TPU v7x, 256 devices: a whole 4x4x8 slice. The times are simulated.
256 devices in a mesh: dp: 4 (over x), space: 64 (over y, z, core).
Axes of the slice: x: 4, y: 4, z: 8, core: 2. Of those that a mesh axis runs over, the one named last changes fastest.
Arguments:
- video_latent: bfloat16 [4, 8, 128, 16, 256], P('dp', None, 'space'), may hold values from -18 to 18
- frame_counts: int32 [4], P('dp'), may hold values from 1 to 8, as said below
- conv_kernel: bfloat16 [27, 256, 256], replicated, may hold values from -0.078125 to 0.078125
- norm_gain: float32 [256], replicated, may hold values from 0.5 to 1.5
- output_grad: bfloat16 [4, 8, 128, 16, 256], P('dp', None, 'space'), may hold values from -6 to 6
Outputs:
- block_output: bfloat16 [4, 8, 128, 16, 256], P('dp', None, 'space')
- input_grad: bfloat16 [4, 8, 128, 16, 256], P('dp', None, 'space')
- kernel_grad: float32 [256, 27, 256], P('space')
- gain_grad: float32 [256], replicated
Inputs may be any that keep to these rules, and one draw needn't show every extreme that they name: `frame_counts`: frames from this count on are padding.
All inputs are finite; a program needn't handle non-finite values.
Results may differ from a plain program's by a relative error of at most 0.0028.
Values may be sent and summed in bfloat16 or wider, within the bound.
No kernel may reach another device: no remote copies, remote signals or barrier semaphores. Data moves between devices by JAX's collectives and lax.ppermute only.
A program may use at most 128 MiB of HBM per device.

v0:
```python
import jax
import jax.numpy as jnp
from jax import lax
from jax.sharding import PartitionSpec as P

GROUPS = 32


EPSILON = 1e-05


def extended(cells, sides, width):
    for axis, dim in sides:
        count = lax.axis_size(axis)
        ends = count - 1
        head = lax.slice_in_dim(cells, 0, width, axis=dim)
        tail = lax.slice_in_dim(cells, cells.shape[dim] - width, cells.shape[dim], axis=dim)
        cells = jnp.concatenate(
            [
                lax.ppermute(tail, axis, [(i, (i + 1) % count) for i in range(ends)]),
                cells,
                lax.ppermute(head, axis, [((i + 1) % count, i) for i in range(ends)]),
            ],
            axis=dim,
        )
    return cells


def tap_products(padded, kernel, frame_slots):
    clip_count = padded.shape[0]
    local_rows = padded.shape[2] - 2
    width_cols = padded.shape[3] - 2
    channels = padded.shape[4]
    running_sum = jnp.zeros(
        (clip_count * frame_slots * local_rows * width_cols, kernel.shape[2]), jnp.float32
    )
    for tap_time in range(3):
        for tap_row in range(3):
            for tap_col in range(3):
                window = padded[
                    :,
                    tap_time : tap_time + frame_slots,
                    tap_row : tap_row + local_rows,
                    tap_col : tap_col + width_cols,
                    :,
                ]
                running_sum = running_sum + jnp.dot(
                    window.reshape(-1, channels),
                    kernel[(tap_time * 3 + tap_row) * 3 + tap_col],
                    preferred_element_type=jnp.float32,
                )
    return running_sum.reshape(clip_count, frame_slots, local_rows, width_cols, kernel.shape[2])


def kernel_terms(padded, grad_slab):
    frame_slots = grad_slab.shape[1]
    local_rows = grad_slab.shape[2]
    width_cols = grad_slab.shape[3]
    grad_rows = grad_slab.reshape(-1, grad_slab.shape[4])
    tap_terms = []
    for tap_time in range(3):
        for tap_row in range(3):
            for tap_col in range(3):
                window = padded[
                    :,
                    tap_time : tap_time + frame_slots,
                    tap_row : tap_row + local_rows,
                    tap_col : tap_col + width_cols,
                    :,
                ]
                tap_terms.append(
                    lax.dot_general(
                        window.reshape(-1, padded.shape[4]),
                        grad_rows,
                        (((0,), (0,)), ((), ())),
                        preferred_element_type=jnp.float32,
                    )
                )
    return jnp.stack(tap_terms, axis=1)


def flip_kernel(kernel):
    channels = kernel.shape[1]
    reversed_taps = kernel.reshape(3, 3, 3, channels, channels)[::-1, ::-1, ::-1]
    return jnp.swapaxes(reversed_taps, 3, 4).reshape(27, channels, channels)


def group_sums(values):
    shape_now = values.shape
    grouped = values.reshape(
        shape_now[0], shape_now[1], shape_now[2], shape_now[3], GROUPS, shape_now[4] // GROUPS
    )
    return jnp.sum(grouped, axis=(2, 3, 5))


def spread_groups(statistic, channels):
    return jnp.repeat(statistic, channels // GROUPS, axis=2)[:, :, None, None, :]


def local(video_latent, frame_counts, conv_kernel, norm_gain, output_grad):
    clip_count, frame_slots, local_rows, width_cols, channels = video_latent.shape
    cell_count = local_rows * lax.axis_size("space") * width_cols * (channels // GROUPS)
    live_mask = (jnp.arange(frame_slots, dtype=jnp.int32)[None, :] < frame_counts[:, None]).astype(
        jnp.float32
    )
    mask_full = live_mask[:, :, None, None, None]
    latent_float = video_latent.astype(jnp.float32)
    group_mean = lax.psum(group_sums(latent_float), "space") / cell_count
    centered = latent_float - spread_groups(group_mean, channels)
    variance = lax.psum(group_sums(centered * centered), "space") / cell_count
    inverse_std = spread_groups(lax.rsqrt(variance + EPSILON), channels)
    normalized = centered * inverse_std
    gated_input = normalized * norm_gain
    activated = jax.nn.silu(gated_input).astype(jnp.bfloat16)
    rows_padded = extended(activated, (("space", 2),), 1)
    padded = jnp.pad(rows_padded, ((0, 0), (2, 0), (0, 0), (1, 1), (0, 0)))
    conv_out = tap_products(padded, conv_kernel, frame_slots)
    block_output = ((latent_float + conv_out) * mask_full).astype(jnp.bfloat16)
    masked_grad = (output_grad.astype(jnp.float32) * mask_full).astype(jnp.bfloat16)
    grad_rows_padded = extended(masked_grad, (("space", 2),), 1)
    grad_padded = jnp.pad(grad_rows_padded, ((0, 0), (0, 2), (0, 0), (1, 1), (0, 0)))
    act_grad = tap_products(grad_padded, flip_kernel(conv_kernel), frame_slots)
    sigmoid_value = jax.nn.sigmoid(gated_input)
    pre_grad = act_grad * sigmoid_value * (1.0 + gated_input * (1.0 - sigmoid_value))
    scaled_grad = pre_grad * norm_gain
    first_back, second_back = lax.psum(
        (group_sums(scaled_grad), group_sums(scaled_grad * normalized)), "space"
    )
    norm_grad = inverse_std * (
        scaled_grad
        - spread_groups(first_back / cell_count, channels)
        - normalized * spread_groups(second_back / cell_count, channels)
    )
    input_grad = (masked_grad.astype(jnp.float32) + norm_grad).astype(jnp.bfloat16)
    gain_grad = lax.psum(jnp.sum(pre_grad * normalized, axis=(0, 1, 2, 3)), ("dp", "space"))
    full_grad = lax.psum(kernel_terms(padded, masked_grad), "dp")
    kernel_grad = lax.psum_scatter(full_grad, "space", scatter_dimension=0, tiled=True)
    return (block_output, input_grad, kernel_grad, gain_grad)


def solution(mesh):
    placed = (
        P("dp", None, "space", None, None),
        P("dp"),
        P(),
        P(),
        P("dp", None, "space", None, None),
    )
    return jax.shard_map(
        local,
        mesh=mesh,
        in_specs=placed,
        out_specs=(
            P("dp", None, "space", None, None),
            P("dp", None, "space", None, None),
            P("space", None, None),
            P(),
        ),
        check_vma=False,
    )
```

profile of v0, /device:TPU:1, one launch (start us, length us, event | category | flops | bytes accessed | tf_op | source)
XLA Modules:
  0.0 776.0 jit_solution(16906532504973755259)
XLA Ops:
  10.2 4.9 collective-permute-start.2
  15.1 2.1 collective-permute-start.3
  18.4 126.8 %psum.42 = f32[1,8,32]{2,1,0:T(8,128)S(1)} all-reduce(f32[1,8,32]{2,1,0:T(8,128)S(1)} %bitcast.729), channel_id=1, replica_groups=mesh['dp'=4,'space'=64] {'space'}, use_global_device_ids=true, to_apply=%region_2.0 | all-reduce | flops 256 | bytes 2048 | tf_op jit(solution)/shard_map/psum | solution.py:108
  146.6 128.0 %psum.43 = f32[1,8,32]{2,1,0:T(8,128)S(1)} all-reduce(f32[1,8,32]{2,1,0:T(8,128)S(1)} %bitcast.730), channel_id=1, replica_groups=mesh['dp'=4,'space'=64] {'space'}, use_global_device_ids=true, to_apply=%region_5.6 | all-reduce | flops 256 | bytes 2048 | tf_op jit(solution)/shard_map/psum | solution.py:110
  274.6 2.2 rev.3
  278.6 1.1 fusion.47
  288.1 126.0 %all-reduce.3 = (f32[1,8,32]{2,1,0:T(8,128)S(1)}, f32[1,8,32]{2,1,0:T(8,128)S(1)}) all-reduce(f32[1,8,32]{2,1,0:T(8,128)S(1)} %bitcast.728, f32[1,8,32]{2,1,0:T(8,128)S(1)} %bitcast.727), channel_id=1, replica_groups=mesh['dp'=4,'space'=64] {'space'}, use_global_device_ids=true, to_apply=%region_11.12 | all-reduce | flops 512 | bytes 4096 | tf_op jit(solution)/shard_map/psum | solution.py:126
  414.6 1.8 fusion.69
  416.4 1.9 collective-permute-start
  418.3 2.4 collective-permute-start.1
  420.8 1.3 dynamic-slice
  422.7 73.7 %psum.47 = f32[256]{0:T(256)} all-reduce(f32[256]{0:T(256)S(1)} %get-tuple-element.4), channel_id=1, replica_groups=mesh['dp'=4,'space'=64] {'dp','space'}, use_global_device_ids=true, to_apply=%region_15.16 | all-reduce | flops 256 | bytes 2048 | tf_op jit(solution)/shard_map/psum | solution.py:135
  496.6 1.9 fusion.33
  499.3 1.6 fusion.214
  525.4 1.9 copy-done
  529.6 1.1 convolution_add_fusion.48
  530.7 1.2 convolution_add_fusion.47
  531.9 1.1 convolution_add_fusion.46
  533.1 1.1 convolution_add_fusion.45
  539.4 181.7 %all-reduce.9.cloned.1.call-done = f32[256,27,256]{2,0,1:T(8,128)} async-done(((f32[256,27,256]{2,0,1:T(8,128)}), f32[256,27,256]{2,0,1:T(8,128)}) %all-reduce.9.cloned.1.call-update) | async-done | bytes 7077904
  721.0 1.6 constant_dynamic-slice_fusion
  722.6 1.7 fusion.73
  724.4 43.2 %all-reduce.7.cloned.1.call-done = f32[4,27,256]{2,0,1:T(4,128)} async-done(((f32[4,27,256]{2,0,1:T(4,128)}), f32[4,27,256]{2,0,1:T(4,128)}) %all-reduce.7.cloned.1.call-update) | async-done | bytes 110608 | tf_op jit(solution)/shard_map/psum | solution.py:136
  767.6 1.5 copy.67
  (179 shorter events, 47.5 us)
Async XLA Ops:
  7.2 713.8 %all-reduce.9.cloned.1.call-start = ((), (), s32[]{:S(2)}) async-start(), calls=%async_computation.1 | async-start | bytes 14155776
  7.9 9.4 %copy-start.29 = (f32[8]{0:T(128)}, f32[8]{0:T(128)S(1)}, u32[]{:S(2)}) copy-start(f32[8]{0:T(128)S(1)} %compare_convert_fusion) | copy-start | bytes 100
  10.2 268.4 %collective-permute-start.2 = (bf16[1,8,1,16,256]{4,3,2,1,0:T(8,128)(2,1)}, bf16[1,8,1,16,256]{4,3,2,1,0:T(8,128)(2,1)}, u32[]{:S(2)}, u32[]{:S(2)}) collective-permute-start(bf16[1,8,1,16,256]{4,3,2,1,0:T(8,128)(2,1)} %get-tuple-element.62), channel_id=1, source_target_pairs={{0,1},{1,2},{2,3},{3,4},{4,5},{5,6},{6,7},{7,8},{8,9},{9,10},{10,1... | collective-permute-start | bytes 196616 | tf_op jit(solution)/shard_map/ppermute | solution.py:20
  15.1 263.5 %collective-permute-start.3 = (bf16[1,8,1,16,256]{4,3,2,1,0:T(8,128)(2,1)}, bf16[1,8,1,16,256]{4,3,2,1,0:T(8,128)(2,1)}, u32[]{:S(2)}, u32[]{:S(2)}) collective-permute-start(bf16[1,8,1,16,256]{4,3,2,1,0:T(8,128)(2,1)} %get-tuple-element.63), channel_id=1, source_target_pairs={{1,0},{2,1},{3,2},{4,3},{5,4},{6,5},{7,6},{8,7},{9,8},{10,9},{11,1... | collective-permute-start | bytes 196616 | tf_op jit(solution)/shard_map/ppermute | solution.py:22
  285.3 2.1 copy-start.1
  285.4 2.1 copy-start.31
  416.4 104.2 %copy-start.5 = (bf16[1,8,2,16,256]{4,3,2,1,0:T(8,128)(2,1)}, bf16[1,8,2,16,256]{4,3,2,1,0:T(8,128)(2,1)S(1)}, u32[]{:S(2)}) copy-start(bf16[1,8,2,16,256]{4,3,2,1,0:T(8,128)(2,1)S(1)} %get-tuple-element.59) | copy-start | bytes 393220
  416.4 80.0 %collective-permute-start = (bf16[1,8,1,16,256]{4,3,2,1,0:T(8,128)(2,1)S(1)}, bf16[1,8,1,16,256]{4,3,2,1,0:T(8,128)(2,1)S(1)}, u32[]{:S(2)}, u32[]{:S(2)}) collective-permute-start(bf16[1,8,1,16,256]{4,3,2,1,0:T(8,128)(2,1)S(1)} %get-tuple-element.66), channel_id=1, source_target_pairs={{0,1},{1,2},{2,3},{3,4},{4,5},{5,6},{6,7},{7,8},{8,9},{9,10},{10,1... | collective-permute-start | bytes 196616 | tf_op jit(solution)/shard_map/ppermute | solution.py:20
  418.3 78.1 %collective-permute-start.1 = (bf16[1,8,1,16,256]{4,3,2,1,0:T(8,128)(2,1)S(1)}, bf16[1,8,1,16,256]{4,3,2,1,0:T(8,128)(2,1)S(1)}, u32[]{:S(2)}, u32[]{:S(2)}) collective-permute-start(bf16[1,8,1,16,256]{4,3,2,1,0:T(8,128)(2,1)S(1)} %get-tuple-element.67), channel_id=1, source_target_pairs={{1,0},{2,1},{3,2},{4,3},{5,4},{6,5},{7,6},{8,7},{9,8},{10,9},{11,1... | collective-permute-start | bytes 196616 | tf_op jit(solution)/shard_map/ppermute | solution.py:22
  498.5 2.5 copy-start.4
  517.8 3.8 copy-start.27
  517.8 5.6 copy-start.25
  525.3 2.0 copy-start
  525.4 242.2 %all-reduce.7.cloned.1.call-start = ((), (), s32[]{:S(2)}) async-start(), calls=%async_computation | async-start | bytes 221184 | tf_op jit(solution)/shard_map/psum | solution.py:136
  525.4 8.8 %copy-start.24 = (bf16[1,8,2,16,256]{4,3,2,1,0:T(8,128)(2,1)S(1)}, bf16[1,8,2,16,256]{4,3,2,1,0:T(8,128)(2,1)}, u32[]{:S(2)}) copy-start(bf16[1,8,2,16,256]{4,3,2,1,0:T(8,128)(2,1)} %get-tuple-element.51) | copy-start | bytes 393220
  525.4 9.0 %copy-start.23 = (bf16[1,8,2,16,256]{4,3,2,1,0:T(8,128)(2,1)S(1)}, bf16[1,8,2,16,256]{4,3,2,1,0:T(8,128)(2,1)}, u32[]{:S(2)}) copy-start(bf16[1,8,2,16,256]{4,3,2,1,0:T(8,128)(2,1)} %get-tuple-element.50) | copy-start | bytes 393220
  525.4 9.2 %copy-start.22 = (bf16[1,8,2,16,256]{4,3,2,1,0:T(8,128)(2,1)S(1)}, bf16[1,8,2,16,256]{4,3,2,1,0:T(8,128)(2,1)}, u32[]{:S(2)}) copy-start(bf16[1,8,2,16,256]{4,3,2,1,0:T(8,128)(2,1)} %get-tuple-element.49) | copy-start | bytes 393220
  525.4 9.4 %copy-start.21 = (bf16[1,8,2,16,256]{4,3,2,1,0:T(8,128)(2,1)S(1)}, bf16[1,8,2,16,256]{4,3,2,1,0:T(8,128)(2,1)}, u32[]{:S(2)}) copy-start(bf16[1,8,2,16,256]{4,3,2,1,0:T(8,128)(2,1)} %get-tuple-element.48) | copy-start | bytes 393220
  528.4 6.7 copy-start.20
  529.6 5.7 copy-start.19
  530.7 4.8 copy-start.14
  531.9 3.8 copy-start.18
  533.1 2.9 copy-start.17
  537.0 185.6 %copy-start.30 = (f32[8]{0:T(128)S(1)}, f32[8]{0:T(128)}, u32[]{:S(2)}) copy-start(f32[8]{0:T(128)} %copy-done.29) | copy-start | bytes 100
  (14 other events, 24.6 us)
Sparse Core Ops, SparseCore 0:
  525.5 195.4 all-reduce.8
  724.0 43.5 all-reduce.6
where the time goes:
time: 778 us; the launch traced here: 776 us
  blocking collectives  455 us (58%)
  waiting for transfers between devices  225 us (29%)
  matrix products  43.6 us (6%)
  between operations  16.4 us (2%)
  local copies, waits for them, and re-layouts  15.7 us (2%)
  starting transfers between devices  11.4 us (1%)
  other arithmetic  9.3 us (1%)
    unnamed x3, waiting for transfers between devices  182 us
    psum x1, blocking collectives, local(): variance = lax.psum(group_sums(centered * centered), 'space') / cell_count  128 us
    psum x1, blocking collectives, local(): group_mean = lax.psum(group_sums(latent_float), 'space') / cell_count  127 us
    psum x1, blocking collectives, local(): lax.psum((group_sums(scaled_grad), group_sums(scaled_grad * normalized)),...  126 us
    psum x1, blocking collectives, local(): lax.psum(jnp.sum(pre_grad * normalized, axis=(0, 1, 2, 3)), ('dp', 'space'))  73.7 us
    psum x1, waiting for transfers between devices, local(): full_grad = lax.psum(kernel_terms(padded, masked_grad), 'dp')  43.2 us
    dot_general x27, matrix products, kernel_terms(): lax.dot_general(window.reshape(-1, padded.shape[4]), grad_rows, (((0,), (...  26.2 us
    dot_general x54, matrix products, tap_products(): jnp.dot(window.reshape(-1, channels), kernel[(tap_time * 3 + tap_row) * 3...  17.4 us
  transfers between devices with their start and end apart: 6, of which 2 were waited for; matrix products, arithmetic and copies ran while one was open for 3% of the time, Pallas kernels for 0%

commit v1 on v0

v1 whole, which is shorter than its diff:
```python
import jax
import jax.numpy as jnp
from jax import lax
from jax.experimental import pallas as pl
from jax.experimental.pallas import tpu as pltpu
from jax.sharding import Mesh
from jax.sharding import PartitionSpec as P

F32 = jnp.float32
BF16 = jnp.bfloat16
NX, NY, NZ, NC = 4, 4, 8, 2
SPACE = NY * NZ * NC
FR, ROWS, COLS, CH = 8, 2, 16, 256
CELLS = ROWS * COLS
GROUPS = 32
GC = CH // GROUPS
ASL = CH // NY
BSL = CH // NC
EPSILON = 1e-05
COUNT = CELLS * SPACE * GC
AROWS = FR // 2 * 3 * COLS
GROWS = FR * ROWS * COLS
HI = lax.Precision.HIGHEST


def hdot(a, b):
    return jnp.dot(a, b, preferred_element_type=F32, precision=HI)


def gather_matrix():
    lane = lax.broadcasted_iota(jnp.int32, (CH, GROUPS), 0)
    group = lax.broadcasted_iota(jnp.int32, (CH, GROUPS), 1)
    return (lane // GC == group).astype(F32)


def spread_matrix():
    group = lax.broadcasted_iota(jnp.int32, (GROUPS, CH), 0)
    lane = lax.broadcasted_iota(jnp.int32, (GROUPS, CH), 1)
    return (lane // GC == group).astype(F32)


def frame_mask(shape, count):
    return lax.broadcasted_iota(jnp.int32, shape, 0) < count


def shifted(cells, k):
    if k == 1:
        return cells
    zero = jnp.zeros(cells.shape[:-2] + (1, cells.shape[-1]), cells.dtype)
    if k == 0:
        return jnp.concatenate([zero, cells[..., :-1, :]], axis=-2)
    return jnp.concatenate([cells[..., 1:, :], zero], axis=-2)


def edges_and_sums(x_ref, g_ref, up_ref, dn_ref, st_ref):
    up_ref[0] = x_ref[:, 0]
    up_ref[1] = g_ref[:, 0]
    dn_ref[0] = x_ref[:, 1]
    dn_ref[1] = g_ref[:, 1]
    xf = x_ref[...].astype(F32).reshape(FR, CELLS, CH)
    gather = gather_matrix()
    mean = hdot(jnp.sum(xf, axis=1), gather) / (CELLS * GC)
    centered = xf - hdot(mean, spread_matrix())[:, None, :]
    squares = hdot(jnp.sum(centered * centered, axis=1), gather)
    both = jnp.concatenate([mean, squares], axis=1)
    st_ref[...] = jnp.broadcast_to(both[None], (SPACE, FR, 2 * GROUPS))


def pack_slices(x_ref, g_ref, hp_ref, hn_ref, c_ref, out_ref):
    upper = c_ref[0] == 0
    own = [x_ref[:, 0], x_ref[:, 1]]
    before, after = hp_ref[0], hn_ref[0]
    rows = [
        jnp.where(upper, before, own[0]),
        jnp.where(upper, own[0], own[1]),
        jnp.where(upper, own[1], after),
    ]
    three = jnp.stack(rows, axis=1).reshape(FR // 2, 2, 3, COLS, CH)
    for y in range(NY):
        part = three[..., y * ASL : (y + 1) * ASL]
        pair = jnp.concatenate([part[:, 0], part[:, 1]], axis=-1).reshape(AROWS, 2 * ASL)
        for c in range(NC):
            out_ref[y * NC + c, :AROWS] = pair
            out_ref[y * NC + c, AROWS:] = g_ref[..., c * BSL : (c + 1) * BSL].reshape(GROWS, BSL)


def backward_conv(g_ref, hp_ref, hn_ref, k_ref, n_ref, out_ref, pad_ref):
    count = n_ref[0]
    rows = [hp_ref[1], g_ref[:, 0], g_ref[:, 1], hn_ref[1]]
    for r in range(4):
        cells = rows[r].astype(F32)
        cells = jnp.where(frame_mask(cells.shape, count), cells, 0.0)
        for k in range(3):
            pad_ref[k, :FR, r] = shifted(cells, k).astype(BF16)
    pad_ref[:, FR:] = jnp.zeros((3, 2, 4, COLS, CH), BF16)
    total = jnp.zeros((FR * CELLS, CH), F32)
    for i in range(3):
        for j in range(3):
            for k in range(3):
                window = pad_ref[2 - k, 2 - i : 2 - i + FR, 2 - j : 4 - j]
                total = total + lax.dot_general(
                    window.reshape(FR * CELLS, CH),
                    k_ref[(i * 3 + j) * 3 + k],
                    (((1,), (1,)), ((), ())),
                    preferred_element_type=F32,
                )
    out_ref[...] = total


def group_terms(st_ref, x_ref, ag_ref, gain_ref, out_ref, sc_ref, mean_ref, inv_ref):
    means = st_ref[:, :, :GROUPS]
    squares = st_ref[:, :, GROUPS:]
    mean = jnp.sum(means, axis=0) / SPACE
    apart = means - mean[None]
    whole = jnp.sum(squares + (CELLS * GC) * (apart * apart), axis=0)
    spread = spread_matrix()
    mean_all = hdot(mean, spread)
    inv_all = hdot(lax.rsqrt(whole / COUNT + EPSILON), spread)
    mean_ref[...] = mean_all
    inv_ref[...] = inv_all
    gain = gain_ref[...][None]
    xf = x_ref[...].astype(F32).reshape(FR, CELLS, CH)
    normalized = (xf - mean_all[:, None, :]) * inv_all[:, None, :]
    gated = normalized * gain
    sig = jax.nn.sigmoid(gated)
    pre = ag_ref[...].reshape(FR, CELLS, CH) * sig * (1.0 + gated * (1.0 - sig))
    scaled = pre * gain
    sc_ref[...] = scaled
    gather = gather_matrix()
    first = hdot(jnp.sum(scaled, axis=1), gather)
    by_channel = jnp.sum(pre * normalized, axis=1)
    second = hdot(by_channel * gain_ref[...], gather)
    gain_part = jnp.sum(by_channel, axis=0, keepdims=True)
    row = lax.broadcasted_iota(jnp.int32, (FR, CH), 0)
    lane = lax.broadcasted_iota(jnp.int32, (FR, CH), 1)
    folded = jnp.where(lane // GROUPS == row, jnp.broadcast_to(gain_part, (FR, CH)), 0.0)
    fold_lane = lax.broadcasted_iota(jnp.int32, (CH, GROUPS), 0)
    fold_at = lax.broadcasted_iota(jnp.int32, (CH, GROUPS), 1)
    folded = hdot(folded, (fold_lane % GROUPS == fold_at).astype(F32))
    everything = jnp.concatenate([first, second, folded], axis=1)
    out_ref[...] = jnp.broadcast_to(everything[None], (SPACE, FR, 3 * GROUPS))


def kernel_part(in_ref, mean_ref, inv_ref, gain_ref, at_ref, out_ref, pad_ref, grad_ref, sum_ref):
    count, y_at, z_at = at_ref[0], at_ref[1], at_ref[2]
    lane = lax.broadcasted_iota(jnp.int32, (CH, 2 * ASL), 0)
    slot = lax.broadcasted_iota(jnp.int32, (CH, 2 * ASL), 1)
    pick = (lane == y_at * ASL + slot % ASL).astype(F32)
    mean2 = hdot(mean_ref[...], pick)
    inv2 = hdot(inv_ref[...], pick)
    gain2 = hdot(gain_ref[...], pick)
    low = lax.broadcasted_iota(jnp.int32, (1, 2 * ASL), 1) < ASL
    lowest = lax.broadcasted_iota(jnp.int32, (3, COLS, 2 * ASL), 2) < ASL
    top = (lax.broadcasted_iota(jnp.int32, (3, COLS, 2 * ASL), 0) == 0) & (z_at == 0)
    bottom = (lax.broadcasted_iota(jnp.int32, (3, COLS, 2 * ASL), 0) == 2) & (z_at == NZ - 1)
    for y in range(NY):
        for c in range(NC):
            before = jnp.zeros((3, COLS, 2 * ASL), F32)
            block = 3 * COLS
            for m in range(FR // 2 + 1):
                if m < FR // 2:
                    raw = in_ref[y * NC + c, m * block : (m + 1) * block].astype(F32)
                    center = jnp.where(low, mean2[2 * m : 2 * m + 1], mean2[2 * m + 1 : 2 * m + 2])
                    scale = jnp.where(low, inv2[2 * m : 2 * m + 1], inv2[2 * m + 1 : 2 * m + 2])
                    gated = (raw - center) * scale * gain2
                    act = (gated * jax.nn.sigmoid(gated)).reshape(3, COLS, 2 * ASL)
                    if y == 0 and c == 0:
                        act = jnp.where(top, 0.0, act)
                    if y == NY - 1 and c == NC - 1:
                        act = jnp.where(bottom, 0.0, act)
                else:
                    act = jnp.zeros((3, COLS, 2 * ASL), F32)
                turned = pltpu.roll(act, ASL, 2)
                odd = jnp.where(lowest, before, turned)
                before = turned
                for k in range(3):
                    if m < FR // 2:
                        pad_ref[k, 2 * m + 2, y, 3 * c : 3 * c + 3] = shifted(act, k).astype(BF16)
                    pad_ref[k, 2 * m + 1, y, 3 * c : 3 * c + 3] = shifted(odd, k).astype(BF16)
            cells = in_ref[y * NC + c, AROWS:].reshape(FR, ROWS, COLS, BSL)
            live = frame_mask(cells.shape, count)
            cells = jnp.where(live, cells.astype(F32), 0.0)
            grad_ref[:, y, 2 * c : 2 * c + 2] = cells
    pad_ref[:, 0] = jnp.zeros((3, NY, 6, COLS, 2 * ASL), BF16)
    turned_grad = grad_ref[...].reshape(FR * NY * 4 * COLS, BSL).T.astype(BF16)
    for j in range(3):
        for k in range(3):
            early = pad_ref[k, 0:FR, :, j : j + 4].reshape(FR * NY * 4 * COLS, 2 * ASL)
            late = pad_ref[k, 2 : 2 + FR, :, j : j + 4].reshape(FR * NY * 4 * COLS, 2 * ASL)
            product = jnp.dot(
                turned_grad,
                jnp.concatenate([early, late], axis=1),
                preferred_element_type=F32,
            ).T
            for i in range(3):
                tap = (i * 3 + j) * 3 + k
                piece = product[i * ASL : (i + 1) * ASL].reshape(NZ, ASL // NZ, BSL)
                sum_ref[:, tap * 8 : tap * 8 + 8] = piece
    out_ref[...] = sum_ref[...].astype(BF16)


def forward_conv(x_ref, hp_ref, hn_ref, mean_ref, inv_ref, gain_ref, k_ref, at_ref, out_ref, pad_ref):
    count, s_at = at_ref[0], at_ref[3]
    rows = [hp_ref[0], x_ref[:, 0], x_ref[:, 1], hn_ref[0]]
    mean = mean_ref[...][:, None, :]
    inv = inv_ref[...][:, None, :]
    gain = gain_ref[...][None]
    for r in range(4):
        gated = (rows[r].astype(F32) - mean) * inv * gain
        act = gated * jax.nn.sigmoid(gated)
        if r == 0:
            act = jnp.where(s_at == 0, 0.0, act)
        if r == 3:
            act = jnp.where(s_at == SPACE - 1, 0.0, act)
        for k in range(3):
            pad_ref[k, 2:, r] = shifted(act, k).astype(BF16)
    pad_ref[:, :2] = jnp.zeros((3, 2, 4, COLS, CH), BF16)
    total = jnp.zeros((FR * CELLS, CH), F32)
    for i in range(3):
        for j in range(3):
            for k in range(3):
                window = pad_ref[k, i : i + FR, j : j + 2]
                total = total + jnp.dot(
                    window.reshape(FR * CELLS, CH),
                    k_ref[(i * 3 + j) * 3 + k],
                    preferred_element_type=F32,
                )
    cells = total.reshape(FR, ROWS, COLS, CH) + x_ref[...].astype(F32)
    out_ref[...] = jnp.where(frame_mask(cells.shape, count), cells, 0.0).astype(BF16)


def finish_input(b_ref, sc_ref, x_ref, g_ref, mean_ref, inv_ref, at_ref, out_ref, gain_ref):
    count = at_ref[0]
    sums = jnp.sum(b_ref[...], axis=0)
    spread = spread_matrix()
    first = hdot(sums[:, :GROUPS] / COUNT, spread)[:, None, :]
    second = hdot(sums[:, GROUPS : 2 * GROUPS] / COUNT, spread)[:, None, :]
    inv = inv_ref[...][:, None, :]
    xf = x_ref[...].astype(F32).reshape(FR, CELLS, CH)
    normalized = (xf - mean_ref[...][:, None, :]) * inv
    norm_grad = inv * (sc_ref[...] - first - normalized * second)
    grad = g_ref[...].astype(F32).reshape(FR, CELLS, CH)
    grad = jnp.where(frame_mask(grad.shape, count), grad, 0.0)
    out_ref[...] = (grad + norm_grad).astype(BF16).reshape(FR, ROWS, COLS, CH)
    fold_at = lax.broadcasted_iota(jnp.int32, (GROUPS, CH), 0)
    fold_lane = lax.broadcasted_iota(jnp.int32, (GROUPS, CH), 1)
    wide = hdot(sums[:, 2 * GROUPS :], (fold_lane % GROUPS == fold_at).astype(F32))
    row = lax.broadcasted_iota(jnp.int32, (FR, CH), 0)
    lane = lax.broadcasted_iota(jnp.int32, (FR, CH), 1)
    gain = jnp.sum(jnp.where(lane // GROUPS == row, wide, 0.0), axis=0, keepdims=True)
    gain_ref[0:1] = gain[:, :BSL]
    gain_ref[1:2] = gain[:, BSL:]


def sum_rows(in_ref, gain_ref, out_ref):
    total = jnp.sum(in_ref[...].astype(F32), axis=0).reshape(27, 8, BSL)
    gain = jnp.concatenate([gain_ref[...], jnp.zeros((2, BSL), F32)], axis=0)
    for x in range(NX):
        for c in range(NC):
            out_ref[x * NC + c, :27] = total[:, 4 * c : 4 * c + 4]
            out_ref[x * NC + c, 27] = gain


def sum_clips(in_ref, kg_ref, gain_ref):
    for c in range(NC):
        total = in_ref[c]
        for x in range(1, NX):
            total = total + in_ref[x * NC + c]
        kg_ref[:, :, c * BSL : (c + 1) * BSL] = total[:27]
        if c == 0:
            gain_ref[:, :BSL] = total[27, 0:1]
            gain_ref[:, BSL:] = total[27, 1:2]


def run(body, outs, args, scratch=(), smem=(), flops=0, out_tuple=True):
    specs = [
        pl.BlockSpec(memory_space=pltpu.SMEM if at in smem else pltpu.VMEM) for at in range(len(args))
    ]
    size = sum(a.size * a.dtype.itemsize for a in args)
    return pl.pallas_call(
        body,
        out_shape=tuple(jax.ShapeDtypeStruct(s, d) for s, d in outs),
        in_specs=specs,
        out_specs=tuple(pl.BlockSpec(memory_space=pltpu.VMEM) for _ in outs),
        scratch_shapes=list(scratch),
        compiler_params=pltpu.CompilerParams(vmem_limit_bytes=44 * 2**20),
        cost_estimate=pl.CostEstimate(flops=flops, bytes_accessed=size, transcendentals=0),
        name=body.__name__,
    )(*args)


def local(video_latent, frame_counts, conv_kernel, norm_gain, output_grad):
    x = video_latent.reshape(FR, ROWS, COLS, CH)
    g = output_grad.reshape(FR, ROWS, COLS, CH)
    gain = norm_gain.reshape(1, CH)
    y_at, z_at, c_at = lax.axis_index("y"), lax.axis_index("z"), lax.axis_index("c")
    s_at = (y_at * NZ + z_at) * NC + c_at
    at = jnp.stack([frame_counts[0], y_at, z_at, s_at]).astype(jnp.int32)
    space = ("y", "z", "c")
    cells = (FR, ROWS, COLS, CH)
    wide = (FR, CH)

    up, dn, stats = run(
        edges_and_sums,
        [((2, FR, COLS, CH), BF16), ((2, FR, COLS, CH), BF16), ((SPACE, FR, 2 * GROUPS), F32)],
        (x, g),
    )
    hp = lax.ppermute(dn, space, [(i, i + 1) for i in range(SPACE - 1)])
    hn = lax.ppermute(up, space, [(i + 1, i) for i in range(SPACE - 1)])
    stats = lax.all_to_all(stats, space, 0, 0)
    (packed,) = run(
        pack_slices,
        [((NY * NC, AROWS + GROWS, BSL), BF16)],
        (x, g, hp, hn, c_at.reshape(1).astype(jnp.int32)),
        smem=(4,),
    )
    packed = lax.all_to_all(packed, ("y", "c"), 0, 0)
    conv_flops = 2 * 27 * FR * CELLS * CH * CH
    padded = pltpu.VMEM((3, FR + 2, 4, COLS, CH), BF16)
    (act_grad,) = run(
        backward_conv,
        [((FR * CELLS, CH), F32)],
        (g, hp, hn, conv_kernel, at),
        scratch=[padded],
        smem=(4,),
        flops=conv_flops,
    )
    terms, scaled, mean, inv = run(
        group_terms,
        [((SPACE, FR, 3 * GROUPS), F32), ((FR, CELLS, CH), F32), (wide, F32), (wide, F32)],
        (stats, x, act_grad, gain),
    )
    terms = lax.all_to_all(terms, space, 0, 0)
    (partial,) = run(
        kernel_part,
        [((NZ, 27 * 8, BSL), BF16)],
        (packed, mean, inv, gain, at),
        scratch=[
            pltpu.VMEM((3, FR + 2, NY, 6, COLS, 2 * ASL), BF16),
            pltpu.VMEM((FR, NY, 4, COLS, BSL), F32),
            pltpu.VMEM((NZ, 27 * 8, BSL), F32),
        ],
        smem=(4,),
        flops=conv_flops,
    )
    partial = lax.all_to_all(partial, "z", 0, 0)
    (block_output,) = run(
        forward_conv,
        [(cells, BF16)],
        (x, hp, hn, mean, inv, gain, conv_kernel, at),
        scratch=[padded],
        smem=(7,),
        flops=conv_flops,
    )
    input_grad, gain_sum = run(
        finish_input,
        [(cells, BF16), ((2, BSL), F32)],
        (terms, scaled, x, g, mean, inv, at),
        smem=(6,),
    )
    (sums,) = run(sum_rows, [((NX * NC, 28, 4, BSL), F32)], (partial, gain_sum))
    sums = lax.all_to_all(sums, ("x", "c"), 0, 0)
    kernel_grad, gain_grad = run(sum_clips, [((27, 4, CH), F32), ((1, CH), F32)], (sums,))
    whole = (1,) + cells
    return (
        block_output.reshape(whole),
        input_grad.reshape(whole),
        jnp.swapaxes(kernel_grad, 0, 1),
        gain_grad.reshape(CH),
    )


def solution(mesh):
    fine = Mesh(mesh.devices.reshape(NX, NY, NZ, NC), ("x", "y", "z", "c"))
    space = ("y", "z", "c")
    cells = P("x", None, space, None, None)
    return jax.shard_map(
        local,
        mesh=fine,
        in_specs=(cells, P("x"), P(), P(), cells),
        out_specs=(cells, cells, P(space, None, None), P()),
        check_vma=False,
    )
```

time: 778 us -> 117 us (0.15)
  blocking collectives: 455 us -> 0 us
  waiting for transfers between devices: 225 us -> 25.2 us
  matrix products: 43.6 us -> 0 us
  starting transfers between devices: 11.4 us -> 42.8 us
  Pallas kernels: 0 us -> 16.1 us
  between operations: 16.4 us -> 1.48 us
  local copies, waits for them, and re-layouts: 15.7 us -> 27.5 us
    psum x4 -> x0, blocking collectives: 455 us -> none  [the longest x1 128 us: local(): variance = lax.psum(group_sums(centered * centered), 'space') / cell_count]
    unnamed x3 -> x0, waiting for transfers between devices: 182 us -> none
    dot_general x81 -> x0, matrix products: 43.6 us -> none  [the longest x27 26.2 us: kernel_terms(): lax.dot_general(window.reshape(-1, padded.shape[4]), grad_rows, (((0,), (...]
    psum x1 -> x0, waiting for transfers between devices: 43.2 us -> none  [local(): full_grad = lax.psum(kernel_terms(padded, masked_grad), 'dp')]
    all_to_all x0 -> x5, starting transfers between devices: none -> 37.3 us  [the longest x1 13.3 us: local(): stats = lax.all_to_all(stats, space, 0, 0)]
    all_to_all x0 -> x5, waiting for transfers between devices: none -> 20.4 us  [the longest x1 10.2 us: local(): partial = lax.all_to_all(partial, 'z', 0, 0)]
    unnamed x67 -> x64, local copies, waits for them, and re-layouts: 7.07 us -> 27 us
    pallas_call x0 -> x9, Pallas kernels: none -> 16.1 us  [run(): pl.pallas_call(body, out_shape=tuple((jax.ShapeDtypeStruct(s, d) for s, d...]
  transfers between devices with their start and end apart: 6 -> 7, of which waited for: 2 -> 5; matrix products, arithmetic and copies ran while one was open for 3% -> 4% of each run, Pallas kernels for 0% -> 11%
where the time goes in v1:
time: 117 us; the launch traced here: 116 us
  starting transfers between devices  42.8 us (37%)
  local copies, waits for them, and re-layouts  27.5 us (24%)
  waiting for transfers between devices  25.2 us (22%)
  Pallas kernels  16.1 us (14%)
  other arithmetic  2.59 us (2%)
  between operations  1.48 us (1%)
    unnamed x64, local copies, waits for them, and re-layouts  27 us
    pallas_call x9, Pallas kernels, run(): pl.pallas_call(body, out_shape=tuple((jax.ShapeDtypeStruct(s, d) for s, d...  16.1 us
    all_to_all x1, starting transfers between devices, local(): stats = lax.all_to_all(stats, space, 0, 0)  13.3 us
    all_to_all x1, waiting for transfers between devices, local(): partial = lax.all_to_all(partial, 'z', 0, 0)  10.2 us
    all_to_all x1, starting transfers between devices, local(): terms = lax.all_to_all(terms, space, 0, 0)  9.92 us
    all_to_all x1, waiting for transfers between devices, local(): terms = lax.all_to_all(terms, space, 0, 0)  6.21 us
    all_to_all x1, starting transfers between devices, local(): packed = lax.all_to_all(packed, ('y', 'c'), 0, 0)  5.13 us
    all_to_all x1, starting transfers between devices, local(): sums = lax.all_to_all(sums, ('x', 'c'), 0, 0)  4.79 us
  transfers between devices with their start and end apart: 7, of which 5 were waited for; matrix products, arithmetic and copies ran while one was open for 4% of the time, Pallas kernels for 11%

profile of v1, /device:TPU:1, one launch (start us, length us, event | category | flops | bytes accessed | tf_op | source)
XLA Modules:
  0.0 115.5 jit_solution(7805093661959042199)
XLA Ops:
  0.7 1.0 copy-done.2
  1.7 1.0 copy-done.7
  5.4 1.8 %reshape.36 = f32[64,1,512]{2,1,0:T(1,128)} reshape(f32[64,8,64]{2,1,0:T(8,128)} %copy-done.16) | data formatting | bytes 262144
  7.2 13.3 %all-to-all-start = ((f32[64,1,512]{2,1,0:T(1,128)}), f32[64,1,512]{2,1,0:T(1,128)}, u32[]{:S(2)}, u32[]{:S(2)}) async-start(f32[64,1,512]{2,1,0:T(1,128)} %reshape.36), calls=%async_computation | async-start | bytes 262144 | tf_op jit(solution)/shard_map/all_to_all | solution.py:310
  20.5 3.5 %collective-permute-start = (bf16[2,8,16,256]{3,2,1,0:T(8,128)(2,1)}, bf16[2,8,16,256]{3,2,1,0:T(8,128)(2,1)}, u32[]{:S(2)}, u32[]{:S(2)}) collective-permute-start(bf16[2,8,16,256]{3,2,1,0:T(8,128)(2,1)} %copy-done.30), channel_id=1, source_target_pairs={{0,1},{1,2},{2,3},{3,4},{4,5},{5,6},{6,7},{7,8},{8,9},{9,10},{10,1... | collective-permute-start | bytes 393224 | tf_op jit(solution)/shard_map/ppermute | solution.py:308
  24.1 1.9 %collective-permute-start.1 = (bf16[2,8,16,256]{3,2,1,0:T(8,128)(2,1)}, bf16[2,8,16,256]{3,2,1,0:T(8,128)(2,1)}, u32[]{:S(2)}, u32[]{:S(2)}) collective-permute-start(bf16[2,8,16,256]{3,2,1,0:T(8,128)(2,1)} %copy-done.29), channel_id=1, source_target_pairs={{1,0},{2,1},{3,2},{4,3},{5,4},{6,5},{7,6},{8,7},{9,8},{10,9},{11,1... | collective-permute-start | bytes 393224 | tf_op jit(solution)/shard_map/ppermute | solution.py:309
  26.6 4.2 %collective-permute-done.1.hn_ref = bf16[2,8,16,256]{3,2,1,0:T(8,128)(2,1)} collective-permute-done((bf16[2,8,16,256]{3,2,1,0:T(8,128)(2,1)}, bf16[2,8,16,256]{3,2,1,0:T(8,128)(2,1)}, u32[]{:S(2)}, u32[]{:S(2)}) %collective-permute-start.1) | collective-permute-done | bytes 131104 | tf_op jit(solution)/shard_map/ppermute | solution.py:309
  32.6 1.2 %pack_slices.1 = bf16[8,448,128]{2,1,0:T(8,128)(2,1)S(1)} custom-call(bf16[8,2,16,256]{3,2,1,0:T(8,128)(2,1)S(1)} %bitcast.12, bf16[8,2,16,256]{3,2,1,0:T(8,128)(2,1)S(1)} %bitcast.17, bf16[2,8,16,256]{3,2,1,0:T(8,128)(2,1)} %collective-permute-done.hp_ref, bf16[2,8,16,256]{3,2,1,0:T(8,128)(2,1)} %collective-permute-done.1.hn_ref, s32[1]{0:T(128)} %bitcast.8.c_ref), custom_call_target="tpu_custom_call" | custom-call | bytes 524292 | tf_op jit(solution)/shard_map/pack_slices/pallas_call | solution.py:280
  34.7 5.1 %all-to-all-start.2 = ((bf16[8,448,128]{2,1,0:T(8,128)(2,1)}), bf16[8,448,128]{2,1,0:T(8,128)(2,1)}, u32[]{:S(2)}, u32[]{:S(2)}) async-start(bf16[8,448,128]{2,1,0:T(8,128)(2,1)} %copy-done.1), calls=%async_computation.2 | async-start | bytes 1835008 | tf_op jit(solution)/shard_map/all_to_all | solution.py:317
  41.5 2.1 %backward_conv.1.ag_ref = f32[256,256]{1,0:T(8,128)S(1)} custom-call(bf16[8,2,16,256]{3,2,1,0:T(8,128)(2,1)S(1)} %bitcast.18, bf16[2,8,16,256]{3,2,1,0:T(8,128)(2,1)} %collective-permute-done.hp_ref, bf16[2,8,16,256]{3,2,1,0:T(8,128)(2,1)} %collective-permute-done.1.hn_ref, bf16[27,256,256]{2,1,0:T(8,128)(2,1)S(1)} %copy-done, s32[4]{0:T(128)S(1)} %pad_add_fusion.n_ref.at_ref), custom_call_target="tpu_custom_call" | custom-call | flops 905969664 | bytes 3932176 | tf_op jit(solution)/shard_map/backward_conv/pallas_call | solution.py:280
  45.3 2.5 %reduce = f32[64,512]{1,0:T(8,128)} reduce(f32[64,1,512]{2,1,0:T(1,128)} %all-to-all-done, f32[]{:T(128)} %broadcast), dimensions={1}, to_apply=%all_to_all.15.reduce_sub_computation | reduce | bytes 262148 | tf_op jit(solution)/shard_map/all_to_all | solution.py:310
  47.8 1.7 %reshape.37.st_ref = f32[64,8,64]{2,1,0:T(8,128)} reshape(f32[64,512]{1,0:T(8,128)} %reduce) | data formatting | bytes 262144
  53.0 1.0 group_terms.1
  55.4 9.9 %all-to-all-start.1 = ((f32[64,8,96]{2,1,0:T(8,128)}), f32[64,8,96]{2,1,0:T(8,128)}, u32[]{:S(2)}, u32[]{:S(2)}) async-start(f32[64,8,96]{2,1,0:T(8,128)} %copy-done.17), calls=%async_computation.1 | async-start | bytes 524288 | tf_op jit(solution)/shard_map/all_to_all | solution.py:333
  66.7 3.6 %kernel_part.1 = bf16[8,216,128]{2,1,0:T(8,128)(2,1)S(1)} custom-call(bf16[8,448,128]{2,1,0:T(8,128)(2,1)} %all-to-all-done.2.in_ref, f32[8,256]{1,0:T(8,128)S(1)} %get-tuple-element.18.mean_ref, f32[8,256]{1,0:T(8,128)S(1)} %get-tuple-element.19.inv_ref, f32[1,256]{1,0:T(1,128)S(1)} %bitcast.21, s32[4]{0:T(128)S(1)} %copy-done.21), custom_call_target="tpu_custom_call" | custom-call | flops 905969664 | bytes 934928 | tf_op jit(solution)/shard_map/kernel_part/pallas_call | solution.py:280
  71.1 6.2 %all-to-all-done.1.b_ref = f32[64,8,96]{2,1,0:T(8,128)} async-done(((f32[64,8,96]{2,1,0:T(8,128)}), f32[64,8,96]{2,1,0:T(8,128)}, u32[]{:S(2)}, u32[]{:S(2)}) %all-to-all-start.1) | async-done | bytes 196640 | tf_op jit(solution)/shard_map/all_to_all | solution.py:333
  77.3 4.1 %all-to-all-start.3 = ((bf16[8,216,128]{2,1,0:T(8,128)(2,1)}), bf16[8,216,128]{2,1,0:T(8,128)(2,1)}, u32[]{:S(2)}, u32[]{:S(2)}) async-start(bf16[8,216,128]{2,1,0:T(8,128)(2,1)} %copy-done.15), calls=%async_computation.3 | async-start | bytes 884736 | tf_op jit(solution)/shard_map/all_to_all | solution.py:346
  84.8 2.0 %finish_input.1 = (bf16[8,2,16,256]{3,2,1,0:T(8,128)(2,1)}, f32[2,128]{1,0:T(2,128)S(1)}) custom-call(f32[64,8,96]{2,1,0:T(8,128)} %all-to-all-done.1.b_ref, f32[8,32,256]{2,1,0:T(8,128)S(1)} %copy-done.19, bf16[8,2,16,256]{3,2,1,0:T(8,128)(2,1)S(1)} %bitcast.14, bf16[8,2,16,256]{3,2,1,0:T(8,128)(2,1)S(1)} %bitcast.19, ...), custom_call_target="tpu_custom_call" | custom-call | bytes 737296 | tf_op jit(solution)/shard_map/finish_input/pallas_call | solution.py:280
  87.4 10.2 %all-to-all-done.3.in_ref = bf16[8,216,128]{2,1,0:T(8,128)(2,1)} async-done(((bf16[8,216,128]{2,1,0:T(8,128)(2,1)}), bf16[8,216,128]{2,1,0:T(8,128)(2,1)}, u32[]{:S(2)}, u32[]{:S(2)}) %all-to-all-start.3) | async-done | bytes 442400 | tf_op jit(solution)/shard_map/all_to_all | solution.py:346
  98.3 1.1 sum_rows.1
  100.1 4.8 %all-to-all-start.4 = ((f32[8,28,4,128]{3,2,1,0:T(4,128)}), f32[8,28,4,128]{3,2,1,0:T(4,128)}, u32[]{:S(2)}, u32[]{:S(2)}) async-start(f32[8,28,4,128]{3,2,1,0:T(4,128)} %copy-done.11), calls=%async_computation.4 | async-start | bytes 917504 | tf_op jit(solution)/shard_map/all_to_all | solution.py:362
  107.2 2.7 %forward_conv.1 = bf16[8,2,16,256]{3,2,1,0:T(8,128)(2,1)} custom-call(bf16[8,2,16,256]{3,2,1,0:T(8,128)(2,1)S(1)} %bitcast.15, bf16[2,8,16,256]{3,2,1,0:T(8,128)(2,1)} %collective-permute-done.hp_ref, bf16[2,8,16,256]{3,2,1,0:T(8,128)(2,1)} %collective-permute-done.1.hn_ref, f32[8,256]{1,0:T(8,128)S(1)} %get-tuple-element.18.mean_ref, ...), custom_call_target="tpu_custom_call" | custom-call | flops 905969664 | bytes 3949584 | tf_op jit(solution)/shard_map/forward_conv/pallas_call | solution.py:280
  109.9 3.9 %all-to-all-done.4.in_ref = f32[8,28,4,128]{3,2,1,0:T(4,128)} async-done(((f32[8,28,4,128]{3,2,1,0:T(4,128)}), f32[8,28,4,128]{3,2,1,0:T(4,128)}, u32[]{:S(2)}, u32[]{:S(2)}) %all-to-all-start.4) | async-done | bytes 458784 | tf_op jit(solution)/shard_map/all_to_all | solution.py:362
  113.8 1.7 %sum_clips.1 = (f32[27,4,256]{2,1,0:T(4,128)}, f32[1,256]{1,0:T(1,128)}) custom-call(f32[8,28,4,128]{3,2,1,0:T(4,128)} %all-to-all-done.4.in_ref), custom_call_target="tpu_custom_call" | custom-call | bytes 458752 | tf_op jit(solution)/shard_map/sum_clips/pallas_call | solution.py:280
  (66 shorter events, 23.3 us)
Async XLA Ops:
  0.6 40.0 %copy-start = (bf16[27,256,256]{2,1,0:T(8,128)(2,1)S(1)}, bf16[27,256,256]{2,1,0:T(8,128)(2,1)}, u32[]{:S(2)}) copy-start(bf16[27,256,256]{2,1,0:T(8,128)(2,1)} %k_ref.3) | copy-start | bytes 10616836
  0.6 1.1 copy-start.2
  1.7 1.0 copy-start.7
  7.2 27.6 %all-to-all-start = ((f32[64,1,512]{2,1,0:T(1,128)}), f32[64,1,512]{2,1,0:T(1,128)}, u32[]{:S(2)}, u32[]{:S(2)}) async-start(f32[64,1,512]{2,1,0:T(1,128)} %reshape.36), calls=%async_computation | async-start | bytes 262144 | tf_op jit(solution)/shard_map/all_to_all | solution.py:310
  20.5 6.0 %collective-permute-start = (bf16[2,8,16,256]{3,2,1,0:T(8,128)(2,1)}, bf16[2,8,16,256]{3,2,1,0:T(8,128)(2,1)}, u32[]{:S(2)}, u32[]{:S(2)}) collective-permute-start(bf16[2,8,16,256]{3,2,1,0:T(8,128)(2,1)} %copy-done.30), channel_id=1, source_target_pairs={{0,1},{1,2},{2,3},{3,4},{4,5},{5,6},{6,7},{7,8},{8,9},{9,10},{10,1... | collective-permute-start | bytes 393224 | tf_op jit(solution)/shard_map/ppermute | solution.py:308
  24.1 6.7 %collective-permute-start.1 = (bf16[2,8,16,256]{3,2,1,0:T(8,128)(2,1)}, bf16[2,8,16,256]{3,2,1,0:T(8,128)(2,1)}, u32[]{:S(2)}, u32[]{:S(2)}) collective-permute-start(bf16[2,8,16,256]{3,2,1,0:T(8,128)(2,1)} %copy-done.29), channel_id=1, source_target_pairs={{1,0},{2,1},{3,2},{4,3},{5,4},{6,5},{7,6},{8,7},{9,8},{10,9},{11,1... | collective-permute-start | bytes 393224 | tf_op jit(solution)/shard_map/ppermute | solution.py:309
  30.8 0.9 copy-start.3
  31.7 0.9 copy-start.8
  33.8 0.9 copy-start.1
  34.7 20.7 %all-to-all-start.2 = ((bf16[8,448,128]{2,1,0:T(8,128)(2,1)}), bf16[8,448,128]{2,1,0:T(8,128)(2,1)}, u32[]{:S(2)}, u32[]{:S(2)}) async-start(bf16[8,448,128]{2,1,0:T(8,128)(2,1)} %copy-done.1), calls=%async_computation.2 | async-start | bytes 1835008 | tf_op jit(solution)/shard_map/all_to_all | solution.py:317
  40.6 0.9 copy-start.9
  49.6 0.9 copy-start.4
  50.5 0.9 copy-start.13
  51.4 0.9 copy-start.14
  54.0 0.7 copy-start.17
  55.4 21.8 %all-to-all-start.1 = ((f32[64,8,96]{2,1,0:T(8,128)}), f32[64,8,96]{2,1,0:T(8,128)}, u32[]{:S(2)}, u32[]{:S(2)}) async-start(f32[64,8,96]{2,1,0:T(8,128)} %copy-done.17), calls=%async_computation.1 | async-start | bytes 524288 | tf_op jit(solution)/shard_map/all_to_all | solution.py:333
  70.3 0.8 copy-start.15
  77.3 20.3 %all-to-all-start.3 = ((bf16[8,216,128]{2,1,0:T(8,128)(2,1)}), bf16[8,216,128]{2,1,0:T(8,128)(2,1)}, u32[]{:S(2)}, u32[]{:S(2)}) async-start(bf16[8,216,128]{2,1,0:T(8,128)(2,1)} %copy-done.15), calls=%async_computation.3 | async-start | bytes 884736 | tf_op jit(solution)/shard_map/all_to_all | solution.py:346
  81.4 0.9 copy-start.5
  82.3 0.9 copy-start.10
  83.2 0.9 copy-start.19
  99.4 0.8 copy-start.11
  100.1 13.7 %all-to-all-start.4 = ((f32[8,28,4,128]{3,2,1,0:T(4,128)}), f32[8,28,4,128]{3,2,1,0:T(4,128)}, u32[]{:S(2)}, u32[]{:S(2)}) async-start(f32[8,28,4,128]{3,2,1,0:T(4,128)} %copy-done.11), calls=%async_computation.4 | async-start | bytes 917504 | tf_op jit(solution)/shard_map/all_to_all | solution.py:362
  104.9 0.9 copy-start.6
  (14 other events, 9.2 us)

commit v2 on v1

v2 whole, which is shorter than its diff:
```python
import jax
import jax.numpy as jnp
from jax import lax
from jax.experimental import pallas as pl
from jax.experimental.pallas import tpu as pltpu
from jax.sharding import Mesh
from jax.sharding import PartitionSpec as P

F32 = jnp.float32
BF16 = jnp.bfloat16
NX, NY, NZ, NC = 4, 4, 8, 2
SPACE = NY * NZ * NC
FR, ROWS, COLS, CH = 8, 2, 16, 256
CELLS = ROWS * COLS
GROUPS = 32
GC = CH // GROUPS
ASL = CH // NY
BSL = CH // NC
EPSILON = 1e-05
COUNT = CELLS * SPACE * GC
AROWS = FR // 2 * 3 * COLS
GROWS = FR * ROWS * COLS
TAPS = 27
PROWS = 112
HI = lax.Precision.HIGHEST


def hdot(a, b):
    return jnp.dot(a, b, preferred_element_type=F32, precision=HI)


def gather_matrix():
    lane = lax.broadcasted_iota(jnp.int32, (CH, GROUPS), 0)
    group = lax.broadcasted_iota(jnp.int32, (CH, GROUPS), 1)
    return (lane // GC == group).astype(F32)


def spread_matrix():
    group = lax.broadcasted_iota(jnp.int32, (GROUPS, CH), 0)
    lane = lax.broadcasted_iota(jnp.int32, (GROUPS, CH), 1)
    return (lane // GC == group).astype(F32)


def shifted(cells, k):
    if k == 1:
        return cells
    zero = jnp.zeros(cells.shape[:-2] + (1, cells.shape[-1]), cells.dtype)
    if k == 0:
        return jnp.concatenate([zero, cells[..., :-1, :]], axis=-2)
    return jnp.concatenate([cells[..., 1:, :], zero], axis=-2)


def edges_and_sums(x_ref, g_ref, n_ref, up_ref, dn_ref, st_ref, live_ref):
    up_ref[0] = x_ref[:, 0]
    up_ref[1] = g_ref[:, 0]
    dn_ref[0] = x_ref[:, 1]
    dn_ref[1] = g_ref[:, 1]
    live_ref[...] = (lax.broadcasted_iota(jnp.int32, (FR, CH), 0) < n_ref[0]).astype(F32)
    xf = x_ref[...].astype(F32).reshape(FR, CELLS, CH)
    gather = gather_matrix()
    mean = hdot(jnp.sum(xf, axis=1), gather) / (CELLS * GC)
    centered = xf - hdot(mean, spread_matrix())[:, None, :]
    squares = hdot(jnp.sum(centered * centered, axis=1), gather)
    st_ref[...] = jnp.concatenate([mean, squares, jnp.zeros((FR, 2 * GROUPS), F32)], axis=1)


def combined(parts, squares, each):
    count = parts.shape[0]
    mean = jnp.sum(parts, axis=0) / count
    apart = parts - mean[None]
    return mean, jnp.sum(squares + each * (apart * apart), axis=0)


def pair_sums(own_ref, other_ref, out_ref):
    both = jnp.stack([own_ref[...], other_ref[...]])
    mean, squares = combined(both[:, :, :GROUPS], both[:, :, GROUPS : 2 * GROUPS], CELLS * GC)
    row = jnp.concatenate([mean, squares, jnp.zeros((FR, 2 * GROUPS), F32)], axis=1)
    out_ref[...] = jnp.broadcast_to(row[None], (NY * NZ, FR, 128))


def pack_slices(x_ref, g_ref, hp_ref, hn_ref, out_ref):
    upper = lax.axis_index("c") == 0
    own = [x_ref[:, 0], x_ref[:, 1]]
    before, after = hp_ref[0], hn_ref[0]
    rows = [
        jnp.where(upper, before, own[0]),
        jnp.where(upper, own[0], own[1]),
        jnp.where(upper, own[1], after),
    ]
    three = jnp.stack(rows, axis=1).reshape(FR // 2, 2, 3, COLS, CH)
    for y in range(NY):
        part = three[..., y * ASL : (y + 1) * ASL]
        pair = jnp.concatenate([part[:, 0], part[:, 1]], axis=-1)
        out_ref[y, :AROWS] = pair.reshape(AROWS, 2 * ASL)
        for c in range(NC):
            at = AROWS + c * GROWS
            out_ref[y, at : at + GROWS] = g_ref[..., c * BSL : (c + 1) * BSL].reshape(GROWS, BSL)


def backward_conv(g_ref, hp_ref, hn_ref, k_ref, live_ref, out_ref, pad_ref):
    live = live_ref[...][:, None, :]
    rows = [hp_ref[1], g_ref[:, 0], g_ref[:, 1], hn_ref[1]]
    for r in range(4):
        cells = rows[r].astype(F32) * live
        for k in range(3):
            pad_ref[k, :FR, r] = shifted(cells, k).astype(BF16)
    pad_ref[:, FR:] = jnp.zeros((3, 2, 4, COLS, CH), BF16)
    total = jnp.zeros((FR * CELLS, CH), F32)
    for i in range(3):
        for j in range(3):
            for k in range(3):
                window = pad_ref[2 - k, 2 - i : 2 - i + FR, 2 - j : 4 - j]
                total = total + lax.dot_general(
                    window.reshape(FR * CELLS, CH),
                    k_ref[(i * 3 + j) * 3 + k],
                    (((1,), (1,)), ((), ())),
                    preferred_element_type=F32,
                )
    out_ref[...] = total


def group_terms(st_ref, x_ref, ag_ref, gain_ref, out_ref, sc_ref, mean_ref, inv_ref):
    mean, whole = combined(
        st_ref[:, :, :GROUPS], st_ref[:, :, GROUPS : 2 * GROUPS], NC * CELLS * GC
    )
    spread = spread_matrix()
    mean_all = hdot(mean, spread)
    inv_all = hdot(lax.rsqrt(whole / COUNT + EPSILON), spread)
    mean_ref[...] = mean_all
    inv_ref[...] = inv_all
    gain = gain_ref[...][None]
    xf = x_ref[...].astype(F32).reshape(FR, CELLS, CH)
    normalized = (xf - mean_all[:, None, :]) * inv_all[:, None, :]
    gated = normalized * gain
    sig = jax.nn.sigmoid(gated)
    pre = ag_ref[...].reshape(FR, CELLS, CH) * sig * (1.0 + gated * (1.0 - sig))
    scaled = pre * gain
    sc_ref[...] = scaled
    gather = gather_matrix()
    first = hdot(jnp.sum(scaled, axis=1), gather)
    by_channel = jnp.sum(pre * normalized, axis=1)
    second = hdot(by_channel * gain_ref[...], gather)
    gain_part = jnp.sum(by_channel, axis=0, keepdims=True)
    row = lax.broadcasted_iota(jnp.int32, (FR, CH), 0)
    lane = lax.broadcasted_iota(jnp.int32, (FR, CH), 1)
    folded = jnp.where(lane // GROUPS == row, jnp.broadcast_to(gain_part, (FR, CH)), 0.0)
    fold_lane = lax.broadcasted_iota(jnp.int32, (CH, GROUPS), 0)
    fold_at = lax.broadcasted_iota(jnp.int32, (CH, GROUPS), 1)
    folded = hdot(folded, (fold_lane % GROUPS == fold_at).astype(F32))
    everything = jnp.concatenate([first, second, folded, jnp.zeros((FR, GROUPS), F32)], axis=1)
    out_ref[...] = jnp.broadcast_to(everything[None], (NY * NC, FR, 128))


def kernel_part(*refs):
    blocks, (mean_h, inv_h, gain_h, live_h, keep_h, give_h) = refs[:8], refs[8:14]
    in_ref, mean_ref, inv_ref, gain_ref, live_ref, out_ref, pad_ref, grad_ref, sum_ref, sem = refs[14:]
    y_at, z_at, c_at = lax.axis_index("y"), lax.axis_index("z"), lax.axis_index("c")
    grads_at = pl.multiple_of(AROWS + c_at * GROWS, 64)
    copies = []
    for n in range(8):
        copies.append(
            pltpu.make_async_copy(blocks[n].at[:AROWS], in_ref.at[n, :AROWS], sem.at[2 * n])
        )
        copies.append(
            pltpu.make_async_copy(
                blocks[n].at[pl.ds(grads_at, GROWS)], in_ref.at[n, AROWS:], sem.at[2 * n + 1]
            )
        )
    for n, (src, dst) in enumerate(
        ((mean_h, mean_ref), (inv_h, inv_ref), (gain_h, gain_ref), (live_h, live_ref))
    ):
        copies.append(pltpu.make_async_copy(src, dst, sem.at[16 + n]))
    for copy in copies:
        copy.start()
    pad_ref[:, 0] = jnp.zeros((3, NY, 6, COLS, 2 * ASL), BF16)
    for copy in copies[16:]:
        copy.wait()
    lane = lax.broadcasted_iota(jnp.int32, (CH, 2 * ASL), 0)
    slot = lax.broadcasted_iota(jnp.int32, (CH, 2 * ASL), 1)
    pick = (lane == y_at * ASL + slot % ASL).astype(F32)
    mean2 = hdot(mean_ref[...], pick)
    inv2 = hdot(inv_ref[...], pick)
    gain2 = hdot(gain_ref[...], pick)
    live = live_ref[:, :BSL][:, None, None, :]
    shape = (3, COLS, 2 * ASL)
    low = lax.broadcasted_iota(jnp.int32, (1, 2 * ASL), 1) < ASL
    lowest = lax.broadcasted_iota(jnp.int32, shape, 2) < ASL
    row = lax.broadcasted_iota(jnp.int32, shape, 0)
    block = 3 * COLS
    for n in range(8):
        copies[2 * n].wait()
        copies[2 * n + 1].wait()
        d = n % 4
        y = lax.rem(y_at + NY - d, NY)
        c = c_at if n < 4 else 1 - c_at
        top = (y == 0) & (z_at == 0) & (c == 0)
        bottom = (y == NY - 1) & (z_at == NZ - 1) & (c == NC - 1)
        edge = jnp.where(top, 0, jnp.where(bottom, 2, 3))
        inside = (row != edge).astype(F32)
        before = jnp.zeros(shape, F32)
        for m in range(FR // 2 + 1):
            if m < FR // 2:
                raw = in_ref[n, m * block : (m + 1) * block].astype(F32)
                center = jnp.where(low, mean2[2 * m : 2 * m + 1], mean2[2 * m + 1 : 2 * m + 2])
                scale = jnp.where(low, inv2[2 * m : 2 * m + 1], inv2[2 * m + 1 : 2 * m + 2])
                gated = (raw - center) * scale * gain2
                act = (gated * jax.nn.sigmoid(gated)).reshape(shape) * inside
            else:
                act = jnp.zeros(shape, F32)
            turned = pltpu.roll(act, ASL, 2)
            odd = jnp.where(lowest, before, turned)
            before = turned
            for k in range(3):
                if m < FR // 2:
                    pad_ref[k, 2 * m + 2, d, pl.ds(3 * c, 3)] = shifted(act, k).astype(BF16)
                pad_ref[k, 2 * m + 1, d, pl.ds(3 * c, 3)] = shifted(odd, k).astype(BF16)
        cells = in_ref[n, AROWS:].astype(F32).reshape(FR, ROWS, COLS, BSL) * live
        grad_ref[:, d, pl.ds(2 * c, 2)] = cells
    turned_grad = grad_ref[...].reshape(FR * NY * 4 * COLS, BSL).T.astype(BF16)
    sum_ref[:, :, 4 * TAPS :] = jnp.zeros((NC, NZ, PROWS - 4 * TAPS, BSL), F32)
    for j in range(3):
        for k in range(3):
            early = pad_ref[k, 0:FR, :, j : j + 4].reshape(FR * NY * 4 * COLS, 2 * ASL)
            late = pad_ref[k, 2 : 2 + FR, :, j : j + 4].reshape(FR * NY * 4 * COLS, 2 * ASL)
            product = jnp.dot(
                turned_grad,
                jnp.concatenate([early, late], axis=1),
                preferred_element_type=F32,
            ).T
            for i in range(3):
                tap = (i * 3 + j) * 3 + k
                piece = product[i * ASL : (i + 1) * ASL].reshape(NZ, ASL // NZ, BSL)
                sum_ref[0, :, tap * 4 : tap * 4 + 4] = piece[:, :4]
                sum_ref[1, :, tap * 4 : tap * 4 + 4] = piece[:, 4:]
    out_ref[...] = sum_ref[...].astype(BF16)
    keep = pltpu.make_async_copy(out_ref.at[c_at], keep_h, sem.at[0])
    give = pltpu.make_async_copy(out_ref.at[1 - c_at], give_h, sem.at[1])
    give.start()
    keep.start()
    give.wait()
    keep.wait()


def merge_parts(keep_ref, got_ref, b_ref, out_ref):
    first = lax.axis_index("c") == 0
    keep, got = keep_ref[...], got_ref[...]
    out_ref[:, :PROWS] = jnp.where(first, keep, got)
    out_ref[:, PROWS : 2 * PROWS] = jnp.where(first, got, keep)
    sums = jnp.sum(b_ref[...], axis=0)
    high = sums.astype(BF16).astype(F32)
    middle = (sums - high).astype(BF16).astype(F32)
    low = sums - high - middle
    terms = jnp.concatenate([high, middle, low, jnp.zeros((FR, 128), F32)], axis=0).astype(BF16)
    out_ref[:, 2 * PROWS :] = jnp.broadcast_to(terms[None], (NZ, 4 * FR, 128))


def sum_rows(in_ref, out_ref, sums_ref):
    total = jnp.sum(in_ref[...].astype(F32), axis=0)
    at = 2 * PROWS
    sums = (total[at + 2 * FR : at + 3 * FR] + total[at + FR : at + 2 * FR]) + total[at : at + FR]
    sums_ref[...] = sums
    fold_at = lax.broadcasted_iota(jnp.int32, (GROUPS, CH), 0)
    fold_lane = lax.broadcasted_iota(jnp.int32, (GROUPS, CH), 1)
    wide = hdot(sums[:, 2 * GROUPS : 3 * GROUPS], (fold_lane % GROUPS == fold_at).astype(F32))
    row = lax.broadcasted_iota(jnp.int32, (FR, CH), 0)
    lane = lax.broadcasted_iota(jnp.int32, (FR, CH), 1)
    gain = jnp.sum(jnp.where(lane // GROUPS == row, wide, 0.0), axis=0, keepdims=True)
    out_ref[:, :BSL] = total[:PROWS]
    out_ref[:, BSL:] = total[PROWS : 2 * PROWS]
    out_ref[4 * TAPS : 4 * TAPS + 1] = gain


def forward_conv(x_ref, hp_ref, hn_ref, mean_ref, inv_ref, gain_ref, k_ref, live_ref, out_ref, pad_ref):
    s_at = (lax.axis_index("y") * NZ + lax.axis_index("z")) * NC + lax.axis_index("c")
    rows = [hp_ref[0], x_ref[:, 0], x_ref[:, 1], hn_ref[0]]
    mean = mean_ref[...][:, None, :]
    inv = inv_ref[...][:, None, :]
    gain = gain_ref[...][None]
    for r in range(4):
        gated = (rows[r].astype(F32) - mean) * inv * gain
        act = gated * jax.nn.sigmoid(gated)
        if r == 0:
            act = jnp.where(s_at == 0, 0.0, act)
        if r == 3:
            act = jnp.where(s_at == SPACE - 1, 0.0, act)
        for k in range(3):
            pad_ref[k, 2:, r] = shifted(act, k).astype(BF16)
    pad_ref[:, :2] = jnp.zeros((3, 2, 4, COLS, CH), BF16)
    total = jnp.zeros((FR * CELLS, CH), F32)
    for i in range(3):
        for j in range(3):
            for k in range(3):
                window = pad_ref[k, i : i + FR, j : j + 2]
                total = total + jnp.dot(
                    window.reshape(FR * CELLS, CH),
                    k_ref[(i * 3 + j) * 3 + k],
                    preferred_element_type=F32,
                )
    cells = total.reshape(FR, CELLS, CH) + x_ref[...].astype(F32).reshape(FR, CELLS, CH)
    cells = cells * live_ref[...][:, None, :]
    out_ref[...] = cells.astype(BF16).reshape(FR, ROWS, COLS, CH)


def finish_input(sums_ref, sc_ref, x_ref, g_ref, mean_ref, inv_ref, live_ref, out_ref):
    sums = sums_ref[...]
    spread = spread_matrix()
    first = hdot(sums[:, :GROUPS] / COUNT, spread)[:, None, :]
    second = hdot(sums[:, GROUPS : 2 * GROUPS] / COUNT, spread)[:, None, :]
    inv = inv_ref[...][:, None, :]
    xf = x_ref[...].astype(F32).reshape(FR, CELLS, CH)
    normalized = (xf - mean_ref[...][:, None, :]) * inv
    norm_grad = inv * (sc_ref[...] - first - normalized * second)
    grad = g_ref[...].astype(F32).reshape(FR, CELLS, CH) * live_ref[...][:, None, :]
    out_ref[...] = (grad + norm_grad).astype(BF16).reshape(FR, ROWS, COLS, CH)


def sum_clips(own_h, one_h, two_h, three_h, kg_h, gain_h, in_ref, kg_ref, gain_ref, sem):
    x_at = lax.axis_index("x")
    copies = []
    for d, src in enumerate((own_h, one_h, two_h, three_h)):
        copies.append(
            pltpu.make_async_copy(src, in_ref.at[lax.rem(x_at + NX - d, NX)], sem.at[d])
        )
    for copy in copies:
        copy.start()
    for copy in copies:
        copy.wait()
    total = ((in_ref[0] + in_ref[1]) + in_ref[2]) + in_ref[3]
    for tap in range(TAPS):
        kg_ref[tap] = total[4 * tap : 4 * tap + 4]
    gain_ref[...] = total[4 * TAPS : 4 * TAPS + 1]
    out = (
        pltpu.make_async_copy(kg_ref, kg_h, sem.at[4]),
        pltpu.make_async_copy(gain_ref, gain_h, sem.at[5]),
    )
    for copy in out:
        copy.start()
    for copy in out:
        copy.wait()


HBM = pl.BlockSpec(memory_space=pltpu.HBM)
VMEM = pl.BlockSpec(memory_space=pltpu.VMEM)
SMEM = pl.BlockSpec(memory_space=pltpu.SMEM)


def shapes(outs):
    return tuple(jax.ShapeDtypeStruct(s, d) for s, d in outs)


def call(body, outs, args, specs, scratch, flops=0, limit=32):
    return pl.pallas_call(
        body,
        out_shape=shapes(outs),
        in_specs=specs,
        out_specs=tuple(HBM for _ in outs),
        scratch_shapes=list(scratch),
        compiler_params=pltpu.CompilerParams(vmem_limit_bytes=limit * 2**20),
        cost_estimate=pl.CostEstimate(flops=flops, bytes_accessed=2**20, transcendentals=0),
        name=body.__name__,
    )(*args)


def run(body, outs, args, scratch=(), stay=(), smem=(), flops=0):
    count, outputs = len(args), len(outs)
    moved = [at for at in range(count) if at not in stay and at not in smem]

    def kernel(*refs):
        ins, targets = list(refs[:count]), refs[count : count + outputs]
        rest = refs[count + outputs :]
        buffers, rest = rest[: len(moved)], rest[len(moved) :]
        results, rest = rest[:outputs], rest[outputs:]
        sem, extra = rest[0], rest[1:]
        copies = [
            pltpu.make_async_copy(ins[at], buffers[n], sem.at[n]) for n, at in enumerate(moved)
        ]
        for copy in copies:
            copy.start()
        for n, at in enumerate(moved):
            ins[at] = buffers[n]
        for copy in copies:
            copy.wait()
        body(*ins, *results, *extra)
        copies = [
            pltpu.make_async_copy(results[n], targets[n], sem.at[len(moved) + n])
            for n in range(outputs)
        ]
        for copy in copies:
            copy.start()
        for copy in copies:
            copy.wait()

    kernel.__name__ = body.__name__
    specs = [VMEM if at in stay else SMEM if at in smem else HBM for at in range(count)]
    buffers = [pltpu.VMEM(args[at].shape, args[at].dtype) for at in moved]
    buffers += [pltpu.VMEM(s, d) for s, d in outs]
    buffers += [pltpu.SemaphoreType.DMA((len(moved) + outputs,))]
    return call(kernel, outs, args, specs, buffers + list(scratch), flops)


def pack_body(x_h, g_h, hp_h, hn_h, out0, out1, out2, out3, x_ref, g_ref, hp_ref, hn_ref, buf, sem):
    pairs = ((x_h, x_ref), (g_h, g_ref), (hp_h, hp_ref), (hn_h, hn_ref))
    copies = [pltpu.make_async_copy(a, b, sem.at[n]) for n, (a, b) in enumerate(pairs)]
    for copy in copies:
        copy.start()
    for copy in copies:
        copy.wait()
    pack_slices(x_ref, g_ref, hp_ref, hn_ref, buf)
    y_at = lax.axis_index("y")
    copies = [
        pltpu.make_async_copy(buf.at[lax.rem(y_at + d, NY)], out, sem.at[4 + d])
        for d, out in enumerate((out0, out1, out2, out3))
    ]
    for copy in copies:
        copy.start()
    for copy in copies:
        copy.wait()


def local(video_latent, frame_counts, conv_kernel, norm_gain, output_grad):
    x = video_latent.reshape(FR, ROWS, COLS, CH)
    g = output_grad.reshape(FR, ROWS, COLS, CH)
    gain = norm_gain.reshape(1, CH)
    space = ("y", "z", "c")
    cells = (FR, ROWS, COLS, CH)
    wide = (FR, CH)
    halo = (2, FR, COLS, CH)
    swap = [(0, 1), (1, 0)]
    dma = pltpu.SemaphoreType.DMA

    up, dn, stats, live = run(
        edges_and_sums,
        [(halo, BF16), (halo, BF16), ((FR, 128), F32), (wide, F32)],
        (x, g, frame_counts),
        smem=(2,),
    )
    other = lax.ppermute(stats, "c", swap)
    hp = lax.ppermute(dn, space, [(i, i + 1) for i in range(SPACE - 1)])
    hn = lax.ppermute(up, space, [(i + 1, i) for i in range(SPACE - 1)])
    (stats,) = run(pair_sums, [((NY * NZ, FR, 128), F32)], (stats, other))
    stats, hp, hn = lax.optimization_barrier((stats, hp, hn))
    stats = lax.all_to_all(stats, ("y", "z"), 0, 0)
    block = (AROWS + NC * GROWS, BSL)
    packed = call(
        pack_body,
        [(block, BF16)] * NY,
        (x, g, hp, hn),
        [HBM] * 4,
        [pltpu.VMEM(cells, BF16)] * 2
        + [pltpu.VMEM(halo, BF16)] * 2
        + [pltpu.VMEM((NY,) + block, BF16), dma((8,))],
    )
    near = [packed[0]] + [
        lax.ppermute(packed[d], "y", [(i, (i + d) % NY) for i in range(NY)]) for d in range(1, NY)
    ]
    far = [lax.ppermute(a, "c", swap) for a in near]
    conv_flops = 16 * TAPS * FR * CELLS * CH * CH
    padded = pltpu.VMEM((3, FR + 2, 4, COLS, CH), BF16)
    (act_grad,) = run(
        backward_conv,
        [((FR * CELLS, CH), F32)],
        (g, hp, hn, conv_kernel, live),
        scratch=[padded],
        stay=(3,),
        flops=conv_flops,
    )
    terms, scaled, mean, inv = run(
        group_terms,
        [((NY * NC, FR, 128), F32), ((FR, CELLS, CH), F32), (wide, F32), (wide, F32)],
        (stats, x, act_grad, gain),
    )
    terms = lax.all_to_all(terms, ("y", "c"), 0, 0)
    part = (NZ, PROWS, BSL)
    keep, give = call(
        kernel_part,
        [(part, BF16)] * 2,
        (*near, *far, mean, inv, gain, live),
        [HBM] * 12,
        [
            pltpu.VMEM((8, AROWS + GROWS, BSL), BF16),
            pltpu.VMEM(wide, F32),
            pltpu.VMEM(wide, F32),
            pltpu.VMEM((1, CH), F32),
            pltpu.VMEM(wide, F32),
            pltpu.VMEM((NC,) + part, BF16),
            pltpu.VMEM((3, FR + 2, NY, 6, COLS, 2 * ASL), BF16),
            pltpu.VMEM((FR, NY, 4, COLS, BSL), F32),
            pltpu.VMEM((NC,) + part, F32),
            dma((20,)),
        ],
        flops=conv_flops,
    )
    got = lax.ppermute(give, "c", swap)
    (merged,) = run(
        merge_parts, [((NZ, 2 * PROWS + 4 * FR, BSL), BF16)], (keep, got, terms)
    )
    merged, late_mean = lax.optimization_barrier((merged, mean))
    merged = lax.all_to_all(merged, "z", 0, 0)
    (block_output,) = run(
        forward_conv,
        [(cells, BF16)],
        (x, hp, hn, late_mean, inv, gain, conv_kernel, live),
        scratch=[padded],
        stay=(6,),
        flops=conv_flops,
    )
    merged, block_output = lax.optimization_barrier((merged, block_output))
    rows, sums = run(sum_rows, [((PROWS, CH), F32), ((FR, 128), F32)], (merged,))
    others = [
        lax.ppermute(rows, "x", [(i, (i + d) % NX) for i in range(NX)]) for d in range(1, NX)
    ]
    (input_grad,) = run(
        finish_input, [(cells, BF16)], (sums, scaled, x, g, mean, inv, live)
    )
    kernel_grad, gain_grad = call(
        sum_clips,
        [((TAPS, 4, CH), F32), ((1, CH), F32)],
        (rows, *others),
        [HBM] * 4,
        [
            pltpu.VMEM((NX, PROWS, CH), F32),
            pltpu.VMEM((TAPS, 4, CH), F32),
            pltpu.VMEM((1, CH), F32),
            dma((6,)),
        ],
    )
    whole = (1,) + cells
    return (
        block_output.reshape(whole),
        input_grad.reshape(whole),
        jnp.swapaxes(kernel_grad, 0, 1),
        gain_grad.reshape(CH),
    )


def solution(mesh):
    fine = Mesh(mesh.devices.reshape(NX, NY, NZ, NC), ("x", "y", "z", "c"))
    space = ("y", "z", "c")
    cells = P("x", None, space, None, None)
    return jax.shard_map(
        local,
        mesh=fine,
        in_specs=(cells, P("x"), P(), P(), cells),
        out_specs=(cells, cells, P(space, None, None), P()),
        check_vma=False,
    )
```

time: 117 us -> 95.1 us (0.81)
  local copies, waits for them, and re-layouts: 27.5 us -> 8.52 us
  starting transfers between devices: 42.8 us -> 31.5 us
  blocking collectives: 0 us -> 7.4 us
  Pallas kernels: 16.1 us -> 19.2 us
  other arithmetic: 2.59 us -> 0 us
  waiting for transfers between devices: 25.2 us -> 26.4 us
    all_to_all x5 -> x2, starting transfers between devices: 37.3 us -> 11.2 us  [the longest x1 7.53 us: local(): stats = lax.all_to_all(stats, ('y', 'z'), 0, 0)]
    unnamed x64 -> x20, local copies, waits for them, and re-layouts: 27 us -> 8.52 us
    ppermute x0 -> x12, starting transfers between devices: none -> 13.4 us  [the longest x3 6.08 us: local(): lax.ppermute(packed[d], 'y', [(i, (i + d) % NY) for i in range(NY)])]
    ppermute x0 -> x12, waiting for transfers between devices: none -> 7.46 us  [the longest x3 6.29 us: local(): lax.ppermute(rows, 'x', [(i, (i + d) % NX) for i in range(NX)])]
    all_to_all x0 -> x1, blocking collectives: none -> 7.4 us  [local(): terms = lax.all_to_all(terms, ('y', 'c'), 0, 0)]
    all_to_all x5 -> x2, waiting for transfers between devices: 20.4 us -> 16.6 us  [the longest x1 13.6 us: local(): merged = lax.all_to_all(merged, 'z', 0, 0)]
    pallas_call x9 -> x11, Pallas kernels: 16.1 us -> 19.2 us  [call(): pl.pallas_call(body, out_shape=shapes(outs), in_specs=specs, out_specs=tu...]
    all_to_all x1 -> x0, other arithmetic: 2.51 us -> none  [local(): stats = lax.all_to_all(stats, space, 0, 0)]
  transfers between devices with their start and end apart: 7 -> 16, of which waited for: 5 -> 6; matrix products, arithmetic and copies ran while one was open for 4% -> 0% of each run, Pallas kernels for 11% -> 8%
where the time goes in v2:
time: 95.1 us; the launch traced here: 94.6 us
  starting transfers between devices  31.5 us (33%)
  waiting for transfers between devices  26.4 us (28%)
  Pallas kernels  19.2 us (20%)
  local copies, waits for them, and re-layouts  8.52 us (9%)
  blocking collectives  7.4 us (8%)
  between operations  1.64 us (2%)
    pallas_call x11, Pallas kernels, call(): pl.pallas_call(body, out_shape=shapes(outs), in_specs=specs, out_specs=tu...  19.2 us
    all_to_all x1, waiting for transfers between devices, local(): merged = lax.all_to_all(merged, 'z', 0, 0)  13.6 us
    unnamed x20, local copies, waits for them, and re-layouts  8.52 us
    all_to_all x1, starting transfers between devices, local(): stats = lax.all_to_all(stats, ('y', 'z'), 0, 0)  7.53 us
    all_to_all x1, blocking collectives, local(): terms = lax.all_to_all(terms, ('y', 'c'), 0, 0)  7.4 us
    ppermute x3, waiting for transfers between devices, local(): lax.ppermute(rows, 'x', [(i, (i + d) % NX) for i in range(NX)])  6.29 us
    ppermute x3, starting transfers between devices, local(): lax.ppermute(packed[d], 'y', [(i, (i + d) % NY) for i in range(NY)])  6.08 us
    ppermute x1, starting transfers between devices, local(): hp = lax.ppermute(dn, space, [(i, i + 1) for i in range(SPACE - 1)])  4.94 us
  transfers between devices with their start and end apart: 16, of which 6 were waited for; matrix products, arithmetic and copies ran while one was open for 0% of the time, Pallas kernels for 8%

profile of v2, /device:TPU:1, one launch (start us, length us, event | category | flops | bytes accessed | tf_op | source)
XLA Modules:
  0.0 94.6 jit_solution(18250235778068285219)
XLA Ops:
  3.1 1.4 %edges_and_sums.1 = (bf16[2,8,16,256]{3,2,1,0:T(8,128)(2,1)S(1)}, bf16[2,8,16,256]{3,2,1,0:T(8,128)(2,1)S(1)}, f32[8,128]{1,0:T(8,128)S(1)}, f32[8,256]{1,0:T(8,128)S(1)}) custom-call(bf16[8,2,16,256]{3,2,1,0:T(8,128)(2,1)S(1)} %bitcast.7, bf16[8,2,16,256]{3,2,1,0:T(8,128)(2,1)S(1)} %bitcast.12, s32[1]{0:T(128)S(6)} %copy.9.refs_2_), custom_call_target="tpu_custom_call" | custom-call | bytes 1048576 | tf_op jit(solution)/shard_map/edges_and_sums/pallas_call | solution.py:352
  4.5 4.9 %collective-permute-start.1 = (bf16[2,8,16,256]{3,2,1,0:T(8,128)(2,1)S(1)}, bf16[2,8,16,256]{3,2,1,0:T(8,128)(2,1)S(1)}, u32[]{:S(2)}, u32[]{:S(2)}) collective-permute-start(bf16[2,8,16,256]{3,2,1,0:T(8,128)(2,1)S(1)} %get-tuple-element.30), channel_id=1, source_target_pairs={{0,1},{1,2},{2,3},{3,4},{4,5},{5,6},{6,7},{7,8},{8,9},{9,10},{10,1... | collective-permute-start | bytes 393224 | tf_op jit(solution)/shard_map/ppermute | solution.py:438
  9.4 1.9 %collective-permute-start.2 = (bf16[2,8,16,256]{3,2,1,0:T(8,128)(2,1)S(1)}, bf16[2,8,16,256]{3,2,1,0:T(8,128)(2,1)S(1)}, u32[]{:S(2)}, u32[]{:S(2)}) collective-permute-start(bf16[2,8,16,256]{3,2,1,0:T(8,128)(2,1)S(1)} %get-tuple-element.31), channel_id=1, source_target_pairs={{1,0},{2,1},{3,2},{4,3},{5,4},{6,5},{7,6},{8,7},{9,8},{10,9},{11,1... | collective-permute-start | bytes 393224 | tf_op jit(solution)/shard_map/ppermute | solution.py:439
  13.4 2.3 %collective-permute-done.2.hn_h.refs_2_ = bf16[2,8,16,256]{3,2,1,0:T(8,128)(2,1)S(1)} collective-permute-done((bf16[2,8,16,256]{3,2,1,0:T(8,128)(2,1)S(1)}, bf16[2,8,16,256]{3,2,1,0:T(8,128)(2,1)S(1)}, u32[]{:S(2)}, u32[]{:S(2)}) %collective-permute-start.2) | collective-permute-done | bytes 131104 | tf_op jit(solution)/shard_map/ppermute | solution.py:439
  17.5 1.9 %pack_body.1 = (bf16[704,128]{1,0:T(8,128)(2,1)S(1)}, bf16[704,128]{1,0:T(8,128)(2,1)S(1)}, bf16[704,128]{1,0:T(8,128)(2,1)S(1)}, bf16[704,128]{1,0:T(8,128)(2,1)S(1)}) custom-call(bf16[8,2,16,256]{3,2,1,0:T(8,128)(2,1)S(1)} %bitcast.8, bf16[8,2,16,256]{3,2,1,0:T(8,128)(2,1)S(1)} %bitcast.13, ...), custom_call_target="tpu_custom_call" | custom-call | bytes 1048576 | tf_op jit(solution)/shard_map/pack_body/pallas_call | solution.py:352
  19.4 2.4 %collective-permute-start.3 = (bf16[704,128]{1,0:T(8,128)(2,1)S(1)}, bf16[704,128]{1,0:T(8,128)(2,1)S(1)}, u32[]{:S(2)}, u32[]{:S(2)}) collective-permute-start(bf16[704,128]{1,0:T(8,128)(2,1)S(1)} %get-tuple-element.35), channel_id=1, source_target_pairs={{0,16},{16,32},{32,48},{48,0},{1,17},{17,33},{33,49},{49,1},{2,18}... | collective-permute-start | bytes 540680 | tf_op jit(solution)/shard_map/ppermute | solution.py:454
  21.8 2.9 %collective-permute-start.4 = (bf16[704,128]{1,0:T(8,128)(2,1)S(1)}, bf16[704,128]{1,0:T(8,128)(2,1)S(1)}, u32[]{:S(2)}, u32[]{:S(2)}) collective-permute-start(bf16[704,128]{1,0:T(8,128)(2,1)S(1)} %get-tuple-element.36), channel_id=1, source_target_pairs={{0,32},{16,48},{32,0},{48,16},{1,33},{17,49},{33,1},{49,17},{2,34}... | collective-permute-start | bytes 540680 | tf_op jit(solution)/shard_map/ppermute | solution.py:454
  25.5 7.5 %all-to-all-start = ((f32[32,8,128]{2,1,0:T(8,128)}), f32[32,8,128]{2,1,0:T(8,128)S(1)}, u32[]{:S(2)}, u32[]{:S(2)}) async-start(f32[32,8,128]{2,1,0:T(8,128)} %pair_sums.1), calls=%async_computation | async-start | bytes 262144 | tf_op jit(solution)/shard_map/all_to_all | solution.py:442
  35.5 2.0 %copy-done.8 = bf16[27,256,256]{2,1,0:T(8,128)(2,1)S(1)} copy-done((bf16[27,256,256]{2,1,0:T(8,128)(2,1)S(1)}, bf16[27,256,256]{2,1,0:T(8,128)(2,1)}, u32[]{:S(2)}) %copy-start.8) | copy-done | bytes 3538968
  37.5 1.7 %backward_conv.1.refs_2_ = f32[256,256]{1,0:T(8,128)S(1)} custom-call(bf16[8,2,16,256]{3,2,1,0:T(8,128)(2,1)S(1)} %bitcast.14, bf16[2,8,16,256]{3,2,1,0:T(8,128)(2,1)S(1)} %collective-permute-done.1.hp_h.refs_1_, bf16[2,8,16,256]{3,2,1,0:T(8,128)(2,1)S(1)} %collective-permute-done.2.hn_h.refs_2_, bf16[27,256,256]{2,1,0:T(8,128)(2,1)S(1)} %copy-done.8, ...), custom_call_target="tpu_custom_call" | custom-call | flops 7247757312 | bytes 1048576 | tf_op jit(solution)/shard_map/backward_conv/pallas_call | solution.py:352
  39.2 3.0 %all-to-all-done.refs_0_ = f32[32,8,128]{2,1,0:T(8,128)S(1)} async-done(((f32[32,8,128]{2,1,0:T(8,128)}), f32[32,8,128]{2,1,0:T(8,128)S(1)}, u32[]{:S(2)}, u32[]{:S(2)}) %all-to-all-start) | async-done | bytes 131104 | tf_op jit(solution)/shard_map/all_to_all | solution.py:442
  42.2 1.4 %group_terms.1 = (f32[8,8,128]{2,1,0:T(8,128)S(1)}, f32[8,32,256]{2,1,0:T(8,128)S(1)}, f32[8,256]{1,0:T(8,128)S(1)}, f32[8,256]{1,0:T(8,128)S(1)}) custom-call(f32[32,8,128]{2,1,0:T(8,128)S(1)} %all-to-all-done.refs_0_, bf16[8,2,16,256]{3,2,1,0:T(8,128)(2,1)S(1)} %bitcast.9, f32[256,256]{1,0:T(8,128)S(1)} %backward_conv.1.refs_2_, f32[1,256]{1,0:T(1,128)S(1)} %bitcast.16), custom_call_target="tpu_custom_call" | custom-call | bytes 1048576 | tf_op jit(solution)/shard_map/group_terms/pallas_call | solution.py:352
  43.6 5.0 %kernel_part.1 = (bf16[8,112,128]{2,1,0:T(8,128)(2,1)S(1)}, bf16[8,112,128]{2,1,0:T(8,128)(2,1)S(1)}) custom-call(bf16[704,128]{1,0:T(8,128)(2,1)S(1)} %get-tuple-element.34.refs_0_, bf16[704,128]{1,0:T(8,128)(2,1)S(1)} %collective-permute-done.3.refs_1_, bf16[704,128]{1,0:T(8,128)(2,1)S(1)} %collective-permute-done.4.refs_2_, ...), custom_call_target="tpu_custom_call" | custom-call | flops 7247757312 | bytes 1048576 | tf_op jit(solution)/shard_map/kernel_part/pallas_call | solution.py:352
  48.6 2.0 %collective-permute-start.10 = (bf16[8,112,128]{2,1,0:T(8,128)(2,1)S(1)}, bf16[8,112,128]{2,1,0:T(8,128)(2,1)S(1)}, u32[]{:S(2)}, u32[]{:S(2)}) collective-permute-start(bf16[8,112,128]{2,1,0:T(8,128)(2,1)S(1)} %get-tuple-element.43), channel_id=1, source_target_pairs={{0,1},{1,0},{2,3},{3,2},{4,5},{5,4},{6,7},{7,6},{8,9},{9,8},{10,11... | collective-permute-start | bytes 688136 | tf_op jit(solution)/shard_map/ppermute | solution.py:493
  50.7 7.4 %all_to_all.15.refs_2_ = f32[8,8,128]{2,1,0:T(8,128)S(1)} all-to-all(f32[8,8,128]{2,1,0:T(8,128)S(1)} %get-tuple-element.44), channel_id=1, replica_groups=mesh['x'=4,'y'=4,'z'=8,'c'=2] {'y','c'}, dimensions={0} | all-to-all | bytes 65536 | tf_op jit(solution)/shard_map/all_to_all | solution.py:472
  58.1 1.5 %merge_parts.1 = bf16[8,256,128]{2,1,0:T(8,128)(2,1)} custom-call(bf16[8,112,128]{2,1,0:T(8,128)(2,1)S(1)} %get-tuple-element.42.refs_0_, bf16[8,112,128]{2,1,0:T(8,128)(2,1)S(1)} %collective-permute-done.10.refs_1_, f32[8,8,128]{2,1,0:T(8,128)S(1)} %all_to_all.15.refs_2_), custom_call_target="tpu_custom_call" | custom-call | bytes 1048576 | tf_op jit(solution)/shard_map/merge_parts/pallas_call | solution.py:352
  59.6 3.7 %all-to-all-start.2 = ((bf16[8,256,128]{2,1,0:T(8,128)(2,1)}), bf16[8,256,128]{2,1,0:T(8,128)(2,1)S(1)}, u32[]{:S(2)}, u32[]{:S(2)}) async-start(bf16[8,256,128]{2,1,0:T(8,128)(2,1)} %merge_parts.1), calls=%async_computation.2 | async-start | bytes 1048576 | tf_op jit(solution)/shard_map/all_to_all | solution.py:498
  63.3 2.0 %copy-done.9 = bf16[27,256,256]{2,1,0:T(8,128)(2,1)S(1)} copy-done((bf16[27,256,256]{2,1,0:T(8,128)(2,1)S(1)}, bf16[27,256,256]{2,1,0:T(8,128)(2,1)}, u32[]{:S(2)}) %copy-start.9) | copy-done | bytes 3538968
  65.3 2.3 %forward_conv.1 = bf16[8,2,16,256]{3,2,1,0:T(8,128)(2,1)} custom-call(bf16[8,2,16,256]{3,2,1,0:T(8,128)(2,1)S(1)} %bitcast.10, bf16[2,8,16,256]{3,2,1,0:T(8,128)(2,1)S(1)} %collective-permute-done.1.hp_h.refs_1_, bf16[2,8,16,256]{3,2,1,0:T(8,128)(2,1)S(1)} %collective-permute-done.2.hn_h.refs_2_, f32[8,256]{1,0:T(8,128)S(1)} %get-tuple-element.46.refs_8_.refs_3_.refs_4_, ...), custom_call_target="tpu_custom_call" | custom-call | flops 7247757312 | bytes 1048576 | tf_op jit(solution)/shard_map/forward_conv/pallas_call | solution.py:352
  67.7 13.6 %all-to-all-done.2.refs_0_ = bf16[8,256,128]{2,1,0:T(8,128)(2,1)S(1)} async-done(((bf16[8,256,128]{2,1,0:T(8,128)(2,1)}), bf16[8,256,128]{2,1,0:T(8,128)(2,1)S(1)}, u32[]{:S(2)}, u32[]{:S(2)}) %all-to-all-start.2) | async-done | bytes 524320 | tf_op jit(solution)/shard_map/all_to_all | solution.py:498
  81.8 2.6 %collective-permute-start.13 = (f32[112,256]{1,0:T(8,128)S(1)}, f32[112,256]{1,0:T(8,128)S(1)}, u32[]{:S(2)}, u32[]{:S(2)}) collective-permute-start(f32[112,256]{1,0:T(8,128)S(1)} %get-tuple-element.51.own_h), channel_id=1, source_target_pairs={{0,192},{64,0},{128,64},{192,128},{1,193},{65,1},{129,65},{193,129... | collective-permute-start | bytes 344072 | tf_op jit(solution)/shard_map/ppermute | solution.py:510
  85.5 1.4 %finish_input.1 = bf16[8,2,16,256]{3,2,1,0:T(8,128)(2,1)} custom-call(f32[8,128]{1,0:T(8,128)S(1)} %get-tuple-element.49.refs_0_, f32[8,32,256]{2,1,0:T(8,128)S(1)} %get-tuple-element.50.refs_1_, bf16[8,2,16,256]{3,2,1,0:T(8,128)(2,1)S(1)} %bitcast.11, bf16[8,2,16,256]{3,2,1,0:T(8,128)(2,1)S(1)} %bitcast.15, ...), custom_call_target="tpu_custom_call" | custom-call | bytes 1048576 | tf_op jit(solution)/shard_map/finish_input/pallas_call | solution.py:352
  86.9 2.7 %collective-permute-done.12.two_h = f32[112,256]{1,0:T(8,128)S(1)} collective-permute-done((f32[112,256]{1,0:T(8,128)S(1)}, f32[112,256]{1,0:T(8,128)S(1)}, u32[]{:S(2)}, u32[]{:S(2)}) %collective-permute-start.12) | collective-permute-done | bytes 114720 | tf_op jit(solution)/shard_map/ppermute | solution.py:510
  89.6 3.6 %collective-permute-done.11.one_h = f32[112,256]{1,0:T(8,128)S(1)} collective-permute-done((f32[112,256]{1,0:T(8,128)S(1)}, f32[112,256]{1,0:T(8,128)S(1)}, u32[]{:S(2)}, u32[]{:S(2)}) %collective-permute-start.11) | collective-permute-done | bytes 114720 | tf_op jit(solution)/shard_map/ppermute | solution.py:510
  (40 shorter events, 11.8 us)
Async XLA Ops:
  1.3 0.9 copy-start
  2.2 0.9 copy-start.3
  4.5 8.9 %collective-permute-start.1 = (bf16[2,8,16,256]{3,2,1,0:T(8,128)(2,1)S(1)}, bf16[2,8,16,256]{3,2,1,0:T(8,128)(2,1)S(1)}, u32[]{:S(2)}, u32[]{:S(2)}) collective-permute-start(bf16[2,8,16,256]{3,2,1,0:T(8,128)(2,1)S(1)} %get-tuple-element.30), channel_id=1, source_target_pairs={{0,1},{1,2},{2,3},{3,4},{4,5},{5,6},{6,7},{7,8},{8,9},{9,10},{10,1... | collective-permute-start | bytes 393224 | tf_op jit(solution)/shard_map/ppermute | solution.py:438
  9.4 6.3 %collective-permute-start.2 = (bf16[2,8,16,256]{3,2,1,0:T(8,128)(2,1)S(1)}, bf16[2,8,16,256]{3,2,1,0:T(8,128)(2,1)S(1)}, u32[]{:S(2)}, u32[]{:S(2)}) collective-permute-start(bf16[2,8,16,256]{3,2,1,0:T(8,128)(2,1)S(1)} %get-tuple-element.31), channel_id=1, source_target_pairs={{1,0},{2,1},{3,2},{4,3},{5,4},{6,5},{7,6},{8,7},{9,8},{10,9},{11,1... | collective-permute-start | bytes 393224 | tf_op jit(solution)/shard_map/ppermute | solution.py:439
  11.3 1.3 %collective-permute-start = (f32[8,128]{1,0:T(8,128)S(1)}, f32[8,128]{1,0:T(8,128)S(1)}, u32[]{:S(2)}, u32[]{:S(2)}) collective-permute-start(f32[8,128]{1,0:T(8,128)S(1)} %get-tuple-element.29.refs_0_), channel_id=1, source_target_pairs={{0,1},{1,0},{2,3},{3,2},{4,5},{5,4},{6,7},{7,6},{8,9},{9,8},{10,11... | collective-permute-start | bytes 12296 | tf_op jit(solution)/shard_map/ppermute | solution.py:437
  15.7 0.9 copy-start.1
  19.4 14.5 %collective-permute-start.3 = (bf16[704,128]{1,0:T(8,128)(2,1)S(1)}, bf16[704,128]{1,0:T(8,128)(2,1)S(1)}, u32[]{:S(2)}, u32[]{:S(2)}) collective-permute-start(bf16[704,128]{1,0:T(8,128)(2,1)S(1)} %get-tuple-element.35), channel_id=1, source_target_pairs={{0,16},{16,32},{32,48},{48,0},{1,17},{17,33},{33,49},{49,1},{2,18}... | collective-permute-start | bytes 540680 | tf_op jit(solution)/shard_map/ppermute | solution.py:454
  21.8 12.3 %collective-permute-start.4 = (bf16[704,128]{1,0:T(8,128)(2,1)S(1)}, bf16[704,128]{1,0:T(8,128)(2,1)S(1)}, u32[]{:S(2)}, u32[]{:S(2)}) collective-permute-start(bf16[704,128]{1,0:T(8,128)(2,1)S(1)} %get-tuple-element.36), channel_id=1, source_target_pairs={{0,32},{16,48},{32,0},{48,16},{1,33},{17,49},{33,1},{49,17},{2,34}... | collective-permute-start | bytes 540680 | tf_op jit(solution)/shard_map/ppermute | solution.py:454
  24.7 9.7 %collective-permute-start.5 = (bf16[704,128]{1,0:T(8,128)(2,1)S(1)}, bf16[704,128]{1,0:T(8,128)(2,1)S(1)}, u32[]{:S(2)}, u32[]{:S(2)}) collective-permute-start(bf16[704,128]{1,0:T(8,128)(2,1)S(1)} %get-tuple-element.37), channel_id=1, source_target_pairs={{0,48},{16,0},{32,16},{48,32},{1,49},{17,1},{33,17},{49,33},{2,50}... | collective-permute-start | bytes 540680 | tf_op jit(solution)/shard_map/ppermute | solution.py:454
  25.5 16.7 %all-to-all-start = ((f32[32,8,128]{2,1,0:T(8,128)}), f32[32,8,128]{2,1,0:T(8,128)S(1)}, u32[]{:S(2)}, u32[]{:S(2)}) async-start(f32[32,8,128]{2,1,0:T(8,128)} %pair_sums.1), calls=%async_computation | async-start | bytes 262144 | tf_op jit(solution)/shard_map/all_to_all | solution.py:442
  33.0 10.5 %collective-permute-start.6 = (bf16[704,128]{1,0:T(8,128)(2,1)S(1)}, bf16[704,128]{1,0:T(8,128)(2,1)S(1)}, u32[]{:S(2)}, u32[]{:S(2)}) collective-permute-start(bf16[704,128]{1,0:T(8,128)(2,1)S(1)} %get-tuple-element.34.refs_0_), channel_id=1, source_target_pairs={{0,1},{1,0},{2,3},{3,2},{4,5},{5,4},{6,7},{7,6},{8,9},{9,8},{10,11... | collective-permute-start | bytes 540680 | tf_op jit(solution)/shard_map/ppermute | solution.py:456
  33.9 9.6 %collective-permute-start.7 = (bf16[704,128]{1,0:T(8,128)(2,1)S(1)}, bf16[704,128]{1,0:T(8,128)(2,1)S(1)}, u32[]{:S(2)}, u32[]{:S(2)}) collective-permute-start(bf16[704,128]{1,0:T(8,128)(2,1)S(1)} %collective-permute-done.3.refs_1_), channel_id=1, source_target_pairs={{0,1},{1,0},{2,3},{3,2},{4,5},{5,4},{6,7},{7,6},{8,9},{9,8},{10,11... | collective-permute-start | bytes 540680 | tf_op jit(solution)/shard_map/ppermute | solution.py:456
  34.0 9.5 %collective-permute-start.8 = (bf16[704,128]{1,0:T(8,128)(2,1)S(1)}, bf16[704,128]{1,0:T(8,128)(2,1)S(1)}, u32[]{:S(2)}, u32[]{:S(2)}) collective-permute-start(bf16[704,128]{1,0:T(8,128)(2,1)S(1)} %collective-permute-done.4.refs_2_), channel_id=1, source_target_pairs={{0,1},{1,0},{2,3},{3,2},{4,5},{5,4},{6,7},{7,6},{8,9},{9,8},{10,11... | collective-permute-start | bytes 540680 | tf_op jit(solution)/shard_map/ppermute | solution.py:456
  34.5 9.1 %collective-permute-start.9 = (bf16[704,128]{1,0:T(8,128)(2,1)S(1)}, bf16[704,128]{1,0:T(8,128)(2,1)S(1)}, u32[]{:S(2)}, u32[]{:S(2)}) collective-permute-start(bf16[704,128]{1,0:T(8,128)(2,1)S(1)} %collective-permute-done.5.refs_3_), channel_id=1, source_target_pairs={{0,1},{1,0},{2,3},{3,2},{4,5},{5,4},{6,7},{7,6},{8,9},{9,8},{10,11... | collective-permute-start | bytes 540680 | tf_op jit(solution)/shard_map/ppermute | solution.py:456
  35.5 2.0 %copy-start.8 = (bf16[27,256,256]{2,1,0:T(8,128)(2,1)S(1)}, bf16[27,256,256]{2,1,0:T(8,128)(2,1)}, u32[]{:S(2)}) copy-start(bf16[27,256,256]{2,1,0:T(8,128)(2,1)} %refs_6_.1) | copy-start | bytes 10616836
  37.5 4.7 %copy-start.2 = (bf16[1,8,2,16,256]{4,3,2,1,0:T(8,128)(2,1)S(1)}, bf16[1,8,2,16,256]{4,3,2,1,0:T(8,128)(2,1)}, u32[]{:S(2)}) copy-start(bf16[1,8,2,16,256]{4,3,2,1,0:T(8,128)(2,1)} %param.5) | copy-start | bytes 393220
  37.5 4.7 %copy-start.7 = (f32[256]{0:T(256)S(1)}, f32[256]{0:T(256)}, u32[]{:S(2)}) copy-start(f32[256]{0:T(256)} %param.8) | copy-start | bytes 3076
  48.6 9.5 %collective-permute-start.10 = (bf16[8,112,128]{2,1,0:T(8,128)(2,1)S(1)}, bf16[8,112,128]{2,1,0:T(8,128)(2,1)S(1)}, u32[]{:S(2)}, u32[]{:S(2)}) collective-permute-start(bf16[8,112,128]{2,1,0:T(8,128)(2,1)S(1)} %get-tuple-element.43), channel_id=1, source_target_pairs={{0,1},{1,0},{2,3},{3,2},{4,5},{5,4},{6,7},{7,6},{8,9},{9,8},{10,11... | collective-permute-start | bytes 688136 | tf_op jit(solution)/shard_map/ppermute | solution.py:493
  59.6 21.6 %all-to-all-start.2 = ((bf16[8,256,128]{2,1,0:T(8,128)(2,1)}), bf16[8,256,128]{2,1,0:T(8,128)(2,1)S(1)}, u32[]{:S(2)}, u32[]{:S(2)}) async-start(bf16[8,256,128]{2,1,0:T(8,128)(2,1)} %merge_parts.1), calls=%async_computation.2 | async-start | bytes 1048576 | tf_op jit(solution)/shard_map/all_to_all | solution.py:498
  63.3 2.0 %copy-start.9 = (bf16[27,256,256]{2,1,0:T(8,128)(2,1)S(1)}, bf16[27,256,256]{2,1,0:T(8,128)(2,1)}, u32[]{:S(2)}) copy-start(bf16[27,256,256]{2,1,0:T(8,128)(2,1)} %refs_6_.1) | copy-start | bytes 10616836
  65.3 20.1 %copy-start.6 = (bf16[1,8,2,16,256]{4,3,2,1,0:T(8,128)(2,1)S(1)}, bf16[1,8,2,16,256]{4,3,2,1,0:T(8,128)(2,1)}, u32[]{:S(2)}) copy-start(bf16[1,8,2,16,256]{4,3,2,1,0:T(8,128)(2,1)} %param.9) | copy-start | bytes 393220
  81.8 5.1 %collective-permute-start.13 = (f32[112,256]{1,0:T(8,128)S(1)}, f32[112,256]{1,0:T(8,128)S(1)}, u32[]{:S(2)}, u32[]{:S(2)}) collective-permute-start(f32[112,256]{1,0:T(8,128)S(1)} %get-tuple-element.51.own_h), channel_id=1, source_target_pairs={{0,192},{64,0},{128,64},{192,128},{1,193},{65,1},{129,65},{193,129... | collective-permute-start | bytes 344072 | tf_op jit(solution)/shard_map/ppermute | solution.py:510
  84.3 5.2 %collective-permute-start.12 = (f32[112,256]{1,0:T(8,128)S(1)}, f32[112,256]{1,0:T(8,128)S(1)}, u32[]{:S(2)}, u32[]{:S(2)}) collective-permute-start(f32[112,256]{1,0:T(8,128)S(1)} %get-tuple-element.51.own_h), channel_id=1, source_target_pairs={{0,128},{64,192},{128,0},{192,64},{1,129},{65,193},{129,1},{193,65... | collective-permute-start | bytes 344072 | tf_op jit(solution)/shard_map/ppermute | solution.py:510
  84.8 8.3 %collective-permute-start.11 = (f32[112,256]{1,0:T(8,128)S(1)}, f32[112,256]{1,0:T(8,128)S(1)}, u32[]{:S(2)}, u32[]{:S(2)}) collective-permute-start(f32[112,256]{1,0:T(8,128)S(1)} %get-tuple-element.51.own_h), channel_id=1, source_target_pairs={{0,64},{64,128},{128,192},{192,0},{1,65},{65,129},{129,193},{193,1... | collective-permute-start | bytes 344072 | tf_op jit(solution)/shard_map/ppermute | solution.py:510
  (2 other events, 1.8 us)

commit v3 on v2

--- a/solution.py
+++ b/solution.py
@@ -97,7 +97,7 @@
             out_ref[y, at : at + GROWS] = g_ref[..., c * BSL : (c + 1) * BSL].reshape(GROWS, BSL)
 
 
-def backward_conv(g_ref, hp_ref, hn_ref, k_ref, live_ref, out_ref, pad_ref):
+def backward_conv(g_ref, hp_ref, hn_ref, k_ref, live_ref, out_ref, pad_ref, held):
     live = live_ref[...][:, None, :]
     rows = [hp_ref[1], g_ref[:, 0], g_ref[:, 1], hn_ref[1]]
     for r in range(4):
@@ -105,6 +105,7 @@
         for k in range(3):
             pad_ref[k, :FR, r] = shifted(cells, k).astype(BF16)
     pad_ref[:, FR:] = jnp.zeros((3, 2, 4, COLS, CH), BF16)
+    held.wait()
     total = jnp.zeros((FR * CELLS, CH), F32)
     for i in range(3):
         for j in range(3):
@@ -270,7 +271,7 @@
     out_ref[4 * TAPS : 4 * TAPS + 1] = gain
 
 
-def forward_conv(x_ref, hp_ref, hn_ref, mean_ref, inv_ref, gain_ref, k_ref, live_ref, out_ref, pad_ref):
+def forward_conv(x_ref, hp_ref, hn_ref, mean_ref, inv_ref, gain_ref, k_ref, live_ref, out_ref, pad_ref, held):
     s_at = (lax.axis_index("y") * NZ + lax.axis_index("z")) * NC + lax.axis_index("c")
     rows = [hp_ref[0], x_ref[:, 0], x_ref[:, 1], hn_ref[0]]
     mean = mean_ref[...][:, None, :]
@@ -286,6 +287,7 @@
         for k in range(3):
             pad_ref[k, 2:, r] = shifted(act, k).astype(BF16)
     pad_ref[:, :2] = jnp.zeros((3, 2, 4, COLS, CH), BF16)
+    held.wait()
     total = jnp.zeros((FR * CELLS, CH), F32)
     for i in range(3):
         for j in range(3):
@@ -340,8 +342,11 @@
 
 
 HBM = pl.BlockSpec(memory_space=pltpu.HBM)
-VMEM = pl.BlockSpec(memory_space=pltpu.VMEM)
 SMEM = pl.BlockSpec(memory_space=pltpu.SMEM)
+
+
+def stay_out(array):
+    return pltpu.with_memory_space_constraint(array, pltpu.HBM)
 
 
 def shapes(outs):
@@ -361,9 +366,9 @@
     )(*args)
 
 
-def run(body, outs, args, scratch=(), stay=(), smem=(), flops=0):
+def run(body, outs, args, scratch=(), late=None, smem=(), flops=0):
     count, outputs = len(args), len(outs)
-    moved = [at for at in range(count) if at not in stay and at not in smem]
+    moved = [at for at in range(count) if at not in smem]
 
     def kernel(*refs):
         ins, targets = list(refs[:count]), refs[count : count + outputs]
@@ -378,9 +383,13 @@
             copy.start()
         for n, at in enumerate(moved):
             ins[at] = buffers[n]
+        held = copies.pop(moved.index(late)) if late is not None else None
         for copy in copies:
             copy.wait()
-        body(*ins, *results, *extra)
+        if held is None:
+            body(*ins, *results, *extra)
+        else:
+            body(*ins, *results, *extra, held)
         copies = [
             pltpu.make_async_copy(results[n], targets[n], sem.at[len(moved) + n])
             for n in range(outputs)
@@ -391,7 +400,7 @@
             copy.wait()
 
     kernel.__name__ = body.__name__
-    specs = [VMEM if at in stay else SMEM if at in smem else HBM for at in range(count)]
+    specs = [SMEM if at in smem else HBM for at in range(count)]
     buffers = [pltpu.VMEM(args[at].shape, args[at].dtype) for at in moved]
     buffers += [pltpu.VMEM(s, d) for s, d in outs]
     buffers += [pltpu.SemaphoreType.DMA((len(moved) + outputs,))]
@@ -418,9 +427,10 @@
 
 
 def local(video_latent, frame_counts, conv_kernel, norm_gain, output_grad):
-    x = video_latent.reshape(FR, ROWS, COLS, CH)
-    g = output_grad.reshape(FR, ROWS, COLS, CH)
-    gain = norm_gain.reshape(1, CH)
+    x = stay_out(video_latent.reshape(FR, ROWS, COLS, CH))
+    g = stay_out(output_grad.reshape(FR, ROWS, COLS, CH))
+    gain = stay_out(norm_gain.reshape(1, CH))
+    conv_kernel = stay_out(conv_kernel)
     space = ("y", "z", "c")
     cells = (FR, ROWS, COLS, CH)
     wide = (FR, CH)
@@ -461,8 +471,8 @@
         [((FR * CELLS, CH), F32)],
         (g, hp, hn, conv_kernel, live),
         scratch=[padded],
-        stay=(3,),
-        flops=conv_flops,
+        late=3,
+        flops=0,
     )
     terms, scaled, mean, inv = run(
         group_terms,
@@ -501,7 +511,7 @@
         [(cells, BF16)],
         (x, hp, hn, late_mean, inv, gain, conv_kernel, live),
         scratch=[padded],
-        stay=(6,),
+        late=6,
         flops=conv_flops,
     )
     merged, block_output = lax.optimization_barrier((merged, block_output))

time: 95.1 us -> 90.5 us (0.952)
  local copies, waits for them, and re-layouts: 8.52 us -> 0 us
  Pallas kernels: 19.2 us -> 25.8 us
  waiting for transfers between devices: 26.4 us -> 23 us
    unnamed x20 -> x0, local copies, waits for them, and re-layouts: 8.52 us -> none
    pallas_call x11, Pallas kernels: 19.2 us -> 25.8 us  [call(): pl.pallas_call(body, out_shape=shapes(outs), in_specs=specs, out_specs=tu...]
    ppermute x3, waiting for transfers between devices: 6.29 us -> 3.21 us  [local(): lax.ppermute(rows, 'x', [(i, (i + d) % NX) for i in range(NX)])]
    all_to_all x1, waiting for transfers between devices: 13.6 us -> 12.3 us  [local(): merged = lax.all_to_all(merged, 'z', 0, 0)]
    all_to_all x1, waiting for transfers between devices: 3.01 us -> 4.09 us  [local(): stats = lax.all_to_all(stats, ('y', 'z'), 0, 0)]
  transfers between devices with their start and end apart: 16 -> 16, of which waited for: 6 -> 6; matrix products, arithmetic and copies ran while one was open for 0% -> 0% of each run, Pallas kernels for 8% -> 14%
where the time goes in v3:
time: 90.5 us; the launch traced here: 89.4 us
  starting transfers between devices  31.5 us (35%)
  Pallas kernels  25.8 us (29%)
  waiting for transfers between devices  23 us (25%)
  blocking collectives  7.4 us (8%)
  between operations  1.61 us (2%)
    pallas_call x11, Pallas kernels, call(): pl.pallas_call(body, out_shape=shapes(outs), in_specs=specs, out_specs=tu...  25.8 us
    all_to_all x1, waiting for transfers between devices, local(): merged = lax.all_to_all(merged, 'z', 0, 0)  12.3 us
    all_to_all x1, starting transfers between devices, local(): stats = lax.all_to_all(stats, ('y', 'z'), 0, 0)  7.52 us
    all_to_all x1, blocking collectives, local(): terms = lax.all_to_all(terms, ('y', 'c'), 0, 0)  7.4 us
    ppermute x3, starting transfers between devices, local(): lax.ppermute(packed[d], 'y', [(i, (i + d) % NY) for i in range(NY)])  6.08 us
    ppermute x1, starting transfers between devices, local(): hp = lax.ppermute(dn, space, [(i, i + 1) for i in range(SPACE - 1)])  4.94 us
    all_to_all x1, waiting for transfers between devices, local(): stats = lax.all_to_all(stats, ('y', 'z'), 0, 0)  4.09 us
    all_to_all x1, starting transfers between devices, local(): merged = lax.all_to_all(merged, 'z', 0, 0)  3.68 us
  transfers between devices with their start and end apart: 16, of which 6 were waited for; matrix products, arithmetic and copies ran while one was open for 0% of the time, Pallas kernels for 14%

profile of v3, /device:TPU:1, one launch (start us, length us, event | category | flops | bytes accessed | tf_op | source)
XLA Modules:
  0.0 89.4 jit_solution(17125473243627026313)
XLA Ops:
  1.3 2.0 %edges_and_sums.1 = (bf16[2,8,16,256]{3,2,1,0:T(8,128)(2,1)S(1)}, bf16[2,8,16,256]{3,2,1,0:T(8,128)(2,1)S(1)}, f32[8,128]{1,0:T(8,128)S(1)}, f32[8,256]{1,0:T(8,128)S(1)}) custom-call(bf16[8,2,16,256]{3,2,1,0:T(8,128)(2,1)} %bitcast.11, bf16[8,2,16,256]{3,2,1,0:T(8,128)(2,1)} %bitcast.7, s32[1]{0:T(128)S(6)} %copy.9.refs_2_), custom_call_target="tpu_custom_call" | custom-call | bytes 1048576 | tf_op jit(solution)/shard_map/edges_and_sums/pallas_call | solution.py:357
  3.3 4.9 %collective-permute-start.1 = (bf16[2,8,16,256]{3,2,1,0:T(8,128)(2,1)S(1)}, bf16[2,8,16,256]{3,2,1,0:T(8,128)(2,1)S(1)}, u32[]{:S(2)}, u32[]{:S(2)}) collective-permute-start(bf16[2,8,16,256]{3,2,1,0:T(8,128)(2,1)S(1)} %get-tuple-element.30), channel_id=1, source_target_pairs={{0,1},{1,2},{2,3},{3,4},{4,5},{5,6},{6,7},{7,8},{8,9},{9,10},{10,1... | collective-permute-start | bytes 393224 | tf_op jit(solution)/shard_map/ppermute | solution.py:448
  8.3 1.9 %collective-permute-start.2 = (bf16[2,8,16,256]{3,2,1,0:T(8,128)(2,1)S(1)}, bf16[2,8,16,256]{3,2,1,0:T(8,128)(2,1)S(1)}, u32[]{:S(2)}, u32[]{:S(2)}) collective-permute-start(bf16[2,8,16,256]{3,2,1,0:T(8,128)(2,1)S(1)} %get-tuple-element.31), channel_id=1, source_target_pairs={{1,0},{2,1},{3,2},{4,3},{5,4},{6,5},{7,6},{8,7},{9,8},{10,9},{11,1... | collective-permute-start | bytes 393224 | tf_op jit(solution)/shard_map/ppermute | solution.py:449
  10.3 1.2 %collective-permute-done.refs_1_ = f32[8,128]{1,0:T(8,128)S(1)} collective-permute-done((f32[8,128]{1,0:T(8,128)S(1)}, f32[8,128]{1,0:T(8,128)S(1)}, u32[]{:S(2)}, u32[]{:S(2)}) %collective-permute-start) | collective-permute-done | bytes 4128 | tf_op jit(solution)/shard_map/ppermute | solution.py:447
  12.2 2.3 %collective-permute-done.2.hn_h.refs_2_ = bf16[2,8,16,256]{3,2,1,0:T(8,128)(2,1)S(1)} collective-permute-done((bf16[2,8,16,256]{3,2,1,0:T(8,128)(2,1)S(1)}, bf16[2,8,16,256]{3,2,1,0:T(8,128)(2,1)S(1)}, u32[]{:S(2)}, u32[]{:S(2)}) %collective-permute-start.2) | collective-permute-done | bytes 131104 | tf_op jit(solution)/shard_map/ppermute | solution.py:449
  14.5 2.2 %pack_body.1 = (bf16[704,128]{1,0:T(8,128)(2,1)S(1)}, bf16[704,128]{1,0:T(8,128)(2,1)S(1)}, bf16[704,128]{1,0:T(8,128)(2,1)S(1)}, bf16[704,128]{1,0:T(8,128)(2,1)S(1)}) custom-call(bf16[8,2,16,256]{3,2,1,0:T(8,128)(2,1)} %bitcast.12, bf16[8,2,16,256]{3,2,1,0:T(8,128)(2,1)} %bitcast.8, bf16[2,8,16,256]{3,2,1,0:T(8,128)(2,1)S(1)} %collective-permute-done.1.hp_h.refs_1_, ...), custom_call_target="tpu_custom_call" | custom-call | bytes 1048576 | tf_op jit(solution)/shard_map/pack_body/pallas_call | solution.py:357
  16.8 2.4 %collective-permute-start.3 = (bf16[704,128]{1,0:T(8,128)(2,1)S(1)}, bf16[704,128]{1,0:T(8,128)(2,1)S(1)}, u32[]{:S(2)}, u32[]{:S(2)}) collective-permute-start(bf16[704,128]{1,0:T(8,128)(2,1)S(1)} %get-tuple-element.35), channel_id=1, source_target_pairs={{0,16},{16,32},{32,48},{48,0},{1,17},{17,33},{33,49},{49,1},{2,18}... | collective-permute-start | bytes 540680 | tf_op jit(solution)/shard_map/ppermute | solution.py:464
  19.2 2.9 %collective-permute-start.4 = (bf16[704,128]{1,0:T(8,128)(2,1)S(1)}, bf16[704,128]{1,0:T(8,128)(2,1)S(1)}, u32[]{:S(2)}, u32[]{:S(2)}) collective-permute-start(bf16[704,128]{1,0:T(8,128)(2,1)S(1)} %get-tuple-element.36), channel_id=1, source_target_pairs={{0,32},{16,48},{32,0},{48,16},{1,33},{17,49},{33,1},{49,17},{2,34}... | collective-permute-start | bytes 540680 | tf_op jit(solution)/shard_map/ppermute | solution.py:464
  22.9 7.5 %all-to-all-start = ((f32[32,8,128]{2,1,0:T(8,128)}), f32[32,8,128]{2,1,0:T(8,128)S(1)}, u32[]{:S(2)}, u32[]{:S(2)}) async-start(f32[32,8,128]{2,1,0:T(8,128)} %pair_sums.1), calls=%async_computation | async-start | bytes 262144 | tf_op jit(solution)/shard_map/all_to_all | solution.py:452
  31.9 3.5 %backward_conv.1.refs_2_ = f32[256,256]{1,0:T(8,128)S(1)} custom-call(bf16[8,2,16,256]{3,2,1,0:T(8,128)(2,1)} %bitcast.9, bf16[2,8,16,256]{3,2,1,0:T(8,128)(2,1)S(1)} %collective-permute-done.1.hp_h.refs_1_, bf16[2,8,16,256]{3,2,1,0:T(8,128)(2,1)S(1)} %collective-permute-done.2.hn_h.refs_2_, bf16[27,256,256]{2,1,0:T(8,128)(2,1)} %refs_6_.1, ...), custom_call_target="tpu_custom_call" | custom-call | bytes 1048576 | tf_op jit(solution)/shard_map/backward_conv/pallas_call | solution.py:357
  35.4 4.1 %all-to-all-done.refs_0_ = f32[32,8,128]{2,1,0:T(8,128)S(1)} async-done(((f32[32,8,128]{2,1,0:T(8,128)}), f32[32,8,128]{2,1,0:T(8,128)S(1)}, u32[]{:S(2)}, u32[]{:S(2)}) %all-to-all-start) | async-done | bytes 131104 | tf_op jit(solution)/shard_map/all_to_all | solution.py:452
  39.5 2.1 %group_terms.1 = (f32[8,8,128]{2,1,0:T(8,128)S(1)}, f32[8,32,256]{2,1,0:T(8,128)S(1)}, f32[8,256]{1,0:T(8,128)S(1)}, f32[8,256]{1,0:T(8,128)S(1)}) custom-call(f32[32,8,128]{2,1,0:T(8,128)S(1)} %all-to-all-done.refs_0_, bf16[8,2,16,256]{3,2,1,0:T(8,128)(2,1)} %bitcast.13, f32[256,256]{1,0:T(8,128)S(1)} %backward_conv.1.refs_2_, f32[1,256]{1,0:T(1,128)} %bitcast.17), custom_call_target="tpu_custom_call" | custom-call | bytes 1048576 | tf_op jit(solution)/shard_map/group_terms/pallas_call | solution.py:357
  41.7 5.6 %kernel_part.1 = (bf16[8,112,128]{2,1,0:T(8,128)(2,1)S(1)}, bf16[8,112,128]{2,1,0:T(8,128)(2,1)S(1)}) custom-call(bf16[704,128]{1,0:T(8,128)(2,1)S(1)} %get-tuple-element.34.refs_0_, bf16[704,128]{1,0:T(8,128)(2,1)S(1)} %collective-permute-done.3.refs_1_, bf16[704,128]{1,0:T(8,128)(2,1)S(1)} %collective-permute-done.4.refs_2_, ...), custom_call_target="tpu_custom_call" | custom-call | flops 7247757312 | bytes 1048576 | tf_op jit(solution)/shard_map/kernel_part/pallas_call | solution.py:357
  47.3 2.1 %collective-permute-start.10 = (bf16[8,112,128]{2,1,0:T(8,128)(2,1)S(1)}, bf16[8,112,128]{2,1,0:T(8,128)(2,1)S(1)}, u32[]{:S(2)}, u32[]{:S(2)}) collective-permute-start(bf16[8,112,128]{2,1,0:T(8,128)(2,1)S(1)} %get-tuple-element.43), channel_id=1, source_target_pairs={{0,1},{1,0},{2,3},{3,2},{4,5},{5,4},{6,7},{7,6},{8,9},{9,8},{10,11... | collective-permute-start | bytes 688136 | tf_op jit(solution)/shard_map/ppermute | solution.py:503
  49.4 7.4 %all_to_all.15.refs_2_ = f32[8,8,128]{2,1,0:T(8,128)S(1)} all-to-all(f32[8,8,128]{2,1,0:T(8,128)S(1)} %get-tuple-element.44), channel_id=1, replica_groups=mesh['x'=4,'y'=4,'z'=8,'c'=2] {'y','c'}, dimensions={0} | all-to-all | bytes 65536 | tf_op jit(solution)/shard_map/all_to_all | solution.py:482
  56.8 1.5 %merge_parts.1 = bf16[8,256,128]{2,1,0:T(8,128)(2,1)} custom-call(bf16[8,112,128]{2,1,0:T(8,128)(2,1)S(1)} %get-tuple-element.42.refs_0_, bf16[8,112,128]{2,1,0:T(8,128)(2,1)S(1)} %collective-permute-done.10.refs_1_, f32[8,8,128]{2,1,0:T(8,128)S(1)} %all_to_all.15.refs_2_), custom_call_target="tpu_custom_call" | custom-call | bytes 1048576 | tf_op jit(solution)/shard_map/merge_parts/pallas_call | solution.py:357
  58.3 3.7 %all-to-all-start.2 = ((bf16[8,256,128]{2,1,0:T(8,128)(2,1)}), bf16[8,256,128]{2,1,0:T(8,128)(2,1)S(1)}, u32[]{:S(2)}, u32[]{:S(2)}) async-start(bf16[8,256,128]{2,1,0:T(8,128)(2,1)} %merge_parts.1), calls=%async_computation.2 | async-start | bytes 1048576 | tf_op jit(solution)/shard_map/all_to_all | solution.py:508
  62.0 4.2 %forward_conv.1 = bf16[8,2,16,256]{3,2,1,0:T(8,128)(2,1)} custom-call(bf16[8,2,16,256]{3,2,1,0:T(8,128)(2,1)} %bitcast.14, bf16[2,8,16,256]{3,2,1,0:T(8,128)(2,1)S(1)} %collective-permute-done.1.hp_h.refs_1_, bf16[2,8,16,256]{3,2,1,0:T(8,128)(2,1)S(1)} %collective-permute-done.2.hn_h.refs_2_, f32[8,256]{1,0:T(8,128)S(1)} %get-tuple-element.46.refs_8_.refs_3_.refs_4_, ...), custom_call_target="tpu_custom_call" | custom-call | flops 7247757312 | bytes 1048576 | tf_op jit(solution)/shard_map/forward_conv/pallas_call | solution.py:357
  66.2 12.3 %all-to-all-done.2.refs_0_ = bf16[8,256,128]{2,1,0:T(8,128)(2,1)S(1)} async-done(((bf16[8,256,128]{2,1,0:T(8,128)(2,1)}), bf16[8,256,128]{2,1,0:T(8,128)(2,1)S(1)}, u32[]{:S(2)}, u32[]{:S(2)}) %all-to-all-start.2) | async-done | bytes 524320 | tf_op jit(solution)/shard_map/all_to_all | solution.py:508
  79.0 2.6 %collective-permute-start.13 = (f32[112,256]{1,0:T(8,128)S(1)}, f32[112,256]{1,0:T(8,128)S(1)}, u32[]{:S(2)}, u32[]{:S(2)}) collective-permute-start(f32[112,256]{1,0:T(8,128)S(1)} %get-tuple-element.51.own_h), channel_id=1, source_target_pairs={{0,192},{64,0},{128,64},{192,128},{1,193},{65,1},{129,65},{193,129... | collective-permute-start | bytes 344072 | tf_op jit(solution)/shard_map/ppermute | solution.py:520
  82.7 2.0 %finish_input.1 = bf16[8,2,16,256]{3,2,1,0:T(8,128)(2,1)} custom-call(f32[8,128]{1,0:T(8,128)S(1)} %get-tuple-element.49.refs_0_, f32[8,32,256]{2,1,0:T(8,128)S(1)} %get-tuple-element.50.refs_1_, bf16[8,2,16,256]{3,2,1,0:T(8,128)(2,1)} %bitcast.15, bf16[8,2,16,256]{3,2,1,0:T(8,128)(2,1)} %bitcast.10, f32[8,256]{1,0:T(8,128)S(1)} %get-tuple-element.46.refs_8_.refs_3_.refs_4_, ...), custom_call_target="tpu_custom_call" | custom-call | bytes 1048576 | tf_op jit(solution)/shard_map/finish_input/pallas_call | solution.py:357
  84.7 2.1 %collective-permute-done.12.two_h = f32[112,256]{1,0:T(8,128)S(1)} collective-permute-done((f32[112,256]{1,0:T(8,128)S(1)}, f32[112,256]{1,0:T(8,128)S(1)}, u32[]{:S(2)}, u32[]{:S(2)}) %collective-permute-start.12) | collective-permute-done | bytes 114720 | tf_op jit(solution)/shard_map/ppermute | solution.py:520
  86.8 1.1 %collective-permute-done.11.one_h = f32[112,256]{1,0:T(8,128)S(1)} collective-permute-done((f32[112,256]{1,0:T(8,128)S(1)}, f32[112,256]{1,0:T(8,128)S(1)}, u32[]{:S(2)}, u32[]{:S(2)}) %collective-permute-start.11) | collective-permute-done | bytes 114720 | tf_op jit(solution)/shard_map/ppermute | solution.py:520
  87.9 1.3 %sum_clips.1 = (f32[27,4,256]{2,1,0:T(4,128)}, f32[1,256]{1,0:T(1,128)}) custom-call(f32[112,256]{1,0:T(8,128)S(1)} %get-tuple-element.51.own_h, f32[112,256]{1,0:T(8,128)S(1)} %collective-permute-done.11.one_h, f32[112,256]{1,0:T(8,128)S(1)} %collective-permute-done.12.two_h, f32[112,256]{1,0:T(8,128)S(1)} %collective-permute-done.13.three_h), custom_call_target="tpu_custom_call" | custom-call | bytes 1048576 | tf_op jit(solution)/shard_map/sum_clips/pallas_call | solution.py:357
  (20 shorter events, 4.8 us)
Async XLA Ops:
  3.3 8.9 %collective-permute-start.1 = (bf16[2,8,16,256]{3,2,1,0:T(8,128)(2,1)S(1)}, bf16[2,8,16,256]{3,2,1,0:T(8,128)(2,1)S(1)}, u32[]{:S(2)}, u32[]{:S(2)}) collective-permute-start(bf16[2,8,16,256]{3,2,1,0:T(8,128)(2,1)S(1)} %get-tuple-element.30), channel_id=1, source_target_pairs={{0,1},{1,2},{2,3},{3,4},{4,5},{5,6},{6,7},{7,8},{8,9},{9,10},{10,1... | collective-permute-start | bytes 393224 | tf_op jit(solution)/shard_map/ppermute | solution.py:448
  8.3 6.3 %collective-permute-start.2 = (bf16[2,8,16,256]{3,2,1,0:T(8,128)(2,1)S(1)}, bf16[2,8,16,256]{3,2,1,0:T(8,128)(2,1)S(1)}, u32[]{:S(2)}, u32[]{:S(2)}) collective-permute-start(bf16[2,8,16,256]{3,2,1,0:T(8,128)(2,1)S(1)} %get-tuple-element.31), channel_id=1, source_target_pairs={{1,0},{2,1},{3,2},{4,3},{5,4},{6,5},{7,6},{8,7},{9,8},{10,9},{11,1... | collective-permute-start | bytes 393224 | tf_op jit(solution)/shard_map/ppermute | solution.py:449
  10.2 1.3 %collective-permute-start = (f32[8,128]{1,0:T(8,128)S(1)}, f32[8,128]{1,0:T(8,128)S(1)}, u32[]{:S(2)}, u32[]{:S(2)}) collective-permute-start(f32[8,128]{1,0:T(8,128)S(1)} %get-tuple-element.29.refs_0_), channel_id=1, source_target_pairs={{0,1},{1,0},{2,3},{3,2},{4,5},{5,4},{6,7},{7,6},{8,9},{9,8},{10,11... | collective-permute-start | bytes 12296 | tf_op jit(solution)/shard_map/ppermute | solution.py:447
  16.8 14.5 %collective-permute-start.3 = (bf16[704,128]{1,0:T(8,128)(2,1)S(1)}, bf16[704,128]{1,0:T(8,128)(2,1)S(1)}, u32[]{:S(2)}, u32[]{:S(2)}) collective-permute-start(bf16[704,128]{1,0:T(8,128)(2,1)S(1)} %get-tuple-element.35), channel_id=1, source_target_pairs={{0,16},{16,32},{32,48},{48,0},{1,17},{17,33},{33,49},{49,1},{2,18}... | collective-permute-start | bytes 540680 | tf_op jit(solution)/shard_map/ppermute | solution.py:464
  19.2 12.2 %collective-permute-start.4 = (bf16[704,128]{1,0:T(8,128)(2,1)S(1)}, bf16[704,128]{1,0:T(8,128)(2,1)S(1)}, u32[]{:S(2)}, u32[]{:S(2)}) collective-permute-start(bf16[704,128]{1,0:T(8,128)(2,1)S(1)} %get-tuple-element.36), channel_id=1, source_target_pairs={{0,32},{16,48},{32,0},{48,16},{1,33},{17,49},{33,1},{49,17},{2,34}... | collective-permute-start | bytes 540680 | tf_op jit(solution)/shard_map/ppermute | solution.py:464
  22.1 9.7 %collective-permute-start.5 = (bf16[704,128]{1,0:T(8,128)(2,1)S(1)}, bf16[704,128]{1,0:T(8,128)(2,1)S(1)}, u32[]{:S(2)}, u32[]{:S(2)}) collective-permute-start(bf16[704,128]{1,0:T(8,128)(2,1)S(1)} %get-tuple-element.37), channel_id=1, source_target_pairs={{0,48},{16,0},{32,16},{48,32},{1,49},{17,1},{33,17},{49,33},{2,50}... | collective-permute-start | bytes 540680 | tf_op jit(solution)/shard_map/ppermute | solution.py:464
  22.9 16.7 %all-to-all-start = ((f32[32,8,128]{2,1,0:T(8,128)}), f32[32,8,128]{2,1,0:T(8,128)S(1)}, u32[]{:S(2)}, u32[]{:S(2)}) async-start(f32[32,8,128]{2,1,0:T(8,128)} %pair_sums.1), calls=%async_computation | async-start | bytes 262144 | tf_op jit(solution)/shard_map/all_to_all | solution.py:452
  30.4 11.2 %collective-permute-start.6 = (bf16[704,128]{1,0:T(8,128)(2,1)S(1)}, bf16[704,128]{1,0:T(8,128)(2,1)S(1)}, u32[]{:S(2)}, u32[]{:S(2)}) collective-permute-start(bf16[704,128]{1,0:T(8,128)(2,1)S(1)} %get-tuple-element.34.refs_0_), channel_id=1, source_target_pairs={{0,1},{1,0},{2,3},{3,2},{4,5},{5,4},{6,7},{7,6},{8,9},{9,8},{10,11... | collective-permute-start | bytes 540680 | tf_op jit(solution)/shard_map/ppermute | solution.py:466
  31.3 10.3 %collective-permute-start.7 = (bf16[704,128]{1,0:T(8,128)(2,1)S(1)}, bf16[704,128]{1,0:T(8,128)(2,1)S(1)}, u32[]{:S(2)}, u32[]{:S(2)}) collective-permute-start(bf16[704,128]{1,0:T(8,128)(2,1)S(1)} %collective-permute-done.3.refs_1_), channel_id=1, source_target_pairs={{0,1},{1,0},{2,3},{3,2},{4,5},{5,4},{6,7},{7,6},{8,9},{9,8},{10,11... | collective-permute-start | bytes 540680 | tf_op jit(solution)/shard_map/ppermute | solution.py:466
  31.4 10.2 %collective-permute-start.8 = (bf16[704,128]{1,0:T(8,128)(2,1)S(1)}, bf16[704,128]{1,0:T(8,128)(2,1)S(1)}, u32[]{:S(2)}, u32[]{:S(2)}) collective-permute-start(bf16[704,128]{1,0:T(8,128)(2,1)S(1)} %collective-permute-done.4.refs_2_), channel_id=1, source_target_pairs={{0,1},{1,0},{2,3},{3,2},{4,5},{5,4},{6,7},{7,6},{8,9},{9,8},{10,11... | collective-permute-start | bytes 540680 | tf_op jit(solution)/shard_map/ppermute | solution.py:466
  31.8 9.8 %collective-permute-start.9 = (bf16[704,128]{1,0:T(8,128)(2,1)S(1)}, bf16[704,128]{1,0:T(8,128)(2,1)S(1)}, u32[]{:S(2)}, u32[]{:S(2)}) collective-permute-start(bf16[704,128]{1,0:T(8,128)(2,1)S(1)} %collective-permute-done.5.refs_3_), channel_id=1, source_target_pairs={{0,1},{1,0},{2,3},{3,2},{4,5},{5,4},{6,7},{7,6},{8,9},{9,8},{10,11... | collective-permute-start | bytes 540680 | tf_op jit(solution)/shard_map/ppermute | solution.py:466
  47.3 9.5 %collective-permute-start.10 = (bf16[8,112,128]{2,1,0:T(8,128)(2,1)S(1)}, bf16[8,112,128]{2,1,0:T(8,128)(2,1)S(1)}, u32[]{:S(2)}, u32[]{:S(2)}) collective-permute-start(bf16[8,112,128]{2,1,0:T(8,128)(2,1)S(1)} %get-tuple-element.43), channel_id=1, source_target_pairs={{0,1},{1,0},{2,3},{3,2},{4,5},{5,4},{6,7},{7,6},{8,9},{9,8},{10,11... | collective-permute-start | bytes 688136 | tf_op jit(solution)/shard_map/ppermute | solution.py:503
  58.3 20.2 %all-to-all-start.2 = ((bf16[8,256,128]{2,1,0:T(8,128)(2,1)}), bf16[8,256,128]{2,1,0:T(8,128)(2,1)S(1)}, u32[]{:S(2)}, u32[]{:S(2)}) async-start(bf16[8,256,128]{2,1,0:T(8,128)(2,1)} %merge_parts.1), calls=%async_computation.2 | async-start | bytes 1048576 | tf_op jit(solution)/shard_map/all_to_all | solution.py:508
  79.0 5.7 %collective-permute-start.13 = (f32[112,256]{1,0:T(8,128)S(1)}, f32[112,256]{1,0:T(8,128)S(1)}, u32[]{:S(2)}, u32[]{:S(2)}) collective-permute-start(f32[112,256]{1,0:T(8,128)S(1)} %get-tuple-element.51.own_h), channel_id=1, source_target_pairs={{0,192},{64,0},{128,64},{192,128},{1,193},{65,1},{129,65},{193,129... | collective-permute-start | bytes 344072 | tf_op jit(solution)/shard_map/ppermute | solution.py:520
  81.6 5.3 %collective-permute-start.12 = (f32[112,256]{1,0:T(8,128)S(1)}, f32[112,256]{1,0:T(8,128)S(1)}, u32[]{:S(2)}, u32[]{:S(2)}) collective-permute-start(f32[112,256]{1,0:T(8,128)S(1)} %get-tuple-element.51.own_h), channel_id=1, source_target_pairs={{0,128},{64,192},{128,0},{192,64},{1,129},{65,193},{129,1},{193,65... | collective-permute-start | bytes 344072 | tf_op jit(solution)/shard_map/ppermute | solution.py:520
  82.1 5.9 %collective-permute-start.11 = (f32[112,256]{1,0:T(8,128)S(1)}, f32[112,256]{1,0:T(8,128)S(1)}, u32[]{:S(2)}, u32[]{:S(2)}) collective-permute-start(f32[112,256]{1,0:T(8,128)S(1)} %get-tuple-element.51.own_h), channel_id=1, source_target_pairs={{0,64},{64,128},{128,192},{192,0},{1,65},{65,129},{129,193},{193,1... | collective-permute-start | bytes 344072 | tf_op jit(solution)/shard_map/ppermute | solution.py:520

commit v4 on v3

--- a/solution.py
+++ b/solution.py
@@ -21,7 +21,9 @@
 AROWS = FR // 2 * 3 * COLS
 GROWS = FR * ROWS * COLS
 TAPS = 27
-PROWS = 112
+PROWS = 224
+BLOCK = AROWS + NC * GROWS
+TERMS = 32
 HI = lax.Precision.HIGHEST
 
 
@@ -61,7 +63,8 @@
     mean = hdot(jnp.sum(xf, axis=1), gather) / (CELLS * GC)
     centered = xf - hdot(mean, spread_matrix())[:, None, :]
     squares = hdot(jnp.sum(centered * centered, axis=1), gather)
-    st_ref[...] = jnp.concatenate([mean, squares, jnp.zeros((FR, 2 * GROUPS), F32)], axis=1)
+    row = jnp.concatenate([mean, squares, jnp.zeros((FR, 2 * GROUPS), F32)], axis=1)
+    st_ref[...] = jnp.broadcast_to(row[None], (NZ * NC, FR, 128))
 
 
 def combined(parts, squares, each):
@@ -71,14 +74,25 @@
     return mean, jnp.sum(squares + each * (apart * apart), axis=0)
 
 
-def pair_sums(own_ref, other_ref, out_ref):
-    both = jnp.stack([own_ref[...], other_ref[...]])
-    mean, squares = combined(both[:, :, :GROUPS], both[:, :, GROUPS : 2 * GROUPS], CELLS * GC)
-    row = jnp.concatenate([mean, squares, jnp.zeros((FR, 2 * GROUPS), F32)], axis=1)
-    out_ref[...] = jnp.broadcast_to(row[None], (NY * NZ, FR, 128))
-
-
-def pack_slices(x_ref, g_ref, hp_ref, hn_ref, out_ref):
+def as_terms(values):
+    high = values.astype(BF16).astype(F32)
+    middle = (values - high).astype(BF16).astype(F32)
+    low = values - high - middle
+    return jnp.concatenate([high, middle, low, jnp.zeros((FR, 128), F32)], axis=0).astype(BF16)
+
+
+def from_terms(terms):
+    terms = terms.astype(F32)
+    return (terms[2 * FR : 3 * FR] + terms[FR : 2 * FR]) + terms[:FR]
+
+
+def pack_slices(x_ref, g_ref, hp_ref, hn_ref, st_ref, out_ref):
+    mean, squares = combined(
+        st_ref[:, :, :GROUPS], st_ref[:, :, GROUPS : 2 * GROUPS], CELLS * GC
+    )
+    sums = as_terms(
+        jnp.concatenate([mean, squares, jnp.zeros((FR, 2 * GROUPS), F32)], axis=1)
+    )
     upper = lax.axis_index("c") == 0
     own = [x_ref[:, 0], x_ref[:, 1]]
     before, after = hp_ref[0], hn_ref[0]
@@ -95,6 +109,7 @@
         for c in range(NC):
             at = AROWS + c * GROWS
             out_ref[y, at : at + GROWS] = g_ref[..., c * BSL : (c + 1) * BSL].reshape(GROWS, BSL)
+        out_ref[y, BLOCK:] = sums
 
 
 def backward_conv(g_ref, hp_ref, hn_ref, k_ref, live_ref, out_ref, pad_ref, held):
@@ -120,9 +135,10 @@
     out_ref[...] = total
 
 
-def group_terms(st_ref, x_ref, ag_ref, gain_ref, out_ref, sc_ref, mean_ref, inv_ref):
+def group_terms(a_ref, b_ref, c_ref, d_ref, x_ref, ag_ref, gain_ref, out_ref, sc_ref, mean_ref, inv_ref):
+    parts = jnp.stack([from_terms(ref[...]) for ref in (a_ref, b_ref, c_ref, d_ref)])
     mean, whole = combined(
-        st_ref[:, :, :GROUPS], st_ref[:, :, GROUPS : 2 * GROUPS], NC * CELLS * GC
+        parts[:, :, :GROUPS], parts[:, :, GROUPS : 2 * GROUPS], NZ * NC * CELLS * GC
     )
     spread = spread_matrix()
     mean_all = hdot(mean, spread)
@@ -153,8 +169,8 @@
 
 
 def kernel_part(*refs):
-    blocks, (mean_h, inv_h, gain_h, live_h, keep_h, give_h) = refs[:8], refs[8:14]
-    in_ref, mean_ref, inv_ref, gain_ref, live_ref, out_ref, pad_ref, grad_ref, sum_ref, sem = refs[14:]
+    blocks, (mean_h, inv_h, gain_h, live_h, out_h) = refs[:8], refs[8:13]
+    in_ref, mean_ref, inv_ref, gain_ref, live_ref, out_ref, pad_ref, grad_ref, sum_ref, sem = refs[13:]
     y_at, z_at, c_at = lax.axis_index("y"), lax.axis_index("z"), lax.axis_index("c")
     grads_at = pl.multiple_of(AROWS + c_at * GROWS, 64)
     copies = []
@@ -218,7 +234,7 @@
         cells = in_ref[n, AROWS:].astype(F32).reshape(FR, ROWS, COLS, BSL) * live
         grad_ref[:, d, pl.ds(2 * c, 2)] = cells
     turned_grad = grad_ref[...].reshape(FR * NY * 4 * COLS, BSL).T.astype(BF16)
-    sum_ref[:, :, 4 * TAPS :] = jnp.zeros((NC, NZ, PROWS - 4 * TAPS, BSL), F32)
+    sum_ref[:, 8 * TAPS :] = jnp.zeros((NZ, PROWS - 8 * TAPS, BSL), F32)
     for j in range(3):
         for k in range(3):
             early = pad_ref[k, 0:FR, :, j : j + 4].reshape(FR * NY * 4 * COLS, 2 * ASL)
@@ -231,34 +247,27 @@
             for i in range(3):
                 tap = (i * 3 + j) * 3 + k
                 piece = product[i * ASL : (i + 1) * ASL].reshape(NZ, ASL // NZ, BSL)
-                sum_ref[0, :, tap * 4 : tap * 4 + 4] = piece[:, :4]
-                sum_ref[1, :, tap * 4 : tap * 4 + 4] = piece[:, 4:]
+                sum_ref[:, tap * 8 : tap * 8 + 8] = piece
     out_ref[...] = sum_ref[...].astype(BF16)
-    keep = pltpu.make_async_copy(out_ref.at[c_at], keep_h, sem.at[0])
-    give = pltpu.make_async_copy(out_ref.at[1 - c_at], give_h, sem.at[1])
-    give.start()
-    keep.start()
-    give.wait()
-    keep.wait()
-
-
-def merge_parts(keep_ref, got_ref, b_ref, out_ref):
-    first = lax.axis_index("c") == 0
-    keep, got = keep_ref[...], got_ref[...]
-    out_ref[:, :PROWS] = jnp.where(first, keep, got)
-    out_ref[:, PROWS : 2 * PROWS] = jnp.where(first, got, keep)
-    sums = jnp.sum(b_ref[...], axis=0)
-    high = sums.astype(BF16).astype(F32)
-    middle = (sums - high).astype(BF16).astype(F32)
-    low = sums - high - middle
-    terms = jnp.concatenate([high, middle, low, jnp.zeros((FR, 128), F32)], axis=0).astype(BF16)
-    out_ref[:, 2 * PROWS :] = jnp.broadcast_to(terms[None], (NZ, 4 * FR, 128))
+    copy = pltpu.make_async_copy(out_ref, out_h.at[:, :PROWS], sem.at[0])
+    copy.start()
+    copy.wait()
+
+
+def add_sums(part_h, b_h, out_h, b_ref, out_ref, sem):
+    copy = pltpu.make_async_copy(b_h, b_ref, sem.at[0])
+    copy.start()
+    copy.wait()
+    terms = as_terms(jnp.sum(b_ref[...], axis=0))
+    out_ref[...] = jnp.broadcast_to(terms[None], (NZ, TERMS, 128))
+    copy = pltpu.make_async_copy(out_ref, out_h.at[:, PROWS:], sem.at[1])
+    copy.start()
+    copy.wait()
 
 
 def sum_rows(in_ref, out_ref, sums_ref):
     total = jnp.sum(in_ref[...].astype(F32), axis=0)
-    at = 2 * PROWS
-    sums = (total[at + 2 * FR : at + 3 * FR] + total[at + FR : at + 2 * FR]) + total[at : at + FR]
+    sums = from_terms(total[PROWS:])
     sums_ref[...] = sums
     fold_at = lax.broadcasted_iota(jnp.int32, (GROUPS, CH), 0)
     fold_lane = lax.broadcasted_iota(jnp.int32, (GROUPS, CH), 1)
@@ -266,9 +275,9 @@
     row = lax.broadcasted_iota(jnp.int32, (FR, CH), 0)
     lane = lax.broadcasted_iota(jnp.int32, (FR, CH), 1)
     gain = jnp.sum(jnp.where(lane // GROUPS == row, wide, 0.0), axis=0, keepdims=True)
-    out_ref[:, :BSL] = total[:PROWS]
-    out_ref[:, BSL:] = total[PROWS : 2 * PROWS]
-    out_ref[4 * TAPS : 4 * TAPS + 1] = gain
+    out_ref[...] = total[:PROWS]
+    out_ref[8 * TAPS : 8 * TAPS + 1] = gain[:, :BSL]
+    out_ref[8 * TAPS + 1 : 8 * TAPS + 2] = gain[:, BSL:]
 
 
 def forward_conv(x_ref, hp_ref, hn_ref, mean_ref, inv_ref, gain_ref, k_ref, live_ref, out_ref, pad_ref, held):
@@ -316,24 +325,28 @@
     out_ref[...] = (grad + norm_grad).astype(BF16).reshape(FR, ROWS, COLS, CH)
 
 
-def sum_clips(own_h, one_h, two_h, three_h, kg_h, gain_h, in_ref, kg_ref, gain_ref, sem):
-    x_at = lax.axis_index("x")
+def sum_clips(*refs):
+    kg_h, gain_h, in_ref, kg_ref, gain_ref, sem = refs[8:]
+    x_at, c_at = lax.axis_index("x"), lax.axis_index("c")
     copies = []
-    for d, src in enumerate((own_h, one_h, two_h, three_h)):
-        copies.append(
-            pltpu.make_async_copy(src, in_ref.at[lax.rem(x_at + NX - d, NX)], sem.at[d])
-        )
+    for n, src in enumerate(refs[:8]):
+        c = c_at if n < 4 else 1 - c_at
+        slot = in_ref.at[c, lax.rem(x_at + NX - n % 4, NX)]
+        copies.append(pltpu.make_async_copy(src, slot, sem.at[n]))
     for copy in copies:
         copy.start()
     for copy in copies:
         copy.wait()
-    total = ((in_ref[0] + in_ref[1]) + in_ref[2]) + in_ref[3]
-    for tap in range(TAPS):
-        kg_ref[tap] = total[4 * tap : 4 * tap + 4]
-    gain_ref[...] = total[4 * TAPS : 4 * TAPS + 1]
+    for c in range(NC):
+        total = ((in_ref[c, 0] + in_ref[c, 1]) + in_ref[c, 2]) + in_ref[c, 3]
+        total = total.reshape(TAPS + 1, 8, BSL)
+        kg_ref[:, :, c * BSL : (c + 1) * BSL] = jnp.where(c_at == 0, total[:TAPS, :4], total[:TAPS, 4:])
+        if c == 0:
+            gain_ref[:, :BSL] = total[TAPS, 0:1]
+            gain_ref[:, BSL:] = total[TAPS, 1:2]
     out = (
-        pltpu.make_async_copy(kg_ref, kg_h, sem.at[4]),
-        pltpu.make_async_copy(gain_ref, gain_h, sem.at[5]),
+        pltpu.make_async_copy(kg_ref, kg_h, sem.at[8]),
+        pltpu.make_async_copy(gain_ref, gain_h, sem.at[9]),
     )
     for copy in out:
         copy.start()
@@ -353,20 +366,21 @@
     return tuple(jax.ShapeDtypeStruct(s, d) for s, d in outs)
 
 
-def call(body, outs, args, specs, scratch, flops=0, limit=32):
+def call(body, outs, args, specs, scratch, flops=0, limit=32, aliases={}):
     return pl.pallas_call(
         body,
         out_shape=shapes(outs),
         in_specs=specs,
         out_specs=tuple(HBM for _ in outs),
         scratch_shapes=list(scratch),
+        input_output_aliases=aliases,
         compiler_params=pltpu.CompilerParams(vmem_limit_bytes=limit * 2**20),
         cost_estimate=pl.CostEstimate(flops=flops, bytes_accessed=2**20, transcendentals=0),
         name=body.__name__,
     )(*args)
 
 
-def run(body, outs, args, scratch=(), late=None, smem=(), flops=0):
+def run(body, outs, args, scratch=(), late=None, smem=(), flops=0, rows={}):
     count, outputs = len(args), len(outs)
     moved = [at for at in range(count) if at not in smem]
 
@@ -377,7 +391,10 @@
         results, rest = rest[:outputs], rest[outputs:]
         sem, extra = rest[0], rest[1:]
         copies = [
-            pltpu.make_async_copy(ins[at], buffers[n], sem.at[n]) for n, at in enumerate(moved)
+            pltpu.make_async_copy(
+                ins[at].at[rows[at][0] : rows[at][1]] if at in rows else ins[at], buffers[n], sem.at[n]
+            )
+            for n, at in enumerate(moved)
         ]
         for copy in copies:
             copy.start()
@@ -401,24 +418,31 @@
 
     kernel.__name__ = body.__name__
     specs = [SMEM if at in smem else HBM for at in range(count)]
-    buffers = [pltpu.VMEM(args[at].shape, args[at].dtype) for at in moved]
+    buffers = []
+    for at in moved:
+        shape = args[at].shape
+        if at in rows:
+            shape = (rows[at][1] - rows[at][0],) + shape[1:]
+        buffers.append(pltpu.VMEM(shape, args[at].dtype))
     buffers += [pltpu.VMEM(s, d) for s, d in outs]
     buffers += [pltpu.SemaphoreType.DMA((len(moved) + outputs,))]
     return call(kernel, outs, args, specs, buffers + list(scratch), flops)
 
 
-def pack_body(x_h, g_h, hp_h, hn_h, out0, out1, out2, out3, x_ref, g_ref, hp_ref, hn_ref, buf, sem):
-    pairs = ((x_h, x_ref), (g_h, g_ref), (hp_h, hp_ref), (hn_h, hn_ref))
+def pack_body(*refs):
+    sources, outs = refs[:5], refs[5:9]
+    x_ref, g_ref, hp_ref, hn_ref, st_ref, buf, sem = refs[9:]
+    pairs = tuple(zip(sources, (x_ref, g_ref, hp_ref, hn_ref, st_ref)))
     copies = [pltpu.make_async_copy(a, b, sem.at[n]) for n, (a, b) in enumerate(pairs)]
     for copy in copies:
         copy.start()
     for copy in copies:
         copy.wait()
-    pack_slices(x_ref, g_ref, hp_ref, hn_ref, buf)
+    pack_slices(x_ref, g_ref, hp_ref, hn_ref, st_ref, buf)
     y_at = lax.axis_index("y")
     copies = [
-        pltpu.make_async_copy(buf.at[lax.rem(y_at + d, NY)], out, sem.at[4 + d])
-        for d, out in enumerate((out0, out1, out2, out3))
+        pltpu.make_async_copy(buf.at[lax.rem(y_at + d, NY)], out, sem.at[5 + d])
+        for d, out in enumerate(outs)
     ]
     for copy in copies:
         copy.start()
@@ -440,30 +464,13 @@
 
     up, dn, stats, live = run(
         edges_and_sums,
-        [(halo, BF16), (halo, BF16), ((FR, 128), F32), (wide, F32)],
+        [(halo, BF16), (halo, BF16), ((NZ * NC, FR, 128), F32), (wide, F32)],
         (x, g, frame_counts),
         smem=(2,),
     )
-    other = lax.ppermute(stats, "c", swap)
     hp = lax.ppermute(dn, space, [(i, i + 1) for i in range(SPACE - 1)])
     hn = lax.ppermute(up, space, [(i + 1, i) for i in range(SPACE - 1)])
-    (stats,) = run(pair_sums, [((NY * NZ, FR, 128), F32)], (stats, other))
-    stats, hp, hn = lax.optimization_barrier((stats, hp, hn))
-    stats = lax.all_to_all(stats, ("y", "z"), 0, 0)
-    block = (AROWS + NC * GROWS, BSL)
-    packed = call(
-        pack_body,
-        [(block, BF16)] * NY,
-        (x, g, hp, hn),
-        [HBM] * 4,
-        [pltpu.VMEM(cells, BF16)] * 2
-        + [pltpu.VMEM(halo, BF16)] * 2
-        + [pltpu.VMEM((NY,) + block, BF16), dma((8,))],
-    )
-    near = [packed[0]] + [
-        lax.ppermute(packed[d], "y", [(i, (i + d) % NY) for i in range(NY)]) for d in range(1, NY)
-    ]
-    far = [lax.ppermute(a, "c", swap) for a in near]
+    stats = lax.all_to_all(stats, ("z", "c"), 0, 0)
     conv_flops = 16 * TAPS * FR * CELLS * CH * CH
     padded = pltpu.VMEM((3, FR + 2, 4, COLS, CH), BF16)
     (act_grad,) = run(
@@ -474,16 +481,33 @@
         late=3,
         flops=0,
     )
+    act_grad, hp, hn = lax.optimization_barrier((act_grad, hp, hn))
+    block = (BLOCK + TERMS, BSL)
+    packed = call(
+        pack_body,
+        [(block, BF16)] * NY,
+        (x, g, hp, hn, stats),
+        [HBM] * 5,
+        [pltpu.VMEM(cells, BF16)] * 2
+        + [pltpu.VMEM(halo, BF16)] * 2
+        + [pltpu.VMEM((NZ * NC, FR, 128), F32), pltpu.VMEM((NY,) + block, BF16), dma((9,))],
+    )
+    near = [packed[0]] + [
+        lax.ppermute(packed[d], "y", [(i, (i + d) % NY) for i in range(NY)]) for d in range(1, NY)
+    ]
+    far = [lax.ppermute(a, "c", swap) for a in near]
     terms, scaled, mean, inv = run(
         group_terms,
         [((NY * NC, FR, 128), F32), ((FR, CELLS, CH), F32), (wide, F32), (wide, F32)],
-        (stats, x, act_grad, gain),
+        (*near, x, act_grad, gain),
+        rows={at: (BLOCK, BLOCK + TERMS) for at in range(NY)},
     )
     terms = lax.all_to_all(terms, ("y", "c"), 0, 0)
     part = (NZ, PROWS, BSL)
-    keep, give = call(
+    whole_part = (NZ, PROWS + TERMS, BSL)
+    (partial,) = call(
         kernel_part,
-        [(part, BF16)] * 2,
+        [(whole_part, BF16)],
         (*near, *far, mean, inv, gain, live),
         [HBM] * 12,
         [
@@ -492,17 +516,21 @@
             pltpu.VMEM(wide, F32),
             pltpu.VMEM((1, CH), F32),
             pltpu.VMEM(wide, F32),
-            pltpu.VMEM((NC,) + part, BF16),
+            pltpu.VMEM(part, BF16),
             pltpu.VMEM((3, FR + 2, NY, 6, COLS, 2 * ASL), BF16),
             pltpu.VMEM((FR, NY, 4, COLS, BSL), F32),
-            pltpu.VMEM((NC,) + part, F32),
+            pltpu.VMEM(part, F32),
             dma((20,)),
         ],
         flops=conv_flops,
     )
-    got = lax.ppermute(give, "c", swap)
-    (merged,) = run(
-        merge_parts, [((NZ, 2 * PROWS + 4 * FR, BSL), BF16)], (keep, got, terms)
+    (merged,) = call(
+        add_sums,
+        [(whole_part, BF16)],
+        (partial, terms),
+        [HBM] * 2,
+        [pltpu.VMEM((NY * NC, FR, 128), F32), pltpu.VMEM((NZ, TERMS, 128), BF16), dma((2,))],
+        aliases={0: 0},
     )
     merged, late_mean = lax.optimization_barrier((merged, mean))
     merged = lax.all_to_all(merged, "z", 0, 0)
@@ -515,23 +543,25 @@
         flops=conv_flops,
     )
     merged, block_output = lax.optimization_barrier((merged, block_output))
-    rows, sums = run(sum_rows, [((PROWS, CH), F32), ((FR, 128), F32)], (merged,))
-    others = [
+    rows, sums = run(sum_rows, [((PROWS, BSL), F32), ((FR, 128), F32)], (merged,))
+    others = [rows] + [
         lax.ppermute(rows, "x", [(i, (i + d) % NX) for i in range(NX)]) for d in range(1, NX)
     ]
     (input_grad,) = run(
         finish_input, [(cells, BF16)], (sums, scaled, x, g, mean, inv, live)
     )
+    *others, input_grad = lax.optimization_barrier((*others, input_grad))
+    swapped = [lax.ppermute(a, "c", swap) for a in others]
     kernel_grad, gain_grad = call(
         sum_clips,
         [((TAPS, 4, CH), F32), ((1, CH), F32)],
-        (rows, *others),
-        [HBM] * 4,
+        (*others, *swapped),
+        [HBM] * 8,
         [
-            pltpu.VMEM((NX, PROWS, CH), F32),
+            pltpu.VMEM((NC, NX, PROWS, BSL), F32),
             pltpu.VMEM((TAPS, 4, CH), F32),
             pltpu.VMEM((1, CH), F32),
-            dma((6,)),
+            dma((10,)),
         ],
     )
     whole = (1,) + cells

time: 90.5 us -> 96.3 us (1.064)
  waiting for transfers between devices: 23 us -> 30.9 us
  blocking collectives: 7.4 us -> 0 us
  starting transfers between devices: 31.5 us -> 37.1 us
    all_to_all x1 -> x0, blocking collectives: 7.4 us -> none  [local(): terms = lax.all_to_all(terms, ('y', 'c'), 0, 0)]
    all_to_all x1 -> x2, starting transfers between devices: 7.52 us -> 13.9 us  [the longest x1 9.91 us: local(): stats = lax.all_to_all(stats, ('z', 'c'), 0, 0)]
    ppermute x3, waiting for transfers between devices: 0.01 us -> 5.79 us  [local(): lax.ppermute(packed[d], 'y', [(i, (i + d) % NY) for i in range(NY)])]
    ppermute x3, waiting for transfers between devices: 3.21 us -> 5.75 us  [local(): lax.ppermute(rows, 'x', [(i, (i + d) % NX) for i in range(NX)])]
    ppermute x1, waiting for transfers between devices: 2.31 us -> 0.01 us  [local(): hn = lax.ppermute(up, space, [(i + 1, i) for i in range(SPACE - 1)])]
    all_to_all x1, waiting for transfers between devices: 12.3 us -> 13.8 us  [local(): merged = lax.all_to_all(merged, 'z', 0, 0)]
    ppermute x4, starting transfers between devices: 1.53 us -> 2.86 us  [local(): far = [lax.ppermute(a, 'c', swap) for a in near]]
    ppermute x3, starting transfers between devices: 6.08 us -> 5.06 us  [local(): lax.ppermute(packed[d], 'y', [(i, (i + d) % NY) for i in range(NY)])]
  transfers between devices with their start and end apart: 16 -> 19, of which waited for: 6 -> 10; matrix products, arithmetic and copies ran while one was open for 0% -> 0% of each run, Pallas kernels for 14% -> 19%
where the time goes in v4:
time: 96.3 us; the launch traced here: 95.8 us
  starting transfers between devices  37.1 us (39%)
  waiting for transfers between devices  30.9 us (32%)
  Pallas kernels  26.2 us (27%)
  between operations  1.59 us (2%)
    pallas_call x10, Pallas kernels, call(): pl.pallas_call(body, out_shape=shapes(outs), in_specs=specs, out_specs=tu...  26.2 us
    all_to_all x1, waiting for transfers between devices, local(): merged = lax.all_to_all(merged, 'z', 0, 0)  13.8 us
    all_to_all x1, starting transfers between devices, local(): stats = lax.all_to_all(stats, ('z', 'c'), 0, 0)  9.91 us
    ppermute x3, waiting for transfers between devices, local(): lax.ppermute(packed[d], 'y', [(i, (i + d) % NY) for i in range(NY)])  5.79 us
    ppermute x3, waiting for transfers between devices, local(): lax.ppermute(rows, 'x', [(i, (i + d) % NX) for i in range(NX)])  5.75 us
    ppermute x3, starting transfers between devices, local(): lax.ppermute(packed[d], 'y', [(i, (i + d) % NY) for i in range(NY)])  5.06 us
    ppermute x1, starting transfers between devices, local(): hp = lax.ppermute(dn, space, [(i, i + 1) for i in range(SPACE - 1)])  4.94 us
    all_to_all x1, waiting for transfers between devices, local(): stats = lax.all_to_all(stats, ('z', 'c'), 0, 0)  4.24 us
  transfers between devices with their start and end apart: 19, of which 10 were waited for; matrix products, arithmetic and copies ran while one was open for 0% of the time, Pallas kernels for 19%

profile of v4, /device:TPU:1, one launch (start us, length us, event | category | flops | bytes accessed | tf_op | source)
XLA Modules:
  0.0 95.8 jit_solution(8322672498893396004)
XLA Ops:
  1.3 2.6 %edges_and_sums.1 = (bf16[2,8,16,256]{3,2,1,0:T(8,128)(2,1)S(1)}, bf16[2,8,16,256]{3,2,1,0:T(8,128)(2,1)S(1)}, f32[16,8,128]{2,1,0:T(8,128)}, f32[8,256]{1,0:T(8,128)S(1)}) custom-call(bf16[8,2,16,256]{3,2,1,0:T(8,128)(2,1)} %bitcast.11, bf16[8,2,16,256]{3,2,1,0:T(8,128)(2,1)} %bitcast.7, s32[1]{0:T(128)S(6)} %copy.11.refs_2_), custom_call_target="tpu_custom_call" | custom-call | bytes 1048576 | tf_op jit(solution)/shard_map/edges_and_sums/pallas_call | solution.py:370
  3.9 4.9 %collective-permute-start = (bf16[2,8,16,256]{3,2,1,0:T(8,128)(2,1)S(1)}, bf16[2,8,16,256]{3,2,1,0:T(8,128)(2,1)S(1)}, u32[]{:S(2)}, u32[]{:S(2)}) collective-permute-start(bf16[2,8,16,256]{3,2,1,0:T(8,128)(2,1)S(1)} %get-tuple-element.32), channel_id=1, source_target_pairs={{0,1},{1,2},{2,3},{3,4},{4,5},{5,6},{6,7},{7,8},{8,9},{9,10},{10,1... | collective-permute-start | bytes 393224 | tf_op jit(solution)/shard_map/ppermute | solution.py:471
  8.9 1.9 %collective-permute-start.1 = (bf16[2,8,16,256]{3,2,1,0:T(8,128)(2,1)S(1)}, bf16[2,8,16,256]{3,2,1,0:T(8,128)(2,1)S(1)}, u32[]{:S(2)}, u32[]{:S(2)}) collective-permute-start(bf16[2,8,16,256]{3,2,1,0:T(8,128)(2,1)S(1)} %get-tuple-element.33), channel_id=1, source_target_pairs={{1,0},{2,1},{3,2},{4,3},{5,4},{6,5},{7,6},{8,7},{9,8},{10,9},{11,1... | collective-permute-start | bytes 393224 | tf_op jit(solution)/shard_map/ppermute | solution.py:472
  10.8 9.9 %all-to-all-start = ((f32[16,8,128]{2,1,0:T(8,128)}), f32[16,8,128]{2,1,0:T(8,128)S(1)}, u32[]{:S(2)}, u32[]{:S(2)}) async-start(f32[16,8,128]{2,1,0:T(8,128)} %get-tuple-element.37), calls=%async_computation | async-start | bytes 131072 | tf_op jit(solution)/shard_map/all_to_all | solution.py:473
  20.7 3.5 %backward_conv.1.refs_5_ = f32[256,256]{1,0:T(8,128)S(1)} custom-call(bf16[8,2,16,256]{3,2,1,0:T(8,128)(2,1)} %bitcast.8, bf16[2,8,16,256]{3,2,1,0:T(8,128)(2,1)S(1)} %collective-permute-done.refs_1_.refs_2_, bf16[2,8,16,256]{3,2,1,0:T(8,128)(2,1)S(1)} %collective-permute-done.1.refs_2_.refs_3_, bf16[27,256,256]{2,1,0:T(8,128)(2,1)} %refs_6_.1, ...), custom_call_target="tpu_custom_call" | custom-call | bytes 1048576 | tf_op jit(solution)/shard_map/backward_conv/pallas_call | solution.py:370
  24.3 4.2 %all-to-all-done.refs_4_ = f32[16,8,128]{2,1,0:T(8,128)S(1)} async-done(((f32[16,8,128]{2,1,0:T(8,128)}), f32[16,8,128]{2,1,0:T(8,128)S(1)}, u32[]{:S(2)}, u32[]{:S(2)}) %all-to-all-start) | async-done | bytes 65568 | tf_op jit(solution)/shard_map/all_to_all | solution.py:473
  28.5 2.3 %pack_body.1 = (bf16[736,128]{1,0:T(8,128)(2,1)S(1)}, bf16[736,128]{1,0:T(8,128)(2,1)S(1)}, bf16[736,128]{1,0:T(8,128)(2,1)S(1)}, bf16[736,128]{1,0:T(8,128)(2,1)S(1)}) custom-call(bf16[8,2,16,256]{3,2,1,0:T(8,128)(2,1)} %bitcast.12, bf16[8,2,16,256]{3,2,1,0:T(8,128)(2,1)} %bitcast.9, bf16[2,8,16,256]{3,2,1,0:T(8,128)(2,1)S(1)} %collective-permute-done.refs_1_.refs_2_, ...), custom_call_target="tpu_custom_call" | custom-call | bytes 1048576 | tf_op jit(solution)/shard_map/pack_body/pallas_call | solution.py:370
  30.8 1.4 %collective-permute-start.2 = (bf16[736,128]{1,0:T(8,128)(2,1)S(1)}, bf16[736,128]{1,0:T(8,128)(2,1)S(1)}, u32[]{:S(2)}, u32[]{:S(2)}) collective-permute-start(bf16[736,128]{1,0:T(8,128)(2,1)S(1)} %get-tuple-element.39), channel_id=1, source_target_pairs={{0,16},{16,32},{32,48},{48,0},{1,17},{17,33},{33,49},{49,1},{2,18}... | collective-permute-start | bytes 565256 | tf_op jit(solution)/shard_map/ppermute | solution.py:496
  32.2 2.6 %collective-permute-start.3 = (bf16[736,128]{1,0:T(8,128)(2,1)S(1)}, bf16[736,128]{1,0:T(8,128)(2,1)S(1)}, u32[]{:S(2)}, u32[]{:S(2)}) collective-permute-start(bf16[736,128]{1,0:T(8,128)(2,1)S(1)} %get-tuple-element.40), channel_id=1, source_target_pairs={{0,32},{16,48},{32,0},{48,16},{1,33},{17,49},{33,1},{49,17},{2,34}... | collective-permute-start | bytes 565256 | tf_op jit(solution)/shard_map/ppermute | solution.py:496
  34.8 1.1 %collective-permute-start.4 = (bf16[736,128]{1,0:T(8,128)(2,1)S(1)}, bf16[736,128]{1,0:T(8,128)(2,1)S(1)}, u32[]{:S(2)}, u32[]{:S(2)}) collective-permute-start(bf16[736,128]{1,0:T(8,128)(2,1)S(1)} %get-tuple-element.41), channel_id=1, source_target_pairs={{0,48},{16,0},{32,16},{48,32},{1,49},{17,1},{33,17},{49,33},{2,50}... | collective-permute-start | bytes 565256 | tf_op jit(solution)/shard_map/ppermute | solution.py:496
  35.9 1.0 %collective-permute-start.5 = (bf16[736,128]{1,0:T(8,128)(2,1)S(1)}, bf16[736,128]{1,0:T(8,128)(2,1)S(1)}, u32[]{:S(2)}, u32[]{:S(2)}) collective-permute-start(bf16[736,128]{1,0:T(8,128)(2,1)S(1)} %get-tuple-element.38.refs_0_), channel_id=1, source_target_pairs={{0,1},{1,0},{2,3},{3,2},{4,5},{5,4},{6,7},{7,6},{8,9},{9,8},{10,11... | collective-permute-start | bytes 565256 | tf_op jit(solution)/shard_map/ppermute | solution.py:498
  36.9 1.5 %collective-permute-done.2.refs_1_ = bf16[736,128]{1,0:T(8,128)(2,1)S(1)} collective-permute-done((bf16[736,128]{1,0:T(8,128)(2,1)S(1)}, bf16[736,128]{1,0:T(8,128)(2,1)S(1)}, u32[]{:S(2)}, u32[]{:S(2)}) %collective-permute-start.2) | collective-permute-done | bytes 188448 | tf_op jit(solution)/shard_map/ppermute | solution.py:496
  39.3 4.2 %collective-permute-done.3.refs_2_ = bf16[736,128]{1,0:T(8,128)(2,1)S(1)} collective-permute-done((bf16[736,128]{1,0:T(8,128)(2,1)S(1)}, bf16[736,128]{1,0:T(8,128)(2,1)S(1)}, u32[]{:S(2)}, u32[]{:S(2)}) %collective-permute-start.3) | collective-permute-done | bytes 188448 | tf_op jit(solution)/shard_map/ppermute | solution.py:496
  44.6 2.5 %group_terms.1 = (f32[8,8,128]{2,1,0:T(8,128)}, f32[8,32,256]{2,1,0:T(8,128)S(1)}, f32[8,256]{1,0:T(8,128)S(1)}, f32[8,256]{1,0:T(8,128)S(1)}) custom-call(bf16[736,128]{1,0:T(8,128)(2,1)S(1)} %get-tuple-element.38.refs_0_, bf16[736,128]{1,0:T(8,128)(2,1)S(1)} %collective-permute-done.2.refs_1_, bf16[736,128]{1,0:T(8,128)(2,1)S(1)} %collective-permute-done.3.refs_2_, ...), custom_call_target="tpu_custom_call" | custom-call | bytes 1048576 | tf_op jit(solution)/shard_map/group_terms/pallas_call | solution.py:370
  47.1 3.9 %all-to-all-start.1 = ((f32[8,8,128]{2,1,0:T(8,128)}), f32[8,8,128]{2,1,0:T(8,128)S(1)}, u32[]{:S(2)}, u32[]{:S(2)}) async-start(f32[8,8,128]{2,1,0:T(8,128)} %get-tuple-element.45), calls=%async_computation.1 | async-start | bytes 65536 | tf_op jit(solution)/shard_map/all_to_all | solution.py:505
  51.0 5.8 %kernel_part.1.part_h = bf16[8,256,128]{2,1,0:T(8,128)(2,1)} custom-call(bf16[736,128]{1,0:T(8,128)(2,1)S(1)} %get-tuple-element.38.refs_0_, bf16[736,128]{1,0:T(8,128)(2,1)S(1)} %collective-permute-done.2.refs_1_, bf16[736,128]{1,0:T(8,128)(2,1)S(1)} %collective-permute-done.3.refs_2_, bf16[736,128]{1,0:T(8,128)(2,1)S(1)} %collective-permute-done.4.refs_3_, ...), custom_call_target="tpu_custom_call" | custom-call | flops 7247757312 | bytes 1048576 | tf_op jit(solution)/shard_map/kernel_part/pallas_call | solution.py:370
  57.6 3.5 %all-to-all-start.2 = ((bf16[8,256,128]{2,1,0:T(8,128)(2,1)}), bf16[8,256,128]{2,1,0:T(8,128)(2,1)S(1)}, u32[]{:S(2)}, u32[]{:S(2)}) async-start(bf16[8,256,128]{2,1,0:T(8,128)(2,1)} %add_sums.1), calls=%async_computation.2 | async-start | bytes 1048576 | tf_op jit(solution)/shard_map/all_to_all | solution.py:536
  61.1 4.2 %forward_conv.1 = bf16[8,2,16,256]{3,2,1,0:T(8,128)(2,1)} custom-call(bf16[8,2,16,256]{3,2,1,0:T(8,128)(2,1)} %bitcast.14, bf16[2,8,16,256]{3,2,1,0:T(8,128)(2,1)S(1)} %collective-permute-done.refs_1_.refs_2_, bf16[2,8,16,256]{3,2,1,0:T(8,128)(2,1)S(1)} %collective-permute-done.1.refs_2_.refs_3_, f32[8,256]{1,0:T(8,128)S(1)} %get-tuple-element.47.refs_8_.refs_3_.refs_4_, ...), custom_call_target="tpu_custom_call" | custom-call | flops 7247757312 | bytes 1048576 | tf_op jit(solution)/shard_map/forward_conv/pallas_call | solution.py:370
  65.3 13.8 %all-to-all-done.2.refs_0_ = bf16[8,256,128]{2,1,0:T(8,128)(2,1)S(1)} async-done(((bf16[8,256,128]{2,1,0:T(8,128)(2,1)}), bf16[8,256,128]{2,1,0:T(8,128)(2,1)S(1)}, u32[]{:S(2)}, u32[]{:S(2)}) %all-to-all-start.2) | async-done | bytes 524320 | tf_op jit(solution)/shard_map/all_to_all | solution.py:536
  79.6 2.7 %collective-permute-start.11 = (f32[224,128]{1,0:T(8,128)S(1)}, f32[224,128]{1,0:T(8,128)S(1)}, u32[]{:S(2)}, u32[]{:S(2)}) collective-permute-start(f32[224,128]{1,0:T(8,128)S(1)} %get-tuple-element.54.refs_0_), channel_id=1, source_target_pairs={{0,192},{64,0},{128,64},{192,128},{1,193},{65,1},{129,65},{193,129... | collective-permute-start | bytes 344072 | tf_op jit(solution)/shard_map/ppermute | solution.py:548
  83.5 2.0 %finish_input.1 = bf16[8,2,16,256]{3,2,1,0:T(8,128)(2,1)} custom-call(f32[8,128]{1,0:T(8,128)S(1)} %get-tuple-element.51.refs_0_, f32[8,32,256]{2,1,0:T(8,128)S(1)} %get-tuple-element.52.refs_1_, bf16[8,2,16,256]{3,2,1,0:T(8,128)(2,1)} %bitcast.15, bf16[8,2,16,256]{3,2,1,0:T(8,128)(2,1)} %bitcast.10, f32[8,256]{1,0:T(8,128)S(1)} %get-tuple-element.47.refs_8_.refs_3_.refs_4_, ...), custom_call_target="tpu_custom_call" | custom-call | bytes 1048576 | tf_op jit(solution)/shard_map/finish_input/pallas_call | solution.py:370
  85.5 2.3 %collective-permute-done.10.refs_2_ = f32[224,128]{1,0:T(8,128)S(1)} collective-permute-done((f32[224,128]{1,0:T(8,128)S(1)}, f32[224,128]{1,0:T(8,128)S(1)}, u32[]{:S(2)}, u32[]{:S(2)}) %collective-permute-start.10) | collective-permute-done | bytes 114720 | tf_op jit(solution)/shard_map/ppermute | solution.py:548
  87.8 3.4 %collective-permute-done.9.refs_1_ = f32[224,128]{1,0:T(8,128)S(1)} collective-permute-done((f32[224,128]{1,0:T(8,128)S(1)}, f32[224,128]{1,0:T(8,128)S(1)}, u32[]{:S(2)}, u32[]{:S(2)}) %collective-permute-start.9) | collective-permute-done | bytes 114720 | tf_op jit(solution)/shard_map/ppermute | solution.py:548
  93.7 1.9 %sum_clips.1 = (f32[27,4,256]{2,1,0:T(4,128)}, f32[1,256]{1,0:T(1,128)}) custom-call(f32[224,128]{1,0:T(8,128)S(1)} %get-tuple-element.54.refs_0_, f32[224,128]{1,0:T(8,128)S(1)} %collective-permute-done.9.refs_1_, f32[224,128]{1,0:T(8,128)S(1)} %collective-permute-done.10.refs_2_, f32[224,128]{1,0:T(8,128)S(1)} %collective-permute-done.11.refs_3_, ...), custom_call_target="tpu_custom_call" | custom-call | bytes 1048576 | tf_op jit(solution)/shard_map/sum_clips/pallas_call | solution.py:370
  (24 shorter events, 6.7 us)
Async XLA Ops:
  3.9 16.8 %collective-permute-start = (bf16[2,8,16,256]{3,2,1,0:T(8,128)(2,1)S(1)}, bf16[2,8,16,256]{3,2,1,0:T(8,128)(2,1)S(1)}, u32[]{:S(2)}, u32[]{:S(2)}) collective-permute-start(bf16[2,8,16,256]{3,2,1,0:T(8,128)(2,1)S(1)} %get-tuple-element.32), channel_id=1, source_target_pairs={{0,1},{1,2},{2,3},{3,4},{4,5},{5,6},{6,7},{7,8},{8,9},{9,10},{10,1... | collective-permute-start | bytes 393224 | tf_op jit(solution)/shard_map/ppermute | solution.py:471
  8.9 11.8 %collective-permute-start.1 = (bf16[2,8,16,256]{3,2,1,0:T(8,128)(2,1)S(1)}, bf16[2,8,16,256]{3,2,1,0:T(8,128)(2,1)S(1)}, u32[]{:S(2)}, u32[]{:S(2)}) collective-permute-start(bf16[2,8,16,256]{3,2,1,0:T(8,128)(2,1)S(1)} %get-tuple-element.33), channel_id=1, source_target_pairs={{1,0},{2,1},{3,2},{4,3},{5,4},{6,5},{7,6},{8,7},{9,8},{10,9},{11,1... | collective-permute-start | bytes 393224 | tf_op jit(solution)/shard_map/ppermute | solution.py:472
  10.8 17.7 %all-to-all-start = ((f32[16,8,128]{2,1,0:T(8,128)}), f32[16,8,128]{2,1,0:T(8,128)S(1)}, u32[]{:S(2)}, u32[]{:S(2)}) async-start(f32[16,8,128]{2,1,0:T(8,128)} %get-tuple-element.37), calls=%async_computation | async-start | bytes 131072 | tf_op jit(solution)/shard_map/all_to_all | solution.py:473
  30.8 7.6 %collective-permute-start.2 = (bf16[736,128]{1,0:T(8,128)(2,1)S(1)}, bf16[736,128]{1,0:T(8,128)(2,1)S(1)}, u32[]{:S(2)}, u32[]{:S(2)}) collective-permute-start(bf16[736,128]{1,0:T(8,128)(2,1)S(1)} %get-tuple-element.39), channel_id=1, source_target_pairs={{0,16},{16,32},{32,48},{48,0},{1,17},{17,33},{33,49},{49,1},{2,18}... | collective-permute-start | bytes 565256 | tf_op jit(solution)/shard_map/ppermute | solution.py:496
  32.2 11.4 %collective-permute-start.3 = (bf16[736,128]{1,0:T(8,128)(2,1)S(1)}, bf16[736,128]{1,0:T(8,128)(2,1)S(1)}, u32[]{:S(2)}, u32[]{:S(2)}) collective-permute-start(bf16[736,128]{1,0:T(8,128)(2,1)S(1)} %get-tuple-element.40), channel_id=1, source_target_pairs={{0,32},{16,48},{32,0},{48,16},{1,33},{17,49},{33,1},{49,17},{2,34}... | collective-permute-start | bytes 565256 | tf_op jit(solution)/shard_map/ppermute | solution.py:496
  34.8 9.7 %collective-permute-start.4 = (bf16[736,128]{1,0:T(8,128)(2,1)S(1)}, bf16[736,128]{1,0:T(8,128)(2,1)S(1)}, u32[]{:S(2)}, u32[]{:S(2)}) collective-permute-start(bf16[736,128]{1,0:T(8,128)(2,1)S(1)} %get-tuple-element.41), channel_id=1, source_target_pairs={{0,48},{16,0},{32,16},{48,32},{1,49},{17,1},{33,17},{49,33},{2,50}... | collective-permute-start | bytes 565256 | tf_op jit(solution)/shard_map/ppermute | solution.py:496
  35.9 15.1 %collective-permute-start.5 = (bf16[736,128]{1,0:T(8,128)(2,1)S(1)}, bf16[736,128]{1,0:T(8,128)(2,1)S(1)}, u32[]{:S(2)}, u32[]{:S(2)}) collective-permute-start(bf16[736,128]{1,0:T(8,128)(2,1)S(1)} %get-tuple-element.38.refs_0_), channel_id=1, source_target_pairs={{0,1},{1,0},{2,3},{3,2},{4,5},{5,4},{6,7},{7,6},{8,9},{9,8},{10,11... | collective-permute-start | bytes 565256 | tf_op jit(solution)/shard_map/ppermute | solution.py:498
  38.4 12.6 %collective-permute-start.6 = (bf16[736,128]{1,0:T(8,128)(2,1)S(1)}, bf16[736,128]{1,0:T(8,128)(2,1)S(1)}, u32[]{:S(2)}, u32[]{:S(2)}) collective-permute-start(bf16[736,128]{1,0:T(8,128)(2,1)S(1)} %collective-permute-done.2.refs_1_), channel_id=1, source_target_pairs={{0,1},{1,0},{2,3},{3,2},{4,5},{5,4},{6,7},{7,6},{8,9},{9,8},{10,11... | collective-permute-start | bytes 565256 | tf_op jit(solution)/shard_map/ppermute | solution.py:498
  43.6 7.4 %collective-permute-start.7 = (bf16[736,128]{1,0:T(8,128)(2,1)S(1)}, bf16[736,128]{1,0:T(8,128)(2,1)S(1)}, u32[]{:S(2)}, u32[]{:S(2)}) collective-permute-start(bf16[736,128]{1,0:T(8,128)(2,1)S(1)} %collective-permute-done.3.refs_2_), channel_id=1, source_target_pairs={{0,1},{1,0},{2,3},{3,2},{4,5},{5,4},{6,7},{7,6},{8,9},{9,8},{10,11... | collective-permute-start | bytes 565256 | tf_op jit(solution)/shard_map/ppermute | solution.py:498
  44.5 6.5 %collective-permute-start.8 = (bf16[736,128]{1,0:T(8,128)(2,1)S(1)}, bf16[736,128]{1,0:T(8,128)(2,1)S(1)}, u32[]{:S(2)}, u32[]{:S(2)}) collective-permute-start(bf16[736,128]{1,0:T(8,128)(2,1)S(1)} %collective-permute-done.4.refs_3_), channel_id=1, source_target_pairs={{0,1},{1,0},{2,3},{3,2},{4,5},{5,4},{6,7},{7,6},{8,9},{9,8},{10,11... | collective-permute-start | bytes 565256 | tf_op jit(solution)/shard_map/ppermute | solution.py:498
  47.1 9.8 %all-to-all-start.1 = ((f32[8,8,128]{2,1,0:T(8,128)}), f32[8,8,128]{2,1,0:T(8,128)S(1)}, u32[]{:S(2)}, u32[]{:S(2)}) async-start(f32[8,8,128]{2,1,0:T(8,128)} %get-tuple-element.45), calls=%async_computation.1 | async-start | bytes 65536 | tf_op jit(solution)/shard_map/all_to_all | solution.py:505
  57.6 21.5 %all-to-all-start.2 = ((bf16[8,256,128]{2,1,0:T(8,128)(2,1)}), bf16[8,256,128]{2,1,0:T(8,128)(2,1)S(1)}, u32[]{:S(2)}, u32[]{:S(2)}) async-start(bf16[8,256,128]{2,1,0:T(8,128)(2,1)} %add_sums.1), calls=%async_computation.2 | async-start | bytes 1048576 | tf_op jit(solution)/shard_map/all_to_all | solution.py:536
  79.6 5.9 %collective-permute-start.11 = (f32[224,128]{1,0:T(8,128)S(1)}, f32[224,128]{1,0:T(8,128)S(1)}, u32[]{:S(2)}, u32[]{:S(2)}) collective-permute-start(f32[224,128]{1,0:T(8,128)S(1)} %get-tuple-element.54.refs_0_), channel_id=1, source_target_pairs={{0,192},{64,0},{128,64},{192,128},{1,193},{65,1},{129,65},{193,129... | collective-permute-start | bytes 344072 | tf_op jit(solution)/shard_map/ppermute | solution.py:548
  82.3 5.5 %collective-permute-start.10 = (f32[224,128]{1,0:T(8,128)S(1)}, f32[224,128]{1,0:T(8,128)S(1)}, u32[]{:S(2)}, u32[]{:S(2)}) collective-permute-start(f32[224,128]{1,0:T(8,128)S(1)} %get-tuple-element.54.refs_0_), channel_id=1, source_target_pairs={{0,128},{64,192},{128,0},{192,64},{1,129},{65,193},{129,1},{193,65... | collective-permute-start | bytes 344072 | tf_op jit(solution)/shard_map/ppermute | solution.py:548
  82.8 8.4 %collective-permute-start.9 = (f32[224,128]{1,0:T(8,128)S(1)}, f32[224,128]{1,0:T(8,128)S(1)}, u32[]{:S(2)}, u32[]{:S(2)}) collective-permute-start(f32[224,128]{1,0:T(8,128)S(1)} %get-tuple-element.54.refs_0_), channel_id=1, source_target_pairs={{0,64},{64,128},{128,192},{192,0},{1,65},{65,129},{129,193},{193,1... | collective-permute-start | bytes 344072 | tf_op jit(solution)/shard_map/ppermute | solution.py:548
  91.2 1.6 %collective-permute-start.12 = (f32[224,128]{1,0:T(8,128)S(1)}, f32[224,128]{1,0:T(8,128)S(1)}, u32[]{:S(2)}, u32[]{:S(2)}) collective-permute-start(f32[224,128]{1,0:T(8,128)S(1)} %get-tuple-element.54.refs_0_), channel_id=1, source_target_pairs={{0,1},{1,0},{2,3},{3,2},{4,5},{5,4},{6,7},{7,6},{8,9},{9,8},{10,11... | collective-permute-start | bytes 344072 | tf_op jit(solution)/shard_map/ppermute | solution.py:554
  91.9 1.3 %collective-permute-start.13 = (f32[224,128]{1,0:T(8,128)S(1)}, f32[224,128]{1,0:T(8,128)S(1)}, u32[]{:S(2)}, u32[]{:S(2)}) collective-permute-start(f32[224,128]{1,0:T(8,128)S(1)} %collective-permute-done.9.refs_1_), channel_id=1, source_target_pairs={{0,1},{1,0},{2,3},{3,2},{4,5},{5,4},{6,7},{7,6},{8,9},{9,8},{10,11... | collective-permute-start | bytes 344072 | tf_op jit(solution)/shard_map/ppermute | solution.py:554
  91.9 1.5 %collective-permute-start.14 = (f32[224,128]{1,0:T(8,128)S(1)}, f32[224,128]{1,0:T(8,128)S(1)}, u32[]{:S(2)}, u32[]{:S(2)}) collective-permute-start(f32[224,128]{1,0:T(8,128)S(1)} %collective-permute-done.10.refs_2_), channel_id=1, source_target_pairs={{0,1},{1,0},{2,3},{3,2},{4,5},{5,4},{6,7},{7,6},{8,9},{9,8},{10,11... | collective-permute-start | bytes 344072 | tf_op jit(solution)/shard_map/ppermute | solution.py:554
  92.4 1.3 %collective-permute-start.15 = (f32[224,128]{1,0:T(8,128)S(1)}, f32[224,128]{1,0:T(8,128)S(1)}, u32[]{:S(2)}, u32[]{:S(2)}) collective-permute-start(f32[224,128]{1,0:T(8,128)S(1)} %collective-permute-done.11.refs_3_), channel_id=1, source_target_pairs={{0,1},{1,0},{2,3},{3,2},{4,5},{5,4},{6,7},{7,6},{8,9},{9,8},{10,11... | collective-permute-start | bytes 344072 | tf_op jit(solution)/shard_map/ppermute | solution.py:554

commit v5 on v3

--- a/solution.py
+++ b/solution.py
@@ -22,6 +22,10 @@
 GROWS = FR * ROWS * COLS
 TAPS = 27
 PROWS = 112
+Q = 4
+APART = ASL // NC
+BLOCK = AROWS + NC * GROWS
+TERMS = 16
 HI = lax.Precision.HIGHEST
 
 
@@ -75,7 +79,21 @@
     both = jnp.stack([own_ref[...], other_ref[...]])
     mean, squares = combined(both[:, :, :GROUPS], both[:, :, GROUPS : 2 * GROUPS], CELLS * GC)
     row = jnp.concatenate([mean, squares, jnp.zeros((FR, 2 * GROUPS), F32)], axis=1)
-    out_ref[...] = jnp.broadcast_to(row[None], (NY * NZ, FR, 128))
+    row = jnp.concatenate([row] * 2, axis=0)
+    out_ref[...] = jnp.broadcast_to(row[None], (NY * NZ, 16, 128))
+
+
+def as_terms(values):
+    high = values.astype(BF16).astype(F32)
+    middle = (values - high).astype(BF16).astype(F32)
+    low = values - high - middle
+    upper = jnp.concatenate([high, middle], axis=1)
+    lower = jnp.concatenate([low, jnp.zeros((FR, 128), F32)], axis=1)
+    return jnp.concatenate([upper, lower], axis=0).astype(BF16)
+
+
+def from_terms(terms):
+    return (terms[FR:, :128] + terms[:FR, 128:]) + terms[:FR, :128]
 
 
 def pack_slices(x_ref, g_ref, hp_ref, hn_ref, out_ref):
@@ -122,7 +140,7 @@
 
 def group_terms(st_ref, x_ref, ag_ref, gain_ref, out_ref, sc_ref, mean_ref, inv_ref):
     mean, whole = combined(
-        st_ref[:, :, :GROUPS], st_ref[:, :, GROUPS : 2 * GROUPS], NC * CELLS * GC
+        st_ref[:, :FR, :GROUPS], st_ref[:, :FR, GROUPS : 2 * GROUPS], NC * CELLS * GC
     )
     spread = spread_matrix()
     mean_all = hdot(mean, spread)
@@ -153,44 +171,46 @@
 
 
 def kernel_part(*refs):
-    blocks, (mean_h, inv_h, gain_h, live_h, keep_h, give_h) = refs[:8], refs[8:14]
-    in_ref, mean_ref, inv_ref, gain_ref, live_ref, out_ref, pad_ref, grad_ref, sum_ref, sem = refs[14:]
+    blocks, (mean_h, inv_h, gain_h, live_h, out_h) = refs[:8], refs[8:13]
+    in_ref, mean_ref, inv_ref, gain_ref, live_ref, out_ref, pad_ref, grad_ref, sum_ref, sem = refs[13:]
     y_at, z_at, c_at = lax.axis_index("y"), lax.axis_index("z"), lax.axis_index("c")
-    grads_at = pl.multiple_of(AROWS + c_at * GROWS, 64)
-    copies = []
-    for n in range(8):
-        copies.append(
-            pltpu.make_async_copy(blocks[n].at[:AROWS], in_ref.at[n, :AROWS], sem.at[2 * n])
-        )
-        copies.append(
-            pltpu.make_async_copy(
-                blocks[n].at[pl.ds(grads_at, GROWS)], in_ref.at[n, AROWS:], sem.at[2 * n + 1]
-            )
-        )
-    for n, (src, dst) in enumerate(
-        ((mean_h, mean_ref), (inv_h, inv_ref), (gain_h, gain_ref), (live_h, live_ref))
-    ):
-        copies.append(pltpu.make_async_copy(src, dst, sem.at[16 + n]))
+    pairs = [(blocks[n], in_ref.at[n]) for n in range(8)]
+    pairs += [(mean_h, mean_ref), (inv_h, inv_ref), (gain_h, gain_ref), (live_h, live_ref)]
+    copies = [pltpu.make_async_copy(a, b, sem.at[n]) for n, (a, b) in enumerate(pairs)]
     for copy in copies:
         copy.start()
-    pad_ref[:, 0] = jnp.zeros((3, NY, 6, COLS, 2 * ASL), BF16)
-    for copy in copies[16:]:
+    for copy in copies[8:]:
         copy.wait()
-    lane = lax.broadcasted_iota(jnp.int32, (CH, 2 * ASL), 0)
-    slot = lax.broadcasted_iota(jnp.int32, (CH, 2 * ASL), 1)
-    pick = (lane == y_at * ASL + slot % ASL).astype(F32)
+    width = Q * APART
+    lane = lax.broadcasted_iota(jnp.int32, (CH, width), 0)
+    slot = lax.broadcasted_iota(jnp.int32, (CH, width), 1)
+    channel = GC * ((slot % APART) // 4) + 4 * c_at + slot % 4
+    pick = (lane == y_at * ASL + channel).astype(F32)
     mean2 = hdot(mean_ref[...], pick)
     inv2 = hdot(inv_ref[...], pick)
     gain2 = hdot(gain_ref[...], pick)
     live = live_ref[:, :BSL][:, None, None, :]
-    shape = (3, COLS, 2 * ASL)
-    low = lax.broadcasted_iota(jnp.int32, (1, 2 * ASL), 1) < ASL
-    lowest = lax.broadcasted_iota(jnp.int32, shape, 2) < ASL
+    quarter = lax.broadcasted_iota(jnp.int32, (1, width), 1) // APART
+    centers, scales = [], []
+    for u in range(2):
+        center, scale = mean2[4 * u : 4 * u + 1], inv2[4 * u : 4 * u + 1]
+        for q in range(1, Q):
+            center = jnp.where(quarter == q, mean2[4 * u + q : 4 * u + q + 1], center)
+            scale = jnp.where(quarter == q, inv2[4 * u + q : 4 * u + q + 1], scale)
+        centers.append(center)
+        scales.append(scale * gain2)
+    lane = lax.broadcasted_iota(jnp.int32, (2 * ASL, width), 0)
+    slot = lax.broadcasted_iota(jnp.int32, (2 * ASL, width), 1)
+    channel = GC * ((slot % APART) // 4) + 4 * c_at + slot % 4
+    chosen = [
+        (lane == (slot // APART - 2 * half) * ASL + channel).astype(BF16) for half in range(2)
+    ]
+    shape = (3, COLS, width)
+    place = lax.broadcasted_iota(jnp.int32, shape, 2) // APART
     row = lax.broadcasted_iota(jnp.int32, shape, 0)
     block = 3 * COLS
     for n in range(8):
-        copies[2 * n].wait()
-        copies[2 * n + 1].wait()
+        copies[n].wait()
         d = n % 4
         y = lax.rem(y_at + NY - d, NY)
         c = c_at if n < 4 else 1 - c_at
@@ -198,67 +218,71 @@
         bottom = (y == NY - 1) & (z_at == NZ - 1) & (c == NC - 1)
         edge = jnp.where(top, 0, jnp.where(bottom, 2, 3))
         inside = (row != edge).astype(F32)
-        before = jnp.zeros(shape, F32)
-        for m in range(FR // 2 + 1):
-            if m < FR // 2:
-                raw = in_ref[n, m * block : (m + 1) * block].astype(F32)
-                center = jnp.where(low, mean2[2 * m : 2 * m + 1], mean2[2 * m + 1 : 2 * m + 2])
-                scale = jnp.where(low, inv2[2 * m : 2 * m + 1], inv2[2 * m + 1 : 2 * m + 2])
-                gated = (raw - center) * scale * gain2
-                act = (gated * jax.nn.sigmoid(gated)).reshape(shape) * inside
-            else:
-                act = jnp.zeros(shape, F32)
-            turned = pltpu.roll(act, ASL, 2)
-            odd = jnp.where(lowest, before, turned)
-            before = turned
+        acts = []
+        for u in range(2):
+            at = 2 * u * block
+            raw = jnp.dot(
+                in_ref[n, at : at + block], chosen[0], preferred_element_type=F32
+            ) + jnp.dot(
+                in_ref[n, at + block : at + 2 * block], chosen[1], preferred_element_type=F32
+            )
+            gated = (raw - centers[u]) * scales[u]
+            acts.append((gated * jax.nn.sigmoid(gated)).reshape(shape) * inside)
+        a, b = acts
+        a1, a2, b1 = pltpu.roll(a, 32, 2), pltpu.roll(a, 64, 2), pltpu.roll(b, 32, 2)
+        b2 = pltpu.roll(b, 64, 2)
+        frames = [
+            jnp.where(place < 2, 0.0, a2),
+            jnp.where(place < 1, 0.0, a1),
+            a,
+            pltpu.roll(a, 96, 2),
+            jnp.where(place < 2, a2, b2),
+            jnp.where(place < 1, a1, b1),
+            b,
+            pltpu.roll(b, 96, 2),
+        ]
+        for f in range(FR):
             for k in range(3):
-                if m < FR // 2:
-                    pad_ref[k, 2 * m + 2, d, pl.ds(3 * c, 3)] = shifted(act, k).astype(BF16)
-                pad_ref[k, 2 * m + 1, d, pl.ds(3 * c, 3)] = shifted(odd, k).astype(BF16)
-        cells = in_ref[n, AROWS:].astype(F32).reshape(FR, ROWS, COLS, BSL) * live
-        grad_ref[:, d, pl.ds(2 * c, 2)] = cells
-    turned_grad = grad_ref[...].reshape(FR * NY * 4 * COLS, BSL).T.astype(BF16)
-    sum_ref[:, :, 4 * TAPS :] = jnp.zeros((NC, NZ, PROWS - 4 * TAPS, BSL), F32)
-    for j in range(3):
-        for k in range(3):
-            early = pad_ref[k, 0:FR, :, j : j + 4].reshape(FR * NY * 4 * COLS, 2 * ASL)
-            late = pad_ref[k, 2 : 2 + FR, :, j : j + 4].reshape(FR * NY * 4 * COLS, 2 * ASL)
-            product = jnp.dot(
-                turned_grad,
-                jnp.concatenate([early, late], axis=1),
-                preferred_element_type=F32,
-            ).T
+                pad_ref[k, f, d, pl.ds(3 * c, 3)] = shifted(frames[f], k).astype(BF16)
+        for h in range(NC):
+            at = AROWS + h * GROWS
+            cells = in_ref[n, at : at + GROWS].astype(F32).reshape(FR, ROWS, COLS, BSL) * live
+            grad_ref[:, d, pl.ds(2 * c, 2), :, h * BSL : (h + 1) * BSL] = cells
+    cells = FR * NY * 4 * COLS
+    turned_grad = grad_ref[...].reshape(cells, CH).T.astype(BF16)
+    sum_ref[:, 4 * TAPS :] = jnp.zeros((NZ, PROWS - 4 * TAPS, CH), F32)
+    combos = [(j, k) for j in range(3) for k in range(3)]
+    for first in range(0, 9, 2):
+        group = combos[first : first + 2]
+        windows = [pad_ref[k, :, :, j : j + 4].reshape(cells, width) for j, k in group]
+        window = windows[0] if len(windows) == 1 else jnp.concatenate(windows, axis=1)
+        product = jnp.dot(turned_grad, window, preferred_element_type=F32).T
+        for n, (j, k) in enumerate(group):
             for i in range(3):
                 tap = (i * 3 + j) * 3 + k
-                piece = product[i * ASL : (i + 1) * ASL].reshape(NZ, ASL // NZ, BSL)
-                sum_ref[0, :, tap * 4 : tap * 4 + 4] = piece[:, :4]
-                sum_ref[1, :, tap * 4 : tap * 4 + 4] = piece[:, 4:]
+                at = n * width + i * APART
+                piece = product[at : at + APART].reshape(NZ, 4, CH)
+                sum_ref[:, tap * 4 : tap * 4 + 4] = piece
     out_ref[...] = sum_ref[...].astype(BF16)
-    keep = pltpu.make_async_copy(out_ref.at[c_at], keep_h, sem.at[0])
-    give = pltpu.make_async_copy(out_ref.at[1 - c_at], give_h, sem.at[1])
-    give.start()
-    keep.start()
-    give.wait()
-    keep.wait()
-
-
-def merge_parts(keep_ref, got_ref, b_ref, out_ref):
-    first = lax.axis_index("c") == 0
-    keep, got = keep_ref[...], got_ref[...]
-    out_ref[:, :PROWS] = jnp.where(first, keep, got)
-    out_ref[:, PROWS : 2 * PROWS] = jnp.where(first, got, keep)
-    sums = jnp.sum(b_ref[...], axis=0)
-    high = sums.astype(BF16).astype(F32)
-    middle = (sums - high).astype(BF16).astype(F32)
-    low = sums - high - middle
-    terms = jnp.concatenate([high, middle, low, jnp.zeros((FR, 128), F32)], axis=0).astype(BF16)
-    out_ref[:, 2 * PROWS :] = jnp.broadcast_to(terms[None], (NZ, 4 * FR, 128))
+    copy = pltpu.make_async_copy(out_ref, out_h.at[:, :PROWS], sem.at[0])
+    copy.start()
+    copy.wait()
+
+
+def add_sums(part_h, b_h, out_h, b_ref, out_ref, sem):
+    copy = pltpu.make_async_copy(b_h, b_ref, sem.at[0])
+    copy.start()
+    copy.wait()
+    terms = as_terms(jnp.sum(b_ref[...], axis=0))
+    out_ref[...] = jnp.broadcast_to(terms[None], (NZ, TERMS, CH))
+    copy = pltpu.make_async_copy(out_ref, out_h.at[:, PROWS:], sem.at[1])
+    copy.start()
+    copy.wait()
 
 
 def sum_rows(in_ref, out_ref, sums_ref):
     total = jnp.sum(in_ref[...].astype(F32), axis=0)
-    at = 2 * PROWS
-    sums = (total[at + 2 * FR : at + 3 * FR] + total[at + FR : at + 2 * FR]) + total[at : at + FR]
+    sums = from_terms(total[PROWS:])
     sums_ref[...] = sums
     fold_at = lax.broadcasted_iota(jnp.int32, (GROUPS, CH), 0)
     fold_lane = lax.broadcasted_iota(jnp.int32, (GROUPS, CH), 1)
@@ -266,8 +290,7 @@
     row = lax.broadcasted_iota(jnp.int32, (FR, CH), 0)
     lane = lax.broadcasted_iota(jnp.int32, (FR, CH), 1)
     gain = jnp.sum(jnp.where(lane // GROUPS == row, wide, 0.0), axis=0, keepdims=True)
-    out_ref[:, :BSL] = total[:PROWS]
-    out_ref[:, BSL:] = total[PROWS : 2 * PROWS]
+    out_ref[...] = total[:PROWS]
     out_ref[4 * TAPS : 4 * TAPS + 1] = gain
 
 
@@ -353,20 +376,21 @@
     return tuple(jax.ShapeDtypeStruct(s, d) for s, d in outs)
 
 
-def call(body, outs, args, specs, scratch, flops=0, limit=32):
+def call(body, outs, args, specs, scratch, flops=0, limit=32, aliases={}):
     return pl.pallas_call(
         body,
         out_shape=shapes(outs),
         in_specs=specs,
         out_specs=tuple(HBM for _ in outs),
         scratch_shapes=list(scratch),
+        input_output_aliases=aliases,
         compiler_params=pltpu.CompilerParams(vmem_limit_bytes=limit * 2**20),
         cost_estimate=pl.CostEstimate(flops=flops, bytes_accessed=2**20, transcendentals=0),
         name=body.__name__,
     )(*args)
 
 
-def run(body, outs, args, scratch=(), late=None, smem=(), flops=0):
+def run(body, outs, args, scratch=(), late=None, smem=(), flops=0, rows={}):
     count, outputs = len(args), len(outs)
     moved = [at for at in range(count) if at not in smem]
 
@@ -377,7 +401,10 @@
         results, rest = rest[:outputs], rest[outputs:]
         sem, extra = rest[0], rest[1:]
         copies = [
-            pltpu.make_async_copy(ins[at], buffers[n], sem.at[n]) for n, at in enumerate(moved)
+            pltpu.make_async_copy(
+                ins[at].at[rows[at][0] : rows[at][1]] if at in rows else ins[at], buffers[n], sem.at[n]
+            )
+            for n, at in enumerate(moved)
         ]
         for copy in copies:
             copy.start()
@@ -401,14 +428,21 @@
 
     kernel.__name__ = body.__name__
     specs = [SMEM if at in smem else HBM for at in range(count)]
-    buffers = [pltpu.VMEM(args[at].shape, args[at].dtype) for at in moved]
+    buffers = []
+    for at in moved:
+        shape = args[at].shape
+        if at in rows:
+            shape = (rows[at][1] - rows[at][0],) + shape[1:]
+        buffers.append(pltpu.VMEM(shape, args[at].dtype))
     buffers += [pltpu.VMEM(s, d) for s, d in outs]
     buffers += [pltpu.SemaphoreType.DMA((len(moved) + outputs,))]
     return call(kernel, outs, args, specs, buffers + list(scratch), flops)
 
 
-def pack_body(x_h, g_h, hp_h, hn_h, out0, out1, out2, out3, x_ref, g_ref, hp_ref, hn_ref, buf, sem):
-    pairs = ((x_h, x_ref), (g_h, g_ref), (hp_h, hp_ref), (hn_h, hn_ref))
+def pack_body(*refs):
+    sources, outs = refs[:4], refs[4:8]
+    x_ref, g_ref, hp_ref, hn_ref, buf, sem = refs[8:]
+    pairs = tuple(zip(sources, (x_ref, g_ref, hp_ref, hn_ref)))
     copies = [pltpu.make_async_copy(a, b, sem.at[n]) for n, (a, b) in enumerate(pairs)]
     for copy in copies:
         copy.start()
@@ -418,7 +452,7 @@
     y_at = lax.axis_index("y")
     copies = [
         pltpu.make_async_copy(buf.at[lax.rem(y_at + d, NY)], out, sem.at[4 + d])
-        for d, out in enumerate((out0, out1, out2, out3))
+        for d, out in enumerate(outs)
     ]
     for copy in copies:
         copy.start()
@@ -445,12 +479,12 @@
         smem=(2,),
     )
     other = lax.ppermute(stats, "c", swap)
+    (stats,) = run(pair_sums, [((NY * NZ, 16, 128), F32)], (stats, other))
+    stats, up, dn = lax.optimization_barrier((stats, up, dn))
     hp = lax.ppermute(dn, space, [(i, i + 1) for i in range(SPACE - 1)])
     hn = lax.ppermute(up, space, [(i + 1, i) for i in range(SPACE - 1)])
-    (stats,) = run(pair_sums, [((NY * NZ, FR, 128), F32)], (stats, other))
-    stats, hp, hn = lax.optimization_barrier((stats, hp, hn))
     stats = lax.all_to_all(stats, ("y", "z"), 0, 0)
-    block = (AROWS + NC * GROWS, BSL)
+    block = (BLOCK, BSL)
     packed = call(
         pack_body,
         [(block, BF16)] * NY,
@@ -480,29 +514,34 @@
         (stats, x, act_grad, gain),
     )
     terms = lax.all_to_all(terms, ("y", "c"), 0, 0)
-    part = (NZ, PROWS, BSL)
-    keep, give = call(
+    part = (NZ, PROWS, CH)
+    whole_part = (NZ, PROWS + TERMS, CH)
+    (partial,) = call(
         kernel_part,
-        [(part, BF16)] * 2,
+        [(whole_part, BF16)],
         (*near, *far, mean, inv, gain, live),
         [HBM] * 12,
         [
-            pltpu.VMEM((8, AROWS + GROWS, BSL), BF16),
+            pltpu.VMEM((8, BLOCK, BSL), BF16),
             pltpu.VMEM(wide, F32),
             pltpu.VMEM(wide, F32),
             pltpu.VMEM((1, CH), F32),
             pltpu.VMEM(wide, F32),
-            pltpu.VMEM((NC,) + part, BF16),
-            pltpu.VMEM((3, FR + 2, NY, 6, COLS, 2 * ASL), BF16),
-            pltpu.VMEM((FR, NY, 4, COLS, BSL), F32),
-            pltpu.VMEM((NC,) + part, F32),
-            dma((20,)),
+            pltpu.VMEM(part, BF16),
+            pltpu.VMEM((3, FR, NY, 6, COLS, Q * APART), BF16),
+            pltpu.VMEM((FR, NY, 4, COLS, CH), F32),
+            pltpu.VMEM(part, F32),
+            dma((12,)),
         ],
         flops=conv_flops,
     )
-    got = lax.ppermute(give, "c", swap)
-    (merged,) = run(
-        merge_parts, [((NZ, 2 * PROWS + 4 * FR, BSL), BF16)], (keep, got, terms)
+    (merged,) = call(
+        add_sums,
+        [(whole_part, BF16)],
+        (partial, terms),
+        [HBM] * 2,
+        [pltpu.VMEM((NY * NC, FR, 128), F32), pltpu.VMEM((NZ, TERMS, CH), BF16), dma((2,))],
+        aliases={0: 0},
     )
     merged, late_mean = lax.optimization_barrier((merged, mean))
     merged = lax.all_to_all(merged, "z", 0, 0)
@@ -516,7 +555,7 @@
     )
     merged, block_output = lax.optimization_barrier((merged, block_output))
     rows, sums = run(sum_rows, [((PROWS, CH), F32), ((FR, 128), F32)], (merged,))
-    others = [
+    others = [rows] + [
         lax.ppermute(rows, "x", [(i, (i + d) % NX) for i in range(NX)]) for d in range(1, NX)
     ]
     (input_grad,) = run(
@@ -525,7 +564,7 @@
     kernel_grad, gain_grad = call(
         sum_clips,
         [((TAPS, 4, CH), F32), ((1, CH), F32)],
-        (rows, *others),
+        others,
         [HBM] * 4,
         [
             pltpu.VMEM((NX, PROWS, CH), F32),

time: 90.5 us -> 99.4 us (1.098)
  starting transfers between devices: 31.5 us -> 40.4 us
  blocking collectives: 7.4 us -> 0 us
  waiting for transfers between devices: 23 us -> 29.3 us
  Pallas kernels: 25.8 us -> 27.6 us
    all_to_all x1 -> x0, blocking collectives: 7.4 us -> none  [local(): terms = lax.all_to_all(terms, ('y', 'c'), 0, 0)]
    ppermute x3, waiting for transfers between devices: 0.01 us -> 4.26 us  [local(): lax.ppermute(packed[d], 'y', [(i, (i + d) % NY) for i in range(NY)])]
    all_to_all x1, waiting for transfers between devices: 4.09 us -> 0.01 us  [local(): stats = lax.all_to_all(stats, ('y', 'z'), 0, 0)]
    all_to_all x0 -> x1, starting transfers between devices: none -> 4.01 us  [local(): terms = lax.all_to_all(terms, ('y', 'c'), 0, 0)]
    ppermute x1, starting transfers between devices: 0.09 us -> 3.33 us  [local(): other = lax.ppermute(stats, 'c', swap)]
    ppermute x3, waiting for transfers between devices: 3.21 us -> 5.72 us  [local(): lax.ppermute(rows, 'x', [(i, (i + d) % NX) for i in range(NX)])]
    ppermute x4, starting transfers between devices: 1.53 us -> 3.97 us  [local(): far = [lax.ppermute(a, 'c', swap) for a in near]]
    ppermute x1 -> x0, starting transfers between devices: 2.05 us -> none  [local(): got = lax.ppermute(give, 'c', swap)]
  transfers between devices with their start and end apart: 16 -> 16, of which waited for: 6 -> 8; matrix products, arithmetic and copies ran while one was open for 0% -> 0% of each run, Pallas kernels for 14% -> 23%
where the time goes in v5:
time: 99.4 us; the launch traced here: 98.8 us
  starting transfers between devices  40.4 us (41%)
  waiting for transfers between devices  29.3 us (29%)
  Pallas kernels  27.6 us (28%)
  between operations  1.59 us (2%)
    pallas_call x11, Pallas kernels, call(): pl.pallas_call(body, out_shape=shapes(outs), in_specs=specs, out_specs=tu...  27.6 us
    all_to_all x1, waiting for transfers between devices, local(): merged = lax.all_to_all(merged, 'z', 0, 0)  13.8 us
    all_to_all x1, starting transfers between devices, local(): stats = lax.all_to_all(stats, ('y', 'z'), 0, 0)  9.48 us
    ppermute x3, waiting for transfers between devices, local(): lax.ppermute(rows, 'x', [(i, (i + d) % NX) for i in range(NX)])  5.72 us
    all_to_all x1, starting transfers between devices, local(): merged = lax.all_to_all(merged, 'z', 0, 0)  5.2 us
    ppermute x3, starting transfers between devices, local(): lax.ppermute(packed[d], 'y', [(i, (i + d) % NY) for i in range(NY)])  4.84 us
    ppermute x3, waiting for transfers between devices, local(): lax.ppermute(packed[d], 'y', [(i, (i + d) % NY) for i in range(NY)])  4.26 us
    all_to_all x1, starting transfers between devices, local(): terms = lax.all_to_all(terms, ('y', 'c'), 0, 0)  4.01 us
  transfers between devices with their start and end apart: 16, of which 8 were waited for; matrix products, arithmetic and copies ran while one was open for 0% of the time, Pallas kernels for 23%

profile of v5, /device:TPU:1, one launch (start us, length us, event | category | flops | bytes accessed | tf_op | source)
XLA Modules:
  0.0 98.8 jit_solution(18251976262992462236)
XLA Ops:
  1.3 2.0 %edges_and_sums.1 = (bf16[2,8,16,256]{3,2,1,0:T(8,128)(2,1)S(1)}, bf16[2,8,16,256]{3,2,1,0:T(8,128)(2,1)S(1)}, f32[8,128]{1,0:T(8,128)S(1)}, f32[8,256]{1,0:T(8,128)S(1)}) custom-call(bf16[8,2,16,256]{3,2,1,0:T(8,128)(2,1)} %bitcast.7, bf16[8,2,16,256]{3,2,1,0:T(8,128)(2,1)} %bitcast.12, s32[1]{0:T(128)S(6)} %copy.11.refs_2_), custom_call_target="tpu_custom_call" | custom-call | bytes 1048576 | tf_op jit(solution)/shard_map/edges_and_sums/pallas_call | solution.py:380
  3.3 3.3 %collective-permute-start = (f32[8,128]{1,0:T(8,128)S(1)}, f32[8,128]{1,0:T(8,128)S(1)}, u32[]{:S(2)}, u32[]{:S(2)}) collective-permute-start(f32[8,128]{1,0:T(8,128)S(1)} %get-tuple-element.27.refs_0_), channel_id=1, source_target_pairs={{0,1},{1,0},{2,3},{3,2},{4,5},{5,4},{6,7},{7,6},{8,9},{9,8},{10,11... | collective-permute-start | bytes 12296 | tf_op jit(solution)/shard_map/ppermute | solution.py:481
  8.3 9.5 %all-to-all-start = ((f32[32,16,128]{2,1,0:T(8,128)}), f32[32,16,128]{2,1,0:T(8,128)S(1)}, u32[]{:S(2)}, u32[]{:S(2)}) async-start(f32[32,16,128]{2,1,0:T(8,128)} %pair_sums.1), calls=%async_computation | async-start | bytes 524288 | tf_op jit(solution)/shard_map/all_to_all | solution.py:486
  17.8 3.9 %collective-permute-start.1 = (bf16[2,8,16,256]{3,2,1,0:T(8,128)(2,1)S(1)}, bf16[2,8,16,256]{3,2,1,0:T(8,128)(2,1)S(1)}, u32[]{:S(2)}, u32[]{:S(2)}) collective-permute-start(bf16[2,8,16,256]{3,2,1,0:T(8,128)(2,1)S(1)} %get-tuple-element.30), channel_id=1, source_target_pairs={{0,1},{1,2},{2,3},{3,4},{4,5},{5,6},{6,7},{7,8},{8,9},{9,10},{10,1... | collective-permute-start | bytes 393224 | tf_op jit(solution)/shard_map/ppermute | solution.py:484
  21.7 1.9 %collective-permute-start.2 = (bf16[2,8,16,256]{3,2,1,0:T(8,128)(2,1)S(1)}, bf16[2,8,16,256]{3,2,1,0:T(8,128)(2,1)S(1)}, u32[]{:S(2)}, u32[]{:S(2)}) collective-permute-start(bf16[2,8,16,256]{3,2,1,0:T(8,128)(2,1)S(1)} %get-tuple-element.31), channel_id=1, source_target_pairs={{1,0},{2,1},{3,2},{4,3},{5,4},{6,5},{7,6},{8,7},{9,8},{10,9},{11,1... | collective-permute-start | bytes 393224 | tf_op jit(solution)/shard_map/ppermute | solution.py:485
  24.6 3.7 %collective-permute-done.2.refs_3_.refs_2_ = bf16[2,8,16,256]{3,2,1,0:T(8,128)(2,1)S(1)} collective-permute-done((bf16[2,8,16,256]{3,2,1,0:T(8,128)(2,1)S(1)}, bf16[2,8,16,256]{3,2,1,0:T(8,128)(2,1)S(1)}, u32[]{:S(2)}, u32[]{:S(2)}) %collective-permute-start.2) | collective-permute-done | bytes 131104 | tf_op jit(solution)/shard_map/ppermute | solution.py:485
  28.3 2.2 %pack_body.1 = (bf16[704,128]{1,0:T(8,128)(2,1)S(1)}, bf16[704,128]{1,0:T(8,128)(2,1)S(1)}, bf16[704,128]{1,0:T(8,128)(2,1)S(1)}, bf16[704,128]{1,0:T(8,128)(2,1)S(1)}) custom-call(bf16[8,2,16,256]{3,2,1,0:T(8,128)(2,1)} %bitcast.8, bf16[8,2,16,256]{3,2,1,0:T(8,128)(2,1)} %bitcast.13, bf16[2,8,16,256]{3,2,1,0:T(8,128)(2,1)S(1)} %collective-permute-done.1.refs_2_.refs_1_, ...), custom_call_target="tpu_custom_call" | custom-call | bytes 1048576 | tf_op jit(solution)/shard_map/pack_body/pallas_call | solution.py:380
  30.5 1.3 %collective-permute-start.3 = (bf16[704,128]{1,0:T(8,128)(2,1)S(1)}, bf16[704,128]{1,0:T(8,128)(2,1)S(1)}, u32[]{:S(2)}, u32[]{:S(2)}) collective-permute-start(bf16[704,128]{1,0:T(8,128)(2,1)S(1)} %get-tuple-element.33), channel_id=1, source_target_pairs={{0,16},{16,32},{32,48},{48,0},{1,17},{17,33},{33,49},{49,1},{2,18}... | collective-permute-start | bytes 540680 | tf_op jit(solution)/shard_map/ppermute | solution.py:498
  31.8 2.4 %collective-permute-start.4 = (bf16[704,128]{1,0:T(8,128)(2,1)S(1)}, bf16[704,128]{1,0:T(8,128)(2,1)S(1)}, u32[]{:S(2)}, u32[]{:S(2)}) collective-permute-start(bf16[704,128]{1,0:T(8,128)(2,1)S(1)} %get-tuple-element.34), channel_id=1, source_target_pairs={{0,32},{16,48},{32,0},{48,16},{1,33},{17,49},{33,1},{49,17},{2,34}... | collective-permute-start | bytes 540680 | tf_op jit(solution)/shard_map/ppermute | solution.py:498
  35.4 1.5 %collective-permute-start.6 = (bf16[704,128]{1,0:T(8,128)(2,1)S(1)}, bf16[704,128]{1,0:T(8,128)(2,1)S(1)}, u32[]{:S(2)}, u32[]{:S(2)}) collective-permute-start(bf16[704,128]{1,0:T(8,128)(2,1)S(1)} %get-tuple-element.32.refs_0_), channel_id=1, source_target_pairs={{0,1},{1,0},{2,3},{3,2},{4,5},{5,4},{6,7},{7,6},{8,9},{9,8},{10,11... | collective-permute-start | bytes 540680 | tf_op jit(solution)/shard_map/ppermute | solution.py:500
  38.9 3.2 %collective-permute-done.4.refs_2_ = bf16[704,128]{1,0:T(8,128)(2,1)S(1)} collective-permute-done((bf16[704,128]{1,0:T(8,128)(2,1)S(1)}, bf16[704,128]{1,0:T(8,128)(2,1)S(1)}, u32[]{:S(2)}, u32[]{:S(2)}) %collective-permute-start.4) | collective-permute-done | bytes 180256 | tf_op jit(solution)/shard_map/ppermute | solution.py:498
  42.1 1.5 %collective-permute-start.8 = (bf16[704,128]{1,0:T(8,128)(2,1)S(1)}, bf16[704,128]{1,0:T(8,128)(2,1)S(1)}, u32[]{:S(2)}, u32[]{:S(2)}) collective-permute-start(bf16[704,128]{1,0:T(8,128)(2,1)S(1)} %collective-permute-done.4.refs_2_), channel_id=1, source_target_pairs={{0,1},{1,0},{2,3},{3,2},{4,5},{5,4},{6,7},{7,6},{8,9},{9,8},{10,11... | collective-permute-start | bytes 540680 | tf_op jit(solution)/shard_map/ppermute | solution.py:500
  43.6 3.5 %backward_conv.1.refs_2_ = f32[256,256]{1,0:T(8,128)S(1)} custom-call(bf16[8,2,16,256]{3,2,1,0:T(8,128)(2,1)} %bitcast.14, bf16[2,8,16,256]{3,2,1,0:T(8,128)(2,1)S(1)} %collective-permute-done.1.refs_2_.refs_1_, bf16[2,8,16,256]{3,2,1,0:T(8,128)(2,1)S(1)} %collective-permute-done.2.refs_3_.refs_2_, bf16[27,256,256]{2,1,0:T(8,128)(2,1)} %refs_6_.1, ...), custom_call_target="tpu_custom_call" | custom-call | bytes 1048576 | tf_op jit(solution)/shard_map/backward_conv/pallas_call | solution.py:380
  47.2 2.5 %group_terms.1 = (f32[8,8,128]{2,1,0:T(8,128)}, f32[8,32,256]{2,1,0:T(8,128)S(1)}, f32[8,256]{1,0:T(8,128)S(1)}, f32[8,256]{1,0:T(8,128)S(1)}) custom-call(f32[32,16,128]{2,1,0:T(8,128)S(1)} %all-to-all-done.refs_0_, bf16[8,2,16,256]{3,2,1,0:T(8,128)(2,1)} %bitcast.9, f32[256,256]{1,0:T(8,128)S(1)} %backward_conv.1.refs_2_, f32[1,256]{1,0:T(1,128)} %bitcast.17), custom_call_target="tpu_custom_call" | custom-call | bytes 1048576 | tf_op jit(solution)/shard_map/group_terms/pallas_call | solution.py:380
  49.7 4.0 %all-to-all-start.1 = ((f32[8,8,128]{2,1,0:T(8,128)}), f32[8,8,128]{2,1,0:T(8,128)S(1)}, u32[]{:S(2)}, u32[]{:S(2)}) async-start(f32[8,8,128]{2,1,0:T(8,128)} %get-tuple-element.40), calls=%async_computation.1 | async-start | bytes 65536 | tf_op jit(solution)/shard_map/all_to_all | solution.py:516
  53.7 7.8 %kernel_part.1.part_h = bf16[8,128,256]{2,1,0:T(8,128)(2,1)} custom-call(bf16[704,128]{1,0:T(8,128)(2,1)S(1)} %get-tuple-element.32.refs_0_, bf16[704,128]{1,0:T(8,128)(2,1)S(1)} %collective-permute-done.3.refs_1_, bf16[704,128]{1,0:T(8,128)(2,1)S(1)} %collective-permute-done.4.refs_2_, bf16[704,128]{1,0:T(8,128)(2,1)S(1)} %collective-permute-done.5.refs_3_, ...), custom_call_target="tpu_custom_call" | custom-call | flops 7247757312 | bytes 1048576 | tf_op jit(solution)/shard_map/kernel_part/pallas_call | solution.py:380
  62.2 5.2 %all-to-all-start.2 = ((bf16[8,128,256]{2,1,0:T(8,128)(2,1)}), bf16[8,128,256]{2,1,0:T(8,128)(2,1)S(1)}, u32[]{:S(2)}, u32[]{:S(2)}) async-start(bf16[8,128,256]{2,1,0:T(8,128)(2,1)} %add_sums.1), calls=%async_computation.2 | async-start | bytes 1048576 | tf_op jit(solution)/shard_map/all_to_all | solution.py:547
  67.4 4.2 %forward_conv.1 = bf16[8,2,16,256]{3,2,1,0:T(8,128)(2,1)} custom-call(bf16[8,2,16,256]{3,2,1,0:T(8,128)(2,1)} %bitcast.10, bf16[2,8,16,256]{3,2,1,0:T(8,128)(2,1)S(1)} %collective-permute-done.1.refs_2_.refs_1_, bf16[2,8,16,256]{3,2,1,0:T(8,128)(2,1)S(1)} %collective-permute-done.2.refs_3_.refs_2_, f32[8,256]{1,0:T(8,128)S(1)} %get-tuple-element.42.refs_8_.refs_3_.refs_4_, ...), custom_call_target="tpu_custom_call" | custom-call | flops 7247757312 | bytes 1048576 | tf_op jit(solution)/shard_map/forward_conv/pallas_call | solution.py:380
  71.6 13.8 %all-to-all-done.2.refs_0_ = bf16[8,128,256]{2,1,0:T(8,128)(2,1)S(1)} async-done(((bf16[8,128,256]{2,1,0:T(8,128)(2,1)}), bf16[8,128,256]{2,1,0:T(8,128)(2,1)S(1)}, u32[]{:S(2)}, u32[]{:S(2)}) %all-to-all-start.2) | async-done | bytes 524320 | tf_op jit(solution)/shard_map/all_to_all | solution.py:547
  85.9 2.6 %collective-permute-start.12 = (f32[112,256]{1,0:T(8,128)S(1)}, f32[112,256]{1,0:T(8,128)S(1)}, u32[]{:S(2)}, u32[]{:S(2)}) collective-permute-start(f32[112,256]{1,0:T(8,128)S(1)} %get-tuple-element.47.own_h), channel_id=1, source_target_pairs={{0,192},{64,0},{128,64},{192,128},{1,193},{65,1},{129,65},{193,129... | collective-permute-start | bytes 344072 | tf_op jit(solution)/shard_map/ppermute | solution.py:559
  89.6 2.0 %finish_input.1 = bf16[8,2,16,256]{3,2,1,0:T(8,128)(2,1)} custom-call(f32[8,128]{1,0:T(8,128)S(1)} %get-tuple-element.45.refs_0_, f32[8,32,256]{2,1,0:T(8,128)S(1)} %get-tuple-element.46.refs_1_, bf16[8,2,16,256]{3,2,1,0:T(8,128)(2,1)} %bitcast.11, bf16[8,2,16,256]{3,2,1,0:T(8,128)(2,1)} %bitcast.15, f32[8,256]{1,0:T(8,128)S(1)} %get-tuple-element.42.refs_8_.refs_3_.refs_4_, ...), custom_call_target="tpu_custom_call" | custom-call | bytes 1048576 | tf_op jit(solution)/shard_map/finish_input/pallas_call | solution.py:380
  91.7 2.1 %collective-permute-done.11.two_h = f32[112,256]{1,0:T(8,128)S(1)} collective-permute-done((f32[112,256]{1,0:T(8,128)S(1)}, f32[112,256]{1,0:T(8,128)S(1)}, u32[]{:S(2)}, u32[]{:S(2)}) %collective-permute-start.11) | collective-permute-done | bytes 114720 | tf_op jit(solution)/shard_map/ppermute | solution.py:559
  93.8 3.6 %collective-permute-done.10.one_h = f32[112,256]{1,0:T(8,128)S(1)} collective-permute-done((f32[112,256]{1,0:T(8,128)S(1)}, f32[112,256]{1,0:T(8,128)S(1)}, u32[]{:S(2)}, u32[]{:S(2)}) %collective-permute-start.10) | collective-permute-done | bytes 114720 | tf_op jit(solution)/shard_map/ppermute | solution.py:559
  97.4 1.3 %sum_clips.1 = (f32[27,4,256]{2,1,0:T(4,128)}, f32[1,256]{1,0:T(1,128)}) custom-call(f32[112,256]{1,0:T(8,128)S(1)} %get-tuple-element.47.own_h, f32[112,256]{1,0:T(8,128)S(1)} %collective-permute-done.10.one_h, f32[112,256]{1,0:T(8,128)S(1)} %collective-permute-done.11.two_h, f32[112,256]{1,0:T(8,128)S(1)} %collective-permute-done.12.three_h), custom_call_target="tpu_custom_call" | custom-call | bytes 1048576 | tf_op jit(solution)/shard_map/sum_clips/pallas_call | solution.py:380
  (19 shorter events, 8.2 us)
Async XLA Ops:
  3.3 4.2 %collective-permute-start = (f32[8,128]{1,0:T(8,128)S(1)}, f32[8,128]{1,0:T(8,128)S(1)}, u32[]{:S(2)}, u32[]{:S(2)}) collective-permute-start(f32[8,128]{1,0:T(8,128)S(1)} %get-tuple-element.27.refs_0_), channel_id=1, source_target_pairs={{0,1},{1,0},{2,3},{3,2},{4,5},{5,4},{6,7},{7,6},{8,9},{9,8},{10,11... | collective-permute-start | bytes 12296 | tf_op jit(solution)/shard_map/ppermute | solution.py:481
  8.3 38.9 %all-to-all-start = ((f32[32,16,128]{2,1,0:T(8,128)}), f32[32,16,128]{2,1,0:T(8,128)S(1)}, u32[]{:S(2)}, u32[]{:S(2)}) async-start(f32[32,16,128]{2,1,0:T(8,128)} %pair_sums.1), calls=%async_computation | async-start | bytes 524288 | tf_op jit(solution)/shard_map/all_to_all | solution.py:486
  17.8 6.8 %collective-permute-start.1 = (bf16[2,8,16,256]{3,2,1,0:T(8,128)(2,1)S(1)}, bf16[2,8,16,256]{3,2,1,0:T(8,128)(2,1)S(1)}, u32[]{:S(2)}, u32[]{:S(2)}) collective-permute-start(bf16[2,8,16,256]{3,2,1,0:T(8,128)(2,1)S(1)} %get-tuple-element.30), channel_id=1, source_target_pairs={{0,1},{1,2},{2,3},{3,4},{4,5},{5,6},{6,7},{7,8},{8,9},{9,10},{10,1... | collective-permute-start | bytes 393224 | tf_op jit(solution)/shard_map/ppermute | solution.py:484
  21.7 6.6 %collective-permute-start.2 = (bf16[2,8,16,256]{3,2,1,0:T(8,128)(2,1)S(1)}, bf16[2,8,16,256]{3,2,1,0:T(8,128)(2,1)S(1)}, u32[]{:S(2)}, u32[]{:S(2)}) collective-permute-start(bf16[2,8,16,256]{3,2,1,0:T(8,128)(2,1)S(1)} %get-tuple-element.31), channel_id=1, source_target_pairs={{1,0},{2,1},{3,2},{4,3},{5,4},{6,5},{7,6},{8,7},{9,8},{10,9},{11,1... | collective-permute-start | bytes 393224 | tf_op jit(solution)/shard_map/ppermute | solution.py:485
  30.5 7.3 %collective-permute-start.3 = (bf16[704,128]{1,0:T(8,128)(2,1)S(1)}, bf16[704,128]{1,0:T(8,128)(2,1)S(1)}, u32[]{:S(2)}, u32[]{:S(2)}) collective-permute-start(bf16[704,128]{1,0:T(8,128)(2,1)S(1)} %get-tuple-element.33), channel_id=1, source_target_pairs={{0,16},{16,32},{32,48},{48,0},{1,17},{17,33},{33,49},{49,1},{2,18}... | collective-permute-start | bytes 540680 | tf_op jit(solution)/shard_map/ppermute | solution.py:498
  31.8 10.3 %collective-permute-start.4 = (bf16[704,128]{1,0:T(8,128)(2,1)S(1)}, bf16[704,128]{1,0:T(8,128)(2,1)S(1)}, u32[]{:S(2)}, u32[]{:S(2)}) collective-permute-start(bf16[704,128]{1,0:T(8,128)(2,1)S(1)} %get-tuple-element.34), channel_id=1, source_target_pairs={{0,32},{16,48},{32,0},{48,16},{1,33},{17,49},{33,1},{49,17},{2,34}... | collective-permute-start | bytes 540680 | tf_op jit(solution)/shard_map/ppermute | solution.py:498
  34.2 9.4 %collective-permute-start.5 = (bf16[704,128]{1,0:T(8,128)(2,1)S(1)}, bf16[704,128]{1,0:T(8,128)(2,1)S(1)}, u32[]{:S(2)}, u32[]{:S(2)}) collective-permute-start(bf16[704,128]{1,0:T(8,128)(2,1)S(1)} %get-tuple-element.35), channel_id=1, source_target_pairs={{0,48},{16,0},{32,16},{48,32},{1,49},{17,1},{33,17},{49,33},{2,50}... | collective-permute-start | bytes 540680 | tf_op jit(solution)/shard_map/ppermute | solution.py:498
  35.4 18.3 %collective-permute-start.6 = (bf16[704,128]{1,0:T(8,128)(2,1)S(1)}, bf16[704,128]{1,0:T(8,128)(2,1)S(1)}, u32[]{:S(2)}, u32[]{:S(2)}) collective-permute-start(bf16[704,128]{1,0:T(8,128)(2,1)S(1)} %get-tuple-element.32.refs_0_), channel_id=1, source_target_pairs={{0,1},{1,0},{2,3},{3,2},{4,5},{5,4},{6,7},{7,6},{8,9},{9,8},{10,11... | collective-permute-start | bytes 540680 | tf_op jit(solution)/shard_map/ppermute | solution.py:500
  37.9 15.8 %collective-permute-start.7 = (bf16[704,128]{1,0:T(8,128)(2,1)S(1)}, bf16[704,128]{1,0:T(8,128)(2,1)S(1)}, u32[]{:S(2)}, u32[]{:S(2)}) collective-permute-start(bf16[704,128]{1,0:T(8,128)(2,1)S(1)} %collective-permute-done.3.refs_1_), channel_id=1, source_target_pairs={{0,1},{1,0},{2,3},{3,2},{4,5},{5,4},{6,7},{7,6},{8,9},{9,8},{10,11... | collective-permute-start | bytes 540680 | tf_op jit(solution)/shard_map/ppermute | solution.py:500
  42.1 11.6 %collective-permute-start.8 = (bf16[704,128]{1,0:T(8,128)(2,1)S(1)}, bf16[704,128]{1,0:T(8,128)(2,1)S(1)}, u32[]{:S(2)}, u32[]{:S(2)}) collective-permute-start(bf16[704,128]{1,0:T(8,128)(2,1)S(1)} %collective-permute-done.4.refs_2_), channel_id=1, source_target_pairs={{0,1},{1,0},{2,3},{3,2},{4,5},{5,4},{6,7},{7,6},{8,9},{9,8},{10,11... | collective-permute-start | bytes 540680 | tf_op jit(solution)/shard_map/ppermute | solution.py:500
  43.6 10.1 %collective-permute-start.9 = (bf16[704,128]{1,0:T(8,128)(2,1)S(1)}, bf16[704,128]{1,0:T(8,128)(2,1)S(1)}, u32[]{:S(2)}, u32[]{:S(2)}) collective-permute-start(bf16[704,128]{1,0:T(8,128)(2,1)S(1)} %collective-permute-done.5.refs_3_), channel_id=1, source_target_pairs={{0,1},{1,0},{2,3},{3,2},{4,5},{5,4},{6,7},{7,6},{8,9},{9,8},{10,11... | collective-permute-start | bytes 540680 | tf_op jit(solution)/shard_map/ppermute | solution.py:500
  49.7 11.8 %all-to-all-start.1 = ((f32[8,8,128]{2,1,0:T(8,128)}), f32[8,8,128]{2,1,0:T(8,128)S(1)}, u32[]{:S(2)}, u32[]{:S(2)}) async-start(f32[8,8,128]{2,1,0:T(8,128)} %get-tuple-element.40), calls=%async_computation.1 | async-start | bytes 65536 | tf_op jit(solution)/shard_map/all_to_all | solution.py:516
  62.2 23.2 %all-to-all-start.2 = ((bf16[8,128,256]{2,1,0:T(8,128)(2,1)}), bf16[8,128,256]{2,1,0:T(8,128)(2,1)S(1)}, u32[]{:S(2)}, u32[]{:S(2)}) async-start(bf16[8,128,256]{2,1,0:T(8,128)(2,1)} %add_sums.1), calls=%async_computation.2 | async-start | bytes 1048576 | tf_op jit(solution)/shard_map/all_to_all | solution.py:547
  85.9 5.7 %collective-permute-start.12 = (f32[112,256]{1,0:T(8,128)S(1)}, f32[112,256]{1,0:T(8,128)S(1)}, u32[]{:S(2)}, u32[]{:S(2)}) collective-permute-start(f32[112,256]{1,0:T(8,128)S(1)} %get-tuple-element.47.own_h), channel_id=1, source_target_pairs={{0,192},{64,0},{128,64},{192,128},{1,193},{65,1},{129,65},{193,129... | collective-permute-start | bytes 344072 | tf_op jit(solution)/shard_map/ppermute | solution.py:559
  88.5 5.2 %collective-permute-start.11 = (f32[112,256]{1,0:T(8,128)S(1)}, f32[112,256]{1,0:T(8,128)S(1)}, u32[]{:S(2)}, u32[]{:S(2)}) collective-permute-start(f32[112,256]{1,0:T(8,128)S(1)} %get-tuple-element.47.own_h), channel_id=1, source_target_pairs={{0,128},{64,192},{128,0},{192,64},{1,129},{65,193},{129,1},{193,65... | collective-permute-start | bytes 344072 | tf_op jit(solution)/shard_map/ppermute | solution.py:559
  89.0 8.4 %collective-permute-start.10 = (f32[112,256]{1,0:T(8,128)S(1)}, f32[112,256]{1,0:T(8,128)S(1)}, u32[]{:S(2)}, u32[]{:S(2)}) collective-permute-start(f32[112,256]{1,0:T(8,128)S(1)} %get-tuple-element.47.own_h), channel_id=1, source_target_pairs={{0,64},{64,128},{128,192},{192,0},{1,65},{65,129},{129,193},{193,1... | collective-permute-start | bytes 344072 | tf_op jit(solution)/shard_map/ppermute | solution.py:559

commit v6 on v5

--- a/solution.py
+++ b/solution.py
@@ -26,6 +26,7 @@
 APART = ASL // NC
 BLOCK = AROWS + NC * GROWS
 TERMS = 16
+HALO = FR * COLS
 HI = lax.Precision.HIGHEST
 
 
@@ -54,18 +55,29 @@
     return jnp.concatenate([cells[..., 1:, :], zero], axis=-2)
 
 
-def edges_and_sums(x_ref, g_ref, n_ref, up_ref, dn_ref, st_ref, live_ref):
-    up_ref[0] = x_ref[:, 0]
-    up_ref[1] = g_ref[:, 0]
-    dn_ref[0] = x_ref[:, 1]
-    dn_ref[1] = g_ref[:, 1]
+def edges_and_sums(x_ref, g_ref, n_ref, in_ref, out_ref, st_ref, live_ref):
+    first = lax.axis_index("c") == 0
+    for n, ref in enumerate((x_ref, g_ref)):
+        low, high = ref[:, 0], ref[:, 1]
+        inner, outer = jnp.where(first, high, low), jnp.where(first, low, high)
+        in_ref[n * HALO : (n + 1) * HALO] = inner.reshape(HALO, CH)
+        out_ref[n * HALO : (n + 1) * HALO] = outer.reshape(HALO, CH)
     live_ref[...] = (lax.broadcasted_iota(jnp.int32, (FR, CH), 0) < n_ref[0]).astype(F32)
     xf = x_ref[...].astype(F32).reshape(FR, CELLS, CH)
     gather = gather_matrix()
     mean = hdot(jnp.sum(xf, axis=1), gather) / (CELLS * GC)
     centered = xf - hdot(mean, spread_matrix())[:, None, :]
     squares = hdot(jnp.sum(centered * centered, axis=1), gather)
-    st_ref[...] = jnp.concatenate([mean, squares, jnp.zeros((FR, 2 * GROUPS), F32)], axis=1)
+    sums = jnp.concatenate([mean, squares, jnp.zeros((FR, 2 * GROUPS), F32)], axis=1)
+    st_ref[...] = sums
+    in_ref[2 * HALO :] = as_terms(sums)
+
+
+def outside(in_ref, out_ref):
+    first = lax.axis_index("c") == 0
+    inner = in_ref[...].reshape(FR, COLS, CH)
+    outer = out_ref[...].reshape(FR, COLS, CH)
+    return jnp.where(first, outer, inner), jnp.where(first, inner, outer)
 
 
 def combined(parts, squares, each):
@@ -76,11 +88,10 @@
 
 
 def pair_sums(own_ref, other_ref, out_ref):
-    both = jnp.stack([own_ref[...], other_ref[...]])
+    both = jnp.stack([own_ref[...], from_terms(other_ref[...].astype(F32))])
     mean, squares = combined(both[:, :, :GROUPS], both[:, :, GROUPS : 2 * GROUPS], CELLS * GC)
     row = jnp.concatenate([mean, squares, jnp.zeros((FR, 2 * GROUPS), F32)], axis=1)
-    row = jnp.concatenate([row] * 2, axis=0)
-    out_ref[...] = jnp.broadcast_to(row[None], (NY * NZ, 16, 128))
+    out_ref[...] = jnp.broadcast_to(row[None], (NY * NZ, FR, 128))
 
 
 def as_terms(values):
@@ -99,7 +110,7 @@
 def pack_slices(x_ref, g_ref, hp_ref, hn_ref, out_ref):
     upper = lax.axis_index("c") == 0
     own = [x_ref[:, 0], x_ref[:, 1]]
-    before, after = hp_ref[0], hn_ref[0]
+    before, after = outside(hp_ref, hn_ref)
     rows = [
         jnp.where(upper, before, own[0]),
         jnp.where(upper, own[0], own[1]),
@@ -117,7 +128,8 @@
 
 def backward_conv(g_ref, hp_ref, hn_ref, k_ref, live_ref, out_ref, pad_ref, held):
     live = live_ref[...][:, None, :]
-    rows = [hp_ref[1], g_ref[:, 0], g_ref[:, 1], hn_ref[1]]
+    before, after = outside(hp_ref, hn_ref)
+    rows = [before, g_ref[:, 0], g_ref[:, 1], after]
     for r in range(4):
         cells = rows[r].astype(F32) * live
         for k in range(3):
@@ -296,7 +308,8 @@
 
 def forward_conv(x_ref, hp_ref, hn_ref, mean_ref, inv_ref, gain_ref, k_ref, live_ref, out_ref, pad_ref, held):
     s_at = (lax.axis_index("y") * NZ + lax.axis_index("z")) * NC + lax.axis_index("c")
-    rows = [hp_ref[0], x_ref[:, 0], x_ref[:, 1], hn_ref[0]]
+    before, after = outside(hp_ref, hn_ref)
+    rows = [before, x_ref[:, 0], x_ref[:, 1], after]
     mean = mean_ref[...][:, None, :]
     inv = inv_ref[...][:, None, :]
     gain = gain_ref[...][None]
@@ -442,6 +455,7 @@
 def pack_body(*refs):
     sources, outs = refs[:4], refs[4:8]
     x_ref, g_ref, hp_ref, hn_ref, buf, sem = refs[8:]
+    sources = (sources[0], sources[1], sources[2].at[:HALO], sources[3].at[:HALO])
     pairs = tuple(zip(sources, (x_ref, g_ref, hp_ref, hn_ref)))
     copies = [pltpu.make_async_copy(a, b, sem.at[n]) for n, (a, b) in enumerate(pairs)]
     for copy in copies:
@@ -468,21 +482,32 @@
     space = ("y", "z", "c")
     cells = (FR, ROWS, COLS, CH)
     wide = (FR, CH)
-    halo = (2, FR, COLS, CH)
     swap = [(0, 1), (1, 0)]
     dma = pltpu.SemaphoreType.DMA
 
-    up, dn, stats, live = run(
+    inner, outer, stats, live = run(
         edges_and_sums,
-        [(halo, BF16), (halo, BF16), ((FR, 128), F32), (wide, F32)],
+        [
+            ((2 * HALO + TERMS, CH), BF16),
+            ((2 * HALO, CH), BF16),
+            ((FR, 128), F32),
+            (wide, F32),
+        ],
         (x, g, frame_counts),
         smem=(2,),
     )
-    other = lax.ppermute(stats, "c", swap)
-    (stats,) = run(pair_sums, [((NY * NZ, 16, 128), F32)], (stats, other))
-    stats, up, dn = lax.optimization_barrier((stats, up, dn))
-    hp = lax.ppermute(dn, space, [(i, i + 1) for i in range(SPACE - 1)])
-    hn = lax.ppermute(up, space, [(i + 1, i) for i in range(SPACE - 1)])
+    hp = lax.ppermute(inner, "c", swap)
+    hn = lax.ppermute(
+        outer,
+        space,
+        [(i, i - 1 if i % 2 == 0 else i + 1) for i in range(1, SPACE - 1)],
+    )
+    (stats,) = run(
+        pair_sums,
+        [((NY * NZ, FR, 128), F32)],
+        (stats, hp),
+        rows={1: (2 * HALO, 2 * HALO + TERMS)},
+    )
     stats = lax.all_to_all(stats, ("y", "z"), 0, 0)
     block = (BLOCK, BSL)
     packed = call(
@@ -491,19 +516,19 @@
         (x, g, hp, hn),
         [HBM] * 4,
         [pltpu.VMEM(cells, BF16)] * 2
-        + [pltpu.VMEM(halo, BF16)] * 2
+        + [pltpu.VMEM((HALO, CH), BF16)] * 2
         + [pltpu.VMEM((NY,) + block, BF16), dma((8,))],
     )
     near = [packed[0]] + [
         lax.ppermute(packed[d], "y", [(i, (i + d) % NY) for i in range(NY)]) for d in range(1, NY)
     ]
-    far = [lax.ppermute(a, "c", swap) for a in near]
     conv_flops = 16 * TAPS * FR * CELLS * CH * CH
     padded = pltpu.VMEM((3, FR + 2, 4, COLS, CH), BF16)
     (act_grad,) = run(
         backward_conv,
         [((FR * CELLS, CH), F32)],
         (g, hp, hn, conv_kernel, live),
+        rows={1: (HALO, 2 * HALO), 2: (HALO, 2 * HALO)},
         scratch=[padded],
         late=3,
         flops=0,
@@ -513,7 +538,9 @@
         [((NY * NC, FR, 128), F32), ((FR, CELLS, CH), F32), (wide, F32), (wide, F32)],
         (stats, x, act_grad, gain),
     )
+    *near, terms = lax.optimization_barrier((*near, terms))
     terms = lax.all_to_all(terms, ("y", "c"), 0, 0)
+    far = [lax.ppermute(a, "c", swap) for a in near]
     part = (NZ, PROWS, CH)
     whole_part = (NZ, PROWS + TERMS, CH)
     (partial,) = call(
@@ -549,6 +576,7 @@
         forward_conv,
         [(cells, BF16)],
         (x, hp, hn, late_mean, inv, gain, conv_kernel, live),
+        rows={1: (0, HALO), 2: (0, HALO)},
         scratch=[padded],
         late=6,
         flops=conv_flops,

time: 99.4 us -> 86.6 us (0.87)
  waiting for transfers between devices: 29.3 us -> 21.4 us
  starting transfers between devices: 40.4 us -> 35.7 us
    ppermute x3 -> x2, waiting for transfers between devices: 5.48 us -> 0.01 us  [the longest x1 0.01 us: local(): hp = lax.ppermute(inner, 'c', swap)]
    ppermute x3 -> x2, starting transfers between devices: 9.17 us -> 5.24 us  [the longest x1 3.33 us: local(): hp = lax.ppermute(inner, 'c', swap)]
    ppermute x3, waiting for transfers between devices: 4.26 us -> 1.72 us  [local(): lax.ppermute(packed[d], 'y', [(i, (i + d) % NY) for i in range(NY)])]
    ppermute x4, starting transfers between devices: 3.97 us -> 1.66 us  [local(): far = [lax.ppermute(a, 'c', swap) for a in near]]
  transfers between devices with their start and end apart: 16 -> 15, of which waited for: 8 -> 4; matrix products, arithmetic and copies ran while one was open for 0% -> 0% of each run, Pallas kernels for 23% -> 27%
where the time goes in v6:
time: 86.6 us; the launch traced here: 86.2 us
  starting transfers between devices  35.7 us (41%)
  Pallas kernels  27.4 us (32%)
  waiting for transfers between devices  21.4 us (25%)
  between operations  1.61 us (2%)
    pallas_call x11, Pallas kernels, call(): pl.pallas_call(body, out_shape=shapes(outs), in_specs=specs, out_specs=tu...  27.4 us
    all_to_all x1, waiting for transfers between devices, local(): merged = lax.all_to_all(merged, 'z', 0, 0)  14 us
    all_to_all x1, starting transfers between devices, local(): stats = lax.all_to_all(stats, ('y', 'z'), 0, 0)  10.1 us
    all_to_all x1, starting transfers between devices, local(): merged = lax.all_to_all(merged, 'z', 0, 0)  6.09 us
    ppermute x3, waiting for transfers between devices, local(): lax.ppermute(rows, 'x', [(i, (i + d) % NX) for i in range(NX)])  5.72 us
    ppermute x3, starting transfers between devices, local(): lax.ppermute(packed[d], 'y', [(i, (i + d) % NY) for i in range(NY)])  4.89 us
    all_to_all x1, starting transfers between devices, local(): terms = lax.all_to_all(terms, ('y', 'c'), 0, 0)  4.03 us
    ppermute x3, starting transfers between devices, local(): lax.ppermute(rows, 'x', [(i, (i + d) % NX) for i in range(NX)])  3.68 us
  transfers between devices with their start and end apart: 15, of which 4 were waited for; matrix products, arithmetic and copies ran while one was open for 0% of the time, Pallas kernels for 27%

profile of v6, /device:TPU:1, one launch (start us, length us, event | category | flops | bytes accessed | tf_op | source)
XLA Modules:
  0.0 86.2 jit_solution(10010723114656926182)
XLA Ops:
  1.3 2.1 %edges_and_sums.1 = (bf16[272,256]{1,0:T(8,128)(2,1)S(1)}, bf16[256,256]{1,0:T(8,128)(2,1)S(1)}, f32[8,128]{1,0:T(8,128)S(1)}, f32[8,256]{1,0:T(8,128)S(1)}) custom-call(bf16[8,2,16,256]{3,2,1,0:T(8,128)(2,1)} %bitcast.11, bf16[8,2,16,256]{3,2,1,0:T(8,128)(2,1)} %bitcast.7, s32[1]{0:T(128)S(6)} %copy.11.refs_2_), custom_call_target="tpu_custom_call" | custom-call | bytes 1048576 | tf_op jit(solution)/shard_map/edges_and_sums/pallas_call | solution.py:393
  3.3 3.3 %collective-permute-start = (bf16[272,256]{1,0:T(8,128)(2,1)S(1)}, bf16[272,256]{1,0:T(8,128)(2,1)S(1)}, u32[]{:S(2)}, u32[]{:S(2)}) collective-permute-start(bf16[272,256]{1,0:T(8,128)(2,1)S(1)} %get-tuple-element.29), channel_id=1, source_target_pairs={{0,1},{1,0},{2,3},{3,2},{4,5},{5,4},{6,7},{7,6},{8,9},{9,8},{10,11... | collective-permute-start | bytes 417800 | tf_op jit(solution)/shard_map/ppermute | solution.py:499
  6.7 1.9 %collective-permute-start.1 = (bf16[256,256]{1,0:T(8,128)(2,1)S(1)}, bf16[256,256]{1,0:T(8,128)(2,1)S(1)}, u32[]{:S(2)}, u32[]{:S(2)}) collective-permute-start(bf16[256,256]{1,0:T(8,128)(2,1)S(1)} %get-tuple-element.30), channel_id=1, source_target_pairs={{1,2},{2,1},{3,4},{4,3},{5,6},{6,5},{7,8},{8,7},{9,10},{10,9},{11,... | collective-permute-start | bytes 393224 | tf_op jit(solution)/shard_map/ppermute | solution.py:500
  8.6 0.8 pair_sums.1
  9.4 10.1 %all-to-all-start = ((f32[32,8,128]{2,1,0:T(8,128)}), f32[32,8,128]{2,1,0:T(8,128)S(1)}, u32[]{:S(2)}, u32[]{:S(2)}) async-start(f32[32,8,128]{2,1,0:T(8,128)} %pair_sums.1), calls=%async_computation | async-start | bytes 262144 | tf_op jit(solution)/shard_map/all_to_all | solution.py:511
  19.5 2.2 %pack_body.1 = (bf16[704,128]{1,0:T(8,128)(2,1)S(1)}, bf16[704,128]{1,0:T(8,128)(2,1)S(1)}, bf16[704,128]{1,0:T(8,128)(2,1)S(1)}, bf16[704,128]{1,0:T(8,128)(2,1)S(1)}) custom-call(bf16[8,2,16,256]{3,2,1,0:T(8,128)(2,1)} %bitcast.12, bf16[8,2,16,256]{3,2,1,0:T(8,128)(2,1)} %bitcast.8, bf16[272,256]{1,0:T(8,128)(2,1)S(1)} %collective-permute-done.refs_2_.refs_1_, ...), custom_call_target="tpu_custom_call" | custom-call | bytes 1048576 | tf_op jit(solution)/shard_map/pack_body/pallas_call | solution.py:393
  21.8 1.3 %collective-permute-start.2 = (bf16[704,128]{1,0:T(8,128)(2,1)S(1)}, bf16[704,128]{1,0:T(8,128)(2,1)S(1)}, u32[]{:S(2)}, u32[]{:S(2)}) collective-permute-start(bf16[704,128]{1,0:T(8,128)(2,1)S(1)} %get-tuple-element.32), channel_id=1, source_target_pairs={{0,16},{16,32},{32,48},{48,0},{1,17},{17,33},{33,49},{49,1},{2,18}... | collective-permute-start | bytes 540680 | tf_op jit(solution)/shard_map/ppermute | solution.py:523
  23.1 2.4 %collective-permute-start.3 = (bf16[704,128]{1,0:T(8,128)(2,1)S(1)}, bf16[704,128]{1,0:T(8,128)(2,1)S(1)}, u32[]{:S(2)}, u32[]{:S(2)}) collective-permute-start(bf16[704,128]{1,0:T(8,128)(2,1)S(1)} %get-tuple-element.33), channel_id=1, source_target_pairs={{0,32},{16,48},{32,0},{48,16},{1,33},{17,49},{33,1},{49,17},{2,34}... | collective-permute-start | bytes 540680 | tf_op jit(solution)/shard_map/ppermute | solution.py:523
  25.5 1.1 %collective-permute-start.4 = (bf16[704,128]{1,0:T(8,128)(2,1)S(1)}, bf16[704,128]{1,0:T(8,128)(2,1)S(1)}, u32[]{:S(2)}, u32[]{:S(2)}) collective-permute-start(bf16[704,128]{1,0:T(8,128)(2,1)S(1)} %get-tuple-element.34), channel_id=1, source_target_pairs={{0,48},{16,0},{32,16},{48,32},{1,49},{17,1},{33,17},{49,33},{2,50}... | collective-permute-start | bytes 540680 | tf_op jit(solution)/shard_map/ppermute | solution.py:523
  26.7 3.4 %backward_conv.1.refs_2_ = f32[256,256]{1,0:T(8,128)S(1)} custom-call(bf16[8,2,16,256]{3,2,1,0:T(8,128)(2,1)} %bitcast.9, bf16[272,256]{1,0:T(8,128)(2,1)S(1)} %collective-permute-done.refs_2_.refs_1_, bf16[256,256]{1,0:T(8,128)(2,1)S(1)} %collective-permute-done.1.refs_3_.refs_2_, bf16[27,256,256]{2,1,0:T(8,128)(2,1)} %refs_6_.1, ...), custom_call_target="tpu_custom_call" | custom-call | bytes 1048576 | tf_op jit(solution)/shard_map/backward_conv/pallas_call | solution.py:393
  30.0 2.7 %group_terms.1 = (f32[8,8,128]{2,1,0:T(8,128)}, f32[8,32,256]{2,1,0:T(8,128)S(1)}, f32[8,256]{1,0:T(8,128)S(1)}, f32[8,256]{1,0:T(8,128)S(1)}) custom-call(f32[32,8,128]{2,1,0:T(8,128)S(1)} %all-to-all-done.refs_0_, bf16[8,2,16,256]{3,2,1,0:T(8,128)(2,1)} %bitcast.13, f32[256,256]{1,0:T(8,128)S(1)} %backward_conv.1.refs_2_, f32[1,256]{1,0:T(1,128)} %bitcast.17), custom_call_target="tpu_custom_call" | custom-call | bytes 1048576 | tf_op jit(solution)/shard_map/group_terms/pallas_call | solution.py:393
  32.7 1.7 %collective-permute-done.3.refs_2_ = bf16[704,128]{1,0:T(8,128)(2,1)S(1)} collective-permute-done((bf16[704,128]{1,0:T(8,128)(2,1)S(1)}, bf16[704,128]{1,0:T(8,128)(2,1)S(1)}, u32[]{:S(2)}, u32[]{:S(2)}) %collective-permute-start.3) | collective-permute-done | bytes 180256 | tf_op jit(solution)/shard_map/ppermute | solution.py:523
  34.4 1.1 %collective-permute-start.5 = (bf16[704,128]{1,0:T(8,128)(2,1)S(1)}, bf16[704,128]{1,0:T(8,128)(2,1)S(1)}, u32[]{:S(2)}, u32[]{:S(2)}) collective-permute-start(bf16[704,128]{1,0:T(8,128)(2,1)S(1)} %get-tuple-element.38.refs_0_), channel_id=1, source_target_pairs={{0,1},{1,0},{2,3},{3,2},{4,5},{5,4},{6,7},{7,6},{8,9},{9,8},{10,11... | collective-permute-start | bytes 540680 | tf_op jit(solution)/shard_map/ppermute | solution.py:543
  36.1 4.0 %all-to-all-start.1 = ((f32[8,8,128]{2,1,0:T(8,128)}), f32[8,8,128]{2,1,0:T(8,128)S(1)}, u32[]{:S(2)}, u32[]{:S(2)}) async-start(f32[8,8,128]{2,1,0:T(8,128)} %get-tuple-element.44), calls=%async_computation.1 | async-start | bytes 65536 | tf_op jit(solution)/shard_map/all_to_all | solution.py:542
  40.2 7.8 %kernel_part.1.part_h = bf16[8,128,256]{2,1,0:T(8,128)(2,1)} custom-call(bf16[704,128]{1,0:T(8,128)(2,1)S(1)} %get-tuple-element.38.refs_0_, bf16[704,128]{1,0:T(8,128)(2,1)S(1)} %collective-permute-done.2.refs_1_, bf16[704,128]{1,0:T(8,128)(2,1)S(1)} %collective-permute-done.3.refs_2_, bf16[704,128]{1,0:T(8,128)(2,1)S(1)} %collective-permute-done.4.refs_3_, ...), custom_call_target="tpu_custom_call" | custom-call | flops 7247757312 | bytes 1048576 | tf_op jit(solution)/shard_map/kernel_part/pallas_call | solution.py:393
  47.9 0.7 add_sums.1
  48.7 6.1 %all-to-all-start.2 = ((bf16[8,128,256]{2,1,0:T(8,128)(2,1)}), bf16[8,128,256]{2,1,0:T(8,128)(2,1)S(1)}, u32[]{:S(2)}, u32[]{:S(2)}) async-start(bf16[8,128,256]{2,1,0:T(8,128)(2,1)} %add_sums.1), calls=%async_computation.2 | async-start | bytes 1048576 | tf_op jit(solution)/shard_map/all_to_all | solution.py:574
  54.7 4.0 %forward_conv.1 = bf16[8,2,16,256]{3,2,1,0:T(8,128)(2,1)} custom-call(bf16[8,2,16,256]{3,2,1,0:T(8,128)(2,1)} %bitcast.14, bf16[272,256]{1,0:T(8,128)(2,1)S(1)} %collective-permute-done.refs_2_.refs_1_, bf16[256,256]{1,0:T(8,128)(2,1)S(1)} %collective-permute-done.1.refs_3_.refs_2_, f32[8,256]{1,0:T(8,128)S(1)} %get-tuple-element.46.refs_8_.refs_3_.refs_4_, ...), custom_call_target="tpu_custom_call" | custom-call | flops 7247757312 | bytes 1048576 | tf_op jit(solution)/shard_map/forward_conv/pallas_call | solution.py:393
  58.8 14.0 %all-to-all-done.2.refs_0_ = bf16[8,128,256]{2,1,0:T(8,128)(2,1)S(1)} async-done(((bf16[8,128,256]{2,1,0:T(8,128)(2,1)}), bf16[8,128,256]{2,1,0:T(8,128)(2,1)S(1)}, u32[]{:S(2)}, u32[]{:S(2)}) %all-to-all-start.2) | async-done | bytes 524320 | tf_op jit(solution)/shard_map/all_to_all | solution.py:574
  73.3 2.6 %collective-permute-start.11 = (f32[112,256]{1,0:T(8,128)S(1)}, f32[112,256]{1,0:T(8,128)S(1)}, u32[]{:S(2)}, u32[]{:S(2)}) collective-permute-start(f32[112,256]{1,0:T(8,128)S(1)} %get-tuple-element.51.own_h), channel_id=1, source_target_pairs={{0,192},{64,0},{128,64},{192,128},{1,193},{65,1},{129,65},{193,129... | collective-permute-start | bytes 344072 | tf_op jit(solution)/shard_map/ppermute | solution.py:587
  77.0 2.0 %finish_input.1 = bf16[8,2,16,256]{3,2,1,0:T(8,128)(2,1)} custom-call(f32[8,128]{1,0:T(8,128)S(1)} %get-tuple-element.49.refs_0_, f32[8,32,256]{2,1,0:T(8,128)S(1)} %get-tuple-element.50.refs_1_, bf16[8,2,16,256]{3,2,1,0:T(8,128)(2,1)} %bitcast.15, bf16[8,2,16,256]{3,2,1,0:T(8,128)(2,1)} %bitcast.10, f32[8,256]{1,0:T(8,128)S(1)} %get-tuple-element.46.refs_8_.refs_3_.refs_4_, ...), custom_call_target="tpu_custom_call" | custom-call | bytes 1048576 | tf_op jit(solution)/shard_map/finish_input/pallas_call | solution.py:393
  79.0 2.1 %collective-permute-done.10.two_h = f32[112,256]{1,0:T(8,128)S(1)} collective-permute-done((f32[112,256]{1,0:T(8,128)S(1)}, f32[112,256]{1,0:T(8,128)S(1)}, u32[]{:S(2)}, u32[]{:S(2)}) %collective-permute-start.10) | collective-permute-done | bytes 114720 | tf_op jit(solution)/shard_map/ppermute | solution.py:587
  81.1 3.6 %collective-permute-done.9.one_h = f32[112,256]{1,0:T(8,128)S(1)} collective-permute-done((f32[112,256]{1,0:T(8,128)S(1)}, f32[112,256]{1,0:T(8,128)S(1)}, u32[]{:S(2)}, u32[]{:S(2)}) %collective-permute-start.9) | collective-permute-done | bytes 114720 | tf_op jit(solution)/shard_map/ppermute | solution.py:587
  84.7 1.3 %sum_clips.1 = (f32[27,4,256]{2,1,0:T(4,128)}, f32[1,256]{1,0:T(1,128)}) custom-call(f32[112,256]{1,0:T(8,128)S(1)} %get-tuple-element.51.own_h, f32[112,256]{1,0:T(8,128)S(1)} %collective-permute-done.9.one_h, f32[112,256]{1,0:T(8,128)S(1)} %collective-permute-done.10.two_h, f32[112,256]{1,0:T(8,128)S(1)} %collective-permute-done.11.three_h), custom_call_target="tpu_custom_call" | custom-call | bytes 1048576 | tf_op jit(solution)/shard_map/sum_clips/pallas_call | solution.py:393
  (17 shorter events, 2.2 us)
Async XLA Ops:
  3.3 5.2 %collective-permute-start = (bf16[272,256]{1,0:T(8,128)(2,1)S(1)}, bf16[272,256]{1,0:T(8,128)(2,1)S(1)}, u32[]{:S(2)}, u32[]{:S(2)}) collective-permute-start(bf16[272,256]{1,0:T(8,128)(2,1)S(1)} %get-tuple-element.29), channel_id=1, source_target_pairs={{0,1},{1,0},{2,3},{3,2},{4,5},{5,4},{6,7},{7,6},{8,9},{9,8},{10,11... | collective-permute-start | bytes 417800 | tf_op jit(solution)/shard_map/ppermute | solution.py:499
  6.7 12.9 %collective-permute-start.1 = (bf16[256,256]{1,0:T(8,128)(2,1)S(1)}, bf16[256,256]{1,0:T(8,128)(2,1)S(1)}, u32[]{:S(2)}, u32[]{:S(2)}) collective-permute-start(bf16[256,256]{1,0:T(8,128)(2,1)S(1)} %get-tuple-element.30), channel_id=1, source_target_pairs={{1,2},{2,1},{3,4},{4,3},{5,6},{6,5},{7,8},{8,7},{9,10},{10,9},{11,... | collective-permute-start | bytes 393224 | tf_op jit(solution)/shard_map/ppermute | solution.py:500
  9.4 20.6 %all-to-all-start = ((f32[32,8,128]{2,1,0:T(8,128)}), f32[32,8,128]{2,1,0:T(8,128)S(1)}, u32[]{:S(2)}, u32[]{:S(2)}) async-start(f32[32,8,128]{2,1,0:T(8,128)} %pair_sums.1), calls=%async_computation | async-start | bytes 262144 | tf_op jit(solution)/shard_map/all_to_all | solution.py:511
  21.8 10.9 %collective-permute-start.2 = (bf16[704,128]{1,0:T(8,128)(2,1)S(1)}, bf16[704,128]{1,0:T(8,128)(2,1)S(1)}, u32[]{:S(2)}, u32[]{:S(2)}) collective-permute-start(bf16[704,128]{1,0:T(8,128)(2,1)S(1)} %get-tuple-element.32), channel_id=1, source_target_pairs={{0,16},{16,32},{32,48},{48,0},{1,17},{17,33},{33,49},{49,1},{2,18}... | collective-permute-start | bytes 540680 | tf_op jit(solution)/shard_map/ppermute | solution.py:523
  23.1 11.4 %collective-permute-start.3 = (bf16[704,128]{1,0:T(8,128)(2,1)S(1)}, bf16[704,128]{1,0:T(8,128)(2,1)S(1)}, u32[]{:S(2)}, u32[]{:S(2)}) collective-permute-start(bf16[704,128]{1,0:T(8,128)(2,1)S(1)} %get-tuple-element.33), channel_id=1, source_target_pairs={{0,32},{16,48},{32,0},{48,16},{1,33},{17,49},{33,1},{49,17},{2,34}... | collective-permute-start | bytes 540680 | tf_op jit(solution)/shard_map/ppermute | solution.py:523
  25.5 8.9 %collective-permute-start.4 = (bf16[704,128]{1,0:T(8,128)(2,1)S(1)}, bf16[704,128]{1,0:T(8,128)(2,1)S(1)}, u32[]{:S(2)}, u32[]{:S(2)}) collective-permute-start(bf16[704,128]{1,0:T(8,128)(2,1)S(1)} %get-tuple-element.34), channel_id=1, source_target_pairs={{0,48},{16,0},{32,16},{48,32},{1,49},{17,1},{33,17},{49,33},{2,50}... | collective-permute-start | bytes 540680 | tf_op jit(solution)/shard_map/ppermute | solution.py:523
  34.4 5.7 %collective-permute-start.5 = (bf16[704,128]{1,0:T(8,128)(2,1)S(1)}, bf16[704,128]{1,0:T(8,128)(2,1)S(1)}, u32[]{:S(2)}, u32[]{:S(2)}) collective-permute-start(bf16[704,128]{1,0:T(8,128)(2,1)S(1)} %get-tuple-element.38.refs_0_), channel_id=1, source_target_pairs={{0,1},{1,0},{2,3},{3,2},{4,5},{5,4},{6,7},{7,6},{8,9},{9,8},{10,11... | collective-permute-start | bytes 540680 | tf_op jit(solution)/shard_map/ppermute | solution.py:543
  35.6 4.6 %collective-permute-start.6 = (bf16[704,128]{1,0:T(8,128)(2,1)S(1)}, bf16[704,128]{1,0:T(8,128)(2,1)S(1)}, u32[]{:S(2)}, u32[]{:S(2)}) collective-permute-start(bf16[704,128]{1,0:T(8,128)(2,1)S(1)} %collective-permute-done.2.refs_1_), channel_id=1, source_target_pairs={{0,1},{1,0},{2,3},{3,2},{4,5},{5,4},{6,7},{7,6},{8,9},{9,8},{10,11... | collective-permute-start | bytes 540680 | tf_op jit(solution)/shard_map/ppermute | solution.py:543
  35.6 4.6 %collective-permute-start.7 = (bf16[704,128]{1,0:T(8,128)(2,1)S(1)}, bf16[704,128]{1,0:T(8,128)(2,1)S(1)}, u32[]{:S(2)}, u32[]{:S(2)}) collective-permute-start(bf16[704,128]{1,0:T(8,128)(2,1)S(1)} %collective-permute-done.3.refs_2_), channel_id=1, source_target_pairs={{0,1},{1,0},{2,3},{3,2},{4,5},{5,4},{6,7},{7,6},{8,9},{9,8},{10,11... | collective-permute-start | bytes 540680 | tf_op jit(solution)/shard_map/ppermute | solution.py:543
  36.1 4.1 %collective-permute-start.8 = (bf16[704,128]{1,0:T(8,128)(2,1)S(1)}, bf16[704,128]{1,0:T(8,128)(2,1)S(1)}, u32[]{:S(2)}, u32[]{:S(2)}) collective-permute-start(bf16[704,128]{1,0:T(8,128)(2,1)S(1)} %collective-permute-done.4.refs_3_), channel_id=1, source_target_pairs={{0,1},{1,0},{2,3},{3,2},{4,5},{5,4},{6,7},{7,6},{8,9},{9,8},{10,11... | collective-permute-start | bytes 540680 | tf_op jit(solution)/shard_map/ppermute | solution.py:543
  36.1 11.8 %all-to-all-start.1 = ((f32[8,8,128]{2,1,0:T(8,128)}), f32[8,8,128]{2,1,0:T(8,128)S(1)}, u32[]{:S(2)}, u32[]{:S(2)}) async-start(f32[8,8,128]{2,1,0:T(8,128)} %get-tuple-element.44), calls=%async_computation.1 | async-start | bytes 65536 | tf_op jit(solution)/shard_map/all_to_all | solution.py:542
  48.7 24.1 %all-to-all-start.2 = ((bf16[8,128,256]{2,1,0:T(8,128)(2,1)}), bf16[8,128,256]{2,1,0:T(8,128)(2,1)S(1)}, u32[]{:S(2)}, u32[]{:S(2)}) async-start(bf16[8,128,256]{2,1,0:T(8,128)(2,1)} %add_sums.1), calls=%async_computation.2 | async-start | bytes 1048576 | tf_op jit(solution)/shard_map/all_to_all | solution.py:574
  73.3 5.7 %collective-permute-start.11 = (f32[112,256]{1,0:T(8,128)S(1)}, f32[112,256]{1,0:T(8,128)S(1)}, u32[]{:S(2)}, u32[]{:S(2)}) collective-permute-start(f32[112,256]{1,0:T(8,128)S(1)} %get-tuple-element.51.own_h), channel_id=1, source_target_pairs={{0,192},{64,0},{128,64},{192,128},{1,193},{65,1},{129,65},{193,129... | collective-permute-start | bytes 344072 | tf_op jit(solution)/shard_map/ppermute | solution.py:587
  75.8 5.2 %collective-permute-start.10 = (f32[112,256]{1,0:T(8,128)S(1)}, f32[112,256]{1,0:T(8,128)S(1)}, u32[]{:S(2)}, u32[]{:S(2)}) collective-permute-start(f32[112,256]{1,0:T(8,128)S(1)} %get-tuple-element.51.own_h), channel_id=1, source_target_pairs={{0,128},{64,192},{128,0},{192,64},{1,129},{65,193},{129,1},{193,65... | collective-permute-start | bytes 344072 | tf_op jit(solution)/shard_map/ppermute | solution.py:587
  76.4 8.4 %collective-permute-start.9 = (f32[112,256]{1,0:T(8,128)S(1)}, f32[112,256]{1,0:T(8,128)S(1)}, u32[]{:S(2)}, u32[]{:S(2)}) collective-permute-start(f32[112,256]{1,0:T(8,128)S(1)} %get-tuple-element.51.own_h), channel_id=1, source_target_pairs={{0,64},{64,128},{128,192},{192,0},{1,65},{65,129},{129,193},{193,1... | collective-permute-start | bytes 344072 | tf_op jit(solution)/shard_map/ppermute | solution.py:587

commit v7 on v6

--- a/solution.py
+++ b/solution.py
@@ -55,14 +55,13 @@
     return jnp.concatenate([cells[..., 1:, :], zero], axis=-2)
 
 
-def edges_and_sums(x_ref, g_ref, n_ref, in_ref, out_ref, st_ref, live_ref):
+def edges_and_sums(x_ref, g_ref, in_ref, out_ref, st_ref):
     first = lax.axis_index("c") == 0
     for n, ref in enumerate((x_ref, g_ref)):
         low, high = ref[:, 0], ref[:, 1]
         inner, outer = jnp.where(first, high, low), jnp.where(first, low, high)
         in_ref[n * HALO : (n + 1) * HALO] = inner.reshape(HALO, CH)
         out_ref[n * HALO : (n + 1) * HALO] = outer.reshape(HALO, CH)
-    live_ref[...] = (lax.broadcasted_iota(jnp.int32, (FR, CH), 0) < n_ref[0]).astype(F32)
     xf = x_ref[...].astype(F32).reshape(FR, CELLS, CH)
     gather = gather_matrix()
     mean = hdot(jnp.sum(xf, axis=1), gather) / (CELLS * GC)
@@ -126,7 +125,7 @@
             out_ref[y, at : at + GROWS] = g_ref[..., c * BSL : (c + 1) * BSL].reshape(GROWS, BSL)
 
 
-def backward_conv(g_ref, hp_ref, hn_ref, k_ref, live_ref, out_ref, pad_ref, held):
+def backward_conv(g_ref, hp_ref, hn_ref, k_ref, live_ref, pad_ref, held):
     live = live_ref[...][:, None, :]
     before, after = outside(hp_ref, hn_ref)
     rows = [before, g_ref[:, 0], g_ref[:, 1], after]
@@ -147,10 +146,14 @@
                     (((1,), (1,)), ((), ())),
                     preferred_element_type=F32,
                 )
-    out_ref[...] = total
-
-
-def group_terms(st_ref, x_ref, ag_ref, gain_ref, out_ref, sc_ref, mean_ref, inv_ref):
+    return total
+
+
+def backward_terms(
+    g_ref, hp_ref, hn_ref, k_ref, live_ref, st_ref, x_ref, gain_ref,
+    out_ref, sc_ref, mean_ref, inv_ref, pad_ref, held,
+):
+    act_grad = backward_conv(g_ref, hp_ref, hn_ref, k_ref, live_ref, pad_ref, held)
     mean, whole = combined(
         st_ref[:, :FR, :GROUPS], st_ref[:, :FR, GROUPS : 2 * GROUPS], NC * CELLS * GC
     )
@@ -164,7 +167,7 @@
     normalized = (xf - mean_all[:, None, :]) * inv_all[:, None, :]
     gated = normalized * gain
     sig = jax.nn.sigmoid(gated)
-    pre = ag_ref[...].reshape(FR, CELLS, CH) * sig * (1.0 + gated * (1.0 - sig))
+    pre = act_grad.reshape(FR, CELLS, CH) * sig * (1.0 + gated * (1.0 - sig))
     scaled = pre * gain
     sc_ref[...] = scaled
     gather = gather_matrix()
@@ -201,7 +204,7 @@
     mean2 = hdot(mean_ref[...], pick)
     inv2 = hdot(inv_ref[...], pick)
     gain2 = hdot(gain_ref[...], pick)
-    live = live_ref[:, :BSL][:, None, None, :]
+    live = live_ref[:, :BSL].astype(BF16)[:, None, None, :]
     quarter = lax.broadcasted_iota(jnp.int32, (1, width), 1) // APART
     centers, scales = [], []
     for u in range(2):
@@ -258,17 +261,18 @@
                 pad_ref[k, f, d, pl.ds(3 * c, 3)] = shifted(frames[f], k).astype(BF16)
         for h in range(NC):
             at = AROWS + h * GROWS
-            cells = in_ref[n, at : at + GROWS].astype(F32).reshape(FR, ROWS, COLS, BSL) * live
+            cells = in_ref[n, at : at + GROWS].reshape(FR, ROWS, COLS, BSL) * live
             grad_ref[:, d, pl.ds(2 * c, 2), :, h * BSL : (h + 1) * BSL] = cells
     cells = FR * NY * 4 * COLS
-    turned_grad = grad_ref[...].reshape(cells, CH).T.astype(BF16)
+    turned_grad = grad_ref[...].reshape(cells, CH).T
     sum_ref[:, 4 * TAPS :] = jnp.zeros((NZ, PROWS - 4 * TAPS, CH), F32)
     combos = [(j, k) for j in range(3) for k in range(3)]
     for first in range(0, 9, 2):
         group = combos[first : first + 2]
         windows = [pad_ref[k, :, :, j : j + 4].reshape(cells, width) for j, k in group]
         window = windows[0] if len(windows) == 1 else jnp.concatenate(windows, axis=1)
-        product = jnp.dot(turned_grad, window, preferred_element_type=F32).T
+        product = jnp.dot(turned_grad, window, preferred_element_type=F32)
+        product = product.astype(BF16).T.astype(F32)
         for n, (j, k) in enumerate(group):
             for i in range(3):
                 tap = (i * 3 + j) * 3 + k
@@ -485,17 +489,17 @@
     swap = [(0, 1), (1, 0)]
     dma = pltpu.SemaphoreType.DMA
 
-    inner, outer, stats, live = run(
+    inner, outer, stats = run(
         edges_and_sums,
         [
             ((2 * HALO + TERMS, CH), BF16),
             ((2 * HALO, CH), BF16),
             ((FR, 128), F32),
-            (wide, F32),
         ],
-        (x, g, frame_counts),
-        smem=(2,),
-    )
+        (x, g),
+    )
+    stats, counts = lax.optimization_barrier((stats, frame_counts))
+    live = jnp.broadcast_to(jnp.arange(FR)[:, None] < counts[0], wide).astype(F32)
     hp = lax.ppermute(inner, "c", swap)
     hn = lax.ppermute(
         outer,
@@ -524,19 +528,13 @@
     ]
     conv_flops = 16 * TAPS * FR * CELLS * CH * CH
     padded = pltpu.VMEM((3, FR + 2, 4, COLS, CH), BF16)
-    (act_grad,) = run(
-        backward_conv,
-        [((FR * CELLS, CH), F32)],
-        (g, hp, hn, conv_kernel, live),
+    terms, scaled, mean, inv = run(
+        backward_terms,
+        [((NY * NC, FR, 128), F32), ((FR, CELLS, CH), F32), (wide, F32), (wide, F32)],
+        (g, hp, hn, conv_kernel, live, stats, x, gain),
         rows={1: (HALO, 2 * HALO), 2: (HALO, 2 * HALO)},
         scratch=[padded],
         late=3,
-        flops=0,
-    )
-    terms, scaled, mean, inv = run(
-        group_terms,
-        [((NY * NC, FR, 128), F32), ((FR, CELLS, CH), F32), (wide, F32), (wide, F32)],
-        (stats, x, act_grad, gain),
     )
     *near, terms = lax.optimization_barrier((*near, terms))
     terms = lax.all_to_all(terms, ("y", "c"), 0, 0)
@@ -556,7 +554,7 @@
             pltpu.VMEM(wide, F32),
             pltpu.VMEM(part, BF16),
             pltpu.VMEM((3, FR, NY, 6, COLS, Q * APART), BF16),
-            pltpu.VMEM((FR, NY, 4, COLS, CH), F32),
+            pltpu.VMEM((FR, NY, 4, COLS, CH), BF16),
             pltpu.VMEM(part, F32),
             dma((12,)),
         ],

time: 86.6 us -> 85.8 us (level)
  Pallas kernels: 27.4 us -> 26.2 us
    all_to_all x1, waiting for transfers between devices: 0.01 us -> 1.36 us  [local(): stats = lax.all_to_all(stats, ('y', 'z'), 0, 0)]
    pallas_call x11 -> x10, Pallas kernels: 27.4 us -> 26.2 us  [call(): pl.pallas_call(body, out_shape=shapes(outs), in_specs=specs, out_specs=tu...]
    ppermute x3, waiting for transfers between devices: 1.72 us -> 0.83 us  [local(): lax.ppermute(packed[d], 'y', [(i, (i + d) % NY) for i in range(NY)])]
  transfers between devices with their start and end apart: 15 -> 15, of which waited for: 4 -> 5; matrix products, arithmetic and copies ran while one was open for 0% -> 0% of each run, Pallas kernels for 27% -> 25%
where the time goes in v7:
time: 85.8 us; the launch traced here: 85.3 us
  starting transfers between devices  35.7 us (42%)
  Pallas kernels  26.2 us (31%)
  waiting for transfers between devices  21.9 us (26%)
  between operations  1.45 us (2%)
    pallas_call x10, Pallas kernels, call(): pl.pallas_call(body, out_shape=shapes(outs), in_specs=specs, out_specs=tu...  26.2 us
    all_to_all x1, waiting for transfers between devices, local(): merged = lax.all_to_all(merged, 'z', 0, 0)  14 us
    all_to_all x1, starting transfers between devices, local(): stats = lax.all_to_all(stats, ('y', 'z'), 0, 0)  10.1 us
    all_to_all x1, starting transfers between devices, local(): merged = lax.all_to_all(merged, 'z', 0, 0)  6.06 us
    ppermute x3, waiting for transfers between devices, local(): lax.ppermute(rows, 'x', [(i, (i + d) % NX) for i in range(NX)])  5.71 us
    ppermute x3, starting transfers between devices, local(): lax.ppermute(packed[d], 'y', [(i, (i + d) % NY) for i in range(NY)])  4.89 us
    ppermute x3, starting transfers between devices, local(): lax.ppermute(rows, 'x', [(i, (i + d) % NX) for i in range(NX)])  3.68 us
    all_to_all x1, starting transfers between devices, local(): terms = lax.all_to_all(terms, ('y', 'c'), 0, 0)  3.65 us
  transfers between devices with their start and end apart: 15, of which 5 were waited for; matrix products, arithmetic and copies ran while one was open for 0% of the time, Pallas kernels for 25%

profile of v7, /device:TPU:1, one launch (start us, length us, event | category | flops | bytes accessed | tf_op | source)
XLA Modules:
  0.0 85.3 jit_solution(3925946633855048950)
XLA Ops:
  0.6 2.0 %edges_and_sums.1 = (bf16[272,256]{1,0:T(8,128)(2,1)S(1)}, bf16[256,256]{1,0:T(8,128)(2,1)S(1)}, f32[8,128]{1,0:T(8,128)S(1)}) custom-call(bf16[8,2,16,256]{3,2,1,0:T(8,128)(2,1)} %bitcast.9, bf16[8,2,16,256]{3,2,1,0:T(8,128)(2,1)} %bitcast.14), custom_call_target="tpu_custom_call" | custom-call | bytes 1048576 | tf_op jit(solution)/shard_map/edges_and_sums/pallas_call | solution.py:397
  2.7 3.3 %collective-permute-start = (bf16[272,256]{1,0:T(8,128)(2,1)S(1)}, bf16[272,256]{1,0:T(8,128)(2,1)S(1)}, u32[]{:S(2)}, u32[]{:S(2)}) collective-permute-start(bf16[272,256]{1,0:T(8,128)(2,1)S(1)} %get-tuple-element.30), channel_id=1, source_target_pairs={{0,1},{1,0},{2,3},{3,2},{4,5},{5,4},{6,7},{7,6},{8,9},{9,8},{10,11... | collective-permute-start | bytes 417800 | tf_op jit(solution)/shard_map/ppermute | solution.py:503
  6.0 1.9 %collective-permute-start.1 = (bf16[256,256]{1,0:T(8,128)(2,1)S(1)}, bf16[256,256]{1,0:T(8,128)(2,1)S(1)}, u32[]{:S(2)}, u32[]{:S(2)}) collective-permute-start(bf16[256,256]{1,0:T(8,128)(2,1)S(1)} %get-tuple-element.31), channel_id=1, source_target_pairs={{1,2},{2,1},{3,4},{4,3},{5,6},{6,5},{7,8},{8,7},{9,10},{10,9},{11,... | collective-permute-start | bytes 393224 | tf_op jit(solution)/shard_map/ppermute | solution.py:504
  7.9 0.8 pair_sums.1
  8.7 10.1 %all-to-all-start = ((f32[32,8,128]{2,1,0:T(8,128)}), f32[32,8,128]{2,1,0:T(8,128)S(1)}, u32[]{:S(2)}, u32[]{:S(2)}) async-start(f32[32,8,128]{2,1,0:T(8,128)} %pair_sums.1), calls=%async_computation | async-start | bytes 262144 | tf_op jit(solution)/shard_map/all_to_all | solution.py:515
  18.9 2.2 %pack_body.1 = (bf16[704,128]{1,0:T(8,128)(2,1)S(1)}, bf16[704,128]{1,0:T(8,128)(2,1)S(1)}, bf16[704,128]{1,0:T(8,128)(2,1)S(1)}, bf16[704,128]{1,0:T(8,128)(2,1)S(1)}) custom-call(bf16[8,2,16,256]{3,2,1,0:T(8,128)(2,1)} %bitcast.10, bf16[8,2,16,256]{3,2,1,0:T(8,128)(2,1)} %bitcast.15, bf16[272,256]{1,0:T(8,128)(2,1)S(1)} %collective-permute-done.refs_2_.refs_1_, ...), custom_call_target="tpu_custom_call" | custom-call | bytes 1048576 | tf_op jit(solution)/shard_map/pack_body/pallas_call | solution.py:397
  21.1 1.3 %collective-permute-start.2 = (bf16[704,128]{1,0:T(8,128)(2,1)S(1)}, bf16[704,128]{1,0:T(8,128)(2,1)S(1)}, u32[]{:S(2)}, u32[]{:S(2)}) collective-permute-start(bf16[704,128]{1,0:T(8,128)(2,1)S(1)} %get-tuple-element.33), channel_id=1, source_target_pairs={{0,16},{16,32},{32,48},{48,0},{1,17},{17,33},{33,49},{49,1},{2,18}... | collective-permute-start | bytes 540680 | tf_op jit(solution)/shard_map/ppermute | solution.py:527
  22.4 2.4 %collective-permute-start.3 = (bf16[704,128]{1,0:T(8,128)(2,1)S(1)}, bf16[704,128]{1,0:T(8,128)(2,1)S(1)}, u32[]{:S(2)}, u32[]{:S(2)}) collective-permute-start(bf16[704,128]{1,0:T(8,128)(2,1)S(1)} %get-tuple-element.34), channel_id=1, source_target_pairs={{0,32},{16,48},{32,0},{48,16},{1,33},{17,49},{33,1},{49,17},{2,34}... | collective-permute-start | bytes 540680 | tf_op jit(solution)/shard_map/ppermute | solution.py:527
  24.8 1.1 %collective-permute-start.4 = (bf16[704,128]{1,0:T(8,128)(2,1)S(1)}, bf16[704,128]{1,0:T(8,128)(2,1)S(1)}, u32[]{:S(2)}, u32[]{:S(2)}) collective-permute-start(bf16[704,128]{1,0:T(8,128)(2,1)S(1)} %get-tuple-element.35), channel_id=1, source_target_pairs={{0,48},{16,0},{32,16},{48,32},{1,49},{17,1},{33,17},{49,33},{2,50}... | collective-permute-start | bytes 540680 | tf_op jit(solution)/shard_map/ppermute | solution.py:527
  26.7 1.4 %all-to-all-done.refs_5_ = f32[32,8,128]{2,1,0:T(8,128)S(1)} async-done(((f32[32,8,128]{2,1,0:T(8,128)}), f32[32,8,128]{2,1,0:T(8,128)S(1)}, u32[]{:S(2)}, u32[]{:S(2)}) %all-to-all-start) | async-done | bytes 131104 | tf_op jit(solution)/shard_map/all_to_all | solution.py:515
  28.1 4.8 %backward_terms.1 = (f32[8,8,128]{2,1,0:T(8,128)}, f32[8,32,256]{2,1,0:T(8,128)S(1)}, f32[8,256]{1,0:T(8,128)S(1)}, f32[8,256]{1,0:T(8,128)S(1)}) custom-call(bf16[8,2,16,256]{3,2,1,0:T(8,128)(2,1)} %bitcast.16, bf16[272,256]{1,0:T(8,128)(2,1)S(1)} %collective-permute-done.refs_2_.refs_1_, bf16[256,256]{1,0:T(8,128)(2,1)S(1)} %collective-permute-done.1.refs_3_.refs_2_, ...), custom_call_target="tpu_custom_call" | custom-call | bytes 1048576 | tf_op jit(solution)/shard_map/backward_terms/pallas_call | solution.py:397
  32.9 0.8 collective-permute-done.3.refs_2_
  33.8 1.5 %collective-permute-start.5 = (bf16[704,128]{1,0:T(8,128)(2,1)S(1)}, bf16[704,128]{1,0:T(8,128)(2,1)S(1)}, u32[]{:S(2)}, u32[]{:S(2)}) collective-permute-start(bf16[704,128]{1,0:T(8,128)(2,1)S(1)} %get-tuple-element.40.refs_0_), channel_id=1, source_target_pairs={{0,1},{1,0},{2,3},{3,2},{4,5},{5,4},{6,7},{7,6},{8,9},{9,8},{10,11... | collective-permute-start | bytes 540680 | tf_op jit(solution)/shard_map/ppermute | solution.py:541
  35.8 3.7 %all-to-all-start.1 = ((f32[8,8,128]{2,1,0:T(8,128)}), f32[8,8,128]{2,1,0:T(8,128)S(1)}, u32[]{:S(2)}, u32[]{:S(2)}) async-start(f32[8,8,128]{2,1,0:T(8,128)} %get-tuple-element.46), calls=%async_computation.1 | async-start | bytes 65536 | tf_op jit(solution)/shard_map/all_to_all | solution.py:540
  39.5 7.8 %kernel_part.1.part_h = bf16[8,128,256]{2,1,0:T(8,128)(2,1)} custom-call(bf16[704,128]{1,0:T(8,128)(2,1)S(1)} %get-tuple-element.40.refs_0_, bf16[704,128]{1,0:T(8,128)(2,1)S(1)} %collective-permute-done.2.refs_1_, bf16[704,128]{1,0:T(8,128)(2,1)S(1)} %collective-permute-done.3.refs_2_, bf16[704,128]{1,0:T(8,128)(2,1)S(1)} %collective-permute-done.4.refs_3_, ...), custom_call_target="tpu_custom_call" | custom-call | flops 7247757312 | bytes 1048576 | tf_op jit(solution)/shard_map/kernel_part/pallas_call | solution.py:397
  47.3 0.7 add_sums.1
  48.0 6.1 %all-to-all-start.2 = ((bf16[8,128,256]{2,1,0:T(8,128)(2,1)}), bf16[8,128,256]{2,1,0:T(8,128)(2,1)S(1)}, u32[]{:S(2)}, u32[]{:S(2)}) async-start(bf16[8,128,256]{2,1,0:T(8,128)(2,1)} %add_sums.1), calls=%async_computation.2 | async-start | bytes 1048576 | tf_op jit(solution)/shard_map/all_to_all | solution.py:572
  54.1 4.0 %forward_conv.1 = bf16[8,2,16,256]{3,2,1,0:T(8,128)(2,1)} custom-call(bf16[8,2,16,256]{3,2,1,0:T(8,128)(2,1)} %bitcast.12, bf16[272,256]{1,0:T(8,128)(2,1)S(1)} %collective-permute-done.refs_2_.refs_1_, bf16[256,256]{1,0:T(8,128)(2,1)S(1)} %collective-permute-done.1.refs_3_.refs_2_, f32[8,256]{1,0:T(8,128)S(1)} %get-tuple-element.48.refs_8_.refs_3_.refs_4_, ...), custom_call_target="tpu_custom_call" | custom-call | flops 7247757312 | bytes 1048576 | tf_op jit(solution)/shard_map/forward_conv/pallas_call | solution.py:397
  58.1 14.0 %all-to-all-done.2.refs_0_ = bf16[8,128,256]{2,1,0:T(8,128)(2,1)S(1)} async-done(((bf16[8,128,256]{2,1,0:T(8,128)(2,1)}), bf16[8,128,256]{2,1,0:T(8,128)(2,1)S(1)}, u32[]{:S(2)}, u32[]{:S(2)}) %all-to-all-start.2) | async-done | bytes 524320 | tf_op jit(solution)/shard_map/all_to_all | solution.py:572
  72.6 2.6 %collective-permute-start.11 = (f32[112,256]{1,0:T(8,128)S(1)}, f32[112,256]{1,0:T(8,128)S(1)}, u32[]{:S(2)}, u32[]{:S(2)}) collective-permute-start(f32[112,256]{1,0:T(8,128)S(1)} %get-tuple-element.53.own_h), channel_id=1, source_target_pairs={{0,192},{64,0},{128,64},{192,128},{1,193},{65,1},{129,65},{193,129... | collective-permute-start | bytes 344072 | tf_op jit(solution)/shard_map/ppermute | solution.py:585
  76.3 2.0 %finish_input.1 = bf16[8,2,16,256]{3,2,1,0:T(8,128)(2,1)} custom-call(f32[8,128]{1,0:T(8,128)S(1)} %get-tuple-element.51.refs_0_, f32[8,32,256]{2,1,0:T(8,128)S(1)} %get-tuple-element.52.refs_1_, bf16[8,2,16,256]{3,2,1,0:T(8,128)(2,1)} %bitcast.13, bf16[8,2,16,256]{3,2,1,0:T(8,128)(2,1)} %bitcast.17, f32[8,256]{1,0:T(8,128)S(1)} %get-tuple-element.48.refs_8_.refs_3_.refs_4_, ...), custom_call_target="tpu_custom_call" | custom-call | bytes 1048576 | tf_op jit(solution)/shard_map/finish_input/pallas_call | solution.py:397
  78.3 2.1 %collective-permute-done.10.two_h = f32[112,256]{1,0:T(8,128)S(1)} collective-permute-done((f32[112,256]{1,0:T(8,128)S(1)}, f32[112,256]{1,0:T(8,128)S(1)}, u32[]{:S(2)}, u32[]{:S(2)}) %collective-permute-start.10) | collective-permute-done | bytes 114720 | tf_op jit(solution)/shard_map/ppermute | solution.py:585
  80.4 3.6 %collective-permute-done.9.one_h = f32[112,256]{1,0:T(8,128)S(1)} collective-permute-done((f32[112,256]{1,0:T(8,128)S(1)}, f32[112,256]{1,0:T(8,128)S(1)}, u32[]{:S(2)}, u32[]{:S(2)}) %collective-permute-start.9) | collective-permute-done | bytes 114720 | tf_op jit(solution)/shard_map/ppermute | solution.py:585
  84.0 1.3 %sum_clips.1 = (f32[27,4,256]{2,1,0:T(4,128)}, f32[1,256]{1,0:T(1,128)}) custom-call(f32[112,256]{1,0:T(8,128)S(1)} %get-tuple-element.53.own_h, f32[112,256]{1,0:T(8,128)S(1)} %collective-permute-done.9.one_h, f32[112,256]{1,0:T(8,128)S(1)} %collective-permute-done.10.two_h, f32[112,256]{1,0:T(8,128)S(1)} %collective-permute-done.11.three_h), custom_call_target="tpu_custom_call" | custom-call | bytes 1048576 | tf_op jit(solution)/shard_map/sum_clips/pallas_call | solution.py:397
  (18 shorter events, 2.3 us)
Async XLA Ops:
  2.7 5.2 %collective-permute-start = (bf16[272,256]{1,0:T(8,128)(2,1)S(1)}, bf16[272,256]{1,0:T(8,128)(2,1)S(1)}, u32[]{:S(2)}, u32[]{:S(2)}) collective-permute-start(bf16[272,256]{1,0:T(8,128)(2,1)S(1)} %get-tuple-element.30), channel_id=1, source_target_pairs={{0,1},{1,0},{2,3},{3,2},{4,5},{5,4},{6,7},{7,6},{8,9},{9,8},{10,11... | collective-permute-start | bytes 417800 | tf_op jit(solution)/shard_map/ppermute | solution.py:503
  6.0 12.9 %collective-permute-start.1 = (bf16[256,256]{1,0:T(8,128)(2,1)S(1)}, bf16[256,256]{1,0:T(8,128)(2,1)S(1)}, u32[]{:S(2)}, u32[]{:S(2)}) collective-permute-start(bf16[256,256]{1,0:T(8,128)(2,1)S(1)} %get-tuple-element.31), channel_id=1, source_target_pairs={{1,2},{2,1},{3,4},{4,3},{5,6},{6,5},{7,8},{8,7},{9,10},{10,9},{11,... | collective-permute-start | bytes 393224 | tf_op jit(solution)/shard_map/ppermute | solution.py:504
  8.7 19.3 %all-to-all-start = ((f32[32,8,128]{2,1,0:T(8,128)}), f32[32,8,128]{2,1,0:T(8,128)S(1)}, u32[]{:S(2)}, u32[]{:S(2)}) async-start(f32[32,8,128]{2,1,0:T(8,128)} %pair_sums.1), calls=%async_computation | async-start | bytes 262144 | tf_op jit(solution)/shard_map/all_to_all | solution.py:515
  21.1 11.8 %collective-permute-start.2 = (bf16[704,128]{1,0:T(8,128)(2,1)S(1)}, bf16[704,128]{1,0:T(8,128)(2,1)S(1)}, u32[]{:S(2)}, u32[]{:S(2)}) collective-permute-start(bf16[704,128]{1,0:T(8,128)(2,1)S(1)} %get-tuple-element.33), channel_id=1, source_target_pairs={{0,16},{16,32},{32,48},{48,0},{1,17},{17,33},{33,49},{49,1},{2,18}... | collective-permute-start | bytes 540680 | tf_op jit(solution)/shard_map/ppermute | solution.py:527
  22.4 11.4 %collective-permute-start.3 = (bf16[704,128]{1,0:T(8,128)(2,1)S(1)}, bf16[704,128]{1,0:T(8,128)(2,1)S(1)}, u32[]{:S(2)}, u32[]{:S(2)}) collective-permute-start(bf16[704,128]{1,0:T(8,128)(2,1)S(1)} %get-tuple-element.34), channel_id=1, source_target_pairs={{0,32},{16,48},{32,0},{48,16},{1,33},{17,49},{33,1},{49,17},{2,34}... | collective-permute-start | bytes 540680 | tf_op jit(solution)/shard_map/ppermute | solution.py:527
  24.8 8.9 %collective-permute-start.4 = (bf16[704,128]{1,0:T(8,128)(2,1)S(1)}, bf16[704,128]{1,0:T(8,128)(2,1)S(1)}, u32[]{:S(2)}, u32[]{:S(2)}) collective-permute-start(bf16[704,128]{1,0:T(8,128)(2,1)S(1)} %get-tuple-element.35), channel_id=1, source_target_pairs={{0,48},{16,0},{32,16},{48,32},{1,49},{17,1},{33,17},{49,33},{2,50}... | collective-permute-start | bytes 540680 | tf_op jit(solution)/shard_map/ppermute | solution.py:527
  33.8 5.7 %collective-permute-start.5 = (bf16[704,128]{1,0:T(8,128)(2,1)S(1)}, bf16[704,128]{1,0:T(8,128)(2,1)S(1)}, u32[]{:S(2)}, u32[]{:S(2)}) collective-permute-start(bf16[704,128]{1,0:T(8,128)(2,1)S(1)} %get-tuple-element.40.refs_0_), channel_id=1, source_target_pairs={{0,1},{1,0},{2,3},{3,2},{4,5},{5,4},{6,7},{7,6},{8,9},{9,8},{10,11... | collective-permute-start | bytes 540680 | tf_op jit(solution)/shard_map/ppermute | solution.py:541
  35.2 4.3 %collective-permute-start.6 = (bf16[704,128]{1,0:T(8,128)(2,1)S(1)}, bf16[704,128]{1,0:T(8,128)(2,1)S(1)}, u32[]{:S(2)}, u32[]{:S(2)}) collective-permute-start(bf16[704,128]{1,0:T(8,128)(2,1)S(1)} %collective-permute-done.2.refs_1_), channel_id=1, source_target_pairs={{0,1},{1,0},{2,3},{3,2},{4,5},{5,4},{6,7},{7,6},{8,9},{9,8},{10,11... | collective-permute-start | bytes 540680 | tf_op jit(solution)/shard_map/ppermute | solution.py:541
  35.3 4.2 %collective-permute-start.7 = (bf16[704,128]{1,0:T(8,128)(2,1)S(1)}, bf16[704,128]{1,0:T(8,128)(2,1)S(1)}, u32[]{:S(2)}, u32[]{:S(2)}) collective-permute-start(bf16[704,128]{1,0:T(8,128)(2,1)S(1)} %collective-permute-done.3.refs_2_), channel_id=1, source_target_pairs={{0,1},{1,0},{2,3},{3,2},{4,5},{5,4},{6,7},{7,6},{8,9},{9,8},{10,11... | collective-permute-start | bytes 540680 | tf_op jit(solution)/shard_map/ppermute | solution.py:541
  35.7 3.8 %collective-permute-start.8 = (bf16[704,128]{1,0:T(8,128)(2,1)S(1)}, bf16[704,128]{1,0:T(8,128)(2,1)S(1)}, u32[]{:S(2)}, u32[]{:S(2)}) collective-permute-start(bf16[704,128]{1,0:T(8,128)(2,1)S(1)} %collective-permute-done.4.refs_3_), channel_id=1, source_target_pairs={{0,1},{1,0},{2,3},{3,2},{4,5},{5,4},{6,7},{7,6},{8,9},{9,8},{10,11... | collective-permute-start | bytes 540680 | tf_op jit(solution)/shard_map/ppermute | solution.py:541
  35.8 11.4 %all-to-all-start.1 = ((f32[8,8,128]{2,1,0:T(8,128)}), f32[8,8,128]{2,1,0:T(8,128)S(1)}, u32[]{:S(2)}, u32[]{:S(2)}) async-start(f32[8,8,128]{2,1,0:T(8,128)} %get-tuple-element.46), calls=%async_computation.1 | async-start | bytes 65536 | tf_op jit(solution)/shard_map/all_to_all | solution.py:540
  48.0 24.1 %all-to-all-start.2 = ((bf16[8,128,256]{2,1,0:T(8,128)(2,1)}), bf16[8,128,256]{2,1,0:T(8,128)(2,1)S(1)}, u32[]{:S(2)}, u32[]{:S(2)}) async-start(bf16[8,128,256]{2,1,0:T(8,128)(2,1)} %add_sums.1), calls=%async_computation.2 | async-start | bytes 1048576 | tf_op jit(solution)/shard_map/all_to_all | solution.py:572
  72.6 5.7 %collective-permute-start.11 = (f32[112,256]{1,0:T(8,128)S(1)}, f32[112,256]{1,0:T(8,128)S(1)}, u32[]{:S(2)}, u32[]{:S(2)}) collective-permute-start(f32[112,256]{1,0:T(8,128)S(1)} %get-tuple-element.53.own_h), channel_id=1, source_target_pairs={{0,192},{64,0},{128,64},{192,128},{1,193},{65,1},{129,65},{193,129... | collective-permute-start | bytes 344072 | tf_op jit(solution)/shard_map/ppermute | solution.py:585
  75.2 5.2 %collective-permute-start.10 = (f32[112,256]{1,0:T(8,128)S(1)}, f32[112,256]{1,0:T(8,128)S(1)}, u32[]{:S(2)}, u32[]{:S(2)}) collective-permute-start(f32[112,256]{1,0:T(8,128)S(1)} %get-tuple-element.53.own_h), channel_id=1, source_target_pairs={{0,128},{64,192},{128,0},{192,64},{1,129},{65,193},{129,1},{193,65... | collective-permute-start | bytes 344072 | tf_op jit(solution)/shard_map/ppermute | solution.py:585
  75.7 8.4 %collective-permute-start.9 = (f32[112,256]{1,0:T(8,128)S(1)}, f32[112,256]{1,0:T(8,128)S(1)}, u32[]{:S(2)}, u32[]{:S(2)}) collective-permute-start(f32[112,256]{1,0:T(8,128)S(1)} %get-tuple-element.53.own_h), channel_id=1, source_target_pairs={{0,64},{64,128},{128,192},{192,0},{1,65},{65,129},{129,193},{193,1... | collective-permute-start | bytes 344072 | tf_op jit(solution)/shard_map/ppermute | solution.py:585

commit v8 on v7

--- a/solution.py
+++ b/solution.py
@@ -106,7 +106,7 @@
     return (terms[FR:, :128] + terms[:FR, 128:]) + terms[:FR, :128]
 
 
-def pack_slices(x_ref, g_ref, hp_ref, hn_ref, out_ref):
+def pack_slices(x_ref, hp_ref, hn_ref, out_ref):
     upper = lax.axis_index("c") == 0
     own = [x_ref[:, 0], x_ref[:, 1]]
     before, after = outside(hp_ref, hn_ref)
@@ -119,10 +119,7 @@
     for y in range(NY):
         part = three[..., y * ASL : (y + 1) * ASL]
         pair = jnp.concatenate([part[:, 0], part[:, 1]], axis=-1)
-        out_ref[y, :AROWS] = pair.reshape(AROWS, 2 * ASL)
-        for c in range(NC):
-            at = AROWS + c * GROWS
-            out_ref[y, at : at + GROWS] = g_ref[..., c * BSL : (c + 1) * BSL].reshape(GROWS, BSL)
+        out_ref[y] = pair.reshape(AROWS, 2 * ASL)
 
 
 def backward_conv(g_ref, hp_ref, hn_ref, k_ref, live_ref, pad_ref, held):
@@ -224,8 +221,9 @@
     place = lax.broadcasted_iota(jnp.int32, shape, 2) // APART
     row = lax.broadcasted_iota(jnp.int32, shape, 0)
     block = 3 * COLS
+    for copy in copies[:8]:
+        copy.wait()
     for n in range(8):
-        copies[n].wait()
         d = n % 4
         y = lax.rem(y_at + NY - d, NY)
         c = c_at if n < 4 else 1 - c_at
@@ -423,11 +421,11 @@
             )
             for n, at in enumerate(moved)
         ]
-        for copy in copies:
+        held = copies.pop(moved.index(late)) if late is not None else None
+        for copy in copies + ([held] if held is not None else []):
             copy.start()
         for n, at in enumerate(moved):
             ins[at] = buffers[n]
-        held = copies.pop(moved.index(late)) if late is not None else None
         for copy in copies:
             copy.wait()
         if held is None:
@@ -456,25 +454,39 @@
     return call(kernel, outs, args, specs, buffers + list(scratch), flops)
 
 
-def pack_body(*refs):
-    sources, outs = refs[:4], refs[4:8]
-    x_ref, g_ref, hp_ref, hn_ref, buf, sem = refs[8:]
-    sources = (sources[0], sources[1], sources[2].at[:HALO], sources[3].at[:HALO])
-    pairs = tuple(zip(sources, (x_ref, g_ref, hp_ref, hn_ref)))
+def pack_body(x_h, g_h, hp_h, hn_h, *refs):
+    outs = refs[:NY]
+    x_ref, hp_ref, hn_ref, buf, sem = refs[NY:]
+    pairs = ((x_h, x_ref), (hp_h.at[:HALO], hp_ref), (hn_h.at[:HALO], hn_ref))
     copies = [pltpu.make_async_copy(a, b, sem.at[n]) for n, (a, b) in enumerate(pairs)]
     for copy in copies:
         copy.start()
+    straight = []
+    for d, out in enumerate(outs):
+        for c in range(NC):
+            at = AROWS + c * GROWS
+            straight.append(
+                pltpu.make_async_copy(
+                    g_h.at[:, c * BSL : (c + 1) * BSL],
+                    out.at[at : at + GROWS],
+                    sem.at[3 + NC * d + c],
+                )
+            )
+    for copy in straight:
+        copy.start()
     for copy in copies:
         copy.wait()
-    pack_slices(x_ref, g_ref, hp_ref, hn_ref, buf)
+    pack_slices(x_ref, hp_ref, hn_ref, buf)
     y_at = lax.axis_index("y")
     copies = [
-        pltpu.make_async_copy(buf.at[lax.rem(y_at + d, NY)], out, sem.at[4 + d])
+        pltpu.make_async_copy(
+            buf.at[lax.rem(y_at + d, NY)], out.at[:AROWS], sem.at[3 + NC * NY + d]
+        )
         for d, out in enumerate(outs)
     ]
     for copy in copies:
         copy.start()
-    for copy in copies:
+    for copy in straight + copies:
         copy.wait()
 
 
@@ -517,11 +529,11 @@
     packed = call(
         pack_body,
         [(block, BF16)] * NY,
-        (x, g, hp, hn),
+        (x, stay_out(output_grad.reshape(GROWS, CH)), hp, hn),
         [HBM] * 4,
-        [pltpu.VMEM(cells, BF16)] * 2
+        [pltpu.VMEM(cells, BF16)]
         + [pltpu.VMEM((HALO, CH), BF16)] * 2
-        + [pltpu.VMEM((NY,) + block, BF16), dma((8,))],
+        + [pltpu.VMEM((NY, AROWS, BSL), BF16), dma((3 + NC * NY + NY,))],
     )
     near = [packed[0]] + [
         lax.ppermute(packed[d], "y", [(i, (i + d) % NY) for i in range(NY)]) for d in range(1, NY)

time: 85.8 us -> 83.8 us (0.977)
  Pallas kernels: 26.2 us -> 24.4 us
    pallas_call x10, Pallas kernels: 26.2 us -> 24.4 us  [call(): pl.pallas_call(body, out_shape=shapes(outs), in_specs=specs, out_specs=tu...]
    all_to_all x1, starting transfers between devices: 6.06 us -> 5.18 us  [local(): merged = lax.all_to_all(merged, 'z', 0, 0)]
  transfers between devices with their start and end apart: 15 -> 15, of which waited for: 5 -> 5; matrix products, arithmetic and copies ran while one was open for 0% -> 0% of each run, Pallas kernels for 25% -> 24%
where the time goes in v8:
time: 83.8 us; the launch traced here: 83.3 us
  starting transfers between devices  35.5 us (42%)
  Pallas kernels  24.4 us (29%)
  waiting for transfers between devices  21.9 us (26%)
  between operations  1.45 us (2%)
    pallas_call x10, Pallas kernels, call(): pl.pallas_call(body, out_shape=shapes(outs), in_specs=specs, out_specs=tu...  24.4 us
    all_to_all x1, waiting for transfers between devices, local(): merged = lax.all_to_all(merged, 'z', 0, 0)  14 us
    all_to_all x1, starting transfers between devices, local(): stats = lax.all_to_all(stats, ('y', 'z'), 0, 0)  10.1 us
    ppermute x3, waiting for transfers between devices, local(): lax.ppermute(rows, 'x', [(i, (i + d) % NX) for i in range(NX)])  5.73 us
    all_to_all x1, starting transfers between devices, local(): merged = lax.all_to_all(merged, 'z', 0, 0)  5.18 us
    ppermute x3, starting transfers between devices, local(): lax.ppermute(packed[d], 'y', [(i, (i + d) % NY) for i in range(NY)])  4.89 us
    ppermute x3, starting transfers between devices, local(): lax.ppermute(rows, 'x', [(i, (i + d) % NX) for i in range(NX)])  3.67 us
    all_to_all x1, starting transfers between devices, local(): terms = lax.all_to_all(terms, ('y', 'c'), 0, 0)  3.65 us
  transfers between devices with their start and end apart: 15, of which 5 were waited for; matrix products, arithmetic and copies ran while one was open for 0% of the time, Pallas kernels for 24%

profile of v8, /device:TPU:1, one launch (start us, length us, event | category | flops | bytes accessed | tf_op | source)
XLA Modules:
  0.0 83.3 jit_solution(14388268480473067599)
XLA Ops:
  0.6 2.0 %edges_and_sums.1 = (bf16[272,256]{1,0:T(8,128)(2,1)S(1)}, bf16[256,256]{1,0:T(8,128)(2,1)S(1)}, f32[8,128]{1,0:T(8,128)S(1)}) custom-call(bf16[8,2,16,256]{3,2,1,0:T(8,128)(2,1)} %bitcast.10, bf16[8,2,16,256]{3,2,1,0:T(8,128)(2,1)} %bitcast.15), custom_call_target="tpu_custom_call" | custom-call | bytes 1048576 | tf_op jit(solution)/shard_map/edges_and_sums/pallas_call | solution.py:395
  2.7 3.3 %collective-permute-start = (bf16[272,256]{1,0:T(8,128)(2,1)S(1)}, bf16[272,256]{1,0:T(8,128)(2,1)S(1)}, u32[]{:S(2)}, u32[]{:S(2)}) collective-permute-start(bf16[272,256]{1,0:T(8,128)(2,1)S(1)} %get-tuple-element.30), channel_id=1, source_target_pairs={{0,1},{1,0},{2,3},{3,2},{4,5},{5,4},{6,7},{7,6},{8,9},{9,8},{10,11... | collective-permute-start | bytes 417800 | tf_op jit(solution)/shard_map/ppermute | solution.py:515
  6.0 1.9 %collective-permute-start.1 = (bf16[256,256]{1,0:T(8,128)(2,1)S(1)}, bf16[256,256]{1,0:T(8,128)(2,1)S(1)}, u32[]{:S(2)}, u32[]{:S(2)}) collective-permute-start(bf16[256,256]{1,0:T(8,128)(2,1)S(1)} %get-tuple-element.31), channel_id=1, source_target_pairs={{1,2},{2,1},{3,4},{4,3},{5,6},{6,5},{7,8},{8,7},{9,10},{10,9},{11,... | collective-permute-start | bytes 393224 | tf_op jit(solution)/shard_map/ppermute | solution.py:516
  7.9 0.8 pair_sums.1
  8.7 10.1 %all-to-all-start = ((f32[32,8,128]{2,1,0:T(8,128)}), f32[32,8,128]{2,1,0:T(8,128)S(1)}, u32[]{:S(2)}, u32[]{:S(2)}) async-start(f32[32,8,128]{2,1,0:T(8,128)} %pair_sums.1), calls=%async_computation | async-start | bytes 262144 | tf_op jit(solution)/shard_map/all_to_all | solution.py:527
  18.9 1.5 %pack_body.1 = (bf16[704,128]{1,0:T(8,128)(2,1)S(1)}, bf16[704,128]{1,0:T(8,128)(2,1)S(1)}, bf16[704,128]{1,0:T(8,128)(2,1)S(1)}, bf16[704,128]{1,0:T(8,128)(2,1)S(1)}) custom-call(bf16[8,2,16,256]{3,2,1,0:T(8,128)(2,1)} %bitcast.11, bf16[256,256]{1,0:T(8,128)(2,1)} %bitcast.16, bf16[272,256]{1,0:T(8,128)(2,1)S(1)} %collective-permute-done.hp_h.refs_1_, ...), custom_call_target="tpu_custom_call" | custom-call | bytes 1048576 | tf_op jit(solution)/shard_map/pack_body/pallas_call | solution.py:395
  20.4 1.3 %collective-permute-start.2 = (bf16[704,128]{1,0:T(8,128)(2,1)S(1)}, bf16[704,128]{1,0:T(8,128)(2,1)S(1)}, u32[]{:S(2)}, u32[]{:S(2)}) collective-permute-start(bf16[704,128]{1,0:T(8,128)(2,1)S(1)} %get-tuple-element.33), channel_id=1, source_target_pairs={{0,16},{16,32},{32,48},{48,0},{1,17},{17,33},{33,49},{49,1},{2,18}... | collective-permute-start | bytes 540680 | tf_op jit(solution)/shard_map/ppermute | solution.py:539
  21.7 2.4 %collective-permute-start.3 = (bf16[704,128]{1,0:T(8,128)(2,1)S(1)}, bf16[704,128]{1,0:T(8,128)(2,1)S(1)}, u32[]{:S(2)}, u32[]{:S(2)}) collective-permute-start(bf16[704,128]{1,0:T(8,128)(2,1)S(1)} %get-tuple-element.34), channel_id=1, source_target_pairs={{0,32},{16,48},{32,0},{48,16},{1,33},{17,49},{33,1},{49,17},{2,34}... | collective-permute-start | bytes 540680 | tf_op jit(solution)/shard_map/ppermute | solution.py:539
  24.1 1.1 %collective-permute-start.4 = (bf16[704,128]{1,0:T(8,128)(2,1)S(1)}, bf16[704,128]{1,0:T(8,128)(2,1)S(1)}, u32[]{:S(2)}, u32[]{:S(2)}) collective-permute-start(bf16[704,128]{1,0:T(8,128)(2,1)S(1)} %get-tuple-element.35), channel_id=1, source_target_pairs={{0,48},{16,0},{32,16},{48,32},{1,49},{17,1},{33,17},{49,33},{2,50}... | collective-permute-start | bytes 540680 | tf_op jit(solution)/shard_map/ppermute | solution.py:539
  25.9 2.1 %all-to-all-done.refs_5_ = f32[32,8,128]{2,1,0:T(8,128)S(1)} async-done(((f32[32,8,128]{2,1,0:T(8,128)}), f32[32,8,128]{2,1,0:T(8,128)S(1)}, u32[]{:S(2)}, u32[]{:S(2)}) %all-to-all-start) | async-done | bytes 131104 | tf_op jit(solution)/shard_map/all_to_all | solution.py:527
  28.1 5.0 %backward_terms.1 = (f32[8,8,128]{2,1,0:T(8,128)}, f32[8,32,256]{2,1,0:T(8,128)S(1)}, f32[8,256]{1,0:T(8,128)S(1)}, f32[8,256]{1,0:T(8,128)S(1)}) custom-call(bf16[8,2,16,256]{3,2,1,0:T(8,128)(2,1)} %bitcast.17, bf16[272,256]{1,0:T(8,128)(2,1)S(1)} %collective-permute-done.hp_h.refs_1_, bf16[256,256]{1,0:T(8,128)(2,1)S(1)} %collective-permute-done.1.hn_h.refs_2_, ...), custom_call_target="tpu_custom_call" | custom-call | bytes 1048576 | tf_op jit(solution)/shard_map/backward_terms/pallas_call | solution.py:395
  33.2 2.2 %collective-permute-start.5 = (bf16[704,128]{1,0:T(8,128)(2,1)S(1)}, bf16[704,128]{1,0:T(8,128)(2,1)S(1)}, u32[]{:S(2)}, u32[]{:S(2)}) collective-permute-start(bf16[704,128]{1,0:T(8,128)(2,1)S(1)} %get-tuple-element.40.refs_0_), channel_id=1, source_target_pairs={{0,1},{1,0},{2,3},{3,2},{4,5},{5,4},{6,7},{7,6},{8,9},{9,8},{10,11... | collective-permute-start | bytes 540680 | tf_op jit(solution)/shard_map/ppermute | solution.py:553
  36.0 3.7 %all-to-all-start.1 = ((f32[8,8,128]{2,1,0:T(8,128)}), f32[8,8,128]{2,1,0:T(8,128)S(1)}, u32[]{:S(2)}, u32[]{:S(2)}) async-start(f32[8,8,128]{2,1,0:T(8,128)} %get-tuple-element.46), calls=%async_computation.1 | async-start | bytes 65536 | tf_op jit(solution)/shard_map/all_to_all | solution.py:552
  39.7 6.5 %kernel_part.1.part_h = bf16[8,128,256]{2,1,0:T(8,128)(2,1)} custom-call(bf16[704,128]{1,0:T(8,128)(2,1)S(1)} %get-tuple-element.40.refs_0_, bf16[704,128]{1,0:T(8,128)(2,1)S(1)} %collective-permute-done.2.refs_1_, bf16[704,128]{1,0:T(8,128)(2,1)S(1)} %collective-permute-done.3.refs_2_, bf16[704,128]{1,0:T(8,128)(2,1)S(1)} %collective-permute-done.4.refs_3_, ...), custom_call_target="tpu_custom_call" | custom-call | flops 7247757312 | bytes 1048576 | tf_op jit(solution)/shard_map/kernel_part/pallas_call | solution.py:395
  46.2 0.7 add_sums.1
  46.9 5.2 %all-to-all-start.2 = ((bf16[8,128,256]{2,1,0:T(8,128)(2,1)}), bf16[8,128,256]{2,1,0:T(8,128)(2,1)S(1)}, u32[]{:S(2)}, u32[]{:S(2)}) async-start(bf16[8,128,256]{2,1,0:T(8,128)(2,1)} %add_sums.1), calls=%async_computation.2 | async-start | bytes 1048576 | tf_op jit(solution)/shard_map/all_to_all | solution.py:584
  52.1 4.0 %forward_conv.1 = bf16[8,2,16,256]{3,2,1,0:T(8,128)(2,1)} custom-call(bf16[8,2,16,256]{3,2,1,0:T(8,128)(2,1)} %bitcast.13, bf16[272,256]{1,0:T(8,128)(2,1)S(1)} %collective-permute-done.hp_h.refs_1_, bf16[256,256]{1,0:T(8,128)(2,1)S(1)} %collective-permute-done.1.hn_h.refs_2_, f32[8,256]{1,0:T(8,128)S(1)} %get-tuple-element.48.refs_8_.refs_3_.refs_4_, ...), custom_call_target="tpu_custom_call" | custom-call | flops 7247757312 | bytes 1048576 | tf_op jit(solution)/shard_map/forward_conv/pallas_call | solution.py:395
  56.1 14.0 %all-to-all-done.2.refs_0_ = bf16[8,128,256]{2,1,0:T(8,128)(2,1)S(1)} async-done(((bf16[8,128,256]{2,1,0:T(8,128)(2,1)}), bf16[8,128,256]{2,1,0:T(8,128)(2,1)S(1)}, u32[]{:S(2)}, u32[]{:S(2)}) %all-to-all-start.2) | async-done | bytes 524320 | tf_op jit(solution)/shard_map/all_to_all | solution.py:584
  70.6 2.6 %collective-permute-start.11 = (f32[112,256]{1,0:T(8,128)S(1)}, f32[112,256]{1,0:T(8,128)S(1)}, u32[]{:S(2)}, u32[]{:S(2)}) collective-permute-start(f32[112,256]{1,0:T(8,128)S(1)} %get-tuple-element.53.own_h), channel_id=1, source_target_pairs={{0,192},{64,0},{128,64},{192,128},{1,193},{65,1},{129,65},{193,129... | collective-permute-start | bytes 344072 | tf_op jit(solution)/shard_map/ppermute | solution.py:597
  73.7 0.6 collective-permute-start.9
  74.3 2.0 %finish_input.1 = bf16[8,2,16,256]{3,2,1,0:T(8,128)(2,1)} custom-call(f32[8,128]{1,0:T(8,128)S(1)} %get-tuple-element.51.refs_0_, f32[8,32,256]{2,1,0:T(8,128)S(1)} %get-tuple-element.52.refs_1_, bf16[8,2,16,256]{3,2,1,0:T(8,128)(2,1)} %bitcast.14, bf16[8,2,16,256]{3,2,1,0:T(8,128)(2,1)} %bitcast.18, f32[8,256]{1,0:T(8,128)S(1)} %get-tuple-element.48.refs_8_.refs_3_.refs_4_, ...), custom_call_target="tpu_custom_call" | custom-call | bytes 1048576 | tf_op jit(solution)/shard_map/finish_input/pallas_call | solution.py:395
  76.3 2.1 %collective-permute-done.10.two_h = f32[112,256]{1,0:T(8,128)S(1)} collective-permute-done((f32[112,256]{1,0:T(8,128)S(1)}, f32[112,256]{1,0:T(8,128)S(1)}, u32[]{:S(2)}, u32[]{:S(2)}) %collective-permute-start.10) | collective-permute-done | bytes 114720 | tf_op jit(solution)/shard_map/ppermute | solution.py:597
  78.4 3.6 %collective-permute-done.9.one_h = f32[112,256]{1,0:T(8,128)S(1)} collective-permute-done((f32[112,256]{1,0:T(8,128)S(1)}, f32[112,256]{1,0:T(8,128)S(1)}, u32[]{:S(2)}, u32[]{:S(2)}) %collective-permute-start.9) | collective-permute-done | bytes 114720 | tf_op jit(solution)/shard_map/ppermute | solution.py:597
  82.0 1.3 %sum_clips.1 = (f32[27,4,256]{2,1,0:T(4,128)}, f32[1,256]{1,0:T(1,128)}) custom-call(f32[112,256]{1,0:T(8,128)S(1)} %get-tuple-element.53.own_h, f32[112,256]{1,0:T(8,128)S(1)} %collective-permute-done.9.one_h, f32[112,256]{1,0:T(8,128)S(1)} %collective-permute-done.10.two_h, f32[112,256]{1,0:T(8,128)S(1)} %collective-permute-done.11.three_h), custom_call_target="tpu_custom_call" | custom-call | bytes 1048576 | tf_op jit(solution)/shard_map/sum_clips/pallas_call | solution.py:395
  (18 shorter events, 1.8 us)
Async XLA Ops:
  2.7 5.2 %collective-permute-start = (bf16[272,256]{1,0:T(8,128)(2,1)S(1)}, bf16[272,256]{1,0:T(8,128)(2,1)S(1)}, u32[]{:S(2)}, u32[]{:S(2)}) collective-permute-start(bf16[272,256]{1,0:T(8,128)(2,1)S(1)} %get-tuple-element.30), channel_id=1, source_target_pairs={{0,1},{1,0},{2,3},{3,2},{4,5},{5,4},{6,7},{7,6},{8,9},{9,8},{10,11... | collective-permute-start | bytes 417800 | tf_op jit(solution)/shard_map/ppermute | solution.py:515
  6.0 12.9 %collective-permute-start.1 = (bf16[256,256]{1,0:T(8,128)(2,1)S(1)}, bf16[256,256]{1,0:T(8,128)(2,1)S(1)}, u32[]{:S(2)}, u32[]{:S(2)}) collective-permute-start(bf16[256,256]{1,0:T(8,128)(2,1)S(1)} %get-tuple-element.31), channel_id=1, source_target_pairs={{1,2},{2,1},{3,4},{4,3},{5,6},{6,5},{7,8},{8,7},{9,10},{10,9},{11,... | collective-permute-start | bytes 393224 | tf_op jit(solution)/shard_map/ppermute | solution.py:516
  8.7 19.3 %all-to-all-start = ((f32[32,8,128]{2,1,0:T(8,128)}), f32[32,8,128]{2,1,0:T(8,128)S(1)}, u32[]{:S(2)}, u32[]{:S(2)}) async-start(f32[32,8,128]{2,1,0:T(8,128)} %pair_sums.1), calls=%async_computation | async-start | bytes 262144 | tf_op jit(solution)/shard_map/all_to_all | solution.py:527
  20.4 12.7 %collective-permute-start.2 = (bf16[704,128]{1,0:T(8,128)(2,1)S(1)}, bf16[704,128]{1,0:T(8,128)(2,1)S(1)}, u32[]{:S(2)}, u32[]{:S(2)}) collective-permute-start(bf16[704,128]{1,0:T(8,128)(2,1)S(1)} %get-tuple-element.33), channel_id=1, source_target_pairs={{0,16},{16,32},{32,48},{48,0},{1,17},{17,33},{33,49},{49,1},{2,18}... | collective-permute-start | bytes 540680 | tf_op jit(solution)/shard_map/ppermute | solution.py:539
  21.7 11.5 %collective-permute-start.3 = (bf16[704,128]{1,0:T(8,128)(2,1)S(1)}, bf16[704,128]{1,0:T(8,128)(2,1)S(1)}, u32[]{:S(2)}, u32[]{:S(2)}) collective-permute-start(bf16[704,128]{1,0:T(8,128)(2,1)S(1)} %get-tuple-element.34), channel_id=1, source_target_pairs={{0,32},{16,48},{32,0},{48,16},{1,33},{17,49},{33,1},{49,17},{2,34}... | collective-permute-start | bytes 540680 | tf_op jit(solution)/shard_map/ppermute | solution.py:539
  24.1 9.1 %collective-permute-start.4 = (bf16[704,128]{1,0:T(8,128)(2,1)S(1)}, bf16[704,128]{1,0:T(8,128)(2,1)S(1)}, u32[]{:S(2)}, u32[]{:S(2)}) collective-permute-start(bf16[704,128]{1,0:T(8,128)(2,1)S(1)} %get-tuple-element.35), channel_id=1, source_target_pairs={{0,48},{16,0},{32,16},{48,32},{1,49},{17,1},{33,17},{49,33},{2,50}... | collective-permute-start | bytes 540680 | tf_op jit(solution)/shard_map/ppermute | solution.py:539
  33.2 6.4 %collective-permute-start.5 = (bf16[704,128]{1,0:T(8,128)(2,1)S(1)}, bf16[704,128]{1,0:T(8,128)(2,1)S(1)}, u32[]{:S(2)}, u32[]{:S(2)}) collective-permute-start(bf16[704,128]{1,0:T(8,128)(2,1)S(1)} %get-tuple-element.40.refs_0_), channel_id=1, source_target_pairs={{0,1},{1,0},{2,3},{3,2},{4,5},{5,4},{6,7},{7,6},{8,9},{9,8},{10,11... | collective-permute-start | bytes 540680 | tf_op jit(solution)/shard_map/ppermute | solution.py:553
  35.4 4.3 %collective-permute-start.6 = (bf16[704,128]{1,0:T(8,128)(2,1)S(1)}, bf16[704,128]{1,0:T(8,128)(2,1)S(1)}, u32[]{:S(2)}, u32[]{:S(2)}) collective-permute-start(bf16[704,128]{1,0:T(8,128)(2,1)S(1)} %collective-permute-done.2.refs_1_), channel_id=1, source_target_pairs={{0,1},{1,0},{2,3},{3,2},{4,5},{5,4},{6,7},{7,6},{8,9},{9,8},{10,11... | collective-permute-start | bytes 540680 | tf_op jit(solution)/shard_map/ppermute | solution.py:553
  35.5 4.2 %collective-permute-start.7 = (bf16[704,128]{1,0:T(8,128)(2,1)S(1)}, bf16[704,128]{1,0:T(8,128)(2,1)S(1)}, u32[]{:S(2)}, u32[]{:S(2)}) collective-permute-start(bf16[704,128]{1,0:T(8,128)(2,1)S(1)} %collective-permute-done.3.refs_2_), channel_id=1, source_target_pairs={{0,1},{1,0},{2,3},{3,2},{4,5},{5,4},{6,7},{7,6},{8,9},{9,8},{10,11... | collective-permute-start | bytes 540680 | tf_op jit(solution)/shard_map/ppermute | solution.py:553
  35.9 3.8 %collective-permute-start.8 = (bf16[704,128]{1,0:T(8,128)(2,1)S(1)}, bf16[704,128]{1,0:T(8,128)(2,1)S(1)}, u32[]{:S(2)}, u32[]{:S(2)}) collective-permute-start(bf16[704,128]{1,0:T(8,128)(2,1)S(1)} %collective-permute-done.4.refs_3_), channel_id=1, source_target_pairs={{0,1},{1,0},{2,3},{3,2},{4,5},{5,4},{6,7},{7,6},{8,9},{9,8},{10,11... | collective-permute-start | bytes 540680 | tf_op jit(solution)/shard_map/ppermute | solution.py:553
  36.0 10.2 %all-to-all-start.1 = ((f32[8,8,128]{2,1,0:T(8,128)}), f32[8,8,128]{2,1,0:T(8,128)S(1)}, u32[]{:S(2)}, u32[]{:S(2)}) async-start(f32[8,8,128]{2,1,0:T(8,128)} %get-tuple-element.46), calls=%async_computation.1 | async-start | bytes 65536 | tf_op jit(solution)/shard_map/all_to_all | solution.py:552
  46.9 23.2 %all-to-all-start.2 = ((bf16[8,128,256]{2,1,0:T(8,128)(2,1)}), bf16[8,128,256]{2,1,0:T(8,128)(2,1)S(1)}, u32[]{:S(2)}, u32[]{:S(2)}) async-start(bf16[8,128,256]{2,1,0:T(8,128)(2,1)} %add_sums.1), calls=%async_computation.2 | async-start | bytes 1048576 | tf_op jit(solution)/shard_map/all_to_all | solution.py:584
  70.6 5.7 %collective-permute-start.11 = (f32[112,256]{1,0:T(8,128)S(1)}, f32[112,256]{1,0:T(8,128)S(1)}, u32[]{:S(2)}, u32[]{:S(2)}) collective-permute-start(f32[112,256]{1,0:T(8,128)S(1)} %get-tuple-element.53.own_h), channel_id=1, source_target_pairs={{0,192},{64,0},{128,64},{192,128},{1,193},{65,1},{129,65},{193,129... | collective-permute-start | bytes 344072 | tf_op jit(solution)/shard_map/ppermute | solution.py:597
  73.2 5.2 %collective-permute-start.10 = (f32[112,256]{1,0:T(8,128)S(1)}, f32[112,256]{1,0:T(8,128)S(1)}, u32[]{:S(2)}, u32[]{:S(2)}) collective-permute-start(f32[112,256]{1,0:T(8,128)S(1)} %get-tuple-element.53.own_h), channel_id=1, source_target_pairs={{0,128},{64,192},{128,0},{192,64},{1,129},{65,193},{129,1},{193,65... | collective-permute-start | bytes 344072 | tf_op jit(solution)/shard_map/ppermute | solution.py:597
  73.7 8.4 %collective-permute-start.9 = (f32[112,256]{1,0:T(8,128)S(1)}, f32[112,256]{1,0:T(8,128)S(1)}, u32[]{:S(2)}, u32[]{:S(2)}) collective-permute-start(f32[112,256]{1,0:T(8,128)S(1)} %get-tuple-element.53.own_h), channel_id=1, source_target_pairs={{0,64},{64,128},{128,192},{192,0},{1,65},{65,129},{129,193},{193,1... | collective-permute-start | bytes 344072 | tf_op jit(solution)/shard_map/ppermute | solution.py:597

commit v9 on v8

--- a/solution.py
+++ b/solution.py
@@ -26,6 +26,7 @@
 APART = ASL // NC
 BLOCK = AROWS + NC * GROWS
 TERMS = 16
+STEPS = 32000.0
 HALO = FR * COLS
 HI = lax.Precision.HIGHEST
 
@@ -294,6 +295,12 @@
     copy.wait()
 
 
+def scale_of(values):
+    most = jnp.max(jnp.max(jnp.abs(values), axis=0, keepdims=True), axis=1, keepdims=True)
+    most = jnp.broadcast_to(jnp.maximum(most, 1e-36), (1, CH))
+    return jnp.ceil(jnp.log2(most))
+
+
 def sum_rows(in_ref, out_ref, sums_ref):
     total = jnp.sum(in_ref[...].astype(F32), axis=0)
     sums = from_terms(total[PROWS:])
@@ -304,8 +311,14 @@
     row = lax.broadcasted_iota(jnp.int32, (FR, CH), 0)
     lane = lax.broadcasted_iota(jnp.int32, (FR, CH), 1)
     gain = jnp.sum(jnp.where(lane // GROUPS == row, wide, 0.0), axis=0, keepdims=True)
-    out_ref[...] = total[:PROWS]
-    out_ref[4 * TAPS : 4 * TAPS + 1] = gain
+    part = total[: 4 * TAPS]
+    exponent, gain_exponent = scale_of(part), scale_of(gain)
+    code = jnp.floor(part / jnp.exp2(exponent) * STEPS + 0.5)
+    steps = gain / jnp.exp2(gain_exponent) * STEPS
+    upper = jnp.floor(steps + 0.5)
+    lower = jnp.floor((steps - upper) * STEPS + 0.5)
+    rows = jnp.concatenate([code, upper, lower, exponent, gain_exponent], axis=0)
+    out_ref[...] = rows.astype(jnp.int32).astype(jnp.int16)
 
 
 def forward_conv(x_ref, hp_ref, hn_ref, mean_ref, inv_ref, gain_ref, k_ref, live_ref, out_ref, pad_ref, held):
@@ -365,10 +378,17 @@
         copy.start()
     for copy in copies:
         copy.wait()
-    total = ((in_ref[0] + in_ref[1]) + in_ref[2]) + in_ref[3]
+    total = jnp.zeros((4 * TAPS, CH), F32)
+    gain = jnp.zeros((1, CH), F32)
+    at = 4 * TAPS
+    for n in range(NX):
+        rows = in_ref[n].astype(jnp.int32).astype(F32)
+        total = total + rows[:at] / STEPS * jnp.exp2(rows[at + 2 : at + 3])
+        steps = rows[at : at + 1] + rows[at + 1 : at + 2] / STEPS
+        gain = gain + steps / STEPS * jnp.exp2(rows[at + 3 : at + 4])
     for tap in range(TAPS):
         kg_ref[tap] = total[4 * tap : 4 * tap + 4]
-    gain_ref[...] = total[4 * TAPS : 4 * TAPS + 1]
+    gain_ref[...] = gain
     out = (
         pltpu.make_async_copy(kg_ref, kg_h, sem.at[4]),
         pltpu.make_async_copy(gain_ref, gain_h, sem.at[5]),
@@ -592,7 +612,7 @@
         flops=conv_flops,
     )
     merged, block_output = lax.optimization_barrier((merged, block_output))
-    rows, sums = run(sum_rows, [((PROWS, CH), F32), ((FR, 128), F32)], (merged,))
+    rows, sums = run(sum_rows, [((PROWS, CH), jnp.int16), ((FR, 128), F32)], (merged,))
     others = [rows] + [
         lax.ppermute(rows, "x", [(i, (i + d) % NX) for i in range(NX)]) for d in range(1, NX)
     ]
@@ -605,7 +625,7 @@
         others,
         [HBM] * 4,
         [
-            pltpu.VMEM((NX, PROWS, CH), F32),
+            pltpu.VMEM((NX, PROWS, CH), jnp.int16),
             pltpu.VMEM((TAPS, 4, CH), F32),
             pltpu.VMEM((1, CH), F32),
             dma((6,)),

time: 83.8 us -> 80.2 us (0.957)
  waiting for transfers between devices: 21.9 us -> 18.2 us
    ppermute x3, waiting for transfers between devices: 5.73 us -> 1.99 us  [local(): lax.ppermute(rows, 'x', [(i, (i + d) % NX) for i in range(NX)])]
  transfers between devices with their start and end apart: 15 -> 15, of which waited for: 5 -> 5; matrix products, arithmetic and copies ran while one was open for 0% -> 0% of each run, Pallas kernels for 24% -> 25%
where the time goes in v9:
time: 80.2 us; the launch traced here: 79.3 us
  starting transfers between devices  35.5 us (44%)
  Pallas kernels  24.1 us (30%)
  waiting for transfers between devices  18.2 us (23%)
  between operations  1.45 us (2%)
    pallas_call x10, Pallas kernels, call(): pl.pallas_call(body, out_shape=shapes(outs), in_specs=specs, out_specs=tu...  24.1 us
    all_to_all x1, waiting for transfers between devices, local(): merged = lax.all_to_all(merged, 'z', 0, 0)  14 us
    all_to_all x1, starting transfers between devices, local(): stats = lax.all_to_all(stats, ('y', 'z'), 0, 0)  10.1 us
    all_to_all x1, starting transfers between devices, local(): merged = lax.all_to_all(merged, 'z', 0, 0)  5.18 us
    ppermute x3, starting transfers between devices, local(): lax.ppermute(packed[d], 'y', [(i, (i + d) % NY) for i in range(NY)])  4.89 us
    ppermute x3, starting transfers between devices, local(): lax.ppermute(rows, 'x', [(i, (i + d) % NX) for i in range(NX)])  3.67 us
    all_to_all x1, starting transfers between devices, local(): terms = lax.all_to_all(terms, ('y', 'c'), 0, 0)  3.65 us
    ppermute x1, starting transfers between devices, local(): hp = lax.ppermute(inner, 'c', swap)  3.33 us
  transfers between devices with their start and end apart: 15, of which 5 were waited for; matrix products, arithmetic and copies ran while one was open for 0% of the time, Pallas kernels for 25%

profile of v9, /device:TPU:1, one launch (start us, length us, event | category | flops | bytes accessed | tf_op | source)
XLA Modules:
  0.0 79.3 jit_solution(13959529362640018447)
XLA Ops:
  0.6 2.0 %edges_and_sums.1 = (bf16[272,256]{1,0:T(8,128)(2,1)S(1)}, bf16[256,256]{1,0:T(8,128)(2,1)S(1)}, f32[8,128]{1,0:T(8,128)S(1)}) custom-call(bf16[8,2,16,256]{3,2,1,0:T(8,128)(2,1)} %bitcast.10, bf16[8,2,16,256]{3,2,1,0:T(8,128)(2,1)} %bitcast.15), custom_call_target="tpu_custom_call" | custom-call | bytes 1048576 | tf_op jit(solution)/shard_map/edges_and_sums/pallas_call | solution.py:415
  2.7 3.3 %collective-permute-start = (bf16[272,256]{1,0:T(8,128)(2,1)S(1)}, bf16[272,256]{1,0:T(8,128)(2,1)S(1)}, u32[]{:S(2)}, u32[]{:S(2)}) collective-permute-start(bf16[272,256]{1,0:T(8,128)(2,1)S(1)} %get-tuple-element.30), channel_id=1, source_target_pairs={{0,1},{1,0},{2,3},{3,2},{4,5},{5,4},{6,7},{7,6},{8,9},{9,8},{10,11... | collective-permute-start | bytes 417800 | tf_op jit(solution)/shard_map/ppermute | solution.py:535
  6.0 1.9 %collective-permute-start.1 = (bf16[256,256]{1,0:T(8,128)(2,1)S(1)}, bf16[256,256]{1,0:T(8,128)(2,1)S(1)}, u32[]{:S(2)}, u32[]{:S(2)}) collective-permute-start(bf16[256,256]{1,0:T(8,128)(2,1)S(1)} %get-tuple-element.31), channel_id=1, source_target_pairs={{1,2},{2,1},{3,4},{4,3},{5,6},{6,5},{7,8},{8,7},{9,10},{10,9},{11,... | collective-permute-start | bytes 393224 | tf_op jit(solution)/shard_map/ppermute | solution.py:536
  7.9 0.8 pair_sums.1
  8.7 10.1 %all-to-all-start = ((f32[32,8,128]{2,1,0:T(8,128)}), f32[32,8,128]{2,1,0:T(8,128)S(1)}, u32[]{:S(2)}, u32[]{:S(2)}) async-start(f32[32,8,128]{2,1,0:T(8,128)} %pair_sums.1), calls=%async_computation | async-start | bytes 262144 | tf_op jit(solution)/shard_map/all_to_all | solution.py:547
  18.9 1.5 %pack_body.1 = (bf16[704,128]{1,0:T(8,128)(2,1)S(1)}, bf16[704,128]{1,0:T(8,128)(2,1)S(1)}, bf16[704,128]{1,0:T(8,128)(2,1)S(1)}, bf16[704,128]{1,0:T(8,128)(2,1)S(1)}) custom-call(bf16[8,2,16,256]{3,2,1,0:T(8,128)(2,1)} %bitcast.11, bf16[256,256]{1,0:T(8,128)(2,1)} %bitcast.16, bf16[272,256]{1,0:T(8,128)(2,1)S(1)} %collective-permute-done.hp_h.refs_1_, ...), custom_call_target="tpu_custom_call" | custom-call | bytes 1048576 | tf_op jit(solution)/shard_map/pack_body/pallas_call | solution.py:415
  20.4 1.3 %collective-permute-start.2 = (bf16[704,128]{1,0:T(8,128)(2,1)S(1)}, bf16[704,128]{1,0:T(8,128)(2,1)S(1)}, u32[]{:S(2)}, u32[]{:S(2)}) collective-permute-start(bf16[704,128]{1,0:T(8,128)(2,1)S(1)} %get-tuple-element.33), channel_id=1, source_target_pairs={{0,16},{16,32},{32,48},{48,0},{1,17},{17,33},{33,49},{49,1},{2,18}... | collective-permute-start | bytes 540680 | tf_op jit(solution)/shard_map/ppermute | solution.py:559
  21.7 2.4 %collective-permute-start.3 = (bf16[704,128]{1,0:T(8,128)(2,1)S(1)}, bf16[704,128]{1,0:T(8,128)(2,1)S(1)}, u32[]{:S(2)}, u32[]{:S(2)}) collective-permute-start(bf16[704,128]{1,0:T(8,128)(2,1)S(1)} %get-tuple-element.34), channel_id=1, source_target_pairs={{0,32},{16,48},{32,0},{48,16},{1,33},{17,49},{33,1},{49,17},{2,34}... | collective-permute-start | bytes 540680 | tf_op jit(solution)/shard_map/ppermute | solution.py:559
  24.1 1.1 %collective-permute-start.4 = (bf16[704,128]{1,0:T(8,128)(2,1)S(1)}, bf16[704,128]{1,0:T(8,128)(2,1)S(1)}, u32[]{:S(2)}, u32[]{:S(2)}) collective-permute-start(bf16[704,128]{1,0:T(8,128)(2,1)S(1)} %get-tuple-element.35), channel_id=1, source_target_pairs={{0,48},{16,0},{32,16},{48,32},{1,49},{17,1},{33,17},{49,33},{2,50}... | collective-permute-start | bytes 540680 | tf_op jit(solution)/shard_map/ppermute | solution.py:559
  25.9 2.1 %all-to-all-done.refs_5_ = f32[32,8,128]{2,1,0:T(8,128)S(1)} async-done(((f32[32,8,128]{2,1,0:T(8,128)}), f32[32,8,128]{2,1,0:T(8,128)S(1)}, u32[]{:S(2)}, u32[]{:S(2)}) %all-to-all-start) | async-done | bytes 131104 | tf_op jit(solution)/shard_map/all_to_all | solution.py:547
  28.1 5.0 %backward_terms.1 = (f32[8,8,128]{2,1,0:T(8,128)}, f32[8,32,256]{2,1,0:T(8,128)S(1)}, f32[8,256]{1,0:T(8,128)S(1)}, f32[8,256]{1,0:T(8,128)S(1)}) custom-call(bf16[8,2,16,256]{3,2,1,0:T(8,128)(2,1)} %bitcast.17, bf16[272,256]{1,0:T(8,128)(2,1)S(1)} %collective-permute-done.hp_h.refs_1_, bf16[256,256]{1,0:T(8,128)(2,1)S(1)} %collective-permute-done.1.hn_h.refs_2_, ...), custom_call_target="tpu_custom_call" | custom-call | bytes 1048576 | tf_op jit(solution)/shard_map/backward_terms/pallas_call | solution.py:415
  33.2 2.2 %collective-permute-start.5 = (bf16[704,128]{1,0:T(8,128)(2,1)S(1)}, bf16[704,128]{1,0:T(8,128)(2,1)S(1)}, u32[]{:S(2)}, u32[]{:S(2)}) collective-permute-start(bf16[704,128]{1,0:T(8,128)(2,1)S(1)} %get-tuple-element.40.refs_0_), channel_id=1, source_target_pairs={{0,1},{1,0},{2,3},{3,2},{4,5},{5,4},{6,7},{7,6},{8,9},{9,8},{10,11... | collective-permute-start | bytes 540680 | tf_op jit(solution)/shard_map/ppermute | solution.py:573
  36.0 3.7 %all-to-all-start.1 = ((f32[8,8,128]{2,1,0:T(8,128)}), f32[8,8,128]{2,1,0:T(8,128)S(1)}, u32[]{:S(2)}, u32[]{:S(2)}) async-start(f32[8,8,128]{2,1,0:T(8,128)} %get-tuple-element.46), calls=%async_computation.1 | async-start | bytes 65536 | tf_op jit(solution)/shard_map/all_to_all | solution.py:572
  39.7 6.5 %kernel_part.1.part_h = bf16[8,128,256]{2,1,0:T(8,128)(2,1)} custom-call(bf16[704,128]{1,0:T(8,128)(2,1)S(1)} %get-tuple-element.40.refs_0_, bf16[704,128]{1,0:T(8,128)(2,1)S(1)} %collective-permute-done.2.refs_1_, bf16[704,128]{1,0:T(8,128)(2,1)S(1)} %collective-permute-done.3.refs_2_, bf16[704,128]{1,0:T(8,128)(2,1)S(1)} %collective-permute-done.4.refs_3_, ...), custom_call_target="tpu_custom_call" | custom-call | flops 7247757312 | bytes 1048576 | tf_op jit(solution)/shard_map/kernel_part/pallas_call | solution.py:415
  46.2 0.7 add_sums.1
  46.9 5.2 %all-to-all-start.2 = ((bf16[8,128,256]{2,1,0:T(8,128)(2,1)}), bf16[8,128,256]{2,1,0:T(8,128)(2,1)S(1)}, u32[]{:S(2)}, u32[]{:S(2)}) async-start(bf16[8,128,256]{2,1,0:T(8,128)(2,1)} %add_sums.1), calls=%async_computation.2 | async-start | bytes 1048576 | tf_op jit(solution)/shard_map/all_to_all | solution.py:604
  52.1 4.0 %forward_conv.1 = bf16[8,2,16,256]{3,2,1,0:T(8,128)(2,1)} custom-call(bf16[8,2,16,256]{3,2,1,0:T(8,128)(2,1)} %bitcast.13, bf16[272,256]{1,0:T(8,128)(2,1)S(1)} %collective-permute-done.hp_h.refs_1_, bf16[256,256]{1,0:T(8,128)(2,1)S(1)} %collective-permute-done.1.hn_h.refs_2_, f32[8,256]{1,0:T(8,128)S(1)} %get-tuple-element.48.refs_8_.refs_3_.refs_4_, ...), custom_call_target="tpu_custom_call" | custom-call | flops 7247757312 | bytes 1048576 | tf_op jit(solution)/shard_map/forward_conv/pallas_call | solution.py:415
  56.1 14.0 %all-to-all-done.2.refs_0_ = bf16[8,128,256]{2,1,0:T(8,128)(2,1)S(1)} async-done(((bf16[8,128,256]{2,1,0:T(8,128)(2,1)}), bf16[8,128,256]{2,1,0:T(8,128)(2,1)S(1)}, u32[]{:S(2)}, u32[]{:S(2)}) %all-to-all-start.2) | async-done | bytes 524320 | tf_op jit(solution)/shard_map/all_to_all | solution.py:604
  70.6 2.6 %collective-permute-start.11 = (s16[112,256]{1,0:T(8,128)(2,1)S(1)}, s16[112,256]{1,0:T(8,128)(2,1)S(1)}, u32[]{:S(2)}, u32[]{:S(2)}) collective-permute-start(s16[112,256]{1,0:T(8,128)(2,1)S(1)} %get-tuple-element.53.own_h), channel_id=1, source_target_pairs={{0,192},{64,0},{128,64},{192,128},{1,193},{65,1},{129,65},{193,129... | collective-permute-start | bytes 172040 | tf_op jit(solution)/shard_map/ppermute | solution.py:617
  73.6 0.6 collective-permute-start.9
  74.2 2.0 %finish_input.1 = bf16[8,2,16,256]{3,2,1,0:T(8,128)(2,1)} custom-call(f32[8,128]{1,0:T(8,128)S(1)} %get-tuple-element.51.refs_0_, f32[8,32,256]{2,1,0:T(8,128)S(1)} %get-tuple-element.52.refs_1_, bf16[8,2,16,256]{3,2,1,0:T(8,128)(2,1)} %bitcast.14, bf16[8,2,16,256]{3,2,1,0:T(8,128)(2,1)} %bitcast.18, f32[8,256]{1,0:T(8,128)S(1)} %get-tuple-element.48.refs_8_.refs_3_.refs_4_, ...), custom_call_target="tpu_custom_call" | custom-call | bytes 1048576 | tf_op jit(solution)/shard_map/finish_input/pallas_call | solution.py:415
  76.3 1.4 %collective-permute-done.10.two_h = s16[112,256]{1,0:T(8,128)(2,1)S(1)} collective-permute-done((s16[112,256]{1,0:T(8,128)(2,1)S(1)}, s16[112,256]{1,0:T(8,128)(2,1)S(1)}, u32[]{:S(2)}, u32[]{:S(2)}) %collective-permute-start.10) | collective-permute-done | bytes 57376 | tf_op jit(solution)/shard_map/ppermute | solution.py:617
  77.7 0.6 collective-permute-done.9.one_h
  78.3 1.1 %sum_clips.1 = (f32[27,4,256]{2,1,0:T(4,128)}, f32[1,256]{1,0:T(1,128)}) custom-call(s16[112,256]{1,0:T(8,128)(2,1)S(1)} %get-tuple-element.53.own_h, s16[112,256]{1,0:T(8,128)(2,1)S(1)} %collective-permute-done.9.one_h, s16[112,256]{1,0:T(8,128)(2,1)S(1)} %collective-permute-done.10.two_h, s16[112,256]{1,0:T(8,128)(2,1)S(1)} %collective-permute-done.11.three_h), custom_call_target="tpu_custom_call" | custom-call | bytes 1048576 | tf_op jit(solution)/shard_map/sum_clips/pallas_call | solution.py:415
  (18 shorter events, 1.8 us)
Async XLA Ops:
  2.7 5.2 %collective-permute-start = (bf16[272,256]{1,0:T(8,128)(2,1)S(1)}, bf16[272,256]{1,0:T(8,128)(2,1)S(1)}, u32[]{:S(2)}, u32[]{:S(2)}) collective-permute-start(bf16[272,256]{1,0:T(8,128)(2,1)S(1)} %get-tuple-element.30), channel_id=1, source_target_pairs={{0,1},{1,0},{2,3},{3,2},{4,5},{5,4},{6,7},{7,6},{8,9},{9,8},{10,11... | collective-permute-start | bytes 417800 | tf_op jit(solution)/shard_map/ppermute | solution.py:535
  6.0 12.9 %collective-permute-start.1 = (bf16[256,256]{1,0:T(8,128)(2,1)S(1)}, bf16[256,256]{1,0:T(8,128)(2,1)S(1)}, u32[]{:S(2)}, u32[]{:S(2)}) collective-permute-start(bf16[256,256]{1,0:T(8,128)(2,1)S(1)} %get-tuple-element.31), channel_id=1, source_target_pairs={{1,2},{2,1},{3,4},{4,3},{5,6},{6,5},{7,8},{8,7},{9,10},{10,9},{11,... | collective-permute-start | bytes 393224 | tf_op jit(solution)/shard_map/ppermute | solution.py:536
  8.7 19.3 %all-to-all-start = ((f32[32,8,128]{2,1,0:T(8,128)}), f32[32,8,128]{2,1,0:T(8,128)S(1)}, u32[]{:S(2)}, u32[]{:S(2)}) async-start(f32[32,8,128]{2,1,0:T(8,128)} %pair_sums.1), calls=%async_computation | async-start | bytes 262144 | tf_op jit(solution)/shard_map/all_to_all | solution.py:547
  20.4 12.7 %collective-permute-start.2 = (bf16[704,128]{1,0:T(8,128)(2,1)S(1)}, bf16[704,128]{1,0:T(8,128)(2,1)S(1)}, u32[]{:S(2)}, u32[]{:S(2)}) collective-permute-start(bf16[704,128]{1,0:T(8,128)(2,1)S(1)} %get-tuple-element.33), channel_id=1, source_target_pairs={{0,16},{16,32},{32,48},{48,0},{1,17},{17,33},{33,49},{49,1},{2,18}... | collective-permute-start | bytes 540680 | tf_op jit(solution)/shard_map/ppermute | solution.py:559
  21.7 11.5 %collective-permute-start.3 = (bf16[704,128]{1,0:T(8,128)(2,1)S(1)}, bf16[704,128]{1,0:T(8,128)(2,1)S(1)}, u32[]{:S(2)}, u32[]{:S(2)}) collective-permute-start(bf16[704,128]{1,0:T(8,128)(2,1)S(1)} %get-tuple-element.34), channel_id=1, source_target_pairs={{0,32},{16,48},{32,0},{48,16},{1,33},{17,49},{33,1},{49,17},{2,34}... | collective-permute-start | bytes 540680 | tf_op jit(solution)/shard_map/ppermute | solution.py:559
  24.1 9.1 %collective-permute-start.4 = (bf16[704,128]{1,0:T(8,128)(2,1)S(1)}, bf16[704,128]{1,0:T(8,128)(2,1)S(1)}, u32[]{:S(2)}, u32[]{:S(2)}) collective-permute-start(bf16[704,128]{1,0:T(8,128)(2,1)S(1)} %get-tuple-element.35), channel_id=1, source_target_pairs={{0,48},{16,0},{32,16},{48,32},{1,49},{17,1},{33,17},{49,33},{2,50}... | collective-permute-start | bytes 540680 | tf_op jit(solution)/shard_map/ppermute | solution.py:559
  33.2 6.4 %collective-permute-start.5 = (bf16[704,128]{1,0:T(8,128)(2,1)S(1)}, bf16[704,128]{1,0:T(8,128)(2,1)S(1)}, u32[]{:S(2)}, u32[]{:S(2)}) collective-permute-start(bf16[704,128]{1,0:T(8,128)(2,1)S(1)} %get-tuple-element.40.refs_0_), channel_id=1, source_target_pairs={{0,1},{1,0},{2,3},{3,2},{4,5},{5,4},{6,7},{7,6},{8,9},{9,8},{10,11... | collective-permute-start | bytes 540680 | tf_op jit(solution)/shard_map/ppermute | solution.py:573
  35.4 4.3 %collective-permute-start.6 = (bf16[704,128]{1,0:T(8,128)(2,1)S(1)}, bf16[704,128]{1,0:T(8,128)(2,1)S(1)}, u32[]{:S(2)}, u32[]{:S(2)}) collective-permute-start(bf16[704,128]{1,0:T(8,128)(2,1)S(1)} %collective-permute-done.2.refs_1_), channel_id=1, source_target_pairs={{0,1},{1,0},{2,3},{3,2},{4,5},{5,4},{6,7},{7,6},{8,9},{9,8},{10,11... | collective-permute-start | bytes 540680 | tf_op jit(solution)/shard_map/ppermute | solution.py:573
  35.5 4.2 %collective-permute-start.7 = (bf16[704,128]{1,0:T(8,128)(2,1)S(1)}, bf16[704,128]{1,0:T(8,128)(2,1)S(1)}, u32[]{:S(2)}, u32[]{:S(2)}) collective-permute-start(bf16[704,128]{1,0:T(8,128)(2,1)S(1)} %collective-permute-done.3.refs_2_), channel_id=1, source_target_pairs={{0,1},{1,0},{2,3},{3,2},{4,5},{5,4},{6,7},{7,6},{8,9},{9,8},{10,11... | collective-permute-start | bytes 540680 | tf_op jit(solution)/shard_map/ppermute | solution.py:573
  35.9 3.8 %collective-permute-start.8 = (bf16[704,128]{1,0:T(8,128)(2,1)S(1)}, bf16[704,128]{1,0:T(8,128)(2,1)S(1)}, u32[]{:S(2)}, u32[]{:S(2)}) collective-permute-start(bf16[704,128]{1,0:T(8,128)(2,1)S(1)} %collective-permute-done.4.refs_3_), channel_id=1, source_target_pairs={{0,1},{1,0},{2,3},{3,2},{4,5},{5,4},{6,7},{7,6},{8,9},{9,8},{10,11... | collective-permute-start | bytes 540680 | tf_op jit(solution)/shard_map/ppermute | solution.py:573
  36.0 10.2 %all-to-all-start.1 = ((f32[8,8,128]{2,1,0:T(8,128)}), f32[8,8,128]{2,1,0:T(8,128)S(1)}, u32[]{:S(2)}, u32[]{:S(2)}) async-start(f32[8,8,128]{2,1,0:T(8,128)} %get-tuple-element.46), calls=%async_computation.1 | async-start | bytes 65536 | tf_op jit(solution)/shard_map/all_to_all | solution.py:572
  46.9 23.2 %all-to-all-start.2 = ((bf16[8,128,256]{2,1,0:T(8,128)(2,1)}), bf16[8,128,256]{2,1,0:T(8,128)(2,1)S(1)}, u32[]{:S(2)}, u32[]{:S(2)}) async-start(bf16[8,128,256]{2,1,0:T(8,128)(2,1)} %add_sums.1), calls=%async_computation.2 | async-start | bytes 1048576 | tf_op jit(solution)/shard_map/all_to_all | solution.py:604
  70.6 5.7 %collective-permute-start.11 = (s16[112,256]{1,0:T(8,128)(2,1)S(1)}, s16[112,256]{1,0:T(8,128)(2,1)S(1)}, u32[]{:S(2)}, u32[]{:S(2)}) collective-permute-start(s16[112,256]{1,0:T(8,128)(2,1)S(1)} %get-tuple-element.53.own_h), channel_id=1, source_target_pairs={{0,192},{64,0},{128,64},{192,128},{1,193},{65,1},{129,65},{193,129... | collective-permute-start | bytes 172040 | tf_op jit(solution)/shard_map/ppermute | solution.py:617
  73.1 4.6 %collective-permute-start.10 = (s16[112,256]{1,0:T(8,128)(2,1)S(1)}, s16[112,256]{1,0:T(8,128)(2,1)S(1)}, u32[]{:S(2)}, u32[]{:S(2)}) collective-permute-start(s16[112,256]{1,0:T(8,128)(2,1)S(1)} %get-tuple-element.53.own_h), channel_id=1, source_target_pairs={{0,128},{64,192},{128,0},{192,64},{1,129},{65,193},{129,1},{193,65... | collective-permute-start | bytes 172040 | tf_op jit(solution)/shard_map/ppermute | solution.py:617
  73.6 4.6 %collective-permute-start.9 = (s16[112,256]{1,0:T(8,128)(2,1)S(1)}, s16[112,256]{1,0:T(8,128)(2,1)S(1)}, u32[]{:S(2)}, u32[]{:S(2)}) collective-permute-start(s16[112,256]{1,0:T(8,128)(2,1)S(1)} %get-tuple-element.53.own_h), channel_id=1, source_target_pairs={{0,64},{64,128},{128,192},{192,0},{1,65},{65,129},{129,193},{193,1... | collective-permute-start | bytes 172040 | tf_op jit(solution)/shard_map/ppermute | solution.py:617

commit v10 on v9

--- a/solution.py
+++ b/solution.py
@@ -27,7 +27,7 @@
 BLOCK = AROWS + NC * GROWS
 TERMS = 16
 STEPS = 32000.0
-HALO = FR * COLS
+HALO = FR
 HI = lax.Precision.HIGHEST
 
 
@@ -56,13 +56,18 @@
     return jnp.concatenate([cells[..., 1:, :], zero], axis=-2)
 
 
-def edges_and_sums(x_ref, g_ref, in_ref, out_ref, st_ref):
-    first = lax.axis_index("c") == 0
-    for n, ref in enumerate((x_ref, g_ref)):
-        low, high = ref[:, 0], ref[:, 1]
-        inner, outer = jnp.where(first, high, low), jnp.where(first, low, high)
-        in_ref[n * HALO : (n + 1) * HALO] = inner.reshape(HALO, CH)
-        out_ref[n * HALO : (n + 1) * HALO] = outer.reshape(HALO, CH)
+def edges_and_sums(x_h, g_h, in_h, out_h, st_h, x_ref, st_ref, term_ref, sem):
+    c_at = lax.axis_index("c")
+    load = pltpu.make_async_copy(x_h, x_ref, sem.at[0])
+    load.start()
+    halo = []
+    for n, source in enumerate((x_h, g_h)):
+        part = slice(n * FR, (n + 1) * FR)
+        halo.append(pltpu.make_async_copy(source.at[:, 1 - c_at], in_h.at[part], sem.at[1 + 2 * n]))
+        halo.append(pltpu.make_async_copy(source.at[:, c_at], out_h.at[part], sem.at[2 + 2 * n]))
+    for copy in halo:
+        copy.start()
+    load.wait()
     xf = x_ref[...].astype(F32).reshape(FR, CELLS, CH)
     gather = gather_matrix()
     mean = hdot(jnp.sum(xf, axis=1), gather) / (CELLS * GC)
@@ -70,7 +75,13 @@
     squares = hdot(jnp.sum(centered * centered, axis=1), gather)
     sums = jnp.concatenate([mean, squares, jnp.zeros((FR, 2 * GROUPS), F32)], axis=1)
     st_ref[...] = sums
-    in_ref[2 * HALO :] = as_terms(sums)
+    term_ref[0] = as_terms(sums)
+    halo.append(pltpu.make_async_copy(term_ref, in_h.at[2 * FR :], sem.at[5]))
+    halo.append(pltpu.make_async_copy(st_ref, st_h, sem.at[6]))
+    for copy in halo[4:]:
+        copy.start()
+    for copy in halo:
+        copy.wait()
 
 
 def outside(in_ref, out_ref):
@@ -88,7 +99,7 @@
 
 
 def pair_sums(own_ref, other_ref, out_ref):
-    both = jnp.stack([own_ref[...], from_terms(other_ref[...].astype(F32))])
+    both = jnp.stack([own_ref[...], from_terms(other_ref[0].astype(F32))])
     mean, squares = combined(both[:, :, :GROUPS], both[:, :, GROUPS : 2 * GROUPS], CELLS * GC)
     row = jnp.concatenate([mean, squares, jnp.zeros((FR, 2 * GROUPS), F32)], axis=1)
     out_ref[...] = jnp.broadcast_to(row[None], (NY * NZ, FR, 128))
@@ -521,14 +532,21 @@
     swap = [(0, 1), (1, 0)]
     dma = pltpu.SemaphoreType.DMA
 
-    inner, outer, stats = run(
+    inner, outer, stats = call(
         edges_and_sums,
         [
-            ((2 * HALO + TERMS, CH), BF16),
-            ((2 * HALO, CH), BF16),
+            ((2 * HALO + 1, COLS, CH), BF16),
+            ((2 * HALO, COLS, CH), BF16),
             ((FR, 128), F32),
         ],
         (x, g),
+        [HBM] * 2,
+        [
+            pltpu.VMEM(cells, BF16),
+            pltpu.VMEM((FR, 128), F32),
+            pltpu.VMEM((1, TERMS, CH), BF16),
+            dma((7,)),
+        ],
     )
     stats, counts = lax.optimization_barrier((stats, frame_counts))
     live = jnp.broadcast_to(jnp.arange(FR)[:, None] < counts[0], wide).astype(F32)
@@ -542,7 +560,7 @@
         pair_sums,
         [((NY * NZ, FR, 128), F32)],
         (stats, hp),
-        rows={1: (2 * HALO, 2 * HALO + TERMS)},
+        rows={1: (2 * HALO, 2 * HALO + 1)},
     )
     stats = lax.all_to_all(stats, ("y", "z"), 0, 0)
     block = (BLOCK, BSL)
@@ -552,7 +570,7 @@
         (x, stay_out(output_grad.reshape(GROWS, CH)), hp, hn),
         [HBM] * 4,
         [pltpu.VMEM(cells, BF16)]
-        + [pltpu.VMEM((HALO, CH), BF16)] * 2
+        + [pltpu.VMEM((HALO, COLS, CH), BF16)] * 2
         + [pltpu.VMEM((NY, AROWS, BSL), BF16), dma((3 + NC * NY + NY,))],
     )
     near = [packed[0]] + [
@@ -568,7 +586,8 @@
         scratch=[padded],
         late=3,
     )
-    *near, terms = lax.optimization_barrier((*near, terms))
+    *moved, terms = lax.optimization_barrier((*near[1:], terms))
+    near = [near[0], *moved]
     terms = lax.all_to_all(terms, ("y", "c"), 0, 0)
     far = [lax.ppermute(a, "c", swap) for a in near]
     part = (NZ, PROWS, CH)

time: 80.2 us -> 79.4 us (0.990)
  waiting for transfers between devices: 18.2 us -> 16.7 us
  starting transfers between devices: 35.5 us -> 36.6 us
    all_to_all x1, waiting for transfers between devices: 2.08 us -> 0.56 us  [local(): stats = lax.all_to_all(stats, ('y', 'z'), 0, 0)]
    ppermute x4, starting transfers between devices: 2.77 us -> 4.19 us  [local(): far = [lax.ppermute(a, 'c', swap) for a in near]]
where the time goes in v10:
time: 79.4 us; the launch traced here: 78.5 us
  starting transfers between devices  36.6 us (46%)
  Pallas kernels  23.7 us (30%)
  waiting for transfers between devices  16.7 us (21%)
  between operations  1.45 us (2%)
    pallas_call x10, Pallas kernels, call(): pl.pallas_call(body, out_shape=shapes(outs), in_specs=specs, out_specs=tu...  23.7 us
    all_to_all x1, waiting for transfers between devices, local(): merged = lax.all_to_all(merged, 'z', 0, 0)  14 us
    all_to_all x1, starting transfers between devices, local(): stats = lax.all_to_all(stats, ('y', 'z'), 0, 0)  10.1 us
    all_to_all x1, starting transfers between devices, local(): merged = lax.all_to_all(merged, 'z', 0, 0)  5.19 us
    ppermute x3, starting transfers between devices, local(): lax.ppermute(packed[d], 'y', [(i, (i + d) % NY) for i in range(NY)])  4.89 us
    ppermute x4, starting transfers between devices, local(): far = [lax.ppermute(a, 'c', swap) for a in near]  4.19 us
    ppermute x3, starting transfers between devices, local(): lax.ppermute(rows, 'x', [(i, (i + d) % NX) for i in range(NX)])  3.68 us
    all_to_all x1, starting transfers between devices, local(): terms = lax.all_to_all(terms, ('y', 'c'), 0, 0)  3.34 us
  transfers between devices with their start and end apart: 15, of which 5 were waited for; matrix products, arithmetic and copies ran while one was open for 0% of the time, Pallas kernels for 25%

profile of v10, /device:TPU:1, one launch (start us, length us, event | category | flops | bytes accessed | tf_op | source)
XLA Modules:
  0.0 78.5 jit_solution(2567162096377186178)
XLA Ops:
  0.6 1.7 %edges_and_sums.1 = (bf16[17,16,256]{2,1,0:T(8,128)(2,1)S(1)}, bf16[16,16,256]{2,1,0:T(8,128)(2,1)S(1)}, f32[8,128]{1,0:T(8,128)S(1)}) custom-call(bf16[8,2,16,256]{3,2,1,0:T(8,128)(2,1)} %bitcast.10, bf16[8,2,16,256]{3,2,1,0:T(8,128)(2,1)} %bitcast.15), custom_call_target="tpu_custom_call" | custom-call | bytes 1048576 | tf_op jit(solution)/shard_map/edges_and_sums/pallas_call | solution.py:426
  2.3 3.3 %collective-permute-start = (bf16[17,16,256]{2,1,0:T(8,128)(2,1)S(1)}, bf16[17,16,256]{2,1,0:T(8,128)(2,1)S(1)}, u32[]{:S(2)}, u32[]{:S(2)}) collective-permute-start(bf16[17,16,256]{2,1,0:T(8,128)(2,1)S(1)} %get-tuple-element.29), channel_id=1, source_target_pairs={{0,1},{1,0},{2,3},{3,2},{4,5},{5,4},{6,7},{7,6},{8,9},{9,8},{10,11... | collective-permute-start | bytes 417800 | tf_op jit(solution)/shard_map/ppermute | solution.py:553
  5.6 1.9 %collective-permute-start.1 = (bf16[16,16,256]{2,1,0:T(8,128)(2,1)S(1)}, bf16[16,16,256]{2,1,0:T(8,128)(2,1)S(1)}, u32[]{:S(2)}, u32[]{:S(2)}) collective-permute-start(bf16[16,16,256]{2,1,0:T(8,128)(2,1)S(1)} %get-tuple-element.30), channel_id=1, source_target_pairs={{1,2},{2,1},{3,4},{4,3},{5,6},{6,5},{7,8},{8,7},{9,10},{10,9},{11,... | collective-permute-start | bytes 393224 | tf_op jit(solution)/shard_map/ppermute | solution.py:554
  7.6 0.8 %pair_sums.1 = f32[32,8,128]{2,1,0:T(8,128)} custom-call(f32[8,128]{1,0:T(8,128)S(1)} %get-tuple-element.37.refs_0_, bf16[17,16,256]{2,1,0:T(8,128)(2,1)S(1)} %collective-permute-done.hp_h.refs_1_), custom_call_target="tpu_custom_call" | custom-call | bytes 1048576 | tf_op jit(solution)/shard_map/pair_sums/pallas_call | solution.py:426
  8.4 10.1 %all-to-all-start = ((f32[32,8,128]{2,1,0:T(8,128)}), f32[32,8,128]{2,1,0:T(8,128)S(1)}, u32[]{:S(2)}, u32[]{:S(2)}) async-start(f32[32,8,128]{2,1,0:T(8,128)} %pair_sums.1), calls=%async_computation | async-start | bytes 262144 | tf_op jit(solution)/shard_map/all_to_all | solution.py:565
  18.5 1.5 %pack_body.1 = (bf16[704,128]{1,0:T(8,128)(2,1)S(1)}, bf16[704,128]{1,0:T(8,128)(2,1)S(1)}, bf16[704,128]{1,0:T(8,128)(2,1)S(1)}, bf16[704,128]{1,0:T(8,128)(2,1)S(1)}) custom-call(bf16[8,2,16,256]{3,2,1,0:T(8,128)(2,1)} %bitcast.11, bf16[256,256]{1,0:T(8,128)(2,1)} %bitcast.16, bf16[17,16,256]{2,1,0:T(8,128)(2,1)S(1)} %collective-permute-done.hp_h.refs_1_, ...), custom_call_target="tpu_custom_call" | custom-call | bytes 1048576 | tf_op jit(solution)/shard_map/pack_body/pallas_call | solution.py:426
  20.0 1.3 %collective-permute-start.2 = (bf16[704,128]{1,0:T(8,128)(2,1)S(1)}, bf16[704,128]{1,0:T(8,128)(2,1)S(1)}, u32[]{:S(2)}, u32[]{:S(2)}) collective-permute-start(bf16[704,128]{1,0:T(8,128)(2,1)S(1)} %get-tuple-element.32), channel_id=1, source_target_pairs={{0,16},{16,32},{32,48},{48,0},{1,17},{17,33},{33,49},{49,1},{2,18}... | collective-permute-start | bytes 540680 | tf_op jit(solution)/shard_map/ppermute | solution.py:577
  21.3 2.4 %collective-permute-start.3 = (bf16[704,128]{1,0:T(8,128)(2,1)S(1)}, bf16[704,128]{1,0:T(8,128)(2,1)S(1)}, u32[]{:S(2)}, u32[]{:S(2)}) collective-permute-start(bf16[704,128]{1,0:T(8,128)(2,1)S(1)} %get-tuple-element.33), channel_id=1, source_target_pairs={{0,32},{16,48},{32,0},{48,16},{1,33},{17,49},{33,1},{49,17},{2,34}... | collective-permute-start | bytes 540680 | tf_op jit(solution)/shard_map/ppermute | solution.py:577
  23.8 1.1 %collective-permute-start.4 = (bf16[704,128]{1,0:T(8,128)(2,1)S(1)}, bf16[704,128]{1,0:T(8,128)(2,1)S(1)}, u32[]{:S(2)}, u32[]{:S(2)}) collective-permute-start(bf16[704,128]{1,0:T(8,128)(2,1)S(1)} %get-tuple-element.34), channel_id=1, source_target_pairs={{0,48},{16,0},{32,16},{48,32},{1,49},{17,1},{33,17},{49,33},{2,50}... | collective-permute-start | bytes 540680 | tf_op jit(solution)/shard_map/ppermute | solution.py:577
  25.6 1.5 %collective-permute-start.5 = (bf16[704,128]{1,0:T(8,128)(2,1)S(1)}, bf16[704,128]{1,0:T(8,128)(2,1)S(1)}, u32[]{:S(2)}, u32[]{:S(2)}) collective-permute-start(bf16[704,128]{1,0:T(8,128)(2,1)S(1)} %get-tuple-element.31.refs_0_), channel_id=1, source_target_pairs={{0,1},{1,0},{2,3},{3,2},{4,5},{5,4},{6,7},{7,6},{8,9},{9,8},{10,11... | collective-permute-start | bytes 540680 | tf_op jit(solution)/shard_map/ppermute | solution.py:592
  27.7 5.0 %backward_terms.1 = (f32[8,8,128]{2,1,0:T(8,128)}, f32[8,32,256]{2,1,0:T(8,128)S(1)}, f32[8,256]{1,0:T(8,128)S(1)}, f32[8,256]{1,0:T(8,128)S(1)}) custom-call(bf16[8,2,16,256]{3,2,1,0:T(8,128)(2,1)} %bitcast.17, bf16[17,16,256]{2,1,0:T(8,128)(2,1)S(1)} %collective-permute-done.hp_h.refs_1_, bf16[16,16,256]{2,1,0:T(8,128)(2,1)S(1)} %collective-permute-done.1.hn_h.refs_2_, ...), custom_call_target="tpu_custom_call" | custom-call | bytes 1048576 | tf_op jit(solution)/shard_map/backward_terms/pallas_call | solution.py:426
  32.9 2.2 %collective-permute-start.6 = (bf16[704,128]{1,0:T(8,128)(2,1)S(1)}, bf16[704,128]{1,0:T(8,128)(2,1)S(1)}, u32[]{:S(2)}, u32[]{:S(2)}) collective-permute-start(bf16[704,128]{1,0:T(8,128)(2,1)S(1)} %collective-permute-done.2.refs_1_), channel_id=1, source_target_pairs={{0,1},{1,0},{2,3},{3,2},{4,5},{5,4},{6,7},{7,6},{8,9},{9,8},{10,11... | collective-permute-start | bytes 540680 | tf_op jit(solution)/shard_map/ppermute | solution.py:592
  35.5 3.3 %all-to-all-start.1 = ((f32[8,8,128]{2,1,0:T(8,128)}), f32[8,8,128]{2,1,0:T(8,128)S(1)}, u32[]{:S(2)}, u32[]{:S(2)}) async-start(f32[8,8,128]{2,1,0:T(8,128)} %get-tuple-element.44), calls=%async_computation.1 | async-start | bytes 65536 | tf_op jit(solution)/shard_map/all_to_all | solution.py:591
  38.9 6.5 %kernel_part.1.part_h = bf16[8,128,256]{2,1,0:T(8,128)(2,1)} custom-call(bf16[704,128]{1,0:T(8,128)(2,1)S(1)} %get-tuple-element.31.refs_0_, bf16[704,128]{1,0:T(8,128)(2,1)S(1)} %collective-permute-done.2.refs_1_, bf16[704,128]{1,0:T(8,128)(2,1)S(1)} %collective-permute-done.3.refs_2_, bf16[704,128]{1,0:T(8,128)(2,1)S(1)} %collective-permute-done.4.refs_3_, ...), custom_call_target="tpu_custom_call" | custom-call | flops 7247757312 | bytes 1048576 | tf_op jit(solution)/shard_map/kernel_part/pallas_call | solution.py:426
  45.4 0.7 add_sums.1
  46.1 5.2 %all-to-all-start.2 = ((bf16[8,128,256]{2,1,0:T(8,128)(2,1)}), bf16[8,128,256]{2,1,0:T(8,128)(2,1)S(1)}, u32[]{:S(2)}, u32[]{:S(2)}) async-start(bf16[8,128,256]{2,1,0:T(8,128)(2,1)} %add_sums.1), calls=%async_computation.2 | async-start | bytes 1048576 | tf_op jit(solution)/shard_map/all_to_all | solution.py:623
  51.3 4.0 %forward_conv.1 = bf16[8,2,16,256]{3,2,1,0:T(8,128)(2,1)} custom-call(bf16[8,2,16,256]{3,2,1,0:T(8,128)(2,1)} %bitcast.13, bf16[17,16,256]{2,1,0:T(8,128)(2,1)S(1)} %collective-permute-done.hp_h.refs_1_, bf16[16,16,256]{2,1,0:T(8,128)(2,1)S(1)} %collective-permute-done.1.hn_h.refs_2_, f32[8,256]{1,0:T(8,128)S(1)} %get-tuple-element.46.refs_8_.refs_3_.refs_4_, ...), custom_call_target="tpu_custom_call" | custom-call | flops 7247757312 | bytes 1048576 | tf_op jit(solution)/shard_map/forward_conv/pallas_call | solution.py:426
  55.3 14.0 %all-to-all-done.2.refs_0_ = bf16[8,128,256]{2,1,0:T(8,128)(2,1)S(1)} async-done(((bf16[8,128,256]{2,1,0:T(8,128)(2,1)}), bf16[8,128,256]{2,1,0:T(8,128)(2,1)S(1)}, u32[]{:S(2)}, u32[]{:S(2)}) %all-to-all-start.2) | async-done | bytes 524320 | tf_op jit(solution)/shard_map/all_to_all | solution.py:623
  69.8 2.6 %collective-permute-start.11 = (s16[112,256]{1,0:T(8,128)(2,1)S(1)}, s16[112,256]{1,0:T(8,128)(2,1)S(1)}, u32[]{:S(2)}, u32[]{:S(2)}) collective-permute-start(s16[112,256]{1,0:T(8,128)(2,1)S(1)} %get-tuple-element.51.own_h), channel_id=1, source_target_pairs={{0,192},{64,0},{128,64},{192,128},{1,193},{65,1},{129,65},{193,129... | collective-permute-start | bytes 172040 | tf_op jit(solution)/shard_map/ppermute | solution.py:636
  72.9 0.6 collective-permute-start.9
  73.5 2.0 %finish_input.1 = bf16[8,2,16,256]{3,2,1,0:T(8,128)(2,1)} custom-call(f32[8,128]{1,0:T(8,128)S(1)} %get-tuple-element.49.refs_0_, f32[8,32,256]{2,1,0:T(8,128)S(1)} %get-tuple-element.50.refs_1_, bf16[8,2,16,256]{3,2,1,0:T(8,128)(2,1)} %bitcast.14, bf16[8,2,16,256]{3,2,1,0:T(8,128)(2,1)} %bitcast.18, f32[8,256]{1,0:T(8,128)S(1)} %get-tuple-element.46.refs_8_.refs_3_.refs_4_, ...), custom_call_target="tpu_custom_call" | custom-call | bytes 1048576 | tf_op jit(solution)/shard_map/finish_input/pallas_call | solution.py:426
  75.5 1.4 %collective-permute-done.10.two_h = s16[112,256]{1,0:T(8,128)(2,1)S(1)} collective-permute-done((s16[112,256]{1,0:T(8,128)(2,1)S(1)}, s16[112,256]{1,0:T(8,128)(2,1)S(1)}, u32[]{:S(2)}, u32[]{:S(2)}) %collective-permute-start.10) | collective-permute-done | bytes 57376 | tf_op jit(solution)/shard_map/ppermute | solution.py:636
  76.9 0.6 collective-permute-done.9.one_h
  77.5 1.1 %sum_clips.1 = (f32[27,4,256]{2,1,0:T(4,128)}, f32[1,256]{1,0:T(1,128)}) custom-call(s16[112,256]{1,0:T(8,128)(2,1)S(1)} %get-tuple-element.51.own_h, s16[112,256]{1,0:T(8,128)(2,1)S(1)} %collective-permute-done.9.one_h, s16[112,256]{1,0:T(8,128)(2,1)S(1)} %collective-permute-done.10.two_h, s16[112,256]{1,0:T(8,128)(2,1)S(1)} %collective-permute-done.11.three_h), custom_call_target="tpu_custom_call" | custom-call | bytes 1048576 | tf_op jit(solution)/shard_map/sum_clips/pallas_call | solution.py:426
  (18 shorter events, 2.3 us)
Async XLA Ops:
  2.3 5.2 %collective-permute-start = (bf16[17,16,256]{2,1,0:T(8,128)(2,1)S(1)}, bf16[17,16,256]{2,1,0:T(8,128)(2,1)S(1)}, u32[]{:S(2)}, u32[]{:S(2)}) collective-permute-start(bf16[17,16,256]{2,1,0:T(8,128)(2,1)S(1)} %get-tuple-element.29), channel_id=1, source_target_pairs={{0,1},{1,0},{2,3},{3,2},{4,5},{5,4},{6,7},{7,6},{8,9},{9,8},{10,11... | collective-permute-start | bytes 417800 | tf_op jit(solution)/shard_map/ppermute | solution.py:553
  5.6 12.9 %collective-permute-start.1 = (bf16[16,16,256]{2,1,0:T(8,128)(2,1)S(1)}, bf16[16,16,256]{2,1,0:T(8,128)(2,1)S(1)}, u32[]{:S(2)}, u32[]{:S(2)}) collective-permute-start(bf16[16,16,256]{2,1,0:T(8,128)(2,1)S(1)} %get-tuple-element.30), channel_id=1, source_target_pairs={{1,2},{2,1},{3,4},{4,3},{5,6},{6,5},{7,8},{8,7},{9,10},{10,9},{11,... | collective-permute-start | bytes 393224 | tf_op jit(solution)/shard_map/ppermute | solution.py:554
  8.4 19.3 %all-to-all-start = ((f32[32,8,128]{2,1,0:T(8,128)}), f32[32,8,128]{2,1,0:T(8,128)S(1)}, u32[]{:S(2)}, u32[]{:S(2)}) async-start(f32[32,8,128]{2,1,0:T(8,128)} %pair_sums.1), calls=%async_computation | async-start | bytes 262144 | tf_op jit(solution)/shard_map/all_to_all | solution.py:565
  20.0 12.7 %collective-permute-start.2 = (bf16[704,128]{1,0:T(8,128)(2,1)S(1)}, bf16[704,128]{1,0:T(8,128)(2,1)S(1)}, u32[]{:S(2)}, u32[]{:S(2)}) collective-permute-start(bf16[704,128]{1,0:T(8,128)(2,1)S(1)} %get-tuple-element.32), channel_id=1, source_target_pairs={{0,16},{16,32},{32,48},{48,0},{1,17},{17,33},{33,49},{49,1},{2,18}... | collective-permute-start | bytes 540680 | tf_op jit(solution)/shard_map/ppermute | solution.py:577
  21.3 11.5 %collective-permute-start.3 = (bf16[704,128]{1,0:T(8,128)(2,1)S(1)}, bf16[704,128]{1,0:T(8,128)(2,1)S(1)}, u32[]{:S(2)}, u32[]{:S(2)}) collective-permute-start(bf16[704,128]{1,0:T(8,128)(2,1)S(1)} %get-tuple-element.33), channel_id=1, source_target_pairs={{0,32},{16,48},{32,0},{48,16},{1,33},{17,49},{33,1},{49,17},{2,34}... | collective-permute-start | bytes 540680 | tf_op jit(solution)/shard_map/ppermute | solution.py:577
  23.8 9.1 %collective-permute-start.4 = (bf16[704,128]{1,0:T(8,128)(2,1)S(1)}, bf16[704,128]{1,0:T(8,128)(2,1)S(1)}, u32[]{:S(2)}, u32[]{:S(2)}) collective-permute-start(bf16[704,128]{1,0:T(8,128)(2,1)S(1)} %get-tuple-element.34), channel_id=1, source_target_pairs={{0,48},{16,0},{32,16},{48,32},{1,49},{17,1},{33,17},{49,33},{2,50}... | collective-permute-start | bytes 540680 | tf_op jit(solution)/shard_map/ppermute | solution.py:577
  25.6 13.3 %collective-permute-start.5 = (bf16[704,128]{1,0:T(8,128)(2,1)S(1)}, bf16[704,128]{1,0:T(8,128)(2,1)S(1)}, u32[]{:S(2)}, u32[]{:S(2)}) collective-permute-start(bf16[704,128]{1,0:T(8,128)(2,1)S(1)} %get-tuple-element.31.refs_0_), channel_id=1, source_target_pairs={{0,1},{1,0},{2,3},{3,2},{4,5},{5,4},{6,7},{7,6},{8,9},{9,8},{10,11... | collective-permute-start | bytes 540680 | tf_op jit(solution)/shard_map/ppermute | solution.py:592
  32.9 6.0 %collective-permute-start.6 = (bf16[704,128]{1,0:T(8,128)(2,1)S(1)}, bf16[704,128]{1,0:T(8,128)(2,1)S(1)}, u32[]{:S(2)}, u32[]{:S(2)}) collective-permute-start(bf16[704,128]{1,0:T(8,128)(2,1)S(1)} %collective-permute-done.2.refs_1_), channel_id=1, source_target_pairs={{0,1},{1,0},{2,3},{3,2},{4,5},{5,4},{6,7},{7,6},{8,9},{9,8},{10,11... | collective-permute-start | bytes 540680 | tf_op jit(solution)/shard_map/ppermute | solution.py:592
  35.0 3.9 %collective-permute-start.7 = (bf16[704,128]{1,0:T(8,128)(2,1)S(1)}, bf16[704,128]{1,0:T(8,128)(2,1)S(1)}, u32[]{:S(2)}, u32[]{:S(2)}) collective-permute-start(bf16[704,128]{1,0:T(8,128)(2,1)S(1)} %collective-permute-done.3.refs_2_), channel_id=1, source_target_pairs={{0,1},{1,0},{2,3},{3,2},{4,5},{5,4},{6,7},{7,6},{8,9},{9,8},{10,11... | collective-permute-start | bytes 540680 | tf_op jit(solution)/shard_map/ppermute | solution.py:592
  35.1 3.8 %collective-permute-start.8 = (bf16[704,128]{1,0:T(8,128)(2,1)S(1)}, bf16[704,128]{1,0:T(8,128)(2,1)S(1)}, u32[]{:S(2)}, u32[]{:S(2)}) collective-permute-start(bf16[704,128]{1,0:T(8,128)(2,1)S(1)} %collective-permute-done.4.refs_3_), channel_id=1, source_target_pairs={{0,1},{1,0},{2,3},{3,2},{4,5},{5,4},{6,7},{7,6},{8,9},{9,8},{10,11... | collective-permute-start | bytes 540680 | tf_op jit(solution)/shard_map/ppermute | solution.py:592
  35.5 9.8 %all-to-all-start.1 = ((f32[8,8,128]{2,1,0:T(8,128)}), f32[8,8,128]{2,1,0:T(8,128)S(1)}, u32[]{:S(2)}, u32[]{:S(2)}) async-start(f32[8,8,128]{2,1,0:T(8,128)} %get-tuple-element.44), calls=%async_computation.1 | async-start | bytes 65536 | tf_op jit(solution)/shard_map/all_to_all | solution.py:591
  46.1 23.2 %all-to-all-start.2 = ((bf16[8,128,256]{2,1,0:T(8,128)(2,1)}), bf16[8,128,256]{2,1,0:T(8,128)(2,1)S(1)}, u32[]{:S(2)}, u32[]{:S(2)}) async-start(bf16[8,128,256]{2,1,0:T(8,128)(2,1)} %add_sums.1), calls=%async_computation.2 | async-start | bytes 1048576 | tf_op jit(solution)/shard_map/all_to_all | solution.py:623
  69.8 5.7 %collective-permute-start.11 = (s16[112,256]{1,0:T(8,128)(2,1)S(1)}, s16[112,256]{1,0:T(8,128)(2,1)S(1)}, u32[]{:S(2)}, u32[]{:S(2)}) collective-permute-start(s16[112,256]{1,0:T(8,128)(2,1)S(1)} %get-tuple-element.51.own_h), channel_id=1, source_target_pairs={{0,192},{64,0},{128,64},{192,128},{1,193},{65,1},{129,65},{193,129... | collective-permute-start | bytes 172040 | tf_op jit(solution)/shard_map/ppermute | solution.py:636
  72.3 4.6 %collective-permute-start.10 = (s16[112,256]{1,0:T(8,128)(2,1)S(1)}, s16[112,256]{1,0:T(8,128)(2,1)S(1)}, u32[]{:S(2)}, u32[]{:S(2)}) collective-permute-start(s16[112,256]{1,0:T(8,128)(2,1)S(1)} %get-tuple-element.51.own_h), channel_id=1, source_target_pairs={{0,128},{64,192},{128,0},{192,64},{1,129},{65,193},{129,1},{193,65... | collective-permute-start | bytes 172040 | tf_op jit(solution)/shard_map/ppermute | solution.py:636
  72.9 4.6 %collective-permute-start.9 = (s16[112,256]{1,0:T(8,128)(2,1)S(1)}, s16[112,256]{1,0:T(8,128)(2,1)S(1)}, u32[]{:S(2)}, u32[]{:S(2)}) collective-permute-start(s16[112,256]{1,0:T(8,128)(2,1)S(1)} %get-tuple-element.51.own_h), channel_id=1, source_target_pairs={{0,64},{64,128},{128,192},{192,0},{1,65},{65,129},{129,193},{193,1... | collective-permute-start | bytes 172040 | tf_op jit(solution)/shard_map/ppermute | solution.py:636

commit v11 on v10

--- a/solution.py
+++ b/solution.py
@@ -198,12 +198,13 @@
     blocks, (mean_h, inv_h, gain_h, live_h, out_h) = refs[:8], refs[8:13]
     in_ref, mean_ref, inv_ref, gain_ref, live_ref, out_ref, pad_ref, grad_ref, sum_ref, sem = refs[13:]
     y_at, z_at, c_at = lax.axis_index("y"), lax.axis_index("z"), lax.axis_index("c")
-    pairs = [(blocks[n], in_ref.at[n]) for n in range(8)]
+    pairs = [(blocks[n].at[:AROWS], in_ref.at[n, :AROWS]) for n in range(8)]
     pairs += [(mean_h, mean_ref), (inv_h, inv_ref), (gain_h, gain_ref), (live_h, live_ref)]
+    pairs += [(blocks[n].at[AROWS:], in_ref.at[n, AROWS:]) for n in range(8)]
     copies = [pltpu.make_async_copy(a, b, sem.at[n]) for n, (a, b) in enumerate(pairs)]
     for copy in copies:
         copy.start()
-    for copy in copies[8:]:
+    for copy in copies[8:12]:
         copy.wait()
     width = Q * APART
     lane = lax.broadcasted_iota(jnp.int32, (CH, width), 0)
@@ -269,6 +270,11 @@
         for f in range(FR):
             for k in range(3):
                 pad_ref[k, f, d, pl.ds(3 * c, 3)] = shifted(frames[f], k).astype(BF16)
+    for copy in copies[12:]:
+        copy.wait()
+    for n in range(8):
+        d = n % 4
+        c = c_at if n < 4 else 1 - c_at
         for h in range(NC):
             at = AROWS + h * GROWS
             cells = in_ref[n, at : at + GROWS].reshape(FR, ROWS, COLS, BSL) * live
@@ -607,7 +613,7 @@
             pltpu.VMEM((3, FR, NY, 6, COLS, Q * APART), BF16),
             pltpu.VMEM((FR, NY, 4, COLS, CH), BF16),
             pltpu.VMEM(part, F32),
-            dma((12,)),
+            dma((20,)),
         ],
         flops=conv_flops,
     )

time: 79.4 us -> 78.7 us (level)
  no operation moved by 1% of the time
where the time goes in v11:
time: 78.7 us; the launch traced here: 77.8 us
  starting transfers between devices  36.6 us (47%)
  Pallas kernels  23 us (29%)
  waiting for transfers between devices  16.6 us (21%)
  between operations  1.45 us (2%)
    pallas_call x10, Pallas kernels, call(): pl.pallas_call(body, out_shape=shapes(outs), in_specs=specs, out_specs=tu...  23 us
    all_to_all x1, waiting for transfers between devices, local(): merged = lax.all_to_all(merged, 'z', 0, 0)  14 us
    all_to_all x1, starting transfers between devices, local(): stats = lax.all_to_all(stats, ('y', 'z'), 0, 0)  10.1 us
    all_to_all x1, starting transfers between devices, local(): merged = lax.all_to_all(merged, 'z', 0, 0)  5.2 us
    ppermute x3, starting transfers between devices, local(): lax.ppermute(packed[d], 'y', [(i, (i + d) % NY) for i in range(NY)])  4.89 us
    ppermute x4, starting transfers between devices, local(): far = [lax.ppermute(a, 'c', swap) for a in near]  4.19 us
    ppermute x3, starting transfers between devices, local(): lax.ppermute(rows, 'x', [(i, (i + d) % NX) for i in range(NX)])  3.68 us
    all_to_all x1, starting transfers between devices, local(): terms = lax.all_to_all(terms, ('y', 'c'), 0, 0)  3.34 us
  transfers between devices with their start and end apart: 15, of which 5 were waited for; matrix products, arithmetic and copies ran while one was open for 0% of the time, Pallas kernels for 25%

profile of v11, /device:TPU:1, one launch (start us, length us, event | category | flops | bytes accessed | tf_op | source)
XLA Modules:
  0.0 77.8 jit_solution(6437634758726826718)
XLA Ops:
  0.6 1.7 %edges_and_sums.1 = (bf16[17,16,256]{2,1,0:T(8,128)(2,1)S(1)}, bf16[16,16,256]{2,1,0:T(8,128)(2,1)S(1)}, f32[8,128]{1,0:T(8,128)S(1)}) custom-call(bf16[8,2,16,256]{3,2,1,0:T(8,128)(2,1)} %bitcast.10, bf16[8,2,16,256]{3,2,1,0:T(8,128)(2,1)} %bitcast.15), custom_call_target="tpu_custom_call" | custom-call | bytes 1048576 | tf_op jit(solution)/shard_map/edges_and_sums/pallas_call | solution.py:432
  2.3 3.3 %collective-permute-start = (bf16[17,16,256]{2,1,0:T(8,128)(2,1)S(1)}, bf16[17,16,256]{2,1,0:T(8,128)(2,1)S(1)}, u32[]{:S(2)}, u32[]{:S(2)}) collective-permute-start(bf16[17,16,256]{2,1,0:T(8,128)(2,1)S(1)} %get-tuple-element.29), channel_id=1, source_target_pairs={{0,1},{1,0},{2,3},{3,2},{4,5},{5,4},{6,7},{7,6},{8,9},{9,8},{10,11... | collective-permute-start | bytes 417800 | tf_op jit(solution)/shard_map/ppermute | solution.py:559
  5.6 1.9 %collective-permute-start.1 = (bf16[16,16,256]{2,1,0:T(8,128)(2,1)S(1)}, bf16[16,16,256]{2,1,0:T(8,128)(2,1)S(1)}, u32[]{:S(2)}, u32[]{:S(2)}) collective-permute-start(bf16[16,16,256]{2,1,0:T(8,128)(2,1)S(1)} %get-tuple-element.30), channel_id=1, source_target_pairs={{1,2},{2,1},{3,4},{4,3},{5,6},{6,5},{7,8},{8,7},{9,10},{10,9},{11,... | collective-permute-start | bytes 393224 | tf_op jit(solution)/shard_map/ppermute | solution.py:560
  7.6 0.8 %pair_sums.1 = f32[32,8,128]{2,1,0:T(8,128)} custom-call(f32[8,128]{1,0:T(8,128)S(1)} %get-tuple-element.37.refs_0_, bf16[17,16,256]{2,1,0:T(8,128)(2,1)S(1)} %collective-permute-done.hp_h.refs_1_), custom_call_target="tpu_custom_call" | custom-call | bytes 1048576 | tf_op jit(solution)/shard_map/pair_sums/pallas_call | solution.py:432
  8.4 10.1 %all-to-all-start = ((f32[32,8,128]{2,1,0:T(8,128)}), f32[32,8,128]{2,1,0:T(8,128)S(1)}, u32[]{:S(2)}, u32[]{:S(2)}) async-start(f32[32,8,128]{2,1,0:T(8,128)} %pair_sums.1), calls=%async_computation | async-start | bytes 262144 | tf_op jit(solution)/shard_map/all_to_all | solution.py:571
  18.5 1.5 %pack_body.1 = (bf16[704,128]{1,0:T(8,128)(2,1)S(1)}, bf16[704,128]{1,0:T(8,128)(2,1)S(1)}, bf16[704,128]{1,0:T(8,128)(2,1)S(1)}, bf16[704,128]{1,0:T(8,128)(2,1)S(1)}) custom-call(bf16[8,2,16,256]{3,2,1,0:T(8,128)(2,1)} %bitcast.11, bf16[256,256]{1,0:T(8,128)(2,1)} %bitcast.16, bf16[17,16,256]{2,1,0:T(8,128)(2,1)S(1)} %collective-permute-done.hp_h.refs_1_, ...), custom_call_target="tpu_custom_call" | custom-call | bytes 1048576 | tf_op jit(solution)/shard_map/pack_body/pallas_call | solution.py:432
  20.0 1.3 %collective-permute-start.2 = (bf16[704,128]{1,0:T(8,128)(2,1)S(1)}, bf16[704,128]{1,0:T(8,128)(2,1)S(1)}, u32[]{:S(2)}, u32[]{:S(2)}) collective-permute-start(bf16[704,128]{1,0:T(8,128)(2,1)S(1)} %get-tuple-element.32), channel_id=1, source_target_pairs={{0,16},{16,32},{32,48},{48,0},{1,17},{17,33},{33,49},{49,1},{2,18}... | collective-permute-start | bytes 540680 | tf_op jit(solution)/shard_map/ppermute | solution.py:583
  21.3 2.4 %collective-permute-start.3 = (bf16[704,128]{1,0:T(8,128)(2,1)S(1)}, bf16[704,128]{1,0:T(8,128)(2,1)S(1)}, u32[]{:S(2)}, u32[]{:S(2)}) collective-permute-start(bf16[704,128]{1,0:T(8,128)(2,1)S(1)} %get-tuple-element.33), channel_id=1, source_target_pairs={{0,32},{16,48},{32,0},{48,16},{1,33},{17,49},{33,1},{49,17},{2,34}... | collective-permute-start | bytes 540680 | tf_op jit(solution)/shard_map/ppermute | solution.py:583
  23.8 1.1 %collective-permute-start.4 = (bf16[704,128]{1,0:T(8,128)(2,1)S(1)}, bf16[704,128]{1,0:T(8,128)(2,1)S(1)}, u32[]{:S(2)}, u32[]{:S(2)}) collective-permute-start(bf16[704,128]{1,0:T(8,128)(2,1)S(1)} %get-tuple-element.34), channel_id=1, source_target_pairs={{0,48},{16,0},{32,16},{48,32},{1,49},{17,1},{33,17},{49,33},{2,50}... | collective-permute-start | bytes 540680 | tf_op jit(solution)/shard_map/ppermute | solution.py:583
  25.6 1.5 %collective-permute-start.5 = (bf16[704,128]{1,0:T(8,128)(2,1)S(1)}, bf16[704,128]{1,0:T(8,128)(2,1)S(1)}, u32[]{:S(2)}, u32[]{:S(2)}) collective-permute-start(bf16[704,128]{1,0:T(8,128)(2,1)S(1)} %get-tuple-element.31.refs_0_), channel_id=1, source_target_pairs={{0,1},{1,0},{2,3},{3,2},{4,5},{5,4},{6,7},{7,6},{8,9},{9,8},{10,11... | collective-permute-start | bytes 540680 | tf_op jit(solution)/shard_map/ppermute | solution.py:598
  27.7 5.0 %backward_terms.1 = (f32[8,8,128]{2,1,0:T(8,128)}, f32[8,32,256]{2,1,0:T(8,128)S(1)}, f32[8,256]{1,0:T(8,128)S(1)}, f32[8,256]{1,0:T(8,128)S(1)}) custom-call(bf16[8,2,16,256]{3,2,1,0:T(8,128)(2,1)} %bitcast.17, bf16[17,16,256]{2,1,0:T(8,128)(2,1)S(1)} %collective-permute-done.hp_h.refs_1_, bf16[16,16,256]{2,1,0:T(8,128)(2,1)S(1)} %collective-permute-done.1.hn_h.refs_2_, ...), custom_call_target="tpu_custom_call" | custom-call | bytes 1048576 | tf_op jit(solution)/shard_map/backward_terms/pallas_call | solution.py:432
  32.9 2.2 %collective-permute-start.6 = (bf16[704,128]{1,0:T(8,128)(2,1)S(1)}, bf16[704,128]{1,0:T(8,128)(2,1)S(1)}, u32[]{:S(2)}, u32[]{:S(2)}) collective-permute-start(bf16[704,128]{1,0:T(8,128)(2,1)S(1)} %collective-permute-done.2.refs_1_), channel_id=1, source_target_pairs={{0,1},{1,0},{2,3},{3,2},{4,5},{5,4},{6,7},{7,6},{8,9},{9,8},{10,11... | collective-permute-start | bytes 540680 | tf_op jit(solution)/shard_map/ppermute | solution.py:598
  35.5 3.3 %all-to-all-start.1 = ((f32[8,8,128]{2,1,0:T(8,128)}), f32[8,8,128]{2,1,0:T(8,128)S(1)}, u32[]{:S(2)}, u32[]{:S(2)}) async-start(f32[8,8,128]{2,1,0:T(8,128)} %get-tuple-element.44), calls=%async_computation.1 | async-start | bytes 65536 | tf_op jit(solution)/shard_map/all_to_all | solution.py:597
  38.9 5.8 %kernel_part.1.part_h = bf16[8,128,256]{2,1,0:T(8,128)(2,1)} custom-call(bf16[704,128]{1,0:T(8,128)(2,1)S(1)} %get-tuple-element.31.refs_0_, bf16[704,128]{1,0:T(8,128)(2,1)S(1)} %collective-permute-done.2.refs_1_, bf16[704,128]{1,0:T(8,128)(2,1)S(1)} %collective-permute-done.3.refs_2_, bf16[704,128]{1,0:T(8,128)(2,1)S(1)} %collective-permute-done.4.refs_3_, ...), custom_call_target="tpu_custom_call" | custom-call | flops 7247757312 | bytes 1048576 | tf_op jit(solution)/shard_map/kernel_part/pallas_call | solution.py:432
  44.7 0.7 add_sums.1
  45.4 5.2 %all-to-all-start.2 = ((bf16[8,128,256]{2,1,0:T(8,128)(2,1)}), bf16[8,128,256]{2,1,0:T(8,128)(2,1)S(1)}, u32[]{:S(2)}, u32[]{:S(2)}) async-start(bf16[8,128,256]{2,1,0:T(8,128)(2,1)} %add_sums.1), calls=%async_computation.2 | async-start | bytes 1048576 | tf_op jit(solution)/shard_map/all_to_all | solution.py:629
  50.6 4.0 %forward_conv.1 = bf16[8,2,16,256]{3,2,1,0:T(8,128)(2,1)} custom-call(bf16[8,2,16,256]{3,2,1,0:T(8,128)(2,1)} %bitcast.13, bf16[17,16,256]{2,1,0:T(8,128)(2,1)S(1)} %collective-permute-done.hp_h.refs_1_, bf16[16,16,256]{2,1,0:T(8,128)(2,1)S(1)} %collective-permute-done.1.hn_h.refs_2_, f32[8,256]{1,0:T(8,128)S(1)} %get-tuple-element.46.refs_8_.refs_3_.refs_4_, ...), custom_call_target="tpu_custom_call" | custom-call | flops 7247757312 | bytes 1048576 | tf_op jit(solution)/shard_map/forward_conv/pallas_call | solution.py:432
  54.7 14.0 %all-to-all-done.2.refs_0_ = bf16[8,128,256]{2,1,0:T(8,128)(2,1)S(1)} async-done(((bf16[8,128,256]{2,1,0:T(8,128)(2,1)}), bf16[8,128,256]{2,1,0:T(8,128)(2,1)S(1)}, u32[]{:S(2)}, u32[]{:S(2)}) %all-to-all-start.2) | async-done | bytes 524320 | tf_op jit(solution)/shard_map/all_to_all | solution.py:629
  69.1 2.5 %collective-permute-start.11 = (s16[112,256]{1,0:T(8,128)(2,1)S(1)}, s16[112,256]{1,0:T(8,128)(2,1)S(1)}, u32[]{:S(2)}, u32[]{:S(2)}) collective-permute-start(s16[112,256]{1,0:T(8,128)(2,1)S(1)} %get-tuple-element.51.own_h), channel_id=1, source_target_pairs={{0,192},{64,0},{128,64},{192,128},{1,193},{65,1},{129,65},{193,129... | collective-permute-start | bytes 172040 | tf_op jit(solution)/shard_map/ppermute | solution.py:642
  72.2 0.6 collective-permute-start.9
  72.8 2.0 %finish_input.1 = bf16[8,2,16,256]{3,2,1,0:T(8,128)(2,1)} custom-call(f32[8,128]{1,0:T(8,128)S(1)} %get-tuple-element.49.refs_0_, f32[8,32,256]{2,1,0:T(8,128)S(1)} %get-tuple-element.50.refs_1_, bf16[8,2,16,256]{3,2,1,0:T(8,128)(2,1)} %bitcast.14, bf16[8,2,16,256]{3,2,1,0:T(8,128)(2,1)} %bitcast.18, f32[8,256]{1,0:T(8,128)S(1)} %get-tuple-element.46.refs_8_.refs_3_.refs_4_, ...), custom_call_target="tpu_custom_call" | custom-call | bytes 1048576 | tf_op jit(solution)/shard_map/finish_input/pallas_call | solution.py:432
  74.8 1.4 %collective-permute-done.10.two_h = s16[112,256]{1,0:T(8,128)(2,1)S(1)} collective-permute-done((s16[112,256]{1,0:T(8,128)(2,1)S(1)}, s16[112,256]{1,0:T(8,128)(2,1)S(1)}, u32[]{:S(2)}, u32[]{:S(2)}) %collective-permute-start.10) | collective-permute-done | bytes 57376 | tf_op jit(solution)/shard_map/ppermute | solution.py:642
  76.2 0.6 collective-permute-done.9.one_h
  76.8 1.1 %sum_clips.1 = (f32[27,4,256]{2,1,0:T(4,128)}, f32[1,256]{1,0:T(1,128)}) custom-call(s16[112,256]{1,0:T(8,128)(2,1)S(1)} %get-tuple-element.51.own_h, s16[112,256]{1,0:T(8,128)(2,1)S(1)} %collective-permute-done.9.one_h, s16[112,256]{1,0:T(8,128)(2,1)S(1)} %collective-permute-done.10.two_h, s16[112,256]{1,0:T(8,128)(2,1)S(1)} %collective-permute-done.11.three_h), custom_call_target="tpu_custom_call" | custom-call | bytes 1048576 | tf_op jit(solution)/shard_map/sum_clips/pallas_call | solution.py:432
  (18 shorter events, 2.3 us)
Async XLA Ops:
  2.3 5.2 %collective-permute-start = (bf16[17,16,256]{2,1,0:T(8,128)(2,1)S(1)}, bf16[17,16,256]{2,1,0:T(8,128)(2,1)S(1)}, u32[]{:S(2)}, u32[]{:S(2)}) collective-permute-start(bf16[17,16,256]{2,1,0:T(8,128)(2,1)S(1)} %get-tuple-element.29), channel_id=1, source_target_pairs={{0,1},{1,0},{2,3},{3,2},{4,5},{5,4},{6,7},{7,6},{8,9},{9,8},{10,11... | collective-permute-start | bytes 417800 | tf_op jit(solution)/shard_map/ppermute | solution.py:559
  5.6 12.9 %collective-permute-start.1 = (bf16[16,16,256]{2,1,0:T(8,128)(2,1)S(1)}, bf16[16,16,256]{2,1,0:T(8,128)(2,1)S(1)}, u32[]{:S(2)}, u32[]{:S(2)}) collective-permute-start(bf16[16,16,256]{2,1,0:T(8,128)(2,1)S(1)} %get-tuple-element.30), channel_id=1, source_target_pairs={{1,2},{2,1},{3,4},{4,3},{5,6},{6,5},{7,8},{8,7},{9,10},{10,9},{11,... | collective-permute-start | bytes 393224 | tf_op jit(solution)/shard_map/ppermute | solution.py:560
  8.4 19.3 %all-to-all-start = ((f32[32,8,128]{2,1,0:T(8,128)}), f32[32,8,128]{2,1,0:T(8,128)S(1)}, u32[]{:S(2)}, u32[]{:S(2)}) async-start(f32[32,8,128]{2,1,0:T(8,128)} %pair_sums.1), calls=%async_computation | async-start | bytes 262144 | tf_op jit(solution)/shard_map/all_to_all | solution.py:571
  20.0 12.7 %collective-permute-start.2 = (bf16[704,128]{1,0:T(8,128)(2,1)S(1)}, bf16[704,128]{1,0:T(8,128)(2,1)S(1)}, u32[]{:S(2)}, u32[]{:S(2)}) collective-permute-start(bf16[704,128]{1,0:T(8,128)(2,1)S(1)} %get-tuple-element.32), channel_id=1, source_target_pairs={{0,16},{16,32},{32,48},{48,0},{1,17},{17,33},{33,49},{49,1},{2,18}... | collective-permute-start | bytes 540680 | tf_op jit(solution)/shard_map/ppermute | solution.py:583
  21.3 11.5 %collective-permute-start.3 = (bf16[704,128]{1,0:T(8,128)(2,1)S(1)}, bf16[704,128]{1,0:T(8,128)(2,1)S(1)}, u32[]{:S(2)}, u32[]{:S(2)}) collective-permute-start(bf16[704,128]{1,0:T(8,128)(2,1)S(1)} %get-tuple-element.33), channel_id=1, source_target_pairs={{0,32},{16,48},{32,0},{48,16},{1,33},{17,49},{33,1},{49,17},{2,34}... | collective-permute-start | bytes 540680 | tf_op jit(solution)/shard_map/ppermute | solution.py:583
  23.8 9.1 %collective-permute-start.4 = (bf16[704,128]{1,0:T(8,128)(2,1)S(1)}, bf16[704,128]{1,0:T(8,128)(2,1)S(1)}, u32[]{:S(2)}, u32[]{:S(2)}) collective-permute-start(bf16[704,128]{1,0:T(8,128)(2,1)S(1)} %get-tuple-element.34), channel_id=1, source_target_pairs={{0,48},{16,0},{32,16},{48,32},{1,49},{17,1},{33,17},{49,33},{2,50}... | collective-permute-start | bytes 540680 | tf_op jit(solution)/shard_map/ppermute | solution.py:583
  25.6 13.3 %collective-permute-start.5 = (bf16[704,128]{1,0:T(8,128)(2,1)S(1)}, bf16[704,128]{1,0:T(8,128)(2,1)S(1)}, u32[]{:S(2)}, u32[]{:S(2)}) collective-permute-start(bf16[704,128]{1,0:T(8,128)(2,1)S(1)} %get-tuple-element.31.refs_0_), channel_id=1, source_target_pairs={{0,1},{1,0},{2,3},{3,2},{4,5},{5,4},{6,7},{7,6},{8,9},{9,8},{10,11... | collective-permute-start | bytes 540680 | tf_op jit(solution)/shard_map/ppermute | solution.py:598
  32.9 6.0 %collective-permute-start.6 = (bf16[704,128]{1,0:T(8,128)(2,1)S(1)}, bf16[704,128]{1,0:T(8,128)(2,1)S(1)}, u32[]{:S(2)}, u32[]{:S(2)}) collective-permute-start(bf16[704,128]{1,0:T(8,128)(2,1)S(1)} %collective-permute-done.2.refs_1_), channel_id=1, source_target_pairs={{0,1},{1,0},{2,3},{3,2},{4,5},{5,4},{6,7},{7,6},{8,9},{9,8},{10,11... | collective-permute-start | bytes 540680 | tf_op jit(solution)/shard_map/ppermute | solution.py:598
  35.0 3.9 %collective-permute-start.7 = (bf16[704,128]{1,0:T(8,128)(2,1)S(1)}, bf16[704,128]{1,0:T(8,128)(2,1)S(1)}, u32[]{:S(2)}, u32[]{:S(2)}) collective-permute-start(bf16[704,128]{1,0:T(8,128)(2,1)S(1)} %collective-permute-done.3.refs_2_), channel_id=1, source_target_pairs={{0,1},{1,0},{2,3},{3,2},{4,5},{5,4},{6,7},{7,6},{8,9},{9,8},{10,11... | collective-permute-start | bytes 540680 | tf_op jit(solution)/shard_map/ppermute | solution.py:598
  35.1 3.8 %collective-permute-start.8 = (bf16[704,128]{1,0:T(8,128)(2,1)S(1)}, bf16[704,128]{1,0:T(8,128)(2,1)S(1)}, u32[]{:S(2)}, u32[]{:S(2)}) collective-permute-start(bf16[704,128]{1,0:T(8,128)(2,1)S(1)} %collective-permute-done.4.refs_3_), channel_id=1, source_target_pairs={{0,1},{1,0},{2,3},{3,2},{4,5},{5,4},{6,7},{7,6},{8,9},{9,8},{10,11... | collective-permute-start | bytes 540680 | tf_op jit(solution)/shard_map/ppermute | solution.py:598
  35.5 9.2 %all-to-all-start.1 = ((f32[8,8,128]{2,1,0:T(8,128)}), f32[8,8,128]{2,1,0:T(8,128)S(1)}, u32[]{:S(2)}, u32[]{:S(2)}) async-start(f32[8,8,128]{2,1,0:T(8,128)} %get-tuple-element.44), calls=%async_computation.1 | async-start | bytes 65536 | tf_op jit(solution)/shard_map/all_to_all | solution.py:597
  45.4 23.2 %all-to-all-start.2 = ((bf16[8,128,256]{2,1,0:T(8,128)(2,1)}), bf16[8,128,256]{2,1,0:T(8,128)(2,1)S(1)}, u32[]{:S(2)}, u32[]{:S(2)}) async-start(bf16[8,128,256]{2,1,0:T(8,128)(2,1)} %add_sums.1), calls=%async_computation.2 | async-start | bytes 1048576 | tf_op jit(solution)/shard_map/all_to_all | solution.py:629
  69.1 5.7 %collective-permute-start.11 = (s16[112,256]{1,0:T(8,128)(2,1)S(1)}, s16[112,256]{1,0:T(8,128)(2,1)S(1)}, u32[]{:S(2)}, u32[]{:S(2)}) collective-permute-start(s16[112,256]{1,0:T(8,128)(2,1)S(1)} %get-tuple-element.51.own_h), channel_id=1, source_target_pairs={{0,192},{64,0},{128,64},{192,128},{1,193},{65,1},{129,65},{193,129... | collective-permute-start | bytes 172040 | tf_op jit(solution)/shard_map/ppermute | solution.py:642
  71.6 4.6 %collective-permute-start.10 = (s16[112,256]{1,0:T(8,128)(2,1)S(1)}, s16[112,256]{1,0:T(8,128)(2,1)S(1)}, u32[]{:S(2)}, u32[]{:S(2)}) collective-permute-start(s16[112,256]{1,0:T(8,128)(2,1)S(1)} %get-tuple-element.51.own_h), channel_id=1, source_target_pairs={{0,128},{64,192},{128,0},{192,64},{1,129},{65,193},{129,1},{193,65... | collective-permute-start | bytes 172040 | tf_op jit(solution)/shard_map/ppermute | solution.py:642
  72.2 4.6 %collective-permute-start.9 = (s16[112,256]{1,0:T(8,128)(2,1)S(1)}, s16[112,256]{1,0:T(8,128)(2,1)S(1)}, u32[]{:S(2)}, u32[]{:S(2)}) collective-permute-start(s16[112,256]{1,0:T(8,128)(2,1)S(1)} %get-tuple-element.51.own_h), channel_id=1, source_target_pairs={{0,64},{64,128},{128,192},{192,0},{1,65},{65,129},{129,193},{193,1... | collective-permute-start | bytes 172040 | tf_op jit(solution)/shard_map/ppermute | solution.py:642

commit v12 on v11

--- a/solution.py
+++ b/solution.py
@@ -295,10 +295,17 @@
                 at = n * width + i * APART
                 piece = product[at : at + APART].reshape(NZ, 4, CH)
                 sum_ref[:, tap * 4 : tap * 4 + 4] = piece
-    out_ref[...] = sum_ref[...].astype(BF16)
-    copy = pltpu.make_async_copy(out_ref, out_h.at[:, :PROWS], sem.at[0])
-    copy.start()
-    copy.wait()
+    copies = []
+    for n in range(0, NZ, 2):
+        out_ref[n : n + 2] = sum_ref[n : n + 2].astype(BF16)
+        copies.append(
+            pltpu.make_async_copy(
+                out_ref.at[n : n + 2], out_h.at[n : n + 2, :PROWS], sem.at[n // 2]
+            )
+        )
+        copies[-1].start()
+    for copy in copies:
+        copy.wait()
 
 
 def add_sums(part_h, b_h, out_h, b_ref, out_ref, sem):

time: 78.7 us -> 78.7 us (level)
  no operation moved by 1% of the time
where the time goes in v12:
time: 78.7 us; the launch traced here: 77.8 us
  starting transfers between devices  36.6 us (47%)
  Pallas kernels  23 us (29%)
  waiting for transfers between devices  16.6 us (21%)
  between operations  1.45 us (2%)
    pallas_call x10, Pallas kernels, call(): pl.pallas_call(body, out_shape=shapes(outs), in_specs=specs, out_specs=tu...  23 us
    all_to_all x1, waiting for transfers between devices, local(): merged = lax.all_to_all(merged, 'z', 0, 0)  14 us
    all_to_all x1, starting transfers between devices, local(): stats = lax.all_to_all(stats, ('y', 'z'), 0, 0)  10.1 us
    all_to_all x1, starting transfers between devices, local(): merged = lax.all_to_all(merged, 'z', 0, 0)  5.2 us
    ppermute x3, starting transfers between devices, local(): lax.ppermute(packed[d], 'y', [(i, (i + d) % NY) for i in range(NY)])  4.89 us
    ppermute x4, starting transfers between devices, local(): far = [lax.ppermute(a, 'c', swap) for a in near]  4.19 us
    ppermute x3, starting transfers between devices, local(): lax.ppermute(rows, 'x', [(i, (i + d) % NX) for i in range(NX)])  3.68 us
    all_to_all x1, starting transfers between devices, local(): terms = lax.all_to_all(terms, ('y', 'c'), 0, 0)  3.34 us
  transfers between devices with their start and end apart: 15, of which 5 were waited for; matrix products, arithmetic and copies ran while one was open for 0% of the time, Pallas kernels for 25%

profile of v12, /device:TPU:1, one launch (start us, length us, event | category | flops | bytes accessed | tf_op | source)
XLA Modules:
  0.0 77.8 jit_solution(8623282824598253590)
XLA Ops:
  0.6 1.7 %edges_and_sums.1 = (bf16[17,16,256]{2,1,0:T(8,128)(2,1)S(1)}, bf16[16,16,256]{2,1,0:T(8,128)(2,1)S(1)}, f32[8,128]{1,0:T(8,128)S(1)}) custom-call(bf16[8,2,16,256]{3,2,1,0:T(8,128)(2,1)} %bitcast.10, bf16[8,2,16,256]{3,2,1,0:T(8,128)(2,1)} %bitcast.15), custom_call_target="tpu_custom_call" | custom-call | bytes 1048576 | tf_op jit(solution)/shard_map/edges_and_sums/pallas_call | solution.py:439
  2.3 3.3 %collective-permute-start = (bf16[17,16,256]{2,1,0:T(8,128)(2,1)S(1)}, bf16[17,16,256]{2,1,0:T(8,128)(2,1)S(1)}, u32[]{:S(2)}, u32[]{:S(2)}) collective-permute-start(bf16[17,16,256]{2,1,0:T(8,128)(2,1)S(1)} %get-tuple-element.29), channel_id=1, source_target_pairs={{0,1},{1,0},{2,3},{3,2},{4,5},{5,4},{6,7},{7,6},{8,9},{9,8},{10,11... | collective-permute-start | bytes 417800 | tf_op jit(solution)/shard_map/ppermute | solution.py:566
  5.6 1.9 %collective-permute-start.1 = (bf16[16,16,256]{2,1,0:T(8,128)(2,1)S(1)}, bf16[16,16,256]{2,1,0:T(8,128)(2,1)S(1)}, u32[]{:S(2)}, u32[]{:S(2)}) collective-permute-start(bf16[16,16,256]{2,1,0:T(8,128)(2,1)S(1)} %get-tuple-element.30), channel_id=1, source_target_pairs={{1,2},{2,1},{3,4},{4,3},{5,6},{6,5},{7,8},{8,7},{9,10},{10,9},{11,... | collective-permute-start | bytes 393224 | tf_op jit(solution)/shard_map/ppermute | solution.py:567
  7.6 0.8 %pair_sums.1 = f32[32,8,128]{2,1,0:T(8,128)} custom-call(f32[8,128]{1,0:T(8,128)S(1)} %get-tuple-element.37.refs_0_, bf16[17,16,256]{2,1,0:T(8,128)(2,1)S(1)} %collective-permute-done.hp_h.refs_1_), custom_call_target="tpu_custom_call" | custom-call | bytes 1048576 | tf_op jit(solution)/shard_map/pair_sums/pallas_call | solution.py:439
  8.4 10.1 %all-to-all-start = ((f32[32,8,128]{2,1,0:T(8,128)}), f32[32,8,128]{2,1,0:T(8,128)S(1)}, u32[]{:S(2)}, u32[]{:S(2)}) async-start(f32[32,8,128]{2,1,0:T(8,128)} %pair_sums.1), calls=%async_computation | async-start | bytes 262144 | tf_op jit(solution)/shard_map/all_to_all | solution.py:578
  18.5 1.5 %pack_body.1 = (bf16[704,128]{1,0:T(8,128)(2,1)S(1)}, bf16[704,128]{1,0:T(8,128)(2,1)S(1)}, bf16[704,128]{1,0:T(8,128)(2,1)S(1)}, bf16[704,128]{1,0:T(8,128)(2,1)S(1)}) custom-call(bf16[8,2,16,256]{3,2,1,0:T(8,128)(2,1)} %bitcast.11, bf16[256,256]{1,0:T(8,128)(2,1)} %bitcast.16, bf16[17,16,256]{2,1,0:T(8,128)(2,1)S(1)} %collective-permute-done.hp_h.refs_1_, ...), custom_call_target="tpu_custom_call" | custom-call | bytes 1048576 | tf_op jit(solution)/shard_map/pack_body/pallas_call | solution.py:439
  20.0 1.3 %collective-permute-start.2 = (bf16[704,128]{1,0:T(8,128)(2,1)S(1)}, bf16[704,128]{1,0:T(8,128)(2,1)S(1)}, u32[]{:S(2)}, u32[]{:S(2)}) collective-permute-start(bf16[704,128]{1,0:T(8,128)(2,1)S(1)} %get-tuple-element.32), channel_id=1, source_target_pairs={{0,16},{16,32},{32,48},{48,0},{1,17},{17,33},{33,49},{49,1},{2,18}... | collective-permute-start | bytes 540680 | tf_op jit(solution)/shard_map/ppermute | solution.py:590
  21.3 2.4 %collective-permute-start.3 = (bf16[704,128]{1,0:T(8,128)(2,1)S(1)}, bf16[704,128]{1,0:T(8,128)(2,1)S(1)}, u32[]{:S(2)}, u32[]{:S(2)}) collective-permute-start(bf16[704,128]{1,0:T(8,128)(2,1)S(1)} %get-tuple-element.33), channel_id=1, source_target_pairs={{0,32},{16,48},{32,0},{48,16},{1,33},{17,49},{33,1},{49,17},{2,34}... | collective-permute-start | bytes 540680 | tf_op jit(solution)/shard_map/ppermute | solution.py:590
  23.8 1.1 %collective-permute-start.4 = (bf16[704,128]{1,0:T(8,128)(2,1)S(1)}, bf16[704,128]{1,0:T(8,128)(2,1)S(1)}, u32[]{:S(2)}, u32[]{:S(2)}) collective-permute-start(bf16[704,128]{1,0:T(8,128)(2,1)S(1)} %get-tuple-element.34), channel_id=1, source_target_pairs={{0,48},{16,0},{32,16},{48,32},{1,49},{17,1},{33,17},{49,33},{2,50}... | collective-permute-start | bytes 540680 | tf_op jit(solution)/shard_map/ppermute | solution.py:590
  25.6 1.5 %collective-permute-start.5 = (bf16[704,128]{1,0:T(8,128)(2,1)S(1)}, bf16[704,128]{1,0:T(8,128)(2,1)S(1)}, u32[]{:S(2)}, u32[]{:S(2)}) collective-permute-start(bf16[704,128]{1,0:T(8,128)(2,1)S(1)} %get-tuple-element.31.refs_0_), channel_id=1, source_target_pairs={{0,1},{1,0},{2,3},{3,2},{4,5},{5,4},{6,7},{7,6},{8,9},{9,8},{10,11... | collective-permute-start | bytes 540680 | tf_op jit(solution)/shard_map/ppermute | solution.py:605
  27.7 5.0 %backward_terms.1 = (f32[8,8,128]{2,1,0:T(8,128)}, f32[8,32,256]{2,1,0:T(8,128)S(1)}, f32[8,256]{1,0:T(8,128)S(1)}, f32[8,256]{1,0:T(8,128)S(1)}) custom-call(bf16[8,2,16,256]{3,2,1,0:T(8,128)(2,1)} %bitcast.17, bf16[17,16,256]{2,1,0:T(8,128)(2,1)S(1)} %collective-permute-done.hp_h.refs_1_, bf16[16,16,256]{2,1,0:T(8,128)(2,1)S(1)} %collective-permute-done.1.hn_h.refs_2_, ...), custom_call_target="tpu_custom_call" | custom-call | bytes 1048576 | tf_op jit(solution)/shard_map/backward_terms/pallas_call | solution.py:439
  32.9 2.2 %collective-permute-start.6 = (bf16[704,128]{1,0:T(8,128)(2,1)S(1)}, bf16[704,128]{1,0:T(8,128)(2,1)S(1)}, u32[]{:S(2)}, u32[]{:S(2)}) collective-permute-start(bf16[704,128]{1,0:T(8,128)(2,1)S(1)} %collective-permute-done.2.refs_1_), channel_id=1, source_target_pairs={{0,1},{1,0},{2,3},{3,2},{4,5},{5,4},{6,7},{7,6},{8,9},{9,8},{10,11... | collective-permute-start | bytes 540680 | tf_op jit(solution)/shard_map/ppermute | solution.py:605
  35.5 3.3 %all-to-all-start.1 = ((f32[8,8,128]{2,1,0:T(8,128)}), f32[8,8,128]{2,1,0:T(8,128)S(1)}, u32[]{:S(2)}, u32[]{:S(2)}) async-start(f32[8,8,128]{2,1,0:T(8,128)} %get-tuple-element.44), calls=%async_computation.1 | async-start | bytes 65536 | tf_op jit(solution)/shard_map/all_to_all | solution.py:604
  38.9 5.8 %kernel_part.1.part_h = bf16[8,128,256]{2,1,0:T(8,128)(2,1)} custom-call(bf16[704,128]{1,0:T(8,128)(2,1)S(1)} %get-tuple-element.31.refs_0_, bf16[704,128]{1,0:T(8,128)(2,1)S(1)} %collective-permute-done.2.refs_1_, bf16[704,128]{1,0:T(8,128)(2,1)S(1)} %collective-permute-done.3.refs_2_, bf16[704,128]{1,0:T(8,128)(2,1)S(1)} %collective-permute-done.4.refs_3_, ...), custom_call_target="tpu_custom_call" | custom-call | flops 7247757312 | bytes 1048576 | tf_op jit(solution)/shard_map/kernel_part/pallas_call | solution.py:439
  44.7 0.7 add_sums.1
  45.4 5.2 %all-to-all-start.2 = ((bf16[8,128,256]{2,1,0:T(8,128)(2,1)}), bf16[8,128,256]{2,1,0:T(8,128)(2,1)S(1)}, u32[]{:S(2)}, u32[]{:S(2)}) async-start(bf16[8,128,256]{2,1,0:T(8,128)(2,1)} %add_sums.1), calls=%async_computation.2 | async-start | bytes 1048576 | tf_op jit(solution)/shard_map/all_to_all | solution.py:636
  50.6 4.0 %forward_conv.1 = bf16[8,2,16,256]{3,2,1,0:T(8,128)(2,1)} custom-call(bf16[8,2,16,256]{3,2,1,0:T(8,128)(2,1)} %bitcast.13, bf16[17,16,256]{2,1,0:T(8,128)(2,1)S(1)} %collective-permute-done.hp_h.refs_1_, bf16[16,16,256]{2,1,0:T(8,128)(2,1)S(1)} %collective-permute-done.1.hn_h.refs_2_, f32[8,256]{1,0:T(8,128)S(1)} %get-tuple-element.46.refs_8_.refs_3_.refs_4_, ...), custom_call_target="tpu_custom_call" | custom-call | flops 7247757312 | bytes 1048576 | tf_op jit(solution)/shard_map/forward_conv/pallas_call | solution.py:439
  54.6 14.0 %all-to-all-done.2.refs_0_ = bf16[8,128,256]{2,1,0:T(8,128)(2,1)S(1)} async-done(((bf16[8,128,256]{2,1,0:T(8,128)(2,1)}), bf16[8,128,256]{2,1,0:T(8,128)(2,1)S(1)}, u32[]{:S(2)}, u32[]{:S(2)}) %all-to-all-start.2) | async-done | bytes 524320 | tf_op jit(solution)/shard_map/all_to_all | solution.py:636
  69.1 2.5 %collective-permute-start.11 = (s16[112,256]{1,0:T(8,128)(2,1)S(1)}, s16[112,256]{1,0:T(8,128)(2,1)S(1)}, u32[]{:S(2)}, u32[]{:S(2)}) collective-permute-start(s16[112,256]{1,0:T(8,128)(2,1)S(1)} %get-tuple-element.51.own_h), channel_id=1, source_target_pairs={{0,192},{64,0},{128,64},{192,128},{1,193},{65,1},{129,65},{193,129... | collective-permute-start | bytes 172040 | tf_op jit(solution)/shard_map/ppermute | solution.py:649
  72.2 0.6 collective-permute-start.9
  72.8 2.0 %finish_input.1 = bf16[8,2,16,256]{3,2,1,0:T(8,128)(2,1)} custom-call(f32[8,128]{1,0:T(8,128)S(1)} %get-tuple-element.49.refs_0_, f32[8,32,256]{2,1,0:T(8,128)S(1)} %get-tuple-element.50.refs_1_, bf16[8,2,16,256]{3,2,1,0:T(8,128)(2,1)} %bitcast.14, bf16[8,2,16,256]{3,2,1,0:T(8,128)(2,1)} %bitcast.18, f32[8,256]{1,0:T(8,128)S(1)} %get-tuple-element.46.refs_8_.refs_3_.refs_4_, ...), custom_call_target="tpu_custom_call" | custom-call | bytes 1048576 | tf_op jit(solution)/shard_map/finish_input/pallas_call | solution.py:439
  74.8 1.4 %collective-permute-done.10.two_h = s16[112,256]{1,0:T(8,128)(2,1)S(1)} collective-permute-done((s16[112,256]{1,0:T(8,128)(2,1)S(1)}, s16[112,256]{1,0:T(8,128)(2,1)S(1)}, u32[]{:S(2)}, u32[]{:S(2)}) %collective-permute-start.10) | collective-permute-done | bytes 57376 | tf_op jit(solution)/shard_map/ppermute | solution.py:649
  76.2 0.6 collective-permute-done.9.one_h
  76.8 1.1 %sum_clips.1 = (f32[27,4,256]{2,1,0:T(4,128)}, f32[1,256]{1,0:T(1,128)}) custom-call(s16[112,256]{1,0:T(8,128)(2,1)S(1)} %get-tuple-element.51.own_h, s16[112,256]{1,0:T(8,128)(2,1)S(1)} %collective-permute-done.9.one_h, s16[112,256]{1,0:T(8,128)(2,1)S(1)} %collective-permute-done.10.two_h, s16[112,256]{1,0:T(8,128)(2,1)S(1)} %collective-permute-done.11.three_h), custom_call_target="tpu_custom_call" | custom-call | bytes 1048576 | tf_op jit(solution)/shard_map/sum_clips/pallas_call | solution.py:439
  (18 shorter events, 2.3 us)
Async XLA Ops:
  2.3 5.2 %collective-permute-start = (bf16[17,16,256]{2,1,0:T(8,128)(2,1)S(1)}, bf16[17,16,256]{2,1,0:T(8,128)(2,1)S(1)}, u32[]{:S(2)}, u32[]{:S(2)}) collective-permute-start(bf16[17,16,256]{2,1,0:T(8,128)(2,1)S(1)} %get-tuple-element.29), channel_id=1, source_target_pairs={{0,1},{1,0},{2,3},{3,2},{4,5},{5,4},{6,7},{7,6},{8,9},{9,8},{10,11... | collective-permute-start | bytes 417800 | tf_op jit(solution)/shard_map/ppermute | solution.py:566
  5.6 12.9 %collective-permute-start.1 = (bf16[16,16,256]{2,1,0:T(8,128)(2,1)S(1)}, bf16[16,16,256]{2,1,0:T(8,128)(2,1)S(1)}, u32[]{:S(2)}, u32[]{:S(2)}) collective-permute-start(bf16[16,16,256]{2,1,0:T(8,128)(2,1)S(1)} %get-tuple-element.30), channel_id=1, source_target_pairs={{1,2},{2,1},{3,4},{4,3},{5,6},{6,5},{7,8},{8,7},{9,10},{10,9},{11,... | collective-permute-start | bytes 393224 | tf_op jit(solution)/shard_map/ppermute | solution.py:567
  8.4 19.3 %all-to-all-start = ((f32[32,8,128]{2,1,0:T(8,128)}), f32[32,8,128]{2,1,0:T(8,128)S(1)}, u32[]{:S(2)}, u32[]{:S(2)}) async-start(f32[32,8,128]{2,1,0:T(8,128)} %pair_sums.1), calls=%async_computation | async-start | bytes 262144 | tf_op jit(solution)/shard_map/all_to_all | solution.py:578
  20.0 12.7 %collective-permute-start.2 = (bf16[704,128]{1,0:T(8,128)(2,1)S(1)}, bf16[704,128]{1,0:T(8,128)(2,1)S(1)}, u32[]{:S(2)}, u32[]{:S(2)}) collective-permute-start(bf16[704,128]{1,0:T(8,128)(2,1)S(1)} %get-tuple-element.32), channel_id=1, source_target_pairs={{0,16},{16,32},{32,48},{48,0},{1,17},{17,33},{33,49},{49,1},{2,18}... | collective-permute-start | bytes 540680 | tf_op jit(solution)/shard_map/ppermute | solution.py:590
  21.3 11.5 %collective-permute-start.3 = (bf16[704,128]{1,0:T(8,128)(2,1)S(1)}, bf16[704,128]{1,0:T(8,128)(2,1)S(1)}, u32[]{:S(2)}, u32[]{:S(2)}) collective-permute-start(bf16[704,128]{1,0:T(8,128)(2,1)S(1)} %get-tuple-element.33), channel_id=1, source_target_pairs={{0,32},{16,48},{32,0},{48,16},{1,33},{17,49},{33,1},{49,17},{2,34}... | collective-permute-start | bytes 540680 | tf_op jit(solution)/shard_map/ppermute | solution.py:590
  23.8 9.1 %collective-permute-start.4 = (bf16[704,128]{1,0:T(8,128)(2,1)S(1)}, bf16[704,128]{1,0:T(8,128)(2,1)S(1)}, u32[]{:S(2)}, u32[]{:S(2)}) collective-permute-start(bf16[704,128]{1,0:T(8,128)(2,1)S(1)} %get-tuple-element.34), channel_id=1, source_target_pairs={{0,48},{16,0},{32,16},{48,32},{1,49},{17,1},{33,17},{49,33},{2,50}... | collective-permute-start | bytes 540680 | tf_op jit(solution)/shard_map/ppermute | solution.py:590
  25.6 13.3 %collective-permute-start.5 = (bf16[704,128]{1,0:T(8,128)(2,1)S(1)}, bf16[704,128]{1,0:T(8,128)(2,1)S(1)}, u32[]{:S(2)}, u32[]{:S(2)}) collective-permute-start(bf16[704,128]{1,0:T(8,128)(2,1)S(1)} %get-tuple-element.31.refs_0_), channel_id=1, source_target_pairs={{0,1},{1,0},{2,3},{3,2},{4,5},{5,4},{6,7},{7,6},{8,9},{9,8},{10,11... | collective-permute-start | bytes 540680 | tf_op jit(solution)/shard_map/ppermute | solution.py:605
  32.9 6.0 %collective-permute-start.6 = (bf16[704,128]{1,0:T(8,128)(2,1)S(1)}, bf16[704,128]{1,0:T(8,128)(2,1)S(1)}, u32[]{:S(2)}, u32[]{:S(2)}) collective-permute-start(bf16[704,128]{1,0:T(8,128)(2,1)S(1)} %collective-permute-done.2.refs_1_), channel_id=1, source_target_pairs={{0,1},{1,0},{2,3},{3,2},{4,5},{5,4},{6,7},{7,6},{8,9},{9,8},{10,11... | collective-permute-start | bytes 540680 | tf_op jit(solution)/shard_map/ppermute | solution.py:605
  35.0 3.9 %collective-permute-start.7 = (bf16[704,128]{1,0:T(8,128)(2,1)S(1)}, bf16[704,128]{1,0:T(8,128)(2,1)S(1)}, u32[]{:S(2)}, u32[]{:S(2)}) collective-permute-start(bf16[704,128]{1,0:T(8,128)(2,1)S(1)} %collective-permute-done.3.refs_2_), channel_id=1, source_target_pairs={{0,1},{1,0},{2,3},{3,2},{4,5},{5,4},{6,7},{7,6},{8,9},{9,8},{10,11... | collective-permute-start | bytes 540680 | tf_op jit(solution)/shard_map/ppermute | solution.py:605
  35.1 3.8 %collective-permute-start.8 = (bf16[704,128]{1,0:T(8,128)(2,1)S(1)}, bf16[704,128]{1,0:T(8,128)(2,1)S(1)}, u32[]{:S(2)}, u32[]{:S(2)}) collective-permute-start(bf16[704,128]{1,0:T(8,128)(2,1)S(1)} %collective-permute-done.4.refs_3_), channel_id=1, source_target_pairs={{0,1},{1,0},{2,3},{3,2},{4,5},{5,4},{6,7},{7,6},{8,9},{9,8},{10,11... | collective-permute-start | bytes 540680 | tf_op jit(solution)/shard_map/ppermute | solution.py:605
  35.5 9.2 %all-to-all-start.1 = ((f32[8,8,128]{2,1,0:T(8,128)}), f32[8,8,128]{2,1,0:T(8,128)S(1)}, u32[]{:S(2)}, u32[]{:S(2)}) async-start(f32[8,8,128]{2,1,0:T(8,128)} %get-tuple-element.44), calls=%async_computation.1 | async-start | bytes 65536 | tf_op jit(solution)/shard_map/all_to_all | solution.py:604
  45.4 23.2 %all-to-all-start.2 = ((bf16[8,128,256]{2,1,0:T(8,128)(2,1)}), bf16[8,128,256]{2,1,0:T(8,128)(2,1)S(1)}, u32[]{:S(2)}, u32[]{:S(2)}) async-start(bf16[8,128,256]{2,1,0:T(8,128)(2,1)} %add_sums.1), calls=%async_computation.2 | async-start | bytes 1048576 | tf_op jit(solution)/shard_map/all_to_all | solution.py:636
  69.1 5.7 %collective-permute-start.11 = (s16[112,256]{1,0:T(8,128)(2,1)S(1)}, s16[112,256]{1,0:T(8,128)(2,1)S(1)}, u32[]{:S(2)}, u32[]{:S(2)}) collective-permute-start(s16[112,256]{1,0:T(8,128)(2,1)S(1)} %get-tuple-element.51.own_h), channel_id=1, source_target_pairs={{0,192},{64,0},{128,64},{192,128},{1,193},{65,1},{129,65},{193,129... | collective-permute-start | bytes 172040 | tf_op jit(solution)/shard_map/ppermute | solution.py:649
  71.6 4.6 %collective-permute-start.10 = (s16[112,256]{1,0:T(8,128)(2,1)S(1)}, s16[112,256]{1,0:T(8,128)(2,1)S(1)}, u32[]{:S(2)}, u32[]{:S(2)}) collective-permute-start(s16[112,256]{1,0:T(8,128)(2,1)S(1)} %get-tuple-element.51.own_h), channel_id=1, source_target_pairs={{0,128},{64,192},{128,0},{192,64},{1,129},{65,193},{129,1},{193,65... | collective-permute-start | bytes 172040 | tf_op jit(solution)/shard_map/ppermute | solution.py:649
  72.2 4.6 %collective-permute-start.9 = (s16[112,256]{1,0:T(8,128)(2,1)S(1)}, s16[112,256]{1,0:T(8,128)(2,1)S(1)}, u32[]{:S(2)}, u32[]{:S(2)}) collective-permute-start(s16[112,256]{1,0:T(8,128)(2,1)S(1)} %get-tuple-element.51.own_h), channel_id=1, source_target_pairs={{0,64},{64,128},{128,192},{192,0},{1,65},{65,129},{129,193},{193,1... | collective-permute-start | bytes 172040 | tf_op jit(solution)/shard_map/ppermute | solution.py:649
